TPU v7x, 512 devices: a whole 4x8x8 slice. The times are simulated.
512 devices in a mesh: section: 2 (over core), tp: 64 (over y_hi, x, z), rep: 4 (over y_lo).
Axes of the slice: x: 4, y: 8 (y_hi: 2, y_lo: 4; y = y_hi * 4 + y_lo), z: 8, core: 2. Of those that a mesh axis runs over, the one named last changes fastest.
Arguments:
- hidden: bfloat16 [8, 1024, 7168], P(('section', 'rep'), None, 'tp'), may hold values from -6 to 6
- comp_query: bfloat16 [8, 1024, 1536], P(('section', 'rep'), 'tp'), may hold values from -6 to 6
- kv_down: bfloat16 [7168, 576], P('tp'), may hold values from -2.5 to 2.5
- kv_gain: float32 [512], replicated, may hold values from 0.25 to 1.75
- q_up: bfloat16 [1536, 24576], P(None, 'tp'), may hold values from -2.5 to 2.5
- kv_up: bfloat16 [512, 32768], P(None, 'tp'), may hold values from -0.25 to 0.25
- req_blocks: int32 [8, 3], P('section'), may hold values from 1 to 4, 8 in all within a row
- dest_slot: int32 [2, 12], P('section'), may hold values from 0 to 11, each once within a row
- dec_query: bfloat16 [24, 4, 1536], P(('section', 'rep')), may hold values from -6 to 6
- dec_latent: bfloat16 [24, 4, 576], P(('section', 'rep')), may hold values from -6 to 6
Outputs:
- prefill_out: bfloat16 [8, 1024, 16384], P(('section', 'rep'), None, 'tp')
- decode_out: bfloat16 [24, 4, 16384], P(('section', 'rep'), None, 'tp')
Inputs may be any that keep to these rules, and one draw needn't show every extreme that they name: `req_blocks`: each row sums to 8. `dest_slot`: each row is a permutation of the decode slots of its section.
All inputs are finite; a program needn't handle non-finite values.
Results may differ from a plain program's by a relative error of at most 0.011.
Values may be sent and summed in bfloat16 or wider, within the bound.
No kernel may reach another device: no remote copies, remote signals or barrier semaphores. Data moves between devices by JAX's collectives and lax.ppermute only.
A program may use at most 64 MiB of HBM per device.

v0:
```python
import math

import jax
import jax.numpy as jnp
from jax import lax
from jax.sharding import PartitionSpec as P

KVL = 512
NOPE = 128
ROPE = 64
VD = 128
BLK = 128
NREQ = 3


softmax_gain = (1.0 + 0.1 * math.log(40.0)) ** 2


def rotate(pair_values, positions):
    half_width = pair_values.shape[-1] // 2
    frequency = 10000.0 ** (
        -jnp.arange(half_width, dtype=jnp.float32) * 2.0 / pair_values.shape[-1]
    )
    angles = positions[..., None] * frequency
    cos_part = jnp.cos(angles)
    sine_part = jnp.sin(angles)
    first_half = pair_values[..., :half_width]
    second = pair_values[..., half_width:]
    return jnp.concatenate(
        [first_half * cos_part - second * sine_part, first_half * sine_part + second * cos_part],
        axis=-1,
    )


def request_spans(blocks, block_rows):
    lengths = blocks * block_rows
    starts = jnp.cumsum(lengths, axis=-1) - lengths
    return (starts, lengths)


def row_places(row_index, starts, lengths):
    inside = (row_index[:, None] >= starts[None, :]) & (
        row_index[:, None] < (starts + lengths)[None, :]
    )
    member = inside.astype(jnp.int32)
    segment = jnp.sum(member * jnp.arange(starts.shape[0], dtype=jnp.int32)[None, :], axis=1)
    offset = row_index - jnp.sum(member * starts[None, :], axis=1)
    return (segment, offset)


def norm_latent(latent, kv_gain, offset):
    content = latent[:, :KVL]
    inv_scale = lax.rsqrt(jnp.mean(content * content, axis=1, keepdims=True) + 1e-06)
    rotated_pe = rotate(latent[:, KVL:], offset.astype(jnp.float32))
    return jnp.concatenate([content * inv_scale * kv_gain[None, :], rotated_pe], axis=1).astype(
        jnp.bfloat16
    )


def make_queries(input_rows, q_up, offset):
    projected = jnp.dot(input_rows, q_up, preferred_element_type=jnp.float32)
    projected = projected.reshape(input_rows.shape[0], -1, NOPE + ROPE)
    rotated_pe = rotate(projected[..., NOPE:], offset.astype(jnp.float32)[:, None])
    return jnp.concatenate([projected[..., :NOPE], rotated_pe], axis=-1).astype(jnp.bfloat16)


def attend_group(queries, latent_cache, kv_up, segment):
    group_rows = latent_cache.shape[0]
    expanded = jnp.dot(latent_cache[:, :KVL], kv_up, preferred_element_type=jnp.float32).astype(
        jnp.bfloat16
    )
    expanded = expanded.reshape(group_rows, -1, NOPE + VD)
    row_index = jnp.arange(group_rows, dtype=jnp.int32)
    allowed = (segment[:, None] == segment[None, :]) & (row_index[None, :] <= row_index[:, None])

    def one_head(inputs):
        head_query, key_nope, head_value = inputs
        all_keys = jnp.concatenate([key_nope, latent_cache[:, KVL:]], axis=1)
        scores = lax.dot_general(
            head_query, all_keys, (((1,), (1,)), ((), ())), preferred_element_type=jnp.float32
        ) * (softmax_gain * (NOPE + ROPE) ** (-0.5))
        scores = jnp.where(allowed, scores, -1e30)
        weights = jax.nn.softmax(scores, axis=1).astype(jnp.bfloat16)
        return jnp.dot(weights, head_value, preferred_element_type=jnp.float32).astype(jnp.bfloat16)

    outputs = lax.map(
        one_head,
        (
            jnp.swapaxes(queries, 0, 1),
            jnp.swapaxes(expanded[..., :NOPE], 0, 1),
            jnp.swapaxes(expanded[..., NOPE:], 0, 1),
        ),
    )
    return jnp.swapaxes(outputs, 0, 1).reshape(group_rows, -1)


def decode_request(step_rows, step_latent, latent_cache, row_start, length, q_up, kv_up):
    step_count = step_rows.shape[0]
    group_rows = latent_cache.shape[0]
    projected = jnp.dot(step_rows, q_up, preferred_element_type=jnp.float32).astype(jnp.bfloat16)
    projected = projected.reshape(step_count, -1, NOPE + ROPE)
    new_positions = (length + jnp.arange(step_count, dtype=jnp.int32)).astype(jnp.float32)
    query_pe = rotate(projected[..., NOPE:].astype(jnp.float32), new_positions[:, None]).astype(
        jnp.bfloat16
    )
    absorbed = kv_up.reshape(KVL, -1, NOPE + VD)
    latent_query = jnp.einsum(
        "thn,khn->thk",
        projected[..., :NOPE],
        absorbed[..., :NOPE],
        preferred_element_type=jnp.float32,
    ).astype(jnp.bfloat16)
    new_keys = jnp.concatenate(
        [
            step_latent[:, :KVL],
            rotate(step_latent[:, KVL:].astype(jnp.float32), new_positions).astype(jnp.bfloat16),
        ],
        axis=1,
    )
    all_keys = jnp.concatenate([latent_cache, new_keys], axis=0)
    full_query = jnp.concatenate([latent_query, query_pe], axis=-1)
    scores = jnp.einsum("thl,kl->thk", full_query, all_keys, preferred_element_type=jnp.float32) * (
        softmax_gain * (NOPE + ROPE) ** (-0.5)
    )
    row_index = jnp.arange(group_rows, dtype=jnp.int32)
    old_allowed = (row_index >= row_start) & (row_index < row_start + length)
    step_index = jnp.arange(step_count, dtype=jnp.int32)
    new_allowed = step_index[None, :] <= step_index[:, None]
    allowed = jnp.concatenate(
        [jnp.broadcast_to(old_allowed[None, :], (step_count, group_rows)), new_allowed], axis=1
    )
    scores = jnp.where(allowed[:, None, :], scores, -1e30)
    weights = jax.nn.softmax(scores, axis=-1).astype(jnp.bfloat16)
    mixture = jnp.einsum(
        "thk,kc->thc", weights, all_keys[:, :KVL], preferred_element_type=jnp.float32
    ).astype(jnp.bfloat16)
    result = jnp.einsum(
        "thc,chv->thv", mixture, absorbed[..., NOPE:], preferred_element_type=jnp.float32
    ).astype(jnp.bfloat16)
    return result.reshape(step_count, -1)


def body(
    hidden, comp_query, kv_down, kv_gain, q_up, kv_up, req_blocks, dest_slot, dec_query, dec_latent
):
    rep_count = lax.axis_size("rep")
    rep_index = lax.axis_index("rep")
    block_x = hidden[0]
    group_rows = block_x.shape[0]
    own_blocks = lax.dynamic_index_in_dim(req_blocks, rep_index, 0, keepdims=False)
    starts, lengths = request_spans(own_blocks, BLK)
    row_index = jnp.arange(group_rows, dtype=jnp.int32)
    segment, offset = row_places(row_index, starts, lengths)
    latent = lax.psum(jnp.dot(block_x, kv_down, preferred_element_type=jnp.float32), "tp")
    latent_cache = norm_latent(latent, kv_gain, offset)
    queries = make_queries(lax.all_gather(comp_query[0], "tp", axis=0, tiled=True), q_up, offset)
    prefill_out = attend_group(queries, latent_cache, kv_up, segment)[None]
    slot_table = dest_slot[0]
    slot_numbers = jnp.arange(rep_count * NREQ, dtype=jnp.int32)
    cache_pool = lax.all_gather(latent_cache, "rep", axis=0, tiled=True)
    all_starts, all_lengths = request_spans(req_blocks, BLK)
    flat_starts = all_starts.reshape(-1)
    flat_lengths = all_lengths.reshape(-1)
    results = []
    for slot_index in range(NREQ):
        matched = slot_table == rep_index * NREQ + slot_index
        source = jnp.sum(jnp.where(matched, slot_numbers, 0))
        row_start = jnp.sum(jnp.where(matched, flat_starts, 0))
        length = jnp.sum(jnp.where(matched, flat_lengths, 0))
        source_rows = lax.dynamic_slice_in_dim(
            cache_pool, source // NREQ * group_rows, group_rows, 0
        )
        results.append(
            decode_request(
                dec_query[slot_index],
                dec_latent[slot_index],
                source_rows,
                row_start,
                length,
                q_up,
                kv_up,
            )
        )
    decode_out = jnp.stack(results)
    return (prefill_out, decode_out)


def solution(mesh):
    in_specs = (
        P(("section", "rep"), None, "tp"),
        P(("section", "rep"), "tp", None),
        P("tp", None),
        P(),
        P(None, "tp"),
        P(None, "tp"),
        P("section", None),
        P("section", None),
        P(("section", "rep"), None, None),
        P(("section", "rep"), None, None),
    )
    out_specs = (P(("section", "rep"), None, "tp"), P(("section", "rep"), None, "tp"))
    return jax.shard_map(body, mesh=mesh, in_specs=in_specs, out_specs=out_specs, check_vma=False)
```

profile of v0, /device:TPU:56, one launch (start us, length us, event | category | flops | bytes accessed | tf_op | source)
XLA Modules:
  0.0 1112.9 jit_solution(13470066589915486403)
XLA Ops:
  7.2 3.0 fusion.92
  10.3 0.7 all-gather.6.cloned.1.call-update
  11.1 0.7 fusion.147
  19.5 0.8 select_reduce_fusion.7
  20.3 0.6 add_convert_fusion.10
  20.8 1.3 add_convert_fusion.8
  22.4 0.8 copy.136
  23.2 1.0 copy.122
  26.7 1.2 fusion.128
  29.3 0.7 select_reduce_fusion
  29.9 824.3 %all-reduce.2.cloned.1.call-done = f32[1024,576]{0,1:T(8,128)} async-done(((f32[1024,576]{0,1:T(8,128)}), f32[1024,576]{0,1:T(8,128)}) %all-reduce.2.cloned.1.call-update) | async-done | bytes 2359312 | tf_op jit(solution)/shard_map/psum | solution.py:154
  854.2 1.9 multiply_reduce_fusion
  856.2 2.2 subtract_convert_fusion.1
  858.7 1.1 pad_maximum_fusion.3
  859.8 0.7 fusion.130
  860.7 0.8 copy.131
  861.5 0.8 copy.125
  862.4 0.7 subtract_convert_fusion.2
  863.1 0.7 subtract_convert_fusion.3
  863.8 0.7 subtract_convert_fusion.4
  864.5 1.7 fusion.64
  866.2 1.1 fusion.63
  867.2 1.1 fusion.62
  868.4 0.6 pad_add_fusion.2
  869.0 1.5 copy.119
  870.5 1.8 convolution_convert_fusion
  872.9 120.8 %all-gather.6.cloned.1.call-done = bf16[1,1024,1536]{2,1,0:T(8,128)(2,1)} async-done(((bf16[1,16,1536]{2,1,0:T(8,128)(2,1)}), bf16[1,1024,1536]{2,1,0:T(8,128)(2,1)}) %all-gather.6.cloned.1.call-update) | async-done | bytes 3145744 | tf_op jit(solution)/shard_map/all_gather | solution.py:156
  993.8 3.3 fusion.21
  997.3 0.9 copy-done.5
  998.2 8.8 while.11
  998.2 1.0 slice.373
  999.2 1.8 fusion.217
  1001.0 0.6 fusion.218
  1001.6 1.0 fusion.219
  1002.6 1.0 slice.373
  1003.6 1.8 fusion.217
  1005.4 0.6 fusion.218
  1006.0 1.0 fusion.219
  1007.0 0.5 copy.120
  1007.6 1.1 broadcast_in_dim_reshape.3
  1008.7 84.7 %all-gather.4.cloned.1.call-done = bf16[4096,576]{0,1:T(8,128)(2,1)} async-done(((bf16[1024,576]{0,1:T(8,128)(2,1)}), bf16[4096,576]{0,1:T(8,128)(2,1)}) %all-gather.4.cloned.1.call-update) | async-done | bytes 4718608 | tf_op jit(solution)/shard_map/all_gather | solution.py:160
  1093.4 3.8 constant_dynamic-slice_fusion.1
  1097.2 1.8 fusion.190
  1099.1 1.8 fusion.89
  1101.0 1.8 fusion.195
  1102.8 1.8 fusion.86
  1105.1 0.6 fusion.83
  1105.7 0.6 pad_maximum_fusion.4
  (120 shorter events, 4.2 us)
Async XLA Ops:
  7.2 10.4 copy-start
  7.2 847.0 %all-reduce.2.cloned.1.call-start = ((), (), s32[]{:S(2)}) async-start(), calls=%async_computation | async-start | bytes 4718592 | tf_op jit(solution)/shard_map/psum | solution.py:154
  10.2 0.8 copy-start.21
  10.2 7.3 copy-start.11
  10.3 983.5 %all-gather.6.cloned.1.call-start = ((), (), s32[]{:S(2)}) async-start(), calls=%async_computation.2 | async-start | bytes 3194880 | tf_op jit(solution)/shard_map/all_gather | solution.py:156
  11.0 1082.4 %all-gather.4.cloned.1.call-start = ((), (), s32[]{:S(2)}) async-start(), calls=%async_computation.1 | async-start | bytes 5898240 | tf_op jit(solution)/shard_map/all_gather | solution.py:160
  17.6 1.1 copy-start.16
  17.6 1.8 copy-start.15
  17.9 5.4 copy-start.4
  18.0 6.3 copy-start.12
  18.3 837.8 %copy-start.13 = (bf16[4,2,192]{2,1,0:T(2,128)(2,1)}, bf16[4,2,192]{2,1,0:T(2,128)(2,1)S(1)}, u32[]{:S(2)}) copy-start(bf16[4,2,192]{2,1,0:T(2,128)(2,1)S(1)} %reshape.392) | copy-start | bytes 9220
  18.7 837.5 %copy-start.14 = (bf16[4,2,192]{2,1,0:T(2,128)(2,1)}, bf16[4,2,192]{2,1,0:T(2,128)(2,1)S(1)}, u32[]{:S(2)}) copy-start(bf16[4,2,192]{2,1,0:T(2,128)(2,1)S(1)} %reshape.390) | copy-start | bytes 9220
  24.3 834.2 %copy-start.28 = (f32[512]{0:T(512)S(1)}, f32[512]{0:T(512)}, u32[]{:S(2)}) copy-start(f32[512]{0:T(512)} %param.15) | copy-start | bytes 6148
  854.2 4.2 copy-start.2
  858.7 3.7 slice-start
  858.7 3.7 slice-start.2
  858.7 3.7 slice-start.4
  858.7 5.8 slice-start.1
  858.7 7.5 slice-start.3
  859.8 7.4 slice-start.5
  859.8 9.2 copy-start.1
  872.9 124.3 %copy-start.6 = (f32[1024,32]{0,1:T(8,128)S(1)}, f32[1024,32]{0,1:T(8,128)}, u32[]{:S(2)}) copy-start(f32[1024,32]{0,1:T(8,128)} %get-tuple-element.140) | copy-start | bytes 393220
  872.9 124.3 %copy-start.7 = (f32[1024,32]{0,1:T(8,128)S(1)}, f32[1024,32]{0,1:T(8,128)}, u32[]{:S(2)}) copy-start(f32[1024,32]{0,1:T(8,128)} %get-tuple-element.141) | copy-start | bytes 393220
  997.2 1.0 copy-start.5
  1008.7 88.5 %copy-start.8 = (bf16[4,576]{0,1:T(8,128)(2,1)S(1)}, bf16[4,576]{0,1:T(8,128)(2,1)}, u32[]{:S(2)}) copy-start(bf16[4,576]{0,1:T(8,128)(2,1)} %copy.136) | copy-start | bytes 13828
  1008.7 88.5 %copy-start.17 = (bf16[4,2,512]{2,0,1:T(4,128)(2,1)S(1)}, bf16[4,2,512]{2,0,1:T(4,128)(2,1)}, u32[]{:S(2)}) copy-start(bf16[4,2,512]{2,0,1:T(4,128)(2,1)} %fusion.64) | copy-start | bytes 24580
  1008.7 88.5 %copy-start.20 = (pred[4,1028]{1,0:T(4,128)(4,1)S(1)}, pred[4,1028]{1,0:T(4,128)(4,1)}, u32[]{:S(2)}) copy-start(pred[4,1028]{1,0:T(4,128)(4,1)} %get-tuple-element.170) | copy-start | bytes 12340
  1008.7 88.5 %copy-start.26 = (bf16[4,2,32]{2,0,1:T(4,128)(2,1)S(1)}, bf16[4,2,32]{2,0,1:T(4,128)(2,1)}, u32[]{:S(2)}) copy-start(bf16[4,2,32]{2,0,1:T(4,128)(2,1)} %get-tuple-element.138) | copy-start | bytes 1540
  1008.7 88.5 %copy-start.27 = (bf16[4,2,32]{2,0,1:T(4,128)(2,1)S(1)}, bf16[4,2,32]{2,0,1:T(4,128)(2,1)}, u32[]{:S(2)}) copy-start(bf16[4,2,32]{2,0,1:T(4,128)(2,1)} %get-tuple-element.139) | copy-start | bytes 1540
  1097.2 1.9 copy-start.3
  1099.1 1.8 copy-start.10
  1099.1 1.8 copy-start.19
  1099.1 1.9 copy-start.24
  1099.1 1.9 copy-start.25
  1102.7 1.8 copy-start.9
  1102.8 1.8 copy-start.18
  1102.8 1.9 copy-start.22
  1102.8 1.9 copy-start.23
Sparse Core Ops, SparseCore 0:
  10.9 843.2 all-reduce.1
  859.6 134.1 all-gather.5
  996.1 97.2 all-gather.3
where the time goes:
time: 1110 us
  waiting for transfers between devices  1030 us (93%)
  matrix products  26.7 us (2%)
  between operations  23.8 us (2%)
  other arithmetic  16.9 us (2%)
  local copies, waits for them, and re-layouts  14.8 us (1%)
    psum x1, waiting for transfers between devices, body(): lax.psum(jnp.dot(block_x, kv_down, preferred_element_type=jnp.float32), '...  824 us
    all_gather x1, waiting for transfers between devices, body(): lax.all_gather(comp_query[0], 'tp', axis=0, tiled=True)  121 us
    all_gather x1, waiting for transfers between devices, body(): cache_pool = lax.all_gather(latent_cache, 'rep', axis=0, tiled=True)  84.7 us
  transfers between devices with their start and end apart: 3, of which 3 were waited for; matrix products, arithmetic and copies ran while one was open for 4% of the time, Pallas kernels for 0%

commit v1 on v0

v1 whole, which is shorter than its diff:
```python
import math

import jax
import jax.numpy as jnp
from jax import lax
from jax.sharding import Mesh, PartitionSpec as P

KVL = 512
NOPE = 128
ROPE = 64
VD = 128
BLK = 128
NREQ = 3
STEPS = 4
REACH = 4
NREP = 4
NX = 4

SIGMA = (1.0 + 0.1 * math.log(40.0)) ** 2 * (NOPE + ROPE) ** (-0.5)
bf16 = jnp.bfloat16
f32 = jnp.float32


def cos_sin(positions):
    half = ROPE // 2
    frequency = 10000.0 ** (-jnp.arange(half, dtype=f32) * 2.0 / ROPE)
    angles = positions.astype(f32)[..., None] * frequency
    return jnp.cos(angles), jnp.sin(angles)


def rotate(u, cos_part, sin_part):
    half = ROPE // 2
    a, b = u[..., :half], u[..., half:]
    return jnp.concatenate([a * cos_part - b * sin_part, a * sin_part + b * cos_part], axis=-1)


def spread(a, axes, count):
    copies = jnp.broadcast_to(a[None], (count,) + a.shape)
    return lax.all_to_all(copies, axes, 0, 0, tiled=True)


def body(hidden, comp_query, kv_down, kv_gain, q_up, kv_up, req_blocks, dest_slot, dec_query, dec_latent):
    rep = lax.axis_index("rep")
    yz_index = lax.axis_index(("yh", "z"))
    x_index = lax.axis_index("x")
    block_x = hidden[0]
    rows = block_x.shape[0]
    features = block_x.shape[1]

    lengths_all = req_blocks * BLK
    starts_all = jnp.cumsum(lengths_all, axis=-1) - lengths_all
    lengths = lax.dynamic_index_in_dim(lengths_all, rep, 0, keepdims=False)
    starts = lax.dynamic_index_in_dim(starts_all, rep, 0, keepdims=False)

    def start_of(row):
        inside = (row[:, None] >= starts[None]) & (row[:, None] < (starts + lengths)[None])
        return jnp.sum(jnp.where(inside, starts[None], 0), axis=1)

    row_index = jnp.arange(rows, dtype=jnp.int32)
    row_start = start_of(row_index)
    offset = row_index - row_start

    per_x = rows // NX
    hidden_t = jnp.swapaxes(block_x.reshape(NX, per_x, features), 1, 2)
    packed = jnp.concatenate(
        [hidden_t, jnp.broadcast_to(kv_down[None], (NX,) + kv_down.shape)], axis=2
    )
    packed = lax.all_to_all(packed, "x", 0, 0, tiled=True).reshape(NX * features, -1)
    partial = lax.dot_general(
        packed[:, :per_x], packed[:, per_x:], (((0,), (0,)), ((), ())), preferred_element_type=f32
    )
    chunk = per_x // 16
    pieces = lax.all_to_all(partial.reshape(16, chunk, -1), ("yh", "z"), 0, 0, tiled=True)
    latent = jnp.sum(pieces, axis=0)
    own_rows = x_index * per_x + yz_index * chunk + jnp.arange(chunk, dtype=jnp.int32)
    content = latent[:, :KVL]
    inv_scale = lax.rsqrt(jnp.mean(content * content, axis=1, keepdims=True) + 1e-06)
    cos_o, sin_o = cos_sin(own_rows - start_of(own_rows))
    own_cache = jnp.concatenate(
        [content * inv_scale * kv_gain[None, :], rotate(latent[:, KVL:], cos_o, sin_o)], axis=1
    ).astype(bf16)
    cache = spread(own_cache, ("yh", "z"), 16).reshape(per_x, -1)
    cache = spread(cache, "x", NX).reshape(rows, -1)

    cq = spread(comp_query[0], ("yh", "z"), 16)
    cq = spread(cq.reshape(2, 8 * 16, -1), "x", NX)
    cq = jnp.swapaxes(cq.reshape(NX, 2, 128, -1), 0, 1).reshape(rows, -1)
    heads = q_up.shape[1] // (NOPE + ROPE)
    cos_q, sin_q = cos_sin(offset)
    projected = jnp.dot(cq, q_up, preferred_element_type=f32).reshape(rows, heads, NOPE + ROPE)
    queries = jnp.concatenate(
        [projected[..., :NOPE], rotate(projected[..., NOPE:], cos_q[:, None], sin_q[:, None])], axis=-1
    ).astype(bf16)

    slots = lax.dynamic_slice_in_dim(dest_slot[0], rep * NREQ, NREQ, 0)
    rep_in = spread(jnp.concatenate([dec_query, dec_latent], axis=2), "rep", NREP)
    rep_in = rep_in.reshape(NREP * NREQ, STEPS, -1)
    mine = jnp.take(rep_in, slots, axis=0, mode="clip")
    my_query = mine[..., : dec_query.shape[2]].reshape(NREQ * STEPS, -1)
    my_latent = mine[..., dec_query.shape[2] :].reshape(NREQ * STEPS, -1)
    new_pos = (lengths[:, None] + jnp.arange(STEPS, dtype=jnp.int32)[None]).reshape(-1)
    cos_d, sin_d = cos_sin(new_pos)
    new_keys = jnp.concatenate(
        [my_latent[:, :KVL], rotate(my_latent[:, KVL:].astype(f32), cos_d, sin_d).astype(bf16)], axis=1
    )
    dq = jnp.dot(my_query, q_up, preferred_element_type=f32).astype(bf16)
    dq = dq.reshape(NREQ * STEPS, heads, NOPE + ROPE)
    query_pe = rotate(dq[..., NOPE:].astype(f32), cos_d[:, None], sin_d[:, None]).astype(bf16)
    absorbed = kv_up.reshape(KVL, heads, NOPE + VD)
    latent_query = jnp.einsum(
        "rhn,khn->hrk", dq[..., :NOPE], absorbed[..., :NOPE], preferred_element_type=f32
    ).astype(bf16)
    full_query = jnp.concatenate([latent_query, jnp.swapaxes(query_pe, 0, 1)], axis=-1)
    full_query = full_query.reshape(heads * NREQ * STEPS, -1)
    all_keys = jnp.concatenate([cache, new_keys], axis=0)
    scores = lax.dot_general(
        full_query, all_keys, (((1,), (1,)), ((), ())), preferred_element_type=f32
    ) * SIGMA
    step_row = jnp.arange(NREQ * STEPS, dtype=jnp.int32)
    low = jnp.repeat(starts, STEPS)[:, None]
    high = jnp.repeat(starts + lengths, STEPS)[:, None]
    old_ok = (row_index[None] >= low) & (row_index[None] < high)
    new_ok = (step_row[None] // STEPS == step_row[:, None] // STEPS) & (step_row[None] <= step_row[:, None])
    ok = jnp.tile(jnp.concatenate([old_ok, new_ok], axis=1), (heads, 1))
    scores = jnp.where(ok, scores, -1e30)
    weights = jax.nn.softmax(scores, axis=-1).astype(bf16)
    mixture = jnp.dot(weights, all_keys[:, :KVL], preferred_element_type=f32).astype(bf16)
    mixture = mixture.reshape(heads, NREQ * STEPS, KVL)
    result = jnp.einsum("hrc,chv->rhv", mixture, absorbed[..., NOPE:], preferred_element_type=f32)
    result = result.astype(bf16).reshape(NREQ, STEPS, heads * VD)
    pool = spread(result, "rep", NREP).reshape(NREP * NREQ, STEPS, heads * VD)
    slot_numbers = rep * NREQ + jnp.arange(NREQ, dtype=jnp.int32)
    source = jnp.sum(
        jnp.where(dest_slot[0][None] == slot_numbers[:, None], jnp.arange(NREP * NREQ, dtype=jnp.int32)[None], 0),
        axis=1,
    )
    decode_out = jnp.take(pool, source, axis=0, mode="clip")

    expanded = jnp.dot(cache[:, :KVL], kv_up, preferred_element_type=f32).astype(bf16)
    outs = []
    for h in range(heads):
        base = h * (NOPE + VD)
        keys = jnp.concatenate([expanded[:, base : base + NOPE], cache[:, KVL:]], axis=1)
        values = expanded[:, base + NOPE : base + NOPE + VD]
        blocks = []
        for i in range(rows // BLK):
            first = max(0, i - REACH + 1) * BLK
            last = (i + 1) * BLK
            s = lax.dot_general(
                queries[i * BLK : last, h], keys[first:last], (((1,), (1,)), ((), ())),
                preferred_element_type=f32,
            ) * SIGMA
            column = row_index[first:last][None]
            ok_block = (column >= row_start[i * BLK : last, None]) & (column <= row_index[i * BLK : last, None])
            w = jax.nn.softmax(jnp.where(ok_block, s, -1e30), axis=1).astype(bf16)
            blocks.append(jnp.dot(w, values[first:last], preferred_element_type=f32).astype(bf16))
        outs.append(jnp.concatenate(blocks, axis=0))
    prefill_out = jnp.concatenate(outs, axis=1)[None]
    return prefill_out, decode_out


def solution(mesh):
    fine = Mesh(mesh.devices.reshape(2, 2, 4, 8, 4), ("section", "yh", "x", "z", "rep"))
    tp = ("yh", "x", "z")
    group = ("section", "rep")
    in_specs = (
        P(group, None, tp),
        P(group, tp, None),
        P(tp, None),
        P(),
        P(None, tp),
        P(None, tp),
        P("section", None),
        P("section", None),
        P(group, None, None),
        P(group, None, None),
    )
    out_specs = (P(group, None, tp), P(group, None, tp))
    return jax.shard_map(body, mesh=fine, in_specs=in_specs, out_specs=out_specs, check_vma=False)
```

time: 1110 us -> 206 us (0.19)
  the two profiles are of different devices: /device:TPU:56 before, /device:TPU:64 now
where the time goes in v1:
time: 206 us; the launch traced here: 205 us
  waiting for transfers between devices  88.5 us (43%)
  starting transfers between devices  46.2 us (22%)
  local copies, waits for them, and re-layouts  27.2 us (13%)
  blocking collectives  18.9 us (9%)
  matrix products  14.9 us (7%)
  other arithmetic  7.89 us (4%)
    all_to_all x5, waiting for transfers between devices, spread(): return lax.all_to_all(copies, axes, 0, 0, tiled=True)  59.6 us
    all_to_all x5, starting transfers between devices, spread(): return lax.all_to_all(copies, axes, 0, 0, tiled=True)  26.6 us
    all_to_all x1, blocking collectives, spread(): return lax.all_to_all(copies, axes, 0, 0, tiled=True)  18.9 us
    all_to_all x1, waiting for transfers between devices, body(): lax.all_to_all(partial.reshape(16, chunk, -1), ('yh', 'z'), 0, 0, tiled=T...  17.1 us
    all_to_all x1, starting transfers between devices, body(): lax.all_to_all(partial.reshape(16, chunk, -1), ('yh', 'z'), 0, 0, tiled=T...  15.4 us
    all_to_all x1, waiting for transfers between devices, body(): lax.all_to_all(packed, 'x', 0, 0, tiled=True).reshape(NX * features, -1)  11.8 us
    unnamed x72, local copies, waits for them, and re-layouts  5.81 us
    broadcast_in_dim x8, local copies, waits for them, and re-layouts, spread(): copies = jnp.broadcast_to(a[None], (count,) + a.shape)  5.64 us
  transfers between devices with their start and end apart: 7, of which 7 were waited for; matrix products, arithmetic and copies ran while one was open for 11% of the time, Pallas kernels for 0%

profile of v1, /device:TPU:64, one launch (start us, length us, event | category | flops | bytes accessed | tf_op | source)
XLA Modules:
  0.0 205.1 jit_solution(13609000082283752758)
XLA Ops:
  0.6 1.1 reshape_squeeze.3
  1.8 1.0 broadcast_in_dim.103
  2.7 1.0 pad_maximum_fusion
  3.7 4.3 %all-to-all-start.2 = ((bf16[4,112,832]{2,1,0:T(8,128)(2,1)}), bf16[4,112,832]{2,1,0:T(8,128)(2,1)S(1)}, u32[]{:S(2)}, u32[]{:S(2)}) async-start(bf16[4,112,832]{2,1,0:T(8,128)(2,1)} %pad_maximum_fusion), calls=%async_computation.2 | async-start | bytes 1605632 | tf_op jit(solution)/shard_map/all_to_all | solution.py:68
  8.6 11.8 %all-to-all-done.2 = bf16[4,112,832]{2,1,0:T(8,128)(2,1)S(1)} async-done(((bf16[4,112,832]{2,1,0:T(8,128)(2,1)}), bf16[4,112,832]{2,1,0:T(8,128)(2,1)S(1)}, u32[]{:S(2)}, u32[]{:S(2)}) %all-to-all-start.2) | async-done | bytes 745504 | tf_op jit(solution)/shard_map/all_to_all | solution.py:68
  20.5 1.2 fusion.45
  21.7 15.4 %all-to-all-start.3 = ((f32[16,16,576]{2,1,0:T(8,128)}), f32[16,16,576]{2,1,0:T(8,128)S(1)}, u32[]{:S(2)}, u32[]{:S(2)}) async-start(f32[16,16,576]{2,1,0:T(8,128)} %bitcast.12), calls=%async_computation.3 | async-start | bytes 1310720 | tf_op jit(solution)/shard_map/all_to_all | solution.py:73
  37.3 17.1 %all-to-all-done.3 = f32[16,16,576]{2,1,0:T(8,128)S(1)} async-done(((f32[16,16,576]{2,1,0:T(8,128)}), f32[16,16,576]{2,1,0:T(8,128)S(1)}, u32[]{:S(2)}, u32[]{:S(2)}) %all-to-all-start.3) | async-done | bytes 589856 | tf_op jit(solution)/shard_map/all_to_all | solution.py:73
  54.4 0.7 broadcast_in_dim.117
  55.2 6.0 %all-to-all-start.6 = ((bf16[4,3,4,2112]{3,2,1,0:T(4,128)(2,1)}), bf16[4,3,4,2112]{3,2,1,0:T(4,128)(2,1)S(1)}, u32[]{:S(2)}, u32[]{:S(2)}) async-start(bf16[4,3,4,2112]{3,2,1,0:T(4,128)(2,1)} %broadcast_in_dim.117), calls=%async_computation.6 | async-start | bytes 417792 | tf_op jit(solution)/shard_map/all_to_all | solution.py:39
  61.6 6.3 %all-to-all-done.6 = bf16[4,3,4,2112]{3,2,1,0:T(4,128)(2,1)S(1)} async-done(((bf16[4,3,4,2112]{3,2,1,0:T(4,128)(2,1)}), bf16[4,3,4,2112]{3,2,1,0:T(4,128)(2,1)S(1)}, u32[]{:S(2)}, u32[]{:S(2)}) %all-to-all-start.6) | async-done | bytes 202784 | tf_op jit(solution)/shard_map/all_to_all | solution.py:39
  67.9 0.8 broadcast_in_dim.105
  68.6 7.4 %all-to-all-start.4 = ((bf16[16,16,576]{2,1,0:T(8,128)(2,1)}), bf16[16,16,576]{2,1,0:T(8,128)(2,1)S(1)}, u32[]{:S(2)}, u32[]{:S(2)}) async-start(bf16[16,16,576]{2,1,0:T(8,128)(2,1)} %broadcast_in_dim.105), calls=%async_computation.4 | async-start | bytes 655360 | tf_op jit(solution)/shard_map/all_to_all | solution.py:39
  76.6 0.6 gather_fusion
  77.2 11.1 %all-to-all-done.4 = bf16[16,16,576]{2,1,0:T(8,128)(2,1)S(1)} async-done(((bf16[16,16,576]{2,1,0:T(8,128)(2,1)}), bf16[16,16,576]{2,1,0:T(8,128)(2,1)S(1)}, u32[]{:S(2)}, u32[]{:S(2)}) %all-to-all-start.4) | async-done | bytes 294944 | tf_op jit(solution)/shard_map/all_to_all | solution.py:39
  88.5 1.1 broadcast_in_dim.107
  89.6 3.7 %all-to-all-start.5 = ((bf16[4,256,576]{1,2,0:T(8,128)(2,1)}), bf16[4,256,576]{1,2,0:T(8,128)(2,1)S(1)}, u32[]{:S(2)}, u32[]{:S(2)}) async-start(bf16[4,256,576]{1,2,0:T(8,128)(2,1)} %broadcast_in_dim.107), calls=%async_computation.5 | async-start | bytes 2359296 | tf_op jit(solution)/shard_map/all_to_all | solution.py:39
  93.8 12.0 %all-to-all-done.5 = bf16[4,256,576]{1,2,0:T(8,128)(2,1)S(1)} async-done(((bf16[4,256,576]{1,2,0:T(8,128)(2,1)}), bf16[4,256,576]{1,2,0:T(8,128)(2,1)S(1)}, u32[]{:S(2)}, u32[]{:S(2)}) %all-to-all-start.5) | async-done | bytes 1179680 | tf_op jit(solution)/shard_map/all_to_all | solution.py:39
  105.8 1.0 broadcast_in_dim.99
  106.7 5.7 %all-to-all-start = ((bf16[16,16,1536]{2,1,0:T(8,128)(2,1)}), bf16[16,16,1536]{2,1,0:T(8,128)(2,1)S(1)}, u32[]{:S(2)}, u32[]{:S(2)}) async-start(bf16[16,16,1536]{2,1,0:T(8,128)(2,1)} %broadcast_in_dim.99), calls=%async_computation | async-start | bytes 1572864 | tf_op jit(solution)/shard_map/all_to_all | solution.py:39
  114.9 14.7 %all-to-all-done = bf16[16,16,1536]{2,1,0:T(8,128)(2,1)S(1)} async-done(((bf16[16,16,1536]{2,1,0:T(8,128)(2,1)}), bf16[16,16,1536]{2,1,0:T(8,128)(2,1)S(1)}, u32[]{:S(2)}, u32[]{:S(2)}) %all-to-all-start) | async-done | bytes 786464 | tf_op jit(solution)/shard_map/all_to_all | solution.py:39
  129.6 18.9 %all_to_all.40 = bf16[4,3,4,256]{3,2,1,0:T(4,128)(2,1)} all-to-all(bf16[4,3,4,256]{3,2,1,0:T(4,128)(2,1)S(1)} %broadcast_in_dim.121), channel_id=1, replica_groups=mesh['section'=2,'yh'=2,'x'=4,'z'=8,'rep'=4] {'rep'}, dimensions={0} | all-to-all | bytes 49152 | tf_op jit(solution)/shard_map/all_to_all | solution.py:39
  148.5 1.9 broadcast_in_dim.102
  150.4 3.9 %all-to-all-start.1 = ((bf16[4,2,128,1536]{3,2,1,0:T(8,128)(2,1)}), bf16[4,2,128,1536]{3,2,1,0:T(8,128)(2,1)S(1)}, u32[]{:S(2)}, u32[]{:S(2)}) async-start(bf16[4,2,128,1536]{3,2,1,0:T(8,128)(2,1)} %broadcast_in_dim.102), calls=%async_computation.1 | async-start | bytes 6291456 | tf_op jit(solution)/shard_map/all_to_all | solution.py:39
  154.3 2.4 %copy.46 = bf16[1536,384]{0,1:T(8,128)(2,1)} copy(bf16[1536,384]{1,0:T(8,128)(2,1)} %param.14) | data formatting | bytes 2359296 | tf_op args[4]
  156.8 0.6 slice.407
  157.4 0.5 slice.409
  157.9 0.6 slice.401
  158.5 0.5 slice.403
  159.0 0.6 slice.395
  159.6 0.6 slice.397
  160.2 0.6 slice.389
  160.8 0.5 slice.391
  161.3 0.6 slice.383
  162.4 0.6 slice.377
  163.6 0.6 slice.373
  164.5 0.6 fusion.185
  165.1 1.3 multiply_cosine_fusion
  166.4 0.9 slice.466
  167.3 2.1 %convolution_convert_fusion = bf16[1024,512]{0,1:T(8,128)(2,1)S(1)} fusion(bf16[512,512]{1,0:T(8,128)(2,1)} %param.15, bf16[1024,576]{0,1:T(8,128)(2,1)} %bitcast.134), kind=kOutput, calls=%fused_computation.4 | convolution fusion | flops 537395200 | bytes 2621440 | tf_op jit(solution)/shard_map/dot_general | solution.py:139
  169.4 1.0 copy-done.7
  170.4 0.7 fusion.184
  171.1 1.9 gather_fusion.1
  173.0 15.6 %all-to-all-done.1 = bf16[4,2,128,1536]{3,2,1,0:T(8,128)(2,1)S(1)} async-done(((bf16[4,2,128,1536]{3,2,1,0:T(8,128)(2,1)}), bf16[4,2,128,1536]{3,2,1,0:T(8,128)(2,1)S(1)}, u32[]{:S(2)}, u32[]{:S(2)}) %all-to-all-start.1) | async-done | bytes 3145760 | tf_op jit(solution)/shard_map/all_to_all | solution.py:39
  188.9 0.9 copy-done.3
  189.8 1.4 fusion.203
  191.6 0.7 copy-done.1
  204.3 0.9 maximum_bitcast_fusion
  (204 shorter events, 18.5 us)
Async XLA Ops:
  2.7 5.3 %copy-start.12 = (s32[4,3]{1,0:T(4,128)S(1)}, s32[4,3]{1,0:T(4,128)}, u32[]{:S(2)}) copy-start(s32[4,3]{1,0:T(4,128)} %param.16) | copy-start | bytes 148
  3.7 16.8 %all-to-all-start.2 = ((bf16[4,112,832]{2,1,0:T(8,128)(2,1)}), bf16[4,112,832]{2,1,0:T(8,128)(2,1)S(1)}, u32[]{:S(2)}, u32[]{:S(2)}) async-start(bf16[4,112,832]{2,1,0:T(8,128)(2,1)} %pad_maximum_fusion), calls=%async_computation.2 | async-start | bytes 1605632 | tf_op jit(solution)/shard_map/all_to_all | solution.py:68
  20.5 16.8 %copy-start.10 = (bf16[3,4,1536]{2,1,0:T(4,128)(2,1)S(1)}, bf16[3,4,1536]{2,1,0:T(4,128)(2,1)}, u32[]{:S(2)}) copy-start(bf16[3,4,1536]{2,1,0:T(4,128)(2,1)} %param.18) | copy-start | bytes 110596
  20.5 16.8 %copy-start.11 = (bf16[3,4,576]{2,1,0:T(4,128)(2,1)S(1)}, bf16[3,4,576]{2,1,0:T(4,128)(2,1)}, u32[]{:S(2)}) copy-start(bf16[3,4,576]{2,1,0:T(4,128)(2,1)} %param.19) | copy-start | bytes 41476
  21.7 39.6 %copy-start.14 = (f32[512]{0:T(512)S(1)}, f32[512]{0:T(512)}, u32[]{:S(2)}) copy-start(f32[512]{0:T(512)} %param.13) | copy-start | bytes 6148
  21.7 32.7 %all-to-all-start.3 = ((f32[16,16,576]{2,1,0:T(8,128)}), f32[16,16,576]{2,1,0:T(8,128)S(1)}, u32[]{:S(2)}, u32[]{:S(2)}) async-start(f32[16,16,576]{2,1,0:T(8,128)} %bitcast.12), calls=%async_computation.3 | async-start | bytes 1310720 | tf_op jit(solution)/shard_map/all_to_all | solution.py:73
  37.3 38.9 %copy-start.4 = (bf16[512,512]{1,0:T(8,128)(2,1)S(1)}, bf16[512,512]{1,0:T(8,128)(2,1)}, u32[]{:S(2)}) copy-start(bf16[512,512]{1,0:T(8,128)(2,1)} %param.15) | copy-start | bytes 1572868
  55.2 12.7 %all-to-all-start.6 = ((bf16[4,3,4,2112]{3,2,1,0:T(4,128)(2,1)}), bf16[4,3,4,2112]{3,2,1,0:T(4,128)(2,1)S(1)}, u32[]{:S(2)}, u32[]{:S(2)}) async-start(bf16[4,3,4,2112]{3,2,1,0:T(4,128)(2,1)} %broadcast_in_dim.117), calls=%async_computation.6 | async-start | bytes 417792 | tf_op jit(solution)/shard_map/all_to_all | solution.py:39
  61.2 15.3 %copy-start.28 = (s32[1,12]{1,0:T(1,128)S(1)}, s32[1,12]{1,0:T(1,128)}, u32[]{:S(2)}) copy-start(s32[1,12]{1,0:T(1,128)} %param.17) | copy-start | bytes 148
  68.6 19.7 %all-to-all-start.4 = ((bf16[16,16,576]{2,1,0:T(8,128)(2,1)}), bf16[16,16,576]{2,1,0:T(8,128)(2,1)S(1)}, u32[]{:S(2)}, u32[]{:S(2)}) async-start(bf16[16,16,576]{2,1,0:T(8,128)(2,1)} %broadcast_in_dim.105), calls=%async_computation.4 | async-start | bytes 655360 | tf_op jit(solution)/shard_map/all_to_all | solution.py:39
  89.6 3.7 %copy-start = (bf16[1536,384]{1,0:T(8,128)(2,1)S(1)}, bf16[1536,384]{1,0:T(8,128)(2,1)}, u32[]{:S(2)}) copy-start(bf16[1536,384]{1,0:T(8,128)(2,1)} %param.14) | copy-start | bytes 3538948
  89.6 16.2 %copy-start.9 = (bf16[1,16,1536]{2,1,0:T(8,128)(2,1)S(1)}, bf16[1,16,1536]{2,1,0:T(8,128)(2,1)}, u32[]{:S(2)}) copy-start(bf16[1,16,1536]{2,1,0:T(8,128)(2,1)} %param.11) | copy-start | bytes 147460
  89.6 16.2 %all-to-all-start.5 = ((bf16[4,256,576]{1,2,0:T(8,128)(2,1)}), bf16[4,256,576]{1,2,0:T(8,128)(2,1)S(1)}, u32[]{:S(2)}, u32[]{:S(2)}) async-start(bf16[4,256,576]{1,2,0:T(8,128)(2,1)} %broadcast_in_dim.107), calls=%async_computation.5 | async-start | bytes 2359296 | tf_op jit(solution)/shard_map/all_to_all | solution.py:39
  106.7 22.8 %all-to-all-start = ((bf16[16,16,1536]{2,1,0:T(8,128)(2,1)}), bf16[16,16,1536]{2,1,0:T(8,128)(2,1)S(1)}, u32[]{:S(2)}, u32[]{:S(2)}) async-start(bf16[16,16,1536]{2,1,0:T(8,128)(2,1)} %broadcast_in_dim.99), calls=%async_computation | async-start | bytes 1572864 | tf_op jit(solution)/shard_map/all_to_all | solution.py:39
  113.2 1.0 copy-start.2
  150.4 38.1 %all-to-all-start.1 = ((bf16[4,2,128,1536]{3,2,1,0:T(8,128)(2,1)}), bf16[4,2,128,1536]{3,2,1,0:T(8,128)(2,1)S(1)}, u32[]{:S(2)}, u32[]{:S(2)}) async-start(bf16[4,2,128,1536]{3,2,1,0:T(8,128)(2,1)} %broadcast_in_dim.102), calls=%async_computation.1 | async-start | bytes 6291456 | tf_op jit(solution)/shard_map/all_to_all | solution.py:39
  169.4 1.0 copy-start.7
  188.6 1.3 copy-start.3
  189.8 1.5 copy-start.5
  189.8 1.5 copy-start.6
  191.3 1.0 copy-start.1
  191.3 0.9 copy-start.20
  191.3 0.9 copy-start.27
  191.4 0.9 copy-start.34
  191.5 1.5 copy-start.19
  191.5 1.5 copy-start.26
  191.5 1.5 copy-start.33
  192.6 1.0 copy-start.18
  192.6 1.0 copy-start.25
  192.6 1.0 copy-start.32
  193.3 1.0 copy-start.17
  193.3 1.0 copy-start.24
  193.3 1.0 copy-start.31
  194.0 1.0 copy-start.16
  194.0 1.0 copy-start.23
  194.0 1.0 copy-start.30
  194.7 1.0 copy-start.15
  194.7 1.0 copy-start.22
  194.7 1.0 copy-start.29
  195.4 1.0 copy-start.13
  195.4 1.0 copy-start.21
  196.0 1.4 copy-start.8

commit v2 on v1

--- a/solution.py
+++ b/solution.py
@@ -37,6 +37,10 @@
 def spread(a, axes, count):
     copies = jnp.broadcast_to(a[None], (count,) + a.shape)
     return lax.all_to_all(copies, axes, 0, 0, tiled=True)
+
+
+def shift(count, d):
+    return [(i, (i + d) % count) for i in range(count)]
 
 
 def body(hidden, comp_query, kv_down, kv_gain, q_up, kv_up, req_blocks, dest_slot, dec_query, dec_latent):
@@ -82,18 +86,32 @@
     cache = spread(own_cache, ("yh", "z"), 16).reshape(per_x, -1)
     cache = spread(cache, "x", NX).reshape(rows, -1)
 
-    cq = spread(comp_query[0], ("yh", "z"), 16)
-    cq = spread(cq.reshape(2, 8 * 16, -1), "x", NX)
-    cq = jnp.swapaxes(cq.reshape(NX, 2, 128, -1), 0, 1).reshape(rows, -1)
+    yh_index = lax.axis_index("yh")
+    own = comp_query[0]
+    other = lax.ppermute(own, "yh", shift(2, 1))
+    pair = jnp.where(yh_index == 0, jnp.stack([own, other]), jnp.stack([other, own]))
+    line = jnp.zeros((2, NX) + own.shape, own.dtype)
+    line = lax.dynamic_update_slice_in_dim(line, pair[:, None], x_index, 1)
+    for d in range(1, NX):
+        arrived = lax.ppermute(pair, "x", shift(NX, d))
+        line = lax.dynamic_update_slice_in_dim(line, arrived[:, None], (x_index - d) % NX, 1)
+    cq = lax.all_gather(line.reshape(128, -1), "z", axis=0, tiled=True)
     heads = q_up.shape[1] // (NOPE + ROPE)
-    cos_q, sin_q = cos_sin(offset)
+    q_offset = jnp.swapaxes(offset.reshape(8, 8, 16), 0, 1).reshape(-1)
+    cos_q, sin_q = cos_sin(q_offset)
     projected = jnp.dot(cq, q_up, preferred_element_type=f32).reshape(rows, heads, NOPE + ROPE)
     queries = jnp.concatenate(
         [projected[..., :NOPE], rotate(projected[..., NOPE:], cos_q[:, None], sin_q[:, None])], axis=-1
     ).astype(bf16)
+    queries = jnp.swapaxes(queries.reshape(8, 8, 16, heads, -1), 0, 1).reshape(rows, heads, -1)
 
     slots = lax.dynamic_slice_in_dim(dest_slot[0], rep * NREQ, NREQ, 0)
-    rep_in = spread(jnp.concatenate([dec_query, dec_latent], axis=2), "rep", NREP)
+    rep_own = jnp.concatenate([dec_query, dec_latent], axis=2)
+    rep_in = jnp.zeros((NREP,) + rep_own.shape, rep_own.dtype)
+    rep_in = lax.dynamic_update_slice_in_dim(rep_in, rep_own[None], rep, 0)
+    for d in range(1, NREP):
+        arrived = lax.ppermute(rep_own, "rep", shift(NREP, d))
+        rep_in = lax.dynamic_update_slice_in_dim(rep_in, arrived[None], (rep - d) % NREP, 0)
     rep_in = rep_in.reshape(NREP * NREQ, STEPS, -1)
     mine = jnp.take(rep_in, slots, axis=0, mode="clip")
     my_query = mine[..., : dec_query.shape[2]].reshape(NREQ * STEPS, -1)

time: 206 us -> 182 us (0.88)
  the two profiles are of different devices: /device:TPU:64 before, /device:TPU:56 now
where the time goes in v2:
time: 182 us; the launch traced here: 180 us
  starting transfers between devices  64.6 us (35%)
  waiting for transfers between devices  47 us (26%)
  local copies, waits for them, and re-layouts  25.6 us (14%)
  matrix products  17.4 us (10%)
  between operations  15.1 us (8%)
  other arithmetic  10.3 us (6%)
    all_to_all x3, waiting for transfers between devices, spread(): return lax.all_to_all(copies, axes, 0, 0, tiled=True)  26.3 us
    all_to_all x3, starting transfers between devices, spread(): return lax.all_to_all(copies, axes, 0, 0, tiled=True)  19.6 us
    all_to_all x1, waiting for transfers between devices, body(): lax.all_to_all(partial.reshape(16, chunk, -1), ('yh', 'z'), 0, 0, tiled=T...  16.5 us
    all_to_all x1, starting transfers between devices, body(): lax.all_to_all(partial.reshape(16, chunk, -1), ('yh', 'z'), 0, 0, tiled=T...  14.2 us
    ppermute x3, starting transfers between devices, body(): arrived = lax.ppermute(rep_own, 'rep', shift(NREP, d))  10.8 us
    ppermute x3, starting transfers between devices, body(): arrived = lax.ppermute(pair, 'x', shift(NX, d))  10.6 us
    ppermute x1, starting transfers between devices, body(): other = lax.ppermute(own, 'yh', shift(2, 1))  5.83 us
    dot_general x1, matrix products, body(): jnp.dot(cq, q_up, preferred_element_type=f32)  4.46 us
  transfers between devices with their start and end apart: 13, of which 4 were waited for; matrix products, arithmetic and copies ran while one was open for 16% of the time, Pallas kernels for 0%

profile of v2, /device:TPU:56, one launch (start us, length us, event | category | flops | bytes accessed | tf_op | source)
XLA Modules:
  0.0 180.0 jit_solution(16698957246436643034)
XLA Ops:
  7.2 0.9 constant_dynamic-update-slice_fusion.1
  8.1 0.7 constant_dynamic-update-slice_fusion
  8.8 3.3 %collective-permute-start.6 = (bf16[3,4,2112]{2,1,0:T(4,128)(2,1)S(1)}, bf16[3,4,2112]{2,1,0:T(4,128)(2,1)S(1)}, u32[]{:S(2)}, u32[]{:S(2)}) collective-permute-start(bf16[3,4,2112]{2,1,0:T(4,128)(2,1)S(1)} %constant_dynamic-update-slice_fusion), channel_id=1, source_target_pairs={{0,3},{1,0},{2,1},{3,2},{4,7},{5,4},{6,5},{7,6},{8,11},{9,8},{10,9... | collective-permute-start | bytes 152072 | tf_op jit(solution)/shard_map/ppermute | solution.py:113
  12.1 4.0 %collective-permute-start.5 = (bf16[3,4,2112]{2,1,0:T(4,128)(2,1)S(1)}, bf16[3,4,2112]{2,1,0:T(4,128)(2,1)S(1)}, u32[]{:S(2)}, u32[]{:S(2)}) collective-permute-start(bf16[3,4,2112]{2,1,0:T(4,128)(2,1)S(1)} %constant_dynamic-update-slice_fusion), channel_id=1, source_target_pairs={{0,2},{1,3},{2,0},{3,1},{4,6},{5,7},{6,4},{7,5},{8,10},{9,11},{10,... | collective-permute-start | bytes 152072 | tf_op jit(solution)/shard_map/ppermute | solution.py:113
  16.1 3.5 %collective-permute-start.4 = (bf16[3,4,2112]{2,1,0:T(4,128)(2,1)S(1)}, bf16[3,4,2112]{2,1,0:T(4,128)(2,1)}, u32[]{:S(2)}, u32[]{:S(2)}) collective-permute-start(bf16[3,4,2112]{2,1,0:T(4,128)(2,1)S(1)} %constant_dynamic-update-slice_fusion), channel_id=1, source_target_pairs={{0,1},{1,2},{2,3},{3,0},{4,5},{5,6},{6,7},{7,4},{8,9},{9,10},{10,1... | collective-permute-start | bytes 152072 | tf_op jit(solution)/shard_map/ppermute | solution.py:113
  19.6 5.8 %collective-permute-start = (bf16[16,1536]{1,0:T(8,128)(2,1)}, bf16[16,1536]{1,0:T(8,128)(2,1)S(1)}, u32[]{:S(2)}, u32[]{:S(2)}) collective-permute-start(bf16[16,1536]{1,0:T(8,128)(2,1)} %bitcast.194), channel_id=1, source_target_pairs={{0,128},{128,0},{1,129},{129,1},{2,130},{130,2},{3,131},{131,3},{4... | collective-permute-start | bytes 147464 | tf_op jit(solution)/shard_map/ppermute | solution.py:91
  25.4 1.1 reshape_squeeze.3
  26.6 1.0 broadcast_in_dim.112
  27.6 1.0 pad_maximum_fusion
  28.5 3.6 %all-to-all-start = ((bf16[4,112,832]{2,1,0:T(8,128)(2,1)}), bf16[4,112,832]{2,1,0:T(8,128)(2,1)S(1)}, u32[]{:S(2)}, u32[]{:S(2)}) async-start(bf16[4,112,832]{2,1,0:T(8,128)(2,1)} %pad_maximum_fusion), calls=%async_computation | async-start | bytes 1605632 | tf_op jit(solution)/shard_map/all_to_all | solution.py:72
  32.6 0.6 fusion.186
  34.6 0.6 pad_clamp_fusion
  35.5 1.2 multiply_cosine_fusion
  36.8 0.6 convert_element_type.203
  38.0 0.6 slice.407
  38.5 0.6 slice.403
  39.1 0.6 slice.401
  40.2 0.6 slice.395
  41.4 0.6 slice.389
  42.0 0.6 slice.385
  42.6 0.6 slice.383
  43.7 0.6 slice.377
  45.2 5.0 %collective-permute-start.3 = (bf16[2,16,1536]{2,1,0:T(8,128)(2,1)S(1)}, bf16[2,16,1536]{2,1,0:T(8,128)(2,1)S(1)}, u32[]{:S(2)}, u32[]{:S(2)}) collective-permute-start(bf16[2,16,1536]{2,1,0:T(8,128)(2,1)S(1)} %maximum_select_fusion.1), channel_id=1, source_target_pairs={{0,96},{32,0},{64,32},{96,64},{1,97},{33,1},{65,33},{97,65},{2,98}... | collective-permute-start | bytes 294920 | tf_op jit(solution)/shard_map/ppermute | solution.py:96
  50.2 2.8 %collective-permute-start.2 = (bf16[2,16,1536]{2,1,0:T(8,128)(2,1)S(1)}, bf16[2,16,1536]{2,1,0:T(8,128)(2,1)S(1)}, u32[]{:S(2)}, u32[]{:S(2)}) collective-permute-start(bf16[2,16,1536]{2,1,0:T(8,128)(2,1)S(1)} %maximum_select_fusion.1), channel_id=1, source_target_pairs={{0,64},{32,96},{64,0},{96,32},{1,65},{33,97},{65,1},{97,33},{2,66}... | collective-permute-start | bytes 294920 | tf_op jit(solution)/shard_map/ppermute | solution.py:96
  53.1 2.8 %collective-permute-start.1 = (bf16[2,16,1536]{2,1,0:T(8,128)(2,1)S(1)}, bf16[2,16,1536]{2,1,0:T(8,128)(2,1)S(1)}, u32[]{:S(2)}, u32[]{:S(2)}) collective-permute-start(bf16[2,16,1536]{2,1,0:T(8,128)(2,1)S(1)} %maximum_select_fusion.1), channel_id=1, source_target_pairs={{0,32},{32,64},{64,96},{96,0},{1,33},{33,65},{65,97},{97,1},{2,34}... | collective-permute-start | bytes 294920 | tf_op jit(solution)/shard_map/ppermute | solution.py:96
  55.8 0.8 bitcast_dynamic-update-slice_fusion.5
  56.7 4.1 %collective-permute-done.1 = bf16[2,16,1536]{2,1,0:T(8,128)(2,1)S(1)} collective-permute-done((bf16[2,16,1536]{2,1,0:T(8,128)(2,1)S(1)}, bf16[2,16,1536]{2,1,0:T(8,128)(2,1)S(1)}, u32[]{:S(2)}, u32[]{:S(2)}) %collective-permute-start.1) | collective-permute-done | bytes 98336 | tf_op jit(solution)/shard_map/ppermute | solution.py:96
  60.9 0.7 copy-done.1
  61.6 1.2 fusion.45
  62.9 14.2 %all-to-all-start.1 = ((f32[16,16,576]{2,1,0:T(8,128)}), f32[16,16,576]{2,1,0:T(8,128)S(1)}, u32[]{:S(2)}, u32[]{:S(2)}) async-start(f32[16,16,576]{2,1,0:T(8,128)} %bitcast.22), calls=%async_computation.1 | async-start | bytes 1310720 | tf_op jit(solution)/shard_map/all_to_all | solution.py:77
  77.2 0.6 gather_fusion
  78.3 16.5 %all-to-all-done.1 = f32[16,16,576]{2,1,0:T(8,128)S(1)} async-done(((f32[16,16,576]{2,1,0:T(8,128)}), f32[16,16,576]{2,1,0:T(8,128)S(1)}, u32[]{:S(2)}, u32[]{:S(2)}) %all-to-all-start.1) | async-done | bytes 589856 | tf_op jit(solution)/shard_map/all_to_all | solution.py:77
  95.3 0.8 broadcast_in_dim.114
  96.0 10.8 %all-to-all-start.2 = ((bf16[16,16,576]{2,1,0:T(8,128)(2,1)}), bf16[16,16,576]{2,1,0:T(8,128)(2,1)S(1)}, u32[]{:S(2)}, u32[]{:S(2)}) async-start(bf16[16,16,576]{2,1,0:T(8,128)(2,1)} %broadcast_in_dim.114), calls=%async_computation.2 | async-start | bytes 655360 | tf_op jit(solution)/shard_map/all_to_all | solution.py:39
  107.3 11.6 %all-to-all-done.2 = bf16[16,16,576]{2,1,0:T(8,128)(2,1)S(1)} async-done(((bf16[16,16,576]{2,1,0:T(8,128)(2,1)}), bf16[16,16,576]{2,1,0:T(8,128)(2,1)S(1)}, u32[]{:S(2)}, u32[]{:S(2)}) %all-to-all-start.2) | async-done | bytes 294944 | tf_op jit(solution)/shard_map/all_to_all | solution.py:39
  119.1 1.1 broadcast_in_dim.117
  120.2 3.7 %all-to-all-start.3 = ((bf16[4,256,576]{1,2,0:T(8,128)(2,1)}), bf16[4,256,576]{1,2,0:T(8,128)(2,1)S(1)}, u32[]{:S(2)}, u32[]{:S(2)}) async-start(bf16[4,256,576]{1,2,0:T(8,128)(2,1)} %broadcast_in_dim.117), calls=%async_computation.3 | async-start | bytes 2359296 | tf_op jit(solution)/shard_map/all_to_all | solution.py:39
  124.2 14.6 %all-to-all-done.3 = bf16[4,256,576]{1,2,0:T(8,128)(2,1)S(1)} async-done(((bf16[4,256,576]{1,2,0:T(8,128)(2,1)}), bf16[4,256,576]{1,2,0:T(8,128)(2,1)S(1)}, u32[]{:S(2)}, u32[]{:S(2)}) %all-to-all-start.3) | async-done | bytes 1179680 | tf_op jit(solution)/shard_map/all_to_all | solution.py:39
  140.7 0.6 broadcast_in_dim.133
  141.3 5.1 %all-to-all-start.4 = ((bf16[4,3,4,256]{3,2,1,0:T(4,128)(2,1)}), bf16[4,3,4,256]{3,2,1,0:T(4,128)(2,1)S(1)}, u32[]{:S(2)}, u32[]{:S(2)}) async-start(bf16[4,3,4,256]{3,2,1,0:T(4,128)(2,1)} %broadcast_in_dim.133), calls=%async_computation.4 | async-start | bytes 49152 | tf_op jit(solution)/shard_map/all_to_all | solution.py:39
  146.4 2.0 %convolution_convert_fusion = bf16[1024,512]{0,1:T(8,128)(2,1)S(1)} fusion(bf16[512,512]{1,0:T(8,128)(2,1)S(1)} %copy-done.4, bf16[1024,576]{0,1:T(8,128)(2,1)} %bitcast.189), kind=kOutput, calls=%fused_computation.4 | convolution fusion | flops 537395200 | bytes 2621440 | tf_op jit(solution)/shard_map/dot_general | solution.py:157
  148.4 1.0 copy-done.7
  149.5 0.9 slice.466
  150.4 1.3 gather_fusion.1
  151.7 4.5 %fusion.204 = f32[1024,384]{0,1:T(8,128)} fusion(bf16[1024,1536]{1,0:T(8,128)(2,1)} %all-gather.2.cloned.1.call-done, bf16[1536,384]{1,0:T(8,128)(2,1)S(1)} %copy-done), kind=kOutput, calls=%fused_computation.368 | convolution fusion | flops 1207959552 | bytes 5898240 | tf_op jit(solution)/shard_map/dot_general | solution.py:102
  156.1 1.3 slice.738
  157.8 1.1 subtract_convert_fusion
  172.3 0.9 maximum_bitcast_fusion.1
  (240 shorter events, 22.2 us)
Async XLA Ops:
  7.2 70.7 %copy-start = (bf16[1536,384]{1,0:T(8,128)(2,1)S(1)}, bf16[1536,384]{1,0:T(8,128)(2,1)}, u32[]{:S(2)}) copy-start(bf16[1536,384]{1,0:T(8,128)(2,1)} %param.14) | copy-start | bytes 3538948
  8.8 68.3 %collective-permute-start.6 = (bf16[3,4,2112]{2,1,0:T(4,128)(2,1)S(1)}, bf16[3,4,2112]{2,1,0:T(4,128)(2,1)S(1)}, u32[]{:S(2)}, u32[]{:S(2)}) collective-permute-start(bf16[3,4,2112]{2,1,0:T(4,128)(2,1)S(1)} %constant_dynamic-update-slice_fusion), channel_id=1, source_target_pairs={{0,3},{1,0},{2,1},{3,2},{4,7},{5,4},{6,5},{7,6},{8,11},{9,8},{10,9... | collective-permute-start | bytes 152072 | tf_op jit(solution)/shard_map/ppermute | solution.py:113
  12.1 65.0 %collective-permute-start.5 = (bf16[3,4,2112]{2,1,0:T(4,128)(2,1)S(1)}, bf16[3,4,2112]{2,1,0:T(4,128)(2,1)S(1)}, u32[]{:S(2)}, u32[]{:S(2)}) collective-permute-start(bf16[3,4,2112]{2,1,0:T(4,128)(2,1)S(1)} %constant_dynamic-update-slice_fusion), channel_id=1, source_target_pairs={{0,2},{1,3},{2,0},{3,1},{4,6},{5,7},{6,4},{7,5},{8,10},{9,11},{10,... | collective-permute-start | bytes 152072 | tf_op jit(solution)/shard_map/ppermute | solution.py:113
  16.1 36.9 %collective-permute-start.4 = (bf16[3,4,2112]{2,1,0:T(4,128)(2,1)S(1)}, bf16[3,4,2112]{2,1,0:T(4,128)(2,1)}, u32[]{:S(2)}, u32[]{:S(2)}) collective-permute-start(bf16[3,4,2112]{2,1,0:T(4,128)(2,1)S(1)} %constant_dynamic-update-slice_fusion), channel_id=1, source_target_pairs={{0,1},{1,2},{2,3},{3,0},{4,5},{5,6},{6,7},{7,4},{8,9},{9,10},{10,1... | collective-permute-start | bytes 152072 | tf_op jit(solution)/shard_map/ppermute | solution.py:113
  19.6 25.5 %collective-permute-start = (bf16[16,1536]{1,0:T(8,128)(2,1)}, bf16[16,1536]{1,0:T(8,128)(2,1)S(1)}, u32[]{:S(2)}, u32[]{:S(2)}) collective-permute-start(bf16[16,1536]{1,0:T(8,128)(2,1)} %bitcast.194), channel_id=1, source_target_pairs={{0,128},{128,0},{1,129},{129,1},{2,130},{130,2},{3,131},{131,3},{4... | collective-permute-start | bytes 147464 | tf_op jit(solution)/shard_map/ppermute | solution.py:91
  27.5 4.7 %copy-start.11 = (s32[4,3]{1,0:T(4,128)S(1)}, s32[4,3]{1,0:T(4,128)}, u32[]{:S(2)}) copy-start(s32[4,3]{1,0:T(4,128)} %param.16) | copy-start | bytes 148
  27.5 6.8 %copy-start.32 = (s32[1,12]{1,0:T(1,128)S(1)}, s32[1,12]{1,0:T(1,128)}, u32[]{:S(2)}) copy-start(s32[1,12]{1,0:T(1,128)} %param.17) | copy-start | bytes 148
  28.5 16.3 %copy-start.3 = (bf16[512,512]{1,0:T(8,128)(2,1)S(1)}, bf16[512,512]{1,0:T(8,128)(2,1)}, u32[]{:S(2)}) copy-start(bf16[512,512]{1,0:T(8,128)(2,1)} %param.15) | copy-start | bytes 1572868
  28.5 33.1 %all-to-all-start = ((bf16[4,112,832]{2,1,0:T(8,128)(2,1)}), bf16[4,112,832]{2,1,0:T(8,128)(2,1)S(1)}, u32[]{:S(2)}, u32[]{:S(2)}) async-start(bf16[4,112,832]{2,1,0:T(8,128)(2,1)} %pad_maximum_fusion), calls=%async_computation | async-start | bytes 1605632 | tf_op jit(solution)/shard_map/all_to_all | solution.py:72
  32.1 13.0 %copy-start.9 = (bf16[1,16,1536]{2,1,0:T(8,128)(2,1)S(1)}, bf16[1,16,1536]{2,1,0:T(8,128)(2,1)}, u32[]{:S(2)}) copy-start(bf16[1,16,1536]{2,1,0:T(8,128)(2,1)} %param.11) | copy-start | bytes 147460
  32.2 119.5 %all-gather.2.cloned.1.call-start = ((), (), s32[]{:S(2)}) async-start(), calls=%async_computation.5 | async-start | bytes 3538944 | tf_op jit(solution)/shard_map/all_gather | solution.py:98
  32.2 12.6 %copy-start.12 = (f32[32]{0:T(128)}, f32[32]{0:T(128)S(1)}, u32[]{:S(2)}) copy-start(f32[32]{0:T(128)S(1)} %multiply_power_fusion) | copy-start | bytes 388
  45.2 15.7 %collective-permute-start.3 = (bf16[2,16,1536]{2,1,0:T(8,128)(2,1)S(1)}, bf16[2,16,1536]{2,1,0:T(8,128)(2,1)S(1)}, u32[]{:S(2)}, u32[]{:S(2)}) collective-permute-start(bf16[2,16,1536]{2,1,0:T(8,128)(2,1)S(1)} %maximum_select_fusion.1), channel_id=1, source_target_pairs={{0,96},{32,0},{64,32},{96,64},{1,97},{33,1},{65,33},{97,65},{2,98}... | collective-permute-start | bytes 294920 | tf_op jit(solution)/shard_map/ppermute | solution.py:96
  50.2 10.6 %collective-permute-start.2 = (bf16[2,16,1536]{2,1,0:T(8,128)(2,1)S(1)}, bf16[2,16,1536]{2,1,0:T(8,128)(2,1)S(1)}, u32[]{:S(2)}, u32[]{:S(2)}) collective-permute-start(bf16[2,16,1536]{2,1,0:T(8,128)(2,1)S(1)} %maximum_select_fusion.1), channel_id=1, source_target_pairs={{0,64},{32,96},{64,0},{96,32},{1,65},{33,97},{65,1},{97,33},{2,66}... | collective-permute-start | bytes 294920 | tf_op jit(solution)/shard_map/ppermute | solution.py:96
  53.1 7.7 %collective-permute-start.1 = (bf16[2,16,1536]{2,1,0:T(8,128)(2,1)S(1)}, bf16[2,16,1536]{2,1,0:T(8,128)(2,1)S(1)}, u32[]{:S(2)}, u32[]{:S(2)}) collective-permute-start(bf16[2,16,1536]{2,1,0:T(8,128)(2,1)S(1)} %maximum_select_fusion.1), channel_id=1, source_target_pairs={{0,32},{32,64},{64,96},{96,0},{1,33},{33,65},{65,97},{97,1},{2,34}... | collective-permute-start | bytes 294920 | tf_op jit(solution)/shard_map/ppermute | solution.py:96
  60.9 0.7 copy-start.1
  62.9 32.0 %all-to-all-start.1 = ((f32[16,16,576]{2,1,0:T(8,128)}), f32[16,16,576]{2,1,0:T(8,128)S(1)}, u32[]{:S(2)}, u32[]{:S(2)}) async-start(f32[16,16,576]{2,1,0:T(8,128)} %bitcast.22), calls=%async_computation.1 | async-start | bytes 1310720 | tf_op jit(solution)/shard_map/all_to_all | solution.py:77
  77.0 17.9 %copy-start.13 = (f32[32]{0:T(128)S(1)}, f32[32]{0:T(128)}, u32[]{:S(2)}) copy-start(f32[32]{0:T(128)} %copy-done.12) | copy-start | bytes 388
  77.1 17.9 %copy-start.31 = (f32[16]{0:T(128)S(1)}, f32[16]{0:T(128)}, u32[]{:S(2)}) copy-start(f32[16]{0:T(128)} %subtract_convert_fusion.3) | copy-start | bytes 196
  77.1 18.1 %copy-start.17 = (f32[512]{0:T(512)S(1)}, f32[512]{0:T(512)}, u32[]{:S(2)}) copy-start(f32[512]{0:T(512)} %param.13) | copy-start | bytes 6148
  77.9 29.0 %copy-start.16 = (f32[12]{0:T(128)S(1)}, f32[12]{0:T(128)}, u32[]{:S(2)}) copy-start(f32[12]{0:T(128)} %convert_element_type.203) | copy-start | bytes 148
  78.2 40.9 %copy-start.10 = (bf16[12,2,192]{2,1,0:T(2,128)(2,1)}, bf16[12,2,192]{2,1,0:T(2,128)(2,1)S(1)}, u32[]{:S(2)}) copy-start(bf16[12,2,192]{2,1,0:T(2,128)(2,1)S(1)} %reshape.433) | copy-start | bytes 27652
  96.0 22.9 %all-to-all-start.2 = ((bf16[16,16,576]{2,1,0:T(8,128)(2,1)}), bf16[16,16,576]{2,1,0:T(8,128)(2,1)S(1)}, u32[]{:S(2)}, u32[]{:S(2)}) async-start(bf16[16,16,576]{2,1,0:T(8,128)(2,1)} %broadcast_in_dim.114), calls=%async_computation.2 | async-start | bytes 655360 | tf_op jit(solution)/shard_map/all_to_all | solution.py:39
  120.2 3.7 %slice-start.1 = ((bf16[12,2,192]{2,1,0:T(2,128)(2,1)}), bf16[12,2,64]{2,1,0:T(2,128)(2,1)S(1)}, s32[]{:S(2)}) async-start(bf16[12,2,192]{2,1,0:T(2,128)(2,1)} %copy-done.10), calls=%async_computation.7 | async-start | bytes 12288 | tf_op jit(solution)/shard_map/slice | solution.py:126
  120.2 3.9 %slice-start = ((bf16[12,2,192]{2,1,0:T(2,128)(2,1)}), bf16[12,2,128]{2,1,0:T(2,128)(2,1)S(1)}, s32[]{:S(2)}) async-start(bf16[12,2,192]{2,1,0:T(2,128)(2,1)} %copy-done.10), calls=%async_computation.6 | async-start | bytes 12288 | tf_op jit(solution)/shard_map/slice | solution.py:129
  120.2 18.7 %all-to-all-start.3 = ((bf16[4,256,576]{1,2,0:T(8,128)(2,1)}), bf16[4,256,576]{1,2,0:T(8,128)(2,1)S(1)}, u32[]{:S(2)}, u32[]{:S(2)}) async-start(bf16[4,256,576]{1,2,0:T(8,128)(2,1)} %broadcast_in_dim.117), calls=%async_computation.3 | async-start | bytes 2359296 | tf_op jit(solution)/shard_map/all_to_all | solution.py:39
  139.0 1.0 copy-start.2
  140.1 6.4 %copy-start.4 = (bf16[512,512]{1,0:T(8,128)(2,1)S(1)}, bf16[512,512]{1,0:T(8,128)(2,1)}, u32[]{:S(2)}) copy-start(bf16[512,512]{1,0:T(8,128)(2,1)} %param.15) | copy-start | bytes 1572868
  141.3 9.0 %all-to-all-start.4 = ((bf16[4,3,4,256]{3,2,1,0:T(4,128)(2,1)}), bf16[4,3,4,256]{3,2,1,0:T(4,128)(2,1)S(1)}, u32[]{:S(2)}, u32[]{:S(2)}) async-start(bf16[4,3,4,256]{3,2,1,0:T(4,128)(2,1)} %broadcast_in_dim.133), calls=%async_computation.4 | async-start | bytes 49152 | tf_op jit(solution)/shard_map/all_to_all | solution.py:39
  148.4 1.0 copy-start.7
  156.1 1.6 copy-start.5
  156.1 1.6 copy-start.6
  159.8 1.1 copy-start.14
  159.8 1.1 copy-start.24
  159.9 1.6 copy-start.23
  159.9 1.6 copy-start.30
  160.0 1.6 copy-start.38
  160.9 1.2 copy-start.22
  161.0 1.2 copy-start.29
  161.0 1.2 copy-start.37
  161.8 0.9 copy-start.21
  161.8 0.9 copy-start.28
  161.8 0.9 copy-start.36
  162.7 0.7 copy-start.20
  162.7 0.7 copy-start.27
  163.9 0.7 copy-start.25
  164.0 0.7 copy-start.33
  164.3 1.2 copy-start.8
  (6 other events, 4.0 us)
Sparse Core Ops, SparseCore 0:
  61.7 67.9 all-gather.1

commit v3 on v1

v3 whole, which is shorter than its diff:
```python
import math

import jax
import jax.numpy as jnp
from jax import lax
from jax.experimental import pallas as pl
from jax.experimental.pallas import tpu as pltpu
from jax.sharding import Mesh, PartitionSpec as P

KVL = 512
NOPE = 128
ROPE = 64
VD = 128
BLK = 128
NREQ = 3
STEPS = 4
REACH = 4
NREP = 4
NX = 4
HEADS = 2
PAD = 16

SIGMA = (1.0 + 0.1 * math.log(40.0)) ** 2 * (NOPE + ROPE) ** (-0.5)
bf16 = jnp.bfloat16
f32 = jnp.float32
i32 = jnp.int32
VMEM_LIMIT = 40 * 1024 * 1024


def cos_sin(positions):
    half = ROPE // 2
    frequency = 10000.0 ** (-jnp.arange(half, dtype=f32) * 2.0 / ROPE)
    angles = positions.astype(f32)[..., None] * frequency
    return jnp.cos(angles), jnp.sin(angles)


def rotate(u, cos_part, sin_part):
    half = ROPE // 2
    a, b = u[..., :half], u[..., half:]
    return jnp.concatenate([a * cos_part - b * sin_part, a * sin_part + b * cos_part], axis=-1)


def spread(a, axes, count):
    copies = jnp.broadcast_to(a[None], (count,) + a.shape)
    return lax.all_to_all(copies, axes, 0, 0, tiled=True)


def shift(count, d):
    return [(i, (i + d) % count) for i in range(count)]


def dot_t(a, b):
    return lax.dot_general(a, b, (((1,), (1,)), ((), ())), preferred_element_type=f32)


def norm_kernel(pieces_ref, gain_ref, cos_ref, sin_ref, out_ref):
    latent = jnp.sum(pieces_ref[...], axis=0)
    content = latent[:, :KVL]
    scale = lax.rsqrt(jnp.mean(content * content, axis=1, keepdims=True) + 1e-06)
    content = (content * scale * gain_ref[...]).astype(bf16)
    a = latent[:, KVL : KVL + ROPE // 2]
    b = latent[:, KVL + ROPE // 2 :]
    cos_part, sin_part = cos_ref[...], sin_ref[...]
    first, second = a * cos_part - b * sin_part, a * sin_part + b * cos_part
    pe = jnp.concatenate([first, second, first, second], axis=1).astype(bf16)
    for i in range(out_ref.shape[0]):
        out_ref[i, :, :KVL] = content
        out_ref[i, :, KVL:] = pe


def norm_rows(pieces, gain, cos_part, sin_part):
    count, chunk, _ = pieces.shape
    return pl.pallas_call(
        norm_kernel,
        out_shape=jax.ShapeDtypeStruct((count, chunk, KVL + 2 * ROPE), bf16),
        cost_estimate=pl.CostEstimate(flops=1_000_000, bytes_accessed=1_000_000, transcendentals=16),
        name="norm_rows",
    )(pieces, gain, cos_part, sin_part)


def query_kernel(cq_ref, w_ref, cos_ref, sin_ref, out_ref):
    rows = cq_ref[...].reshape(BLK, -1)
    u = jnp.dot(rows, w_ref[...], preferred_element_type=f32)
    pe = u[:, HEADS * NOPE :]
    lane = lax.broadcasted_iota(i32, pe.shape, 1)
    swapped = jnp.where(lane % ROPE < ROPE // 2, pltpu.roll(pe, 96, 1), pltpu.roll(pe, 32, 1))
    pe = pe * cos_ref[...] + swapped * sin_ref[...]
    for h in range(HEADS):
        out_ref[h, :, :NOPE] = u[:, h * NOPE : (h + 1) * NOPE].astype(bf16)
        out_ref[h, :, NOPE:] = jnp.where(lane // ROPE == h, pe, 0.0).astype(bf16)


def project_queries(cq, weights, cos_part, sin_part):
    width = cq.shape[-1]
    return pl.pallas_call(
        query_kernel,
        grid=(8,),
        in_specs=[
            pl.BlockSpec((8, 1, 16, width), lambda i: (0, i, 0, 0)),
            pl.BlockSpec(weights.shape, lambda i: (0, 0)),
            pl.BlockSpec((BLK, 2 * ROPE), lambda i: (i, 0)),
            pl.BlockSpec((BLK, 2 * ROPE), lambda i: (i, 0)),
        ],
        out_specs=pl.BlockSpec((HEADS, BLK, 2 * NOPE), lambda i: (0, i, 0)),
        out_shape=jax.ShapeDtypeStruct((HEADS, 8 * BLK, 2 * NOPE), bf16),
        compiler_params=pltpu.CompilerParams(vmem_limit_bytes=VMEM_LIMIT),
        cost_estimate=pl.CostEstimate(flops=1_200_000_000, bytes_accessed=5_000_000, transcendentals=0),
        name="project_queries",
    )(cq, weights, cos_part, sin_part)


def decode_kernel(lq_ref, pe_ref, cache_ref, new_ref, low_ref, high_ref, kv_ref, out_ref):
    latent = cache_ref[:, :KVL]
    new_latent = new_ref[:, :KVL]
    old = (dot_t(lq_ref[...], latent) + dot_t(pe_ref[...], cache_ref[:, KVL : KVL + ROPE])) * SIGMA
    new = (dot_t(lq_ref[...], new_latent) + dot_t(pe_ref[...], new_ref[:, KVL:])) * SIGMA
    column = lax.broadcasted_iota(i32, old.shape, 1)
    old = jnp.where((column >= low_ref[...]) & (column < high_ref[...]), old, -1e30)
    step = lax.broadcasted_iota(i32, new.shape, 0) % PAD
    other = lax.broadcasted_iota(i32, new.shape, 1)
    new = jnp.where((step // STEPS == other // STEPS) & (other <= step), new, -1e30)
    top = jnp.maximum(jnp.max(old, axis=1, keepdims=True), jnp.max(new, axis=1, keepdims=True))
    old = jnp.exp(old - top)
    new = jnp.exp(new - top)
    total = jnp.sum(old, axis=1, keepdims=True) + jnp.sum(new, axis=1, keepdims=True)
    old = (old / total).astype(bf16)
    new = (new / total).astype(bf16)
    mixture = (
        jnp.dot(old, latent, preferred_element_type=f32) + jnp.dot(new, new_latent, preferred_element_type=f32)
    ).astype(bf16)
    for h in range(HEADS):
        base = h * (NOPE + VD) + NOPE
        out_ref[:, h * VD : (h + 1) * VD] = jnp.dot(
            mixture[h * PAD : (h + 1) * PAD], kv_ref[:, base : base + VD], preferred_element_type=f32
        ).astype(bf16)


def decode(lq, pe, cache, new_keys, low, high, kv_up):
    return pl.pallas_call(
        decode_kernel,
        out_shape=jax.ShapeDtypeStruct((PAD, HEADS * VD), bf16),
        compiler_params=pltpu.CompilerParams(vmem_limit_bytes=VMEM_LIMIT),
        cost_estimate=pl.CostEstimate(flops=100_000_000, bytes_accessed=2_000_000, transcendentals=40_000),
        name="decode_attention",
    )(lq, pe, cache, new_keys, low, high, kv_up)


def prefill_kernel(start_ref, q_ref, cache_ref, kv_ref, out_ref, key_ref, value_ref):
    for j in range(8):
        rows = slice(j * BLK, (j + 1) * BLK)
        wide = jnp.dot(cache_ref[rows, :KVL], kv_ref[...], preferred_element_type=f32).astype(bf16)
        for h in range(HEADS):
            base = h * (NOPE + VD)
            key_ref[h, rows, :NOPE] = wide[:, base : base + NOPE]
            key_ref[h, rows, NOPE:] = cache_ref[rows, KVL:]
            value_ref[h, rows, :] = wide[:, base + NOPE : base + NOPE + VD]
    for i in range(8):
        first = max(0, i - REACH + 1) * BLK
        last = (i + 1) * BLK
        shape = (BLK, last - first)
        column = lax.broadcasted_iota(i32, shape, 1) + first
        row = lax.broadcasted_iota(i32, shape, 0) + i * BLK
        ok = (column >= start_ref[i]) & (column <= row)
        for h in range(HEADS):
            s = dot_t(q_ref[h, i * BLK : last, :], key_ref[h, first:last, :]) * SIGMA
            s = jnp.where(ok, s, -1e30)
            w = jnp.exp(s - jnp.max(s, axis=1, keepdims=True))
            w = (w / jnp.sum(w, axis=1, keepdims=True)).astype(bf16)
            out_ref[i * BLK : last, h * VD : (h + 1) * VD] = jnp.dot(
                w, value_ref[h, first:last, :], preferred_element_type=f32
            ).astype(bf16)


def prefill(block_starts, queries, cache, kv_up):
    rows = cache.shape[0]
    vmem = pl.BlockSpec(memory_space=pltpu.VMEM)
    return pl.pallas_call(
        prefill_kernel,
        in_specs=[pl.BlockSpec(memory_space=pltpu.SMEM), vmem, vmem, vmem],
        out_specs=vmem,
        out_shape=jax.ShapeDtypeStruct((rows, HEADS * VD), bf16),
        scratch_shapes=[
            pltpu.VMEM((HEADS, rows, 2 * NOPE), bf16),
            pltpu.VMEM((HEADS, rows, VD), bf16),
        ],
        compiler_params=pltpu.CompilerParams(vmem_limit_bytes=VMEM_LIMIT),
        cost_estimate=pl.CostEstimate(flops=1_500_000_000, bytes_accessed=4_000_000, transcendentals=1_000_000),
        name="prefill_attention",
    )(block_starts, queries, cache, kv_up)


def body(hidden, comp_query, kv_down, kv_gain, q_up, kv_up, req_blocks, dest_slot, dec_query, dec_latent):
    rep = lax.axis_index("rep")
    yh_index = lax.axis_index("yh")
    yz_index = lax.axis_index(("yh", "z"))
    x_index = lax.axis_index("x")
    block_x = hidden[0]
    rows, features = block_x.shape

    own = comp_query[0]
    other = lax.ppermute(own, "yh", shift(2, 1))
    per_x = rows // NX
    hidden_t = jnp.swapaxes(block_x.reshape(NX, per_x, features), 1, 2)
    packed = jnp.concatenate(
        [hidden_t, jnp.broadcast_to(kv_down[None], (NX,) + kv_down.shape)], axis=2
    )
    packed = lax.all_to_all(packed, "x", 0, 0, tiled=True)
    pair = jnp.where(yh_index == 0, jnp.stack([own, other]), jnp.stack([other, own]))
    line = jnp.zeros((2, NX) + own.shape, own.dtype)
    line = lax.dynamic_update_slice_in_dim(line, pair[:, None], x_index, 1)
    for d in range(1, NX):
        arrived = lax.ppermute(pair, "x", shift(NX, d))
        line = lax.dynamic_update_slice_in_dim(line, arrived[:, None], (x_index - d) % NX, 1)

    packed, dec_query, dec_latent = lax.optimization_barrier((packed, dec_query, dec_latent))
    packed = packed.reshape(NX * features, -1)
    partial = lax.dot_general(
        packed[:, :per_x], packed[:, per_x:], (((0,), (0,)), ((), ())), preferred_element_type=f32
    )
    cq = lax.all_gather(line.reshape(BLK, -1), "z", axis=0, tiled=True)

    lengths_all = req_blocks * BLK
    starts_all = jnp.cumsum(lengths_all, axis=-1) - lengths_all
    lengths = lax.dynamic_index_in_dim(lengths_all, rep, 0, keepdims=False)
    starts = lax.dynamic_index_in_dim(starts_all, rep, 0, keepdims=False)

    def start_of(row):
        inside = (row[:, None] >= starts[None]) & (row[:, None] < (starts + lengths)[None])
        return jnp.sum(jnp.where(inside, starts[None], 0), axis=1)

    chunk = per_x // 16
    pieces = lax.all_to_all(partial.reshape(16, chunk, -1), ("yh", "z"), 0, 0, tiled=True)
    own_rows = x_index * per_x + yz_index * chunk + jnp.arange(chunk, dtype=i32)
    cos_o, sin_o = cos_sin(own_rows - start_of(own_rows))
    copies = norm_rows(pieces, kv_gain[None, :], cos_o, sin_o)
    cache = lax.all_to_all(copies, ("yh", "z"), 0, 0, tiled=True).reshape(per_x, -1)
    cache = spread(cache, "x", NX).reshape(rows, -1)

    row_index = jnp.arange(rows, dtype=i32)
    cos_q, sin_q = cos_sin(row_index - start_of(row_index))
    by_head = q_up.reshape(-1, HEADS, NOPE + ROPE)
    nope_part = by_head[..., :NOPE].reshape(-1, HEADS * NOPE)
    rope_part = by_head[..., NOPE:].reshape(-1, HEADS * ROPE)
    queries = project_queries(
        cq.reshape(8, 8, 16, -1),
        jnp.concatenate([nope_part, rope_part], axis=1),
        jnp.concatenate([cos_q] * 4, axis=1),
        jnp.concatenate([-sin_q, sin_q] * 2, axis=1),
    )

    slots = lax.dynamic_slice_in_dim(dest_slot[0], rep * NREQ, NREQ, 0)
    rep_own = jnp.concatenate([dec_query, dec_latent], axis=2)
    rep_in = rep_own[None]
    for d in (1, 2):
        met = lax.ppermute(rep_in, "rep", [(i, i ^ d) for i in range(NREP)])
        upper = (rep // d) % 2 == 1
        rep_in = jnp.where(upper, jnp.concatenate([met, rep_in]), jnp.concatenate([rep_in, met]))
    rep_in = rep_in.reshape(NREP * NREQ, STEPS, -1)
    mine = jnp.take(rep_in, slots, axis=0, mode="clip").reshape(NREQ * STEPS, -1)
    mine = jnp.pad(mine, ((0, PAD - NREQ * STEPS), (0, 0)))
    my_query = mine[:, : dec_query.shape[2]]
    my_latent = mine[:, dec_query.shape[2] :]
    new_pos = jnp.pad((lengths[:, None] + jnp.arange(STEPS, dtype=i32)[None]).reshape(-1), (0, PAD - NREQ * STEPS))
    cos_d, sin_d = cos_sin(new_pos)
    new_keys = jnp.concatenate(
        [my_latent[:, :KVL], rotate(my_latent[:, KVL:].astype(f32), cos_d, sin_d).astype(bf16)], axis=1
    )
    dq = jnp.dot(my_query, q_up, preferred_element_type=f32).astype(bf16).reshape(PAD, HEADS, NOPE + ROPE)
    query_pe = rotate(dq[..., NOPE:].astype(f32), cos_d[:, None], sin_d[:, None]).astype(bf16)
    query_pe = jnp.swapaxes(query_pe, 0, 1).reshape(HEADS * PAD, ROPE)
    key_part = kv_up.reshape(KVL, HEADS, NOPE + VD)[..., :NOPE]
    latent_query = jnp.einsum("rhn,khn->hrk", dq[..., :NOPE], key_part, preferred_element_type=f32)
    latent_query = latent_query.astype(bf16).reshape(HEADS * PAD, KVL)
    span = (0, PAD - NREQ * STEPS)
    low = jnp.tile(jnp.pad(jnp.repeat(starts, STEPS), span), HEADS)[:, None]
    high = jnp.tile(jnp.pad(jnp.repeat(starts + lengths, STEPS), span), HEADS)[:, None]
    result = decode(latent_query, query_pe, cache, new_keys, low, high, kv_up)
    result = result[: NREQ * STEPS].reshape(NREQ, STEPS, HEADS * VD)
    pool = spread(result, "rep", NREP)
    block_starts = start_of(jnp.arange(rows // BLK, dtype=i32) * BLK)
    prefill_out = prefill(block_starts, queries, cache, kv_up)[None]
    pool, prefill_out = lax.optimization_barrier((pool, prefill_out))
    pool = pool.reshape(NREP * NREQ, STEPS, HEADS * VD)
    slot_numbers = rep * NREQ + jnp.arange(NREQ, dtype=i32)
    source = jnp.sum(
        jnp.where(dest_slot[0][None] == slot_numbers[:, None], jnp.arange(NREP * NREQ, dtype=i32)[None], 0),
        axis=1,
    )
    decode_out = jnp.take(pool, source, axis=0, mode="clip")
    return prefill_out, decode_out


def solution(mesh):
    fine = Mesh(mesh.devices.reshape(2, 2, 4, 8, 4), ("section", "yh", "x", "z", "rep"))
    tp = ("yh", "x", "z")
    group = ("section", "rep")
    in_specs = (
        P(group, None, tp),
        P(group, tp, None),
        P(tp, None),
        P(),
        P(None, tp),
        P(None, tp),
        P("section", None),
        P("section", None),
        P(group, None, None),
        P(group, None, None),
    )
    out_specs = (P(group, None, tp), P(group, None, tp))
    return jax.shard_map(body, mesh=fine, in_specs=in_specs, out_specs=out_specs, check_vma=False)
```

time: 206 us -> 173 us (0.84)
  the two profiles are of different devices: /device:TPU:64 before, /device:TPU:56 now
where the time goes in v3:
time: 173 us; the launch traced here: 171 us
  starting transfers between devices  62.4 us (36%)
  waiting for transfers between devices  37.6 us (22%)
  local copies, waits for them, and re-layouts  26.4 us (15%)
  Pallas kernels  15.1 us (9%)
  between operations  14.5 us (8%)
  other arithmetic  11.7 us (7%)
  matrix products  3.22 us (2%)
    all_to_all x1, starting transfers between devices, body(): lax.all_to_all(partial.reshape(16, chunk, -1), ('yh', 'z'), 0, 0, tiled=T...  15.7 us
    ppermute x2, waiting for transfers between devices, body(): met = lax.ppermute(rep_in, 'rep', [(i, i ^ d) for i in range(NREP)])  15.3 us
    all_to_all x1, starting transfers between devices, body(): lax.all_to_all(copies, ('yh', 'z'), 0, 0, tiled=True).reshape(per_x, -1)  12 us
    ppermute x3, starting transfers between devices, body(): arrived = lax.ppermute(pair, 'x', shift(NX, d))  12 us
    all_to_all x2, waiting for transfers between devices, spread(): return lax.all_to_all(copies, axes, 0, 0, tiled=True)  10.4 us
    unnamed x42, local copies, waits for them, and re-layouts  9.71 us
    all_to_all x2, starting transfers between devices, spread(): return lax.all_to_all(copies, axes, 0, 0, tiled=True)  8.63 us
    pallas_call x1, Pallas kernels, prefill(): pl.pallas_call(prefill_kernel, in_specs=[pl.BlockSpec(memory_space=pltpu....  8.11 us
  transfers between devices with their start and end apart: 12, of which 5 were waited for; matrix products, arithmetic and copies ran while one was open for 18% of the time, Pallas kernels for 9%

profile of v3, /device:TPU:56, one launch (start us, length us, event | category | flops | bytes accessed | tf_op | source)
XLA Modules:
  0.0 170.9 jit_solution(612451198845972927)
XLA Ops:
  7.2 4.7 %collective-permute-start.2 = (bf16[16,1536]{1,0:T(8,128)(2,1)}, bf16[16,1536]{1,0:T(8,128)(2,1)S(1)}, u32[]{:S(2)}, u32[]{:S(2)}) collective-permute-start(bf16[16,1536]{1,0:T(8,128)(2,1)} %bitcast.68), channel_id=1, source_target_pairs={{0,128},{128,0},{1,129},{129,1},{2,130},{130,2},{3,131},{131,3},{4... | collective-permute-start | bytes 147464 | tf_op jit(solution)/shard_map/ppermute | solution.py:201
  11.9 1.1 reshape_squeeze.3
  13.0 1.0 broadcast_in_dim.73
  14.0 1.0 pad_maximum_fusion.1
  15.0 4.3 %all-to-all-start = ((bf16[4,112,832]{2,1,0:T(8,128)(2,1)}), bf16[4,112,832]{2,1,0:T(8,128)(2,1)S(1)}, u32[]{:S(2)}, u32[]{:S(2)}) async-start(bf16[4,112,832]{2,1,0:T(8,128)(2,1)} %pad_maximum_fusion.1), calls=%async_computation | async-start | bytes 1605632 | tf_op jit(solution)/shard_map/all_to_all | solution.py:207
  19.6 4.1 %collective-permute-start.3 = (bf16[2,16,1536]{2,1,0:T(8,128)(2,1)S(1)}, bf16[2,16,1536]{2,1,0:T(8,128)(2,1)S(1)}, u32[]{:S(2)}, u32[]{:S(2)}) collective-permute-start(bf16[2,16,1536]{2,1,0:T(8,128)(2,1)S(1)} %maximum_select_fusion.3), channel_id=1, source_target_pairs={{0,32},{32,64},{64,96},{96,0},{1,33},{33,65},{65,97},{97,1},{2,34}... | collective-permute-start | bytes 294920 | tf_op jit(solution)/shard_map/ppermute | solution.py:212
  23.7 4.6 %collective-permute-start.4 = (bf16[2,16,1536]{2,1,0:T(8,128)(2,1)S(1)}, bf16[2,16,1536]{2,1,0:T(8,128)(2,1)S(1)}, u32[]{:S(2)}, u32[]{:S(2)}) collective-permute-start(bf16[2,16,1536]{2,1,0:T(8,128)(2,1)S(1)} %maximum_select_fusion.3), channel_id=1, source_target_pairs={{0,64},{32,96},{64,0},{96,32},{1,65},{33,97},{65,1},{97,33},{2,66}... | collective-permute-start | bytes 294920 | tf_op jit(solution)/shard_map/ppermute | solution.py:212
  28.2 3.4 %collective-permute-start.5 = (bf16[2,16,1536]{2,1,0:T(8,128)(2,1)S(1)}, bf16[2,16,1536]{2,1,0:T(8,128)(2,1)S(1)}, u32[]{:S(2)}, u32[]{:S(2)}) collective-permute-start(bf16[2,16,1536]{2,1,0:T(8,128)(2,1)S(1)} %maximum_select_fusion.3), channel_id=1, source_target_pairs={{0,96},{32,0},{64,32},{96,64},{1,97},{33,1},{65,33},{97,65},{2,98}... | collective-permute-start | bytes 294920 | tf_op jit(solution)/shard_map/ppermute | solution.py:212
  31.7 2.6 %collective-permute-done.3 = bf16[2,16,1536]{2,1,0:T(8,128)(2,1)S(1)} collective-permute-done((bf16[2,16,1536]{2,1,0:T(8,128)(2,1)S(1)}, bf16[2,16,1536]{2,1,0:T(8,128)(2,1)S(1)}, u32[]{:S(2)}, u32[]{:S(2)}) %collective-permute-start.3) | collective-permute-done | bytes 98336 | tf_op jit(solution)/shard_map/ppermute | solution.py:212
  34.3 1.3 collective-permute-done.4
  35.7 0.7 copy-done.13
  37.2 1.0 slice.77
  38.2 0.8 slice.78
  39.0 2.4 %copy.65 = bf16[1536,256]{1,0:T(8,128)(2,1)} copy(bf16[1536,256]{0,1:T(8,128)(2,1)} %bitcast.61) | data formatting | bytes 1572864 | tf_op jit(solution)/shard_map/reshape | solution.py:242
  41.4 0.9 copy.62
  42.4 1.0 copy.51
  43.8 0.7 broadcast_in_dim_tile.9.high_ref
  45.7 1.9 %fusion.4 = (f32[1024,32]{1,0:T(8,128)S(1)}, f32[1024,32]{1,0:T(8,128)S(1)}, f32[1024,32]{1,0:T(8,128)S(1)}) fusion(f32[32]{0:T(128)S(1)} %multiply_power_fusion, f32[1024]{0:T(1024)S(1)} %subtract_convert_fusion.2), kind=kLoop, calls=%fused_computation.15 | loop fusion | flops 65536 | bytes 397440 | tf_op jit(solution)/shard_map/neg | solution.py:248
  47.6 0.9 pad_maximum_fusion.2
  48.6 2.4 %collective-permute-start = (bf16[1,3,4,2112]{3,2,1,0:T(4,128)(2,1)S(1)}, bf16[1,3,4,2112]{3,2,1,0:T(4,128)(2,1)S(1)}, u32[]{:S(2)}, u32[]{:S(2)}) collective-permute-start(bf16[1,3,4,2112]{3,2,1,0:T(4,128)(2,1)S(1)} %maximum_bitcast_fusion), channel_id=1, source_target_pairs={{0,1},{1,0},{2,3},{3,2},{4,5},{5,4},{6,7},{7,6},{8,9},{9,8},{10,11... | collective-permute-start | bytes 152072 | tf_op jit(solution)/shard_map/ppermute | solution.py:255
  50.9 1.2 fusion
  52.2 15.7 %all-to-all-start.1 = ((f32[16,16,576]{2,1,0:T(8,128)}), f32[16,16,576]{2,1,0:T(8,128)S(1)}, u32[]{:S(2)}, u32[]{:S(2)}) async-start(f32[16,16,576]{2,1,0:T(8,128)} %bitcast.62), calls=%async_computation.1 | async-start | bytes 1310720 | tf_op jit(solution)/shard_map/all_to_all | solution.py:232
  68.0 2.7 %collective-permute-start.1 = (bf16[2,3,4,2112]{3,2,1,0:T(4,128)(2,1)S(1)}, bf16[2,3,4,2112]{3,2,1,0:T(4,128)(2,1)S(1)}, u32[]{:S(2)}, u32[]{:S(2)}) collective-permute-start(bf16[2,3,4,2112]{3,2,1,0:T(4,128)(2,1)S(1)} %maximum_select_fusion.1), channel_id=1, source_target_pairs={{0,2},{1,3},{2,0},{3,1},{4,6},{5,7},{6,4},{7,5},{8,10},{9,11},{10,... | collective-permute-start | bytes 304136 | tf_op jit(solution)/shard_map/ppermute | solution.py:255
  70.7 15.3 %collective-permute-done.1 = bf16[2,3,4,2112]{3,2,1,0:T(4,128)(2,1)S(1)} collective-permute-done((bf16[2,3,4,2112]{3,2,1,0:T(4,128)(2,1)S(1)}, bf16[2,3,4,2112]{3,2,1,0:T(4,128)(2,1)S(1)}, u32[]{:S(2)}, u32[]{:S(2)}) %collective-permute-start.1) | collective-permute-done | bytes 101408 | tf_op jit(solution)/shard_map/ppermute | solution.py:255
  86.9 0.8 subtract_convert_fusion.1
  87.7 0.8 copy-done.11
  88.5 2.1 %norm_rows.1 = bf16[16,16,640]{2,1,0:T(8,128)(2,1)} custom-call(f32[16,16,576]{2,1,0:T(8,128)} %copy-done.11, f32[1,512]{1,0:T(1,128)} %bitcast.72, f32[16,32]{1,0:T(8,128)} %get-tuple-element.26.cos_ref, f32[16,32]{1,0:T(8,128)} %get-tuple-element.27.sin_ref), custom_call_target="tpu_custom_call" | custom-call | flops 1000000 | bytes 1000000 | tf_op jit(solution)/shard_map/norm_rows/pallas_call | solution.py:73
  90.6 12.0 %all-to-all-start.2 = ((bf16[16,16,640]{2,1,0:T(8,128)(2,1)}), bf16[16,16,640]{2,1,0:T(8,128)(2,1)}, u32[]{:S(2)}, u32[]{:S(2)}) async-start(bf16[16,16,640]{2,1,0:T(8,128)(2,1)} %norm_rows.1), calls=%async_computation.2 | async-start | bytes 655360 | tf_op jit(solution)/shard_map/all_to_all | solution.py:236
  103.2 1.4 pad_maximum_fusion.w_ref
  106.2 7.9 %all-to-all-done.2 = bf16[16,16,640]{2,1,0:T(8,128)(2,1)} async-done(((bf16[16,16,640]{2,1,0:T(8,128)(2,1)}), bf16[16,16,640]{2,1,0:T(8,128)(2,1)}, u32[]{:S(2)}, u32[]{:S(2)}) %all-to-all-start.2) | async-done | bytes 327712 | tf_op jit(solution)/shard_map/all_to_all | solution.py:236
  114.1 2.1 %broadcast_in_dim.131 = bf16[4,256,640]{2,1,0:T(8,128)(2,1)} broadcast(bf16[256,640]{1,0:T(8,128)(2,1)} %bitcast.14), dimensions={1,2} | broadcast | bytes 1638400 | tf_op jit(solution)/shard_map/broadcast_in_dim | solution.py:44
  116.2 3.5 %all-to-all-start.3 = ((bf16[4,256,640]{2,1,0:T(8,128)(2,1)}), bf16[4,256,640]{2,1,0:T(8,128)(2,1)S(1)}, u32[]{:S(2)}, u32[]{:S(2)}) async-start(bf16[4,256,640]{2,1,0:T(8,128)(2,1)} %broadcast_in_dim.131), calls=%async_computation.3 | async-start | bytes 2621440 | tf_op jit(solution)/shard_map/all_to_all | solution.py:45
  120.5 0.8 subtract_convert_fusion
  121.9 0.7 pad_slice_fusion.1
  122.7 1.4 pad_maximum_fusion.4.new_ref
  124.0 1.7 %convolution_convert_fusion = bf16[2,16,512]{2,1,0:T(8,128)(2,1)} fusion(bf16[512,2,256]{0,2,1:T(8,128)(2,1)} %bitcast.65, bf16[16,2,128]{2,1,0:T(2,128)(2,1)} %slice.67), kind=kOutput, calls=%fused_computation.3 | convolution fusion | flops 4210688 | bytes 303104 | tf_op jit(solution)/shard_map/rhn,khn->hrk/dot_general | solution.py:272
  125.7 10.4 %all-to-all-done.3 = bf16[4,256,640]{2,1,0:T(8,128)(2,1)S(1)} async-done(((bf16[4,256,640]{2,1,0:T(8,128)(2,1)}), bf16[4,256,640]{2,1,0:T(8,128)(2,1)S(1)}, u32[]{:S(2)}, u32[]{:S(2)}) %all-to-all-start.3) | async-done | bytes 1310752 | tf_op jit(solution)/shard_map/all_to_all | solution.py:45
  136.2 1.0 copy-done.2
  137.2 0.8 copy-done.4
  138.0 0.7 copy-done.5
  138.7 0.7 copy-done.6
  140.1 1.1 decode_attention.1
  141.8 0.7 broadcast_in_dim.134
  143.2 5.1 %all-to-all-start.4 = ((bf16[4,3,4,256]{3,2,1,0:T(4,128)(2,1)}), bf16[4,3,4,256]{3,2,1,0:T(4,128)(2,1)}, u32[]{:S(2)}, u32[]{:S(2)}) async-start(bf16[4,3,4,256]{3,2,1,0:T(4,128)(2,1)} %broadcast_in_dim.135), calls=%async_computation.4 | async-start | bytes 49152 | tf_op jit(solution)/shard_map/all_to_all | solution.py:45
  148.3 1.9 %copy-done = bf16[1024,1536]{1,0:T(8,128)(2,1)S(1)} copy-done((bf16[1024,1536]{1,0:T(8,128)(2,1)S(1)}, bf16[1024,1536]{1,0:T(8,128)(2,1)}, u32[]{:S(2)}) %copy-start) | copy-done | bytes 3145752
  150.1 3.8 %project_queries.1.q_ref = bf16[2,1024,256]{2,1,0:T(8,128)(2,1)S(1)} custom-call(bf16[8,8,16,1536]{3,2,1,0:T(8,128)(2,1)S(1)} %bitcast.54, bf16[1536,384]{1,0:T(8,128)(2,1)S(1)} %pad_maximum_fusion.w_ref, f32[1024,128]{1,0:T(8,128)S(1)} %get-tuple-element.28.cos_ref, f32[1024,128]{1,0:T(8,128)S(1)} %get-tuple-element.29.sin_ref), custom_call_target="tpu_custom_call" | custom-call | flops 1200000000 | bytes 5000000 | tf_op jit(solution)/shard_map/project_queries/pallas_call | solution.py:95
  154.0 8.1 %prefill_attention.1 = bf16[1024,256]{1,0:T(8,128)(2,1)} custom-call(s32[8]{0:T(128)S(1)} %copy-done.9, bf16[2,1024,256]{2,1,0:T(8,128)(2,1)S(1)} %project_queries.1.q_ref, bf16[1024,640]{1,0:T(8,128)(2,1)S(1)} %bitcast.53, bf16[512,512]{1,0:T(8,128)(2,1)S(1)} %copy-done.3), custom_call_target="tpu_custom_call" | custom-call | flops 1500000000 | bytes 4000000 | tf_op jit(solution)/shard_map/prefill_attention/pallas_call | solution.py:177
  162.1 2.0 %gather_fusion.1 = bf16[3,4,256]{2,1,0:T(4,128)(2,1)} fusion(bf16[12,4,256]{2,1,0:T(4,128)(2,1)} %bitcast.31, s32[1024]{0:T(1024)} %pad_clamp_fusion), kind=kCustom, calls=%fused_computation.1 | custom fusion | bytes 12300 | tf_op jit(solution)/shard_map/jit(_take)/gather | solution.py:289
  (94 shorter events, 9.3 us)
Async XLA Ops:
  7.2 12.4 %collective-permute-start.2 = (bf16[16,1536]{1,0:T(8,128)(2,1)}, bf16[16,1536]{1,0:T(8,128)(2,1)S(1)}, u32[]{:S(2)}, u32[]{:S(2)}) collective-permute-start(bf16[16,1536]{1,0:T(8,128)(2,1)} %bitcast.68), channel_id=1, source_target_pairs={{0,128},{128,0},{1,129},{129,1},{2,130},{130,2},{3,131},{131,3},{4... | collective-permute-start | bytes 147464 | tf_op jit(solution)/shard_map/ppermute | solution.py:201
  14.0 5.3 %copy-start.18 = (s32[4,3]{1,0:T(4,128)S(1)}, s32[4,3]{1,0:T(4,128)}, u32[]{:S(2)}) copy-start(s32[4,3]{1,0:T(4,128)} %param.16) | copy-start | bytes 148
  14.0 5.6 %copy-start.15 = (bf16[1,16,1536]{2,1,0:T(8,128)(2,1)S(1)}, bf16[1,16,1536]{2,1,0:T(8,128)(2,1)}, u32[]{:S(2)}) copy-start(bf16[1,16,1536]{2,1,0:T(8,128)(2,1)} %param.11) | copy-start | bytes 147460
  15.0 33.5 %all-to-all-start = ((bf16[4,112,832]{2,1,0:T(8,128)(2,1)}), bf16[4,112,832]{2,1,0:T(8,128)(2,1)S(1)}, u32[]{:S(2)}, u32[]{:S(2)}) async-start(bf16[4,112,832]{2,1,0:T(8,128)(2,1)} %pad_maximum_fusion.1), calls=%async_computation | async-start | bytes 1605632 | tf_op jit(solution)/shard_map/all_to_all | solution.py:207
  19.3 129.0 %all-gather.2.cloned.1.call-start = ((), (), s32[]{:S(2)}) async-start(), calls=%async_computation.5 | async-start | bytes 3538944 | tf_op jit(solution)/shard_map/all_gather | solution.py:220
  19.5 17.1 %copy-start.10 = (bf16[1536,384]{1,0:T(8,128)(2,1)S(1)}, bf16[1536,384]{1,0:T(8,128)(2,1)}, u32[]{:S(2)}) copy-start(bf16[1536,384]{1,0:T(8,128)(2,1)} %param.14) | copy-start | bytes 3538948
  19.6 14.7 %collective-permute-start.3 = (bf16[2,16,1536]{2,1,0:T(8,128)(2,1)S(1)}, bf16[2,16,1536]{2,1,0:T(8,128)(2,1)S(1)}, u32[]{:S(2)}, u32[]{:S(2)}) collective-permute-start(bf16[2,16,1536]{2,1,0:T(8,128)(2,1)S(1)} %maximum_select_fusion.3), channel_id=1, source_target_pairs={{0,32},{32,64},{64,96},{96,0},{1,33},{33,65},{65,97},{97,1},{2,34}... | collective-permute-start | bytes 294920 | tf_op jit(solution)/shard_map/ppermute | solution.py:212
  23.7 12.0 %collective-permute-start.4 = (bf16[2,16,1536]{2,1,0:T(8,128)(2,1)S(1)}, bf16[2,16,1536]{2,1,0:T(8,128)(2,1)S(1)}, u32[]{:S(2)}, u32[]{:S(2)}) collective-permute-start(bf16[2,16,1536]{2,1,0:T(8,128)(2,1)S(1)} %maximum_select_fusion.3), channel_id=1, source_target_pairs={{0,64},{32,96},{64,0},{96,32},{1,65},{33,97},{65,1},{97,33},{2,66}... | collective-permute-start | bytes 294920 | tf_op jit(solution)/shard_map/ppermute | solution.py:212
  28.2 7.5 %collective-permute-start.5 = (bf16[2,16,1536]{2,1,0:T(8,128)(2,1)S(1)}, bf16[2,16,1536]{2,1,0:T(8,128)(2,1)S(1)}, u32[]{:S(2)}, u32[]{:S(2)}) collective-permute-start(bf16[2,16,1536]{2,1,0:T(8,128)(2,1)S(1)} %maximum_select_fusion.3), channel_id=1, source_target_pairs={{0,96},{32,0},{64,32},{96,64},{1,97},{33,1},{65,33},{97,65},{2,98}... | collective-permute-start | bytes 294920 | tf_op jit(solution)/shard_map/ppermute | solution.py:212
  35.7 0.8 copy-start.13
  39.0 2.4 %copy-start.12 = (bf16[1536,2,64]{0,2,1:T(8,128)(2,1)S(1)}, bf16[1536,2,64]{0,2,1:T(8,128)(2,1)}, u32[]{:S(2)}) copy-start(bf16[1536,2,64]{0,2,1:T(8,128)(2,1)} %slice.78) | copy-start | bytes 1179652
  39.0 3.4 %copy-start.1 = (bf16[512,512]{1,0:T(8,128)(2,1)S(1)}, bf16[512,512]{1,0:T(8,128)(2,1)}, u32[]{:S(2)}) copy-start(bf16[512,512]{1,0:T(8,128)(2,1)} %kv_ref.3) | copy-start | bytes 1572868
  41.4 3.2 %copy-start.19 = (s32[1,12]{1,0:T(1,128)S(1)}, s32[1,12]{1,0:T(1,128)}, u32[]{:S(2)}) copy-start(s32[1,12]{1,0:T(1,128)} %param.17) | copy-start | bytes 148
  47.6 0.9 copy-start.16
  47.6 0.9 copy-start.17
  48.6 19.3 %collective-permute-start = (bf16[1,3,4,2112]{3,2,1,0:T(4,128)(2,1)S(1)}, bf16[1,3,4,2112]{3,2,1,0:T(4,128)(2,1)S(1)}, u32[]{:S(2)}, u32[]{:S(2)}) collective-permute-start(bf16[1,3,4,2112]{3,2,1,0:T(4,128)(2,1)S(1)} %maximum_bitcast_fusion), channel_id=1, source_target_pairs={{0,1},{1,0},{2,3},{3,2},{4,5},{5,4},{6,7},{7,6},{8,9},{9,8},{10,11... | collective-permute-start | bytes 152072 | tf_op jit(solution)/shard_map/ppermute | solution.py:255
  52.2 35.5 %all-to-all-start.1 = ((f32[16,16,576]{2,1,0:T(8,128)}), f32[16,16,576]{2,1,0:T(8,128)S(1)}, u32[]{:S(2)}, u32[]{:S(2)}) async-start(f32[16,16,576]{2,1,0:T(8,128)} %bitcast.62), calls=%async_computation.1 | async-start | bytes 1310720 | tf_op jit(solution)/shard_map/all_to_all | solution.py:232
  68.0 18.0 %collective-permute-start.1 = (bf16[2,3,4,2112]{3,2,1,0:T(4,128)(2,1)S(1)}, bf16[2,3,4,2112]{3,2,1,0:T(4,128)(2,1)S(1)}, u32[]{:S(2)}, u32[]{:S(2)}) collective-permute-start(bf16[2,3,4,2112]{3,2,1,0:T(4,128)(2,1)S(1)} %maximum_select_fusion.1), channel_id=1, source_target_pairs={{0,2},{1,3},{2,0},{3,1},{4,6},{5,7},{6,4},{7,5},{8,10},{9,11},{10,... | collective-permute-start | bytes 304136 | tf_op jit(solution)/shard_map/ppermute | solution.py:255
  86.9 17.7 %copy-start.14 = (bf16[12,2112]{1,0:T(8,128)(2,1)}, bf16[12,2112]{1,0:T(8,128)(2,1)S(1)}, u32[]{:S(2)}) copy-start(bf16[12,2112]{1,0:T(8,128)(2,1)S(1)} %reshape.203) | copy-start | bytes 152068
  87.7 0.8 copy-start.11
  90.6 23.5 %all-to-all-start.2 = ((bf16[16,16,640]{2,1,0:T(8,128)(2,1)}), bf16[16,16,640]{2,1,0:T(8,128)(2,1)}, u32[]{:S(2)}, u32[]{:S(2)}) async-start(bf16[16,16,640]{2,1,0:T(8,128)(2,1)} %norm_rows.1), calls=%async_computation.2 | async-start | bytes 655360 | tf_op jit(solution)/shard_map/all_to_all | solution.py:236
  116.2 19.9 %all-to-all-start.3 = ((bf16[4,256,640]{2,1,0:T(8,128)(2,1)}), bf16[4,256,640]{2,1,0:T(8,128)(2,1)S(1)}, u32[]{:S(2)}, u32[]{:S(2)}) async-start(bf16[4,256,640]{2,1,0:T(8,128)(2,1)} %broadcast_in_dim.131), calls=%async_computation.3 | async-start | bytes 2621440 | tf_op jit(solution)/shard_map/all_to_all | solution.py:45
  136.2 1.0 copy-start.2
  137.2 0.8 copy-start.4
  138.0 0.7 copy-start.5
  138.7 0.7 copy-start.6
  139.4 0.7 copy-start.7
  141.2 0.6 copy-start.8
  143.2 18.9 %all-to-all-start.4 = ((bf16[4,3,4,256]{3,2,1,0:T(4,128)(2,1)}), bf16[4,3,4,256]{3,2,1,0:T(4,128)(2,1)}, u32[]{:S(2)}, u32[]{:S(2)}) async-start(bf16[4,3,4,256]{3,2,1,0:T(4,128)(2,1)} %broadcast_in_dim.135), calls=%async_computation.4 | async-start | bytes 49152 | tf_op jit(solution)/shard_map/all_to_all | solution.py:45
  148.2 1.9 %copy-start = (bf16[1024,1536]{1,0:T(8,128)(2,1)S(1)}, bf16[1024,1536]{1,0:T(8,128)(2,1)}, u32[]{:S(2)}) copy-start(bf16[1024,1536]{1,0:T(8,128)(2,1)} %all-gather.2.cloned.1.call-done) | copy-start | bytes 9437188
  150.1 3.8 %copy-start.3 = (bf16[512,512]{1,0:T(8,128)(2,1)S(1)}, bf16[512,512]{1,0:T(8,128)(2,1)}, u32[]{:S(2)}) copy-start(bf16[512,512]{1,0:T(8,128)(2,1)} %kv_ref.3) | copy-start | bytes 1572868
  150.1 3.8 %copy-start.9 = (s32[8]{0:T(128)S(1)}, s32[8]{0:T(128)}, u32[]{:S(2)}) copy-start(s32[8]{0:T(128)} %select_reduce_fusion.2.start_ref) | copy-start | bytes 100
Sparse Core Ops, SparseCore 0:
  36.6 63.3 all-gather.1

commit v4 on v3

v4 whole, which is shorter than its diff:
```python
import math

import jax
import jax.numpy as jnp
import numpy as np
from jax import lax
from jax.experimental import pallas as pl
from jax.experimental.pallas import tpu as pltpu
from jax.sharding import Mesh, PartitionSpec as P

KVL = 512
NOPE = 128
ROPE = 64
VD = 128
BLK = 128
NREQ = 3
STEPS = 4
REACH = 4
NREP = 4
NX = 4
HEADS = 2
PAD = 16
TABLE = 640
WIDE = KVL + 2 * ROPE
START, LENGTH, BASE, PLACE, FIRST, SOURCE, SLOT, BLOCK = 0, 3, 6, 8, 16, 24, 28, 32

SIGMA = (1.0 + 0.1 * math.log(40.0)) ** 2 * (NOPE + ROPE) ** (-0.5)
bf16 = jnp.bfloat16
f32 = jnp.float32
i32 = jnp.int32
VMEM_LIMIT = 40 * 1024 * 1024


def rotary_table():
    half = ROPE // 2
    frequency = np.float32(10000.0) ** (-np.arange(half, dtype=np.float32) * np.float32(2.0 / ROPE))
    angles = np.arange(TABLE, dtype=np.float32)[:, None] * frequency.astype(np.float32)
    cos_part, sin_part = np.cos(angles), np.sin(angles)
    return np.concatenate([cos_part] * 4, axis=1), np.concatenate([-sin_part, sin_part] * 2, axis=1)


def rotate(u, cos_part, sin_part):
    lane = lax.broadcasted_iota(i32, u.shape, 1)
    swapped = jnp.where(lane % ROPE < ROPE // 2, pltpu.roll(u, 96, 1), pltpu.roll(u, 32, 1))
    return u * cos_part + swapped * sin_part


def split_heads(u):
    a, b, c = u[:, :NOPE], u[:, NOPE : 2 * NOPE], u[:, 2 * NOPE :]
    low = lax.broadcasted_iota(i32, a.shape, 1) < ROPE
    return a, jnp.where(low, pltpu.roll(b, ROPE, 1), pltpu.roll(c, ROPE, 1)), jnp.where(low, b, c)


def spread(a, axes, count):
    copies = jnp.broadcast_to(a[None], (count,) + a.shape)
    return lax.all_to_all(copies, axes, 0, 0, tiled=True)


def shift(count, d):
    return [(i, (i + d) % count) for i in range(count)]


def dot_t(a, b):
    return lax.dot_general(a, b, (((1,), (1,)), ((), ())), preferred_element_type=f32)


def layout_kernel(ids_ref, req_ref, slot_ref, out_ref):
    rep, x, yh, yz = ids_ref[0], ids_ref[1], ids_ref[2], ids_ref[3]
    lengths = [req_ref[rep, r] for r in range(NREQ)]
    starts = [0, lengths[0], lengths[0] + lengths[1]]

    def start_of(block):
        return jnp.where(block >= starts[2], starts[2], jnp.where(block >= starts[1], starts[1], 0))

    for r in range(NREQ):
        out_ref[START + r] = starts[r] * BLK
        out_ref[LENGTH + r] = lengths[r] * BLK
        slot = slot_ref[0, rep * NREQ + r]
        out_ref[SLOT + r] = (lax.div(slot, NREQ) ^ rep) * NREQ + lax.rem(slot, NREQ)
        source = 0
        for m in range(NREP * NREQ):
            source += jnp.where(slot_ref[0, m] == rep * NREQ + r, m, 0)
        out_ref[SOURCE + r] = lax.div(source, NREQ) * PAD + lax.rem(source, NREQ) * STEPS
    out_ref[BASE] = x * 2 * BLK + yz * PAD - start_of(x * 2 + lax.div(yz, 8)) * BLK
    for i in range(8):
        out_ref[PLACE + i] = i - start_of(i)
        out_ref[FIRST + i] = start_of(i) * BLK
        out_ref[BLOCK + i] = lax.rem(x + NX - i % NX, NX) * 2 + (yh ^ (i // NX))


SMEM = pl.BlockSpec(memory_space=pltpu.SMEM)
VMEM = pl.BlockSpec(memory_space=pltpu.VMEM)


def request_layout(ids, req_blocks, dest_slot):
    return pl.pallas_call(
        layout_kernel,
        in_specs=[SMEM] * 3,
        out_specs=SMEM,
        out_shape=jax.ShapeDtypeStruct((64,), i32),
        cost_estimate=pl.CostEstimate(flops=1000, bytes_accessed=1000, transcendentals=0),
        name="request_layout",
    )(ids, req_blocks, dest_slot)


def pack_kernel(hidden_ref, down_ref, out_ref):
    features = hidden_ref.shape[1]
    per_x = hidden_ref.shape[0] // NX
    row = lax.broadcasted_iota(i32, (features, features), 0)
    column = lax.broadcasted_iota(i32, (features, features), 1)
    unit = jnp.where(row == column, 1.0, 0.0).astype(bf16)
    for i in range(NX):
        out_ref[i, :, :per_x] = dot_t(unit, hidden_ref[i * per_x : (i + 1) * per_x, :]).astype(bf16)
        out_ref[i, :, per_x:] = down_ref[...]


def pack(hidden, kv_down):
    rows, features = hidden.shape
    return pl.pallas_call(
        pack_kernel,
        in_specs=[VMEM] * 2,
        out_specs=VMEM,
        out_shape=jax.ShapeDtypeStruct((NX, features, rows // NX + kv_down.shape[1]), bf16),
        cost_estimate=pl.CostEstimate(flops=26_000_000, bytes_accessed=1_200_000, transcendentals=0),
        name="pack_hidden",
    )(hidden, kv_down)


def norm_kernel(layout_ref, pieces_ref, gain_ref, cos_ref, sin_ref, out_ref):
    latent = jnp.sum(pieces_ref[...].astype(f32), axis=0)
    content = latent[:, :KVL]
    scale = lax.rsqrt(jnp.mean(content * content, axis=1, keepdims=True) + 1e-06)
    content = (content * scale * gain_ref[...]).astype(bf16)
    at = pl.ds(pl.multiple_of(layout_ref[BASE], PAD), PAD)
    pe = jnp.concatenate([latent[:, KVL:]] * 2, axis=1)
    pe = rotate(pe, cos_ref[at, :], sin_ref[at, :]).astype(bf16)
    for i in range(out_ref.shape[0]):
        out_ref[i, :, :KVL] = content
        out_ref[i, :, KVL:] = pe


def norm_rows(layout, pieces, gain, cos_part, sin_part):
    count, chunk, _ = pieces.shape
    return pl.pallas_call(
        norm_kernel,
        in_specs=[SMEM] + [VMEM] * 4,
        out_specs=VMEM,
        out_shape=jax.ShapeDtypeStruct((count, chunk, WIDE), bf16),
        cost_estimate=pl.CostEstimate(flops=1_000_000, bytes_accessed=1_000_000, transcendentals=16),
        name="norm_rows",
    )(layout, pieces, gain, cos_part, sin_part)


def query_kernel(layout_ref, cq_ref, w_ref, cos_ref, sin_ref, out_ref):
    rows = cq_ref[...].reshape(BLK, -1)
    u = jnp.dot(rows, w_ref[...], preferred_element_type=f32)
    first, second, pe = split_heads(u)
    pe = rotate(pe, cos_ref[...], sin_ref[...])
    low = lax.broadcasted_iota(i32, pe.shape, 1) < ROPE
    out_ref[0, :, :NOPE] = first.astype(bf16)
    out_ref[0, :, NOPE:] = jnp.where(low, pe, 0.0).astype(bf16)
    out_ref[1, :, :NOPE] = second.astype(bf16)
    out_ref[1, :, NOPE:] = jnp.where(low, 0.0, pe).astype(bf16)


def project_queries(layout, cq, weights, cos_part, sin_part):
    width = cq.shape[-1]
    table = pl.BlockSpec((BLK, 2 * ROPE), lambda i, place: (place[PLACE + i], 0))
    return pl.pallas_call(
        query_kernel,
        grid_spec=pltpu.PrefetchScalarGridSpec(
            num_scalar_prefetch=1,
            grid=(8,),
            in_specs=[
                pl.BlockSpec((8, 1, PAD, width), lambda i, place: (0, place[BLOCK + i], 0, 0)),
                pl.BlockSpec(weights.shape, lambda i, place: (0, 0)),
                table,
                table,
            ],
            out_specs=pl.BlockSpec((HEADS, BLK, 2 * NOPE), lambda i, place: (0, i, 0)),
        ),
        out_shape=jax.ShapeDtypeStruct((HEADS, 8 * BLK, 2 * NOPE), bf16),
        compiler_params=pltpu.CompilerParams(vmem_limit_bytes=VMEM_LIMIT),
        cost_estimate=pl.CostEstimate(flops=1_200_000_000, bytes_accessed=5_000_000, transcendentals=0),
        name="project_queries",
    )(layout, cq, weights, cos_part, sin_part)


def prepare_kernel(layout_ref, rows_ref, w_ref, kv_ref, cos_ref, sin_ref, out_ref, in_ref, cos_at, sin_at):
    query_latent = w_ref.shape[0]
    in_ref[...] = jnp.zeros_like(in_ref)
    cos_at[...] = jnp.zeros_like(cos_at)
    sin_at[...] = jnp.zeros_like(sin_at)
    for r in range(NREQ):
        here = slice(r * STEPS, (r + 1) * STEPS)
        in_ref[here, :] = rows_ref[layout_ref[SLOT + r]].astype(f32)
        at = pl.ds(pl.multiple_of(layout_ref[LENGTH + r], BLK), 8)
        cos_at[here, :] = cos_ref[at, :][:STEPS]
        sin_at[here, :] = sin_ref[at, :][:STEPS]
    cos_part, sin_part = cos_at[...], sin_at[...]
    rows = in_ref[:, :query_latent].astype(bf16)
    u = jnp.dot(rows, w_ref[...], preferred_element_type=f32).astype(bf16).astype(f32)
    first, second, pe = split_heads(u)
    pe = rotate(pe, cos_part, sin_part)
    low = lax.broadcasted_iota(i32, pe.shape, 1) < ROPE
    for h, plain in enumerate((first, second)):
        here = slice(h * PAD, (h + 1) * PAD)
        base = h * (NOPE + VD)
        out_ref[here, :KVL] = dot_t(plain.astype(bf16), kv_ref[:, base : base + NOPE]).astype(bf16)
        out_ref[here, KVL:] = jnp.where(low == (h == 0), pe, 0.0).astype(bf16)
    new = slice(HEADS * PAD, (HEADS + 1) * PAD)
    out_ref[new, :KVL] = in_ref[:, query_latent : query_latent + KVL].astype(bf16)
    new_pe = jnp.concatenate([in_ref[:, query_latent + KVL :]] * 2, axis=1)
    out_ref[new, KVL:] = rotate(new_pe, cos_part, sin_part).astype(bf16)


def prepare_decode(layout, rows, q_up, kv_up, cos_part, sin_part):
    return pl.pallas_call(
        prepare_kernel,
        in_specs=[SMEM] + [VMEM] * 5,
        out_specs=VMEM,
        out_shape=jax.ShapeDtypeStruct(((HEADS + 1) * PAD, WIDE), bf16),
        scratch_shapes=[
            pltpu.VMEM((PAD, rows.shape[-1]), f32),
            pltpu.VMEM((PAD, 2 * ROPE), f32),
            pltpu.VMEM((PAD, 2 * ROPE), f32),
        ],
        compiler_params=pltpu.CompilerParams(vmem_limit_bytes=VMEM_LIMIT),
        cost_estimate=pl.CostEstimate(flops=30_000_000, bytes_accessed=2_500_000, transcendentals=0),
        name="prepare_decode",
    )(layout, rows, q_up, kv_up, cos_part, sin_part)


def decode_kernel(layout_ref, ready_ref, cache_ref, kv_ref, out_ref):
    query = ready_ref[: HEADS * PAD, :]
    fresh = ready_ref[HEADS * PAD :, :]
    old = dot_t(query, cache_ref[...]) * SIGMA
    new = dot_t(query, fresh) * SIGMA
    request = lax.broadcasted_iota(i32, (HEADS * PAD, 1), 0) % PAD // STEPS

    def per_request(values):
        return jnp.where(request == 0, values[0], jnp.where(request == 1, values[1], values[2]))

    low = per_request([layout_ref[START + r] for r in range(NREQ)])
    high = per_request([layout_ref[START + r] + layout_ref[LENGTH + r] for r in range(NREQ)])
    column = lax.broadcasted_iota(i32, old.shape, 1)
    old = jnp.where((column >= low) & (column < high), old, -1e30)
    step = lax.broadcasted_iota(i32, new.shape, 0) % PAD
    other = lax.broadcasted_iota(i32, new.shape, 1)
    new = jnp.where((step // STEPS == other // STEPS) & (other <= step), new, -1e30)
    top = jnp.maximum(jnp.max(old, axis=1, keepdims=True), jnp.max(new, axis=1, keepdims=True))
    old = jnp.exp(old - top)
    new = jnp.exp(new - top)
    inverse = 1.0 / (jnp.sum(old, axis=1, keepdims=True) + jnp.sum(new, axis=1, keepdims=True))
    old = (old * inverse).astype(bf16)
    new = (new * inverse).astype(bf16)
    mixture = (
        jnp.dot(old, cache_ref[:, :KVL], preferred_element_type=f32)
        + jnp.dot(new, fresh[:, :KVL], preferred_element_type=f32)
    ).astype(bf16)
    for h in range(HEADS):
        base = h * (NOPE + VD) + NOPE
        value = jnp.dot(
            mixture[h * PAD : (h + 1) * PAD], kv_ref[:, base : base + VD], preferred_element_type=f32
        ).astype(bf16)
        for i in range(NREP):
            out_ref[i, :, h * VD : (h + 1) * VD] = value


def decode(layout, ready, cache, kv_up):
    return pl.pallas_call(
        decode_kernel,
        in_specs=[SMEM] + [VMEM] * 3,
        out_specs=VMEM,
        out_shape=jax.ShapeDtypeStruct((NREP, PAD, HEADS * VD), bf16),
        compiler_params=pltpu.CompilerParams(vmem_limit_bytes=VMEM_LIMIT),
        cost_estimate=pl.CostEstimate(flops=100_000_000, bytes_accessed=2_000_000, transcendentals=40_000),
        name="decode_attention",
    )(layout, ready, cache, kv_up)


def select_kernel(layout_ref, pool_ref, out_ref):
    pool = pool_ref[...].reshape(NREP * PAD, -1)
    for r in range(NREQ):
        row = lax.broadcasted_iota(i32, (8, NREP * PAD), 0)
        column = lax.broadcasted_iota(i32, (8, NREP * PAD), 1)
        pick = jnp.where(column == layout_ref[SOURCE + r] + row, 1.0, 0.0).astype(bf16)
        out_ref[r] = jnp.dot(pick, pool, preferred_element_type=f32)[:STEPS].astype(bf16)


def select(layout, pool):
    return pl.pallas_call(
        select_kernel,
        in_specs=[SMEM, VMEM],
        out_specs=VMEM,
        out_shape=jax.ShapeDtypeStruct((NREQ, STEPS, HEADS * VD), bf16),
        cost_estimate=pl.CostEstimate(flops=1_000_000, bytes_accessed=50_000, transcendentals=0),
        name="select_slots",
    )(layout, pool)


def prefill_kernel(layout_ref, q_ref, cache_ref, kv_ref, out_ref, key_ref, value_ref):
    for j in range(4):
        rows = slice(j * 2 * BLK, (j + 1) * 2 * BLK)
        wide = jnp.dot(cache_ref[rows, :KVL], kv_ref[...], preferred_element_type=f32).astype(bf16)
        for h in range(HEADS):
            base = h * (NOPE + VD)
            key_ref[h, rows, :NOPE] = wide[:, base : base + NOPE]
            key_ref[h, rows, NOPE:] = cache_ref[rows, KVL:]
            value_ref[h, rows, :] = wide[:, base + NOPE : base + NOPE + VD]
    for i in range(8):
        first = max(0, i - REACH + 1) * BLK
        last = (i + 1) * BLK
        shape = (BLK, last - first)
        column = lax.broadcasted_iota(i32, shape, 1) + first
        row = lax.broadcasted_iota(i32, shape, 0) + i * BLK
        ok = (column >= layout_ref[FIRST + i]) & (column <= row)
        scores = [
            dot_t(q_ref[h, i * BLK : last, :], key_ref[h, first:last, :]) * SIGMA for h in range(HEADS)
        ]
        scores = [jnp.where(ok, s, -1e30) for s in scores]
        weights = [jnp.exp(s - jnp.max(s, axis=1, keepdims=True)) for s in scores]
        weights = [(w * (1.0 / jnp.sum(w, axis=1, keepdims=True))).astype(bf16) for w in weights]
        for h in range(HEADS):
            out_ref[i * BLK : last, h * VD : (h + 1) * VD] = jnp.dot(
                weights[h], value_ref[h, first:last, :], preferred_element_type=f32
            ).astype(bf16)


def prefill(layout, queries, cache, kv_up):
    rows = cache.shape[0]
    return pl.pallas_call(
        prefill_kernel,
        in_specs=[SMEM] + [VMEM] * 3,
        out_specs=VMEM,
        out_shape=jax.ShapeDtypeStruct((rows, HEADS * VD), bf16),
        scratch_shapes=[
            pltpu.VMEM((HEADS, rows, 2 * NOPE), bf16),
            pltpu.VMEM((HEADS, rows, VD), bf16),
        ],
        compiler_params=pltpu.CompilerParams(vmem_limit_bytes=VMEM_LIMIT),
        cost_estimate=pl.CostEstimate(flops=1_500_000_000, bytes_accessed=4_000_000, transcendentals=1_000_000),
        name="prefill_attention",
    )(layout, queries, cache, kv_up)


def body(hidden, comp_query, kv_down, kv_gain, q_up, kv_up, req_blocks, dest_slot, dec_query, dec_latent):
    ids = jnp.stack(
        [lax.axis_index("rep"), lax.axis_index("x"), lax.axis_index("yh"), lax.axis_index(("yh", "z"))]
    ).astype(i32)
    rows, features = hidden.shape[1:]
    per_x = rows // NX
    chunk = per_x // 16
    cos_part, sin_part = rotary_table()

    own = comp_query[0]
    other = lax.ppermute(own, "yh", shift(2, 1))
    packed = lax.all_to_all(pack(hidden[0], kv_down), "x", 0, 0, tiled=True)
    layout = request_layout(ids, req_blocks, dest_slot)
    pair = jnp.stack([own, other])
    line = [pair] + [lax.ppermute(pair, "x", shift(NX, d)) for d in range(1, NX)]
    cq = lax.all_gather(jnp.concatenate(line).reshape(BLK, -1), "z", axis=0, tiled=True)

    packed, dec_query, dec_latent = lax.optimization_barrier((packed, dec_query, dec_latent))
    packed = packed.reshape(NX * features, -1)
    partial = lax.dot_general(
        packed[:, :per_x], packed[:, per_x:], (((0,), (0,)), ((), ())), preferred_element_type=f32
    )
    pieces = lax.all_to_all(partial.reshape(16, chunk, -1), ("yh", "z"), 0, 0, tiled=True)
    copies = norm_rows(layout, pieces, kv_gain[None, :], cos_part, sin_part)
    cache = lax.all_to_all(copies, ("yh", "z"), 0, 0, tiled=True).reshape(per_x, -1)
    cache = spread(cache, "x", NX).reshape(rows, -1)

    rep_in = jnp.concatenate([dec_query, dec_latent], axis=2)
    for d in (1, 2):
        met = lax.ppermute(rep_in, "rep", [(i, i ^ d) for i in range(NREP)])
        rep_in = jnp.concatenate([rep_in, met])
    ready = prepare_decode(layout, rep_in, q_up, kv_up, cos_part, sin_part)

    queries = project_queries(layout, cq.reshape(8, 8, PAD, -1), q_up, cos_part, sin_part)
    cache, queries, ready = lax.optimization_barrier((cache, queries, ready))
    result = decode(layout, ready, cache, kv_up)
    pool = lax.all_to_all(result, "rep", 0, 0, tiled=True)
    prefill_out = prefill(layout, queries, cache, kv_up)[None]
    pool, prefill_out = lax.optimization_barrier((pool, prefill_out))
    return prefill_out, select(layout, pool)


def solution(mesh):
    fine = Mesh(mesh.devices.reshape(2, 2, 4, 8, 4), ("section", "yh", "x", "z", "rep"))
    tp = ("yh", "x", "z")
    group = ("section", "rep")
    in_specs = (
        P(group, None, tp),
        P(group, tp, None),
        P(tp, None),
        P(),
        P(None, tp),
        P(None, tp),
        P("section", None),
        P("section", None),
        P(group, None, None),
        P(group, None, None),
    )
    out_specs = (P(group, None, tp), P(group, None, tp))
    return jax.shard_map(body, mesh=fine, in_specs=in_specs, out_specs=out_specs, check_vma=False)
```

time: 173 us -> 167 us (0.965)
  local copies, waits for them, and re-layouts: 26.4 us -> 10 us
  blocking collectives: 0 us -> 14.5 us
  other arithmetic: 11.7 us -> 1.63 us
  Pallas kernels: 15.1 us -> 21.2 us
  waiting for transfers between devices: 37.6 us -> 42 us
  starting transfers between devices: 62.4 us -> 58.9 us
  matrix products: 3.22 us -> 1.21 us
    all_to_all x1, waiting for transfers between devices: 0.01 us -> 15.4 us  [body(): lax.all_to_all(partial.reshape(16, chunk, -1), ('yh', 'z'), 0, 0, tiled=T...]
    all_to_all x0 -> x1, blocking collectives: none -> 14.5 us  [body(): packed = lax.all_to_all(pack(hidden[0], kv_down), 'x', 0, 0, tiled=True)]
    all_to_all x2 -> x1, waiting for transfers between devices: 10.4 us -> 0.01 us  [spread(): return lax.all_to_all(copies, axes, 0, 0, tiled=True)]
    ppermute x2, waiting for transfers between devices: 15.3 us -> 7.07 us  [body(): met = lax.ppermute(rep_in, 'rep', [(i, i ^ d) for i in range(NREP)])]
    pallas_call x4 -> x8, Pallas kernels: 15.1 us -> 21.2 us  [the longest x1 5.91 us: prefill(): pl.pallas_call(prefill_kernel, in_specs=[SMEM] + [VMEM] * 3, out_specs=VM...]
    ppermute x1, waiting for transfers between devices: 0.01 us -> 5.09 us  [body(): other = lax.ppermute(own, 'yh', shift(2, 1))]
    concatenate x5 -> x2, other arithmetic: 5.25 us -> 0.22 us  [body(): rep_in = jnp.concatenate([rep_in, met])]
    all_to_all x2 -> x1, starting transfers between devices: 8.63 us -> 3.68 us  [spread(): return lax.all_to_all(copies, axes, 0, 0, tiled=True)]
  transfers between devices with their start and end apart: 12 -> 11, of which waited for: 5 -> 6; matrix products, arithmetic and copies ran while one was open for 18% -> 3% of each run, Pallas kernels for 9% -> 11%
where the time goes in v4:
time: 167 us; the launch traced here: 164 us
  starting transfers between devices  58.9 us (35%)
  waiting for transfers between devices  42 us (25%)
  Pallas kernels  21.2 us (13%)
  blocking collectives  14.5 us (9%)
  between operations  14.3 us (9%)
  local copies, waits for them, and re-layouts  10 us (6%)
    all_to_all x1, starting transfers between devices, body(): lax.all_to_all(partial.reshape(16, chunk, -1), ('yh', 'z'), 0, 0, tiled=T...  15.7 us
    all_to_all x1, waiting for transfers between devices, body(): lax.all_to_all(partial.reshape(16, chunk, -1), ('yh', 'z'), 0, 0, tiled=T...  15.4 us
    all_to_all x1, blocking collectives, body(): packed = lax.all_to_all(pack(hidden[0], kv_down), 'x', 0, 0, tiled=True)  14.5 us
    all_to_all x1, starting transfers between devices, body(): lax.all_to_all(copies, ('yh', 'z'), 0, 0, tiled=True).reshape(per_x, -1)  11 us
    ppermute x3, starting transfers between devices, body(): lax.ppermute(pair, 'x', shift(NX, d))  10.2 us
    all_to_all x1, waiting for transfers between devices, body(): lax.all_to_all(copies, ('yh', 'z'), 0, 0, tiled=True).reshape(per_x, -1)  9.5 us
    unnamed x38, local copies, waits for them, and re-layouts  8.86 us
    ppermute x2, starting transfers between devices, body(): met = lax.ppermute(rep_in, 'rep', [(i, i ^ d) for i in range(NREP)])  7.52 us
  transfers between devices with their start and end apart: 11, of which 6 were waited for; matrix products, arithmetic and copies ran while one was open for 3% of the time, Pallas kernels for 11%

profile of v4, /device:TPU:56, one launch (start us, length us, event | category | flops | bytes accessed | tf_op | source)
XLA Modules:
  0.0 163.7 jit_solution(11574869329553237094)
XLA Ops:
  7.2 0.0 all-gather.2.cloned.1.call-start
  7.2 4.8 %collective-permute-start = (bf16[16,1536]{1,0:T(8,128)(2,1)}, bf16[16,1536]{1,0:T(8,128)(2,1)S(1)}, u32[]{:S(2)}, u32[]{:S(2)}) collective-permute-start(bf16[16,1536]{1,0:T(8,128)(2,1)} %bitcast.23), channel_id=1, source_target_pairs={{0,128},{128,0},{1,129},{129,1},{2,130},{130,2},{3,131},{131,3},{4... | collective-permute-start | bytes 147464 | tf_op jit(solution)/shard_map/ppermute | solution.py:357
  12.1 0.8 constant_dynamic-update-slice_fusion.4
  12.9 5.1 %collective-permute-done = bf16[16,1536]{1,0:T(8,128)(2,1)S(1)} collective-permute-done((bf16[16,1536]{1,0:T(8,128)(2,1)}, bf16[16,1536]{1,0:T(8,128)(2,1)S(1)}, u32[]{:S(2)}, u32[]{:S(2)}) %collective-permute-start) | collective-permute-done | bytes 49184 | tf_op jit(solution)/shard_map/ppermute | solution.py:357
  18.0 0.8 pad_maximum_fusion.2
  18.8 4.7 %collective-permute-start.3 = (bf16[2,16,1536]{2,1,0:T(8,128)(2,1)S(1)}, bf16[2,16,1536]{2,1,0:T(8,128)(2,1)S(1)}, u32[]{:S(2)}, u32[]{:S(2)}) collective-permute-start(bf16[2,16,1536]{2,1,0:T(8,128)(2,1)S(1)} %pad_maximum_fusion.2), channel_id=1, source_target_pairs={{0,96},{32,0},{64,32},{96,64},{1,97},{33,1},{65,33},{97,65},{2,98}... | collective-permute-start | bytes 294920 | tf_op jit(solution)/shard_map/ppermute | solution.py:361
  23.5 2.7 %collective-permute-start.2 = (bf16[2,16,1536]{2,1,0:T(8,128)(2,1)S(1)}, bf16[2,16,1536]{2,1,0:T(8,128)(2,1)S(1)}, u32[]{:S(2)}, u32[]{:S(2)}) collective-permute-start(bf16[2,16,1536]{2,1,0:T(8,128)(2,1)S(1)} %pad_maximum_fusion.2), channel_id=1, source_target_pairs={{0,64},{32,96},{64,0},{96,32},{1,65},{33,97},{65,1},{97,33},{2,66}... | collective-permute-start | bytes 294920 | tf_op jit(solution)/shard_map/ppermute | solution.py:361
  26.2 2.8 %collective-permute-start.1 = (bf16[2,16,1536]{2,1,0:T(8,128)(2,1)S(1)}, bf16[2,16,1536]{2,1,0:T(8,128)(2,1)S(1)}, u32[]{:S(2)}, u32[]{:S(2)}) collective-permute-start(bf16[2,16,1536]{2,1,0:T(8,128)(2,1)S(1)} %pad_maximum_fusion.2), channel_id=1, source_target_pairs={{0,32},{32,64},{64,96},{96,0},{1,33},{33,65},{65,97},{97,1},{2,34}... | collective-permute-start | bytes 294920 | tf_op jit(solution)/shard_map/ppermute | solution.py:361
  29.0 4.9 %collective-permute-done.1 = bf16[2,16,1536]{2,1,0:T(8,128)(2,1)S(1)} collective-permute-done((bf16[2,16,1536]{2,1,0:T(8,128)(2,1)S(1)}, bf16[2,16,1536]{2,1,0:T(8,128)(2,1)S(1)}, u32[]{:S(2)}, u32[]{:S(2)}) %collective-permute-start.1) | collective-permute-done | bytes 98336 | tf_op jit(solution)/shard_map/ppermute | solution.py:361
  33.9 0.0 collective-permute-done.2
  33.9 0.0 collective-permute-done.3
  34.0 0.0 copy-start.11
  34.0 0.7 copy-done.11
  34.7 0.0 all-gather.2.cloned.1.call-update
  34.8 0.8 copy.14
  35.6 2.1 %pack_hidden.1 = bf16[4,112,832]{2,1,0:T(8,128)(2,1)} custom-call(bf16[1024,112]{1,0:T(8,128)(2,1)} %bitcast.21, bf16[112,576]{1,0:T(8,128)(2,1)} %down_ref.1), custom_call_target="tpu_custom_call" | custom-call | flops 26000000 | bytes 1200000 | tf_op jit(solution)/shard_map/pack_hidden/pallas_call | solution.py:119
  37.7 14.5 %all_to_all.25 = bf16[4,112,832]{2,1,0:T(8,128)(2,1)S(1)} all-to-all(bf16[4,112,832]{2,1,0:T(8,128)(2,1)} %pack_hidden.1), channel_id=1, replica_groups=mesh['section'=2,'yh'=2,'x'=4,'z'=8,'rep'=4] {'x'}, dimensions={0} | all-to-all | bytes 1490944 | tf_op jit(solution)/shard_map/all_to_all | solution.py:358
  52.2 1.2 fusion
  53.4 15.7 %all-to-all-start.1 = ((f32[16,16,576]{2,1,0:T(8,128)}), f32[16,16,576]{2,1,0:T(8,128)S(1)}, u32[]{:S(2)}, u32[]{:S(2)}) async-start(f32[16,16,576]{2,1,0:T(8,128)} %bitcast.6), calls=%async_computation.1 | async-start | bytes 1310720 | tf_op jit(solution)/shard_map/all_to_all | solution.py:369
  69.1 0.6 pad_add_fusion.ids_ref
  69.7 1.3 request_layout.1.layout_ref
  71.1 15.4 %all-to-all-done.1.pieces_ref = f32[16,16,576]{2,1,0:T(8,128)S(1)} async-done(((f32[16,16,576]{2,1,0:T(8,128)}), f32[16,16,576]{2,1,0:T(8,128)S(1)}, u32[]{:S(2)}, u32[]{:S(2)}) %all-to-all-start.1) | async-done | bytes 589856 | tf_op jit(solution)/shard_map/all_to_all | solution.py:369
  86.4 0.8 copy-done.10
  87.3 2.2 %norm_rows.1 = bf16[16,16,640]{2,1,0:T(8,128)(2,1)} custom-call(s32[64]{0:T(128)} %request_layout.1.layout_ref, f32[16,16,576]{2,1,0:T(8,128)} %copy-done.10, f32[1,512]{1,0:T(1,128)} %bitcast.25, f32[640,128]{1,0:T(8,128)} %constant.24.clone.cos_ref, f32[640,128]{1,0:T(8,128)} %constant.25.clone.sin_ref), custom_call_target="tpu_custom_call" | custom-call | flops 1000000 | bytes 1000000 | tf_op jit(solution)/shard_map/norm_rows/pallas_call | solution.py:144
  89.5 11.0 %all-to-all-start.2 = ((bf16[16,16,640]{2,1,0:T(8,128)(2,1)}), bf16[16,16,640]{2,1,0:T(8,128)(2,1)S(1)}, u32[]{:S(2)}, u32[]{:S(2)}) async-start(bf16[16,16,640]{2,1,0:T(8,128)(2,1)} %norm_rows.1), calls=%async_computation.2 | async-start | bytes 655360 | tf_op jit(solution)/shard_map/all_to_all | solution.py:371
  100.5 9.5 %all-to-all-done.2 = bf16[16,16,640]{2,1,0:T(8,128)(2,1)S(1)} async-done(((bf16[16,16,640]{2,1,0:T(8,128)(2,1)}), bf16[16,16,640]{2,1,0:T(8,128)(2,1)S(1)}, u32[]{:S(2)}, u32[]{:S(2)}) %all-to-all-start.2) | async-done | bytes 327712 | tf_op jit(solution)/shard_map/all_to_all | solution.py:371
  110.0 1.2 broadcast_in_dim.15
  111.2 3.7 %all-to-all-start.3 = ((bf16[4,256,640]{2,1,0:T(8,128)(2,1)}), bf16[4,256,640]{2,1,0:T(8,128)(2,1)S(1)}, u32[]{:S(2)}, u32[]{:S(2)}) async-start(bf16[4,256,640]{2,1,0:T(8,128)(2,1)} %broadcast_in_dim.15), calls=%async_computation.3 | async-start | bytes 2621440 | tf_op jit(solution)/shard_map/all_to_all | solution.py:56
  114.9 3.3 %collective-permute-start.4 = (bf16[3,4,2112]{2,1,0:T(4,128)(2,1)S(1)}, bf16[3,4,2112]{2,1,0:T(4,128)(2,1)S(1)}, u32[]{:S(2)}, u32[]{:S(2)}) collective-permute-start(bf16[3,4,2112]{2,1,0:T(4,128)(2,1)S(1)} %constant_dynamic-update-slice_fusion.5), channel_id=1, source_target_pairs={{0,1},{1,0},{2,3},{3,2},{4,5},{5,4},{6,7},{7,6},{8,9},{9,8},{10,11... | collective-permute-start | bytes 152072 | tf_op jit(solution)/shard_map/ppermute | solution.py:376
  118.2 2.7 %collective-permute-done.4 = bf16[3,4,2112]{2,1,0:T(4,128)(2,1)S(1)} collective-permute-done((bf16[3,4,2112]{2,1,0:T(4,128)(2,1)S(1)}, bf16[3,4,2112]{2,1,0:T(4,128)(2,1)S(1)}, u32[]{:S(2)}, u32[]{:S(2)}) %collective-permute-start.4) | collective-permute-done | bytes 50720 | tf_op jit(solution)/shard_map/ppermute | solution.py:376
  120.9 0.1 pad_maximum_fusion.1
  121.0 4.2 %collective-permute-start.5 = (bf16[6,4,2112]{2,1,0:T(4,128)(2,1)S(1)}, bf16[6,4,2112]{2,1,0:T(4,128)(2,1)S(1)}, u32[]{:S(2)}, u32[]{:S(2)}) collective-permute-start(bf16[6,4,2112]{2,1,0:T(4,128)(2,1)S(1)} %pad_maximum_fusion.1), channel_id=1, source_target_pairs={{0,2},{1,3},{2,0},{3,1},{4,6},{5,7},{6,4},{7,5},{8,10},{9,11},{10,... | collective-permute-start | bytes 304136 | tf_op jit(solution)/shard_map/ppermute | solution.py:376
  125.2 4.4 %collective-permute-done.5 = bf16[6,4,2112]{2,1,0:T(4,128)(2,1)S(1)} collective-permute-done((bf16[6,4,2112]{2,1,0:T(4,128)(2,1)S(1)}, bf16[6,4,2112]{2,1,0:T(4,128)(2,1)S(1)}, u32[]{:S(2)}, u32[]{:S(2)}) %collective-permute-start.5) | collective-permute-done | bytes 101408 | tf_op jit(solution)/shard_map/ppermute | solution.py:376
  129.6 0.1 pad_maximum_fusion.rows_ref
  129.8 0.0 copy-start.4
  129.8 1.0 copy-done.4
  130.8 1.1 prepare_decode.1.ready_ref
  131.9 1.9 %copy-done.1 = bf16[1024,1536]{1,0:T(8,128)(2,1)S(1)} copy-done((bf16[1024,1536]{1,0:T(8,128)(2,1)S(1)}, bf16[1024,1536]{1,0:T(8,128)(2,1)}, u32[]{:S(2)}) %copy-start.1) | copy-done | bytes 3145752
  133.8 4.6 %project_queries.1.q_ref = bf16[2,1024,256]{2,1,0:T(8,128)(2,1)S(1)} custom-call(s32[64]{0:T(128)S(1)} %copy-done.9, bf16[8,8,16,1536]{3,2,1,0:T(8,128)(2,1)S(1)} %bitcast.18, bf16[1536,384]{1,0:T(8,128)(2,1)S(1)} %copy-done, f32[640,128]{1,0:T(8,128)S(1)} %copy-done.3, f32[640,128]{1,0:T(8,128)S(1)} %copy-done.2), custom_call_target="tpu_custom_call" | custom-call | flops 1200000000 | bytes 5000000 | tf_op jit(solution)/shard_map/project_queries/pallas_call | solution.py:169
  138.4 1.0 copy-done.7
  139.4 0.0 all-to-all-done.3
  139.4 1.0 copy-done.5
  140.5 2.5 %decode_attention.1 = bf16[4,16,256]{2,1,0:T(8,128)(2,1)} custom-call(s32[64]{0:T(128)S(1)} %copy-done.9, bf16[48,640]{1,0:T(8,128)(2,1)S(1)} %prepare_decode.1.ready_ref, bf16[1024,640]{1,0:T(8,128)(2,1)S(1)} %bitcast.16, bf16[512,512]{1,0:T(8,128)(2,1)S(1)} %copy-done.5), custom_call_target="tpu_custom_call" | custom-call | flops 100000000 | bytes 2000000 | tf_op jit(solution)/shard_map/decode_attention/pallas_call | solution.py:271
  142.9 5.9 %all-to-all-start.4 = ((bf16[4,16,256]{2,1,0:T(8,128)(2,1)}), bf16[4,16,256]{2,1,0:T(8,128)(2,1)S(1)}, u32[]{:S(2)}, u32[]{:S(2)}) async-start(bf16[4,16,256]{2,1,0:T(8,128)(2,1)} %decode_attention.1), calls=%async_computation.4 | async-start | bytes 65536 | tf_op jit(solution)/shard_map/all_to_all | solution.py:383
  148.8 5.9 %prefill_attention.1 = bf16[1024,256]{1,0:T(8,128)(2,1)} custom-call(s32[64]{0:T(128)S(1)} %copy-done.9, bf16[2,1024,256]{2,1,0:T(8,128)(2,1)S(1)} %copy-done.8, bf16[1024,640]{1,0:T(8,128)(2,1)S(1)} %bitcast.17, bf16[512,512]{1,0:T(8,128)(2,1)S(1)} %copy-done.6), custom_call_target="tpu_custom_call" | custom-call | flops 1500000000 | bytes 4000000 | tf_op jit(solution)/shard_map/prefill_attention/pallas_call | solution.py:332
  154.8 0.0 all-to-all-done.4.pool_ref
  154.8 0.6 copy-done.13
  155.4 1.5 select_slots.1
  (30 shorter events, 0.1 us)
Async XLA Ops:
  7.2 27.6 %copy-start.12 = (bf16[1,1024,112]{1,2,0:T(8,128)(2,1)S(1)}, bf16[1,1024,112]{1,2,0:T(8,128)(2,1)}, u32[]{:S(2)}) copy-start(bf16[1,1024,112]{1,2,0:T(8,128)(2,1)} %param.12) | copy-start | bytes 688132
  7.2 124.7 %all-gather.2.cloned.1.call-start = ((), (), s32[]{:S(2)}) async-start(), calls=%async_computation.5 | async-start | bytes 3538944 | tf_op jit(solution)/shard_map/all_gather | solution.py:362
  7.2 10.8 %collective-permute-start = (bf16[16,1536]{1,0:T(8,128)(2,1)}, bf16[16,1536]{1,0:T(8,128)(2,1)S(1)}, u32[]{:S(2)}, u32[]{:S(2)}) collective-permute-start(bf16[16,1536]{1,0:T(8,128)(2,1)} %bitcast.23), channel_id=1, source_target_pairs={{0,128},{128,0},{1,129},{129,1},{2,130},{130,2},{3,131},{131,3},{4... | collective-permute-start | bytes 147464 | tf_op jit(solution)/shard_map/ppermute | solution.py:357
  18.8 15.2 %collective-permute-start.3 = (bf16[2,16,1536]{2,1,0:T(8,128)(2,1)S(1)}, bf16[2,16,1536]{2,1,0:T(8,128)(2,1)S(1)}, u32[]{:S(2)}, u32[]{:S(2)}) collective-permute-start(bf16[2,16,1536]{2,1,0:T(8,128)(2,1)S(1)} %pad_maximum_fusion.2), channel_id=1, source_target_pairs={{0,96},{32,0},{64,32},{96,64},{1,97},{33,1},{65,33},{97,65},{2,98}... | collective-permute-start | bytes 294920 | tf_op jit(solution)/shard_map/ppermute | solution.py:361
  23.5 10.5 %collective-permute-start.2 = (bf16[2,16,1536]{2,1,0:T(8,128)(2,1)S(1)}, bf16[2,16,1536]{2,1,0:T(8,128)(2,1)S(1)}, u32[]{:S(2)}, u32[]{:S(2)}) collective-permute-start(bf16[2,16,1536]{2,1,0:T(8,128)(2,1)S(1)} %pad_maximum_fusion.2), channel_id=1, source_target_pairs={{0,64},{32,96},{64,0},{96,32},{1,65},{33,97},{65,1},{97,33},{2,66}... | collective-permute-start | bytes 294920 | tf_op jit(solution)/shard_map/ppermute | solution.py:361
  26.2 7.7 %collective-permute-start.1 = (bf16[2,16,1536]{2,1,0:T(8,128)(2,1)S(1)}, bf16[2,16,1536]{2,1,0:T(8,128)(2,1)S(1)}, u32[]{:S(2)}, u32[]{:S(2)}) collective-permute-start(bf16[2,16,1536]{2,1,0:T(8,128)(2,1)S(1)} %pad_maximum_fusion.2), channel_id=1, source_target_pairs={{0,32},{32,64},{64,96},{96,0},{1,33},{33,65},{65,97},{97,1},{2,34}... | collective-permute-start | bytes 294920 | tf_op jit(solution)/shard_map/ppermute | solution.py:361
  34.0 0.7 copy-start.11
  53.4 33.0 %all-to-all-start.1 = ((f32[16,16,576]{2,1,0:T(8,128)}), f32[16,16,576]{2,1,0:T(8,128)S(1)}, u32[]{:S(2)}, u32[]{:S(2)}) async-start(f32[16,16,576]{2,1,0:T(8,128)} %bitcast.6), calls=%async_computation.1 | async-start | bytes 1310720 | tf_op jit(solution)/shard_map/all_to_all | solution.py:369
  69.1 31.4 %copy-start.14 = (bf16[3,4,1536]{2,1,0:T(4,128)(2,1)S(1)}, bf16[3,4,1536]{2,1,0:T(4,128)(2,1)}, u32[]{:S(2)}) copy-start(bf16[3,4,1536]{2,1,0:T(4,128)(2,1)} %param.20) | copy-start | bytes 110596
  86.4 0.8 copy-start.10
  89.5 20.5 %all-to-all-start.2 = ((bf16[16,16,640]{2,1,0:T(8,128)(2,1)}), bf16[16,16,640]{2,1,0:T(8,128)(2,1)S(1)}, u32[]{:S(2)}, u32[]{:S(2)}) async-start(bf16[16,16,640]{2,1,0:T(8,128)(2,1)} %norm_rows.1), calls=%async_computation.2 | async-start | bytes 655360 | tf_op jit(solution)/shard_map/all_to_all | solution.py:371
  111.2 3.7 %copy-start.15 = (bf16[3,4,576]{2,1,0:T(4,128)(2,1)S(1)}, bf16[3,4,576]{2,1,0:T(4,128)(2,1)}, u32[]{:S(2)}) copy-start(bf16[3,4,576]{2,1,0:T(4,128)(2,1)} %param.21) | copy-start | bytes 41476
  111.2 18.6 %copy-start = (bf16[1536,384]{1,0:T(8,128)(2,1)S(1)}, bf16[1536,384]{1,0:T(8,128)(2,1)}, u32[]{:S(2)}) copy-start(bf16[1536,384]{1,0:T(8,128)(2,1)} %w_ref.3) | copy-start | bytes 3538948
  111.2 18.6 %copy-start.2 = (f32[640,128]{1,0:T(8,128)S(1)}, f32[640,128]{1,0:T(8,128)}, u32[]{:S(2)}) copy-start(f32[640,128]{1,0:T(8,128)} %constant.25.clone.sin_ref) | copy-start | bytes 983044
  111.2 18.6 %copy-start.3 = (f32[640,128]{1,0:T(8,128)S(1)}, f32[640,128]{1,0:T(8,128)}, u32[]{:S(2)}) copy-start(f32[640,128]{1,0:T(8,128)} %constant.24.clone.cos_ref) | copy-start | bytes 983044
  111.2 18.6 %copy-start.9 = (s32[64]{0:T(128)S(1)}, s32[64]{0:T(128)}, u32[]{:S(2)}) copy-start(s32[64]{0:T(128)} %request_layout.1.layout_ref) | copy-start | bytes 772
  111.2 28.2 %all-to-all-start.3 = ((bf16[4,256,640]{2,1,0:T(8,128)(2,1)}), bf16[4,256,640]{2,1,0:T(8,128)(2,1)S(1)}, u32[]{:S(2)}, u32[]{:S(2)}) async-start(bf16[4,256,640]{2,1,0:T(8,128)(2,1)} %broadcast_in_dim.15), calls=%async_computation.3 | async-start | bytes 2621440 | tf_op jit(solution)/shard_map/all_to_all | solution.py:56
  114.9 6.0 %collective-permute-start.4 = (bf16[3,4,2112]{2,1,0:T(4,128)(2,1)S(1)}, bf16[3,4,2112]{2,1,0:T(4,128)(2,1)S(1)}, u32[]{:S(2)}, u32[]{:S(2)}) collective-permute-start(bf16[3,4,2112]{2,1,0:T(4,128)(2,1)S(1)} %constant_dynamic-update-slice_fusion.5), channel_id=1, source_target_pairs={{0,1},{1,0},{2,3},{3,2},{4,5},{5,4},{6,7},{7,6},{8,9},{9,8},{10,11... | collective-permute-start | bytes 152072 | tf_op jit(solution)/shard_map/ppermute | solution.py:376
  121.0 8.6 %collective-permute-start.5 = (bf16[6,4,2112]{2,1,0:T(4,128)(2,1)S(1)}, bf16[6,4,2112]{2,1,0:T(4,128)(2,1)S(1)}, u32[]{:S(2)}, u32[]{:S(2)}) collective-permute-start(bf16[6,4,2112]{2,1,0:T(4,128)(2,1)S(1)} %pad_maximum_fusion.1), channel_id=1, source_target_pairs={{0,2},{1,3},{2,0},{3,1},{4,6},{5,7},{6,4},{7,5},{8,10},{9,11},{10,... | collective-permute-start | bytes 304136 | tf_op jit(solution)/shard_map/ppermute | solution.py:376
  129.8 1.0 copy-start.4
  131.9 1.9 %copy-start.1 = (bf16[1024,1536]{1,0:T(8,128)(2,1)S(1)}, bf16[1024,1536]{1,0:T(8,128)(2,1)}, u32[]{:S(2)}) copy-start(bf16[1024,1536]{1,0:T(8,128)(2,1)} %all-gather.2.cloned.1.call-done) | copy-start | bytes 9437188
  138.4 1.0 copy-start.7
  139.4 1.0 copy-start.5
  140.5 8.4 %copy-start.6 = (bf16[512,512]{1,0:T(8,128)(2,1)S(1)}, bf16[512,512]{1,0:T(8,128)(2,1)}, u32[]{:S(2)}) copy-start(bf16[512,512]{1,0:T(8,128)(2,1)} %kv_ref.5) | copy-start | bytes 1572868
  140.5 8.4 %copy-start.8 = (bf16[2,1024,256]{2,1,0:T(8,128)(2,1)S(1)}, bf16[2,1024,256]{2,1,0:T(8,128)(2,1)}, u32[]{:S(2)}) copy-start(bf16[2,1024,256]{2,1,0:T(8,128)(2,1)} %copy-done.7) | copy-start | bytes 3145732
  142.9 11.8 %all-to-all-start.4 = ((bf16[4,16,256]{2,1,0:T(8,128)(2,1)}), bf16[4,16,256]{2,1,0:T(8,128)(2,1)S(1)}, u32[]{:S(2)}, u32[]{:S(2)}) async-start(bf16[4,16,256]{2,1,0:T(8,128)(2,1)} %decode_attention.1), calls=%async_computation.4 | async-start | bytes 65536 | tf_op jit(solution)/shard_map/all_to_all | solution.py:383
  154.8 0.6 copy-start.13
Sparse Core Ops, SparseCore 0:
  34.9 65.0 all-gather.1

commit v5 on v4

--- a/solution.py
+++ b/solution.py
@@ -21,6 +21,7 @@
 HEADS = 2
 PAD = 16
 TABLE = 640
+NORM_FLOPS = 1_000_000
 WIDE = KVL + 2 * ROPE
 START, LENGTH, BASE, PLACE, FIRST, SOURCE, SLOT, BLOCK = 0, 3, 6, 8, 16, 24, 28, 32
 
@@ -65,7 +66,7 @@
 
 
 def layout_kernel(ids_ref, req_ref, slot_ref, out_ref):
-    rep, x, yh, yz = ids_ref[0], ids_ref[1], ids_ref[2], ids_ref[3]
+    rep, x, yh, z = ids_ref[0], ids_ref[1], ids_ref[2], ids_ref[3]
     lengths = [req_ref[rep, r] for r in range(NREQ)]
     starts = [0, lengths[0], lengths[0] + lengths[1]]
 
@@ -81,7 +82,7 @@
         for m in range(NREP * NREQ):
             source += jnp.where(slot_ref[0, m] == rep * NREQ + r, m, 0)
         out_ref[SOURCE + r] = lax.div(source, NREQ) * PAD + lax.rem(source, NREQ) * STEPS
-    out_ref[BASE] = x * 2 * BLK + yz * PAD - start_of(x * 2 + lax.div(yz, 8)) * BLK
+    out_ref[BASE] = x * 2 * BLK + z * 2 * PAD - start_of(x * 2 + lax.div(z, 4)) * BLK
     for i in range(8):
         out_ref[PLACE + i] = i - start_of(i)
         out_ref[FIRST + i] = start_of(i) * BLK
@@ -126,12 +127,12 @@
     )(hidden, kv_down)
 
 
-def norm_kernel(layout_ref, pieces_ref, gain_ref, cos_ref, sin_ref, out_ref):
-    latent = jnp.sum(pieces_ref[...].astype(f32), axis=0)
+def norm_kernel(layout_ref, own_ref, other_ref, gain_ref, cos_ref, sin_ref, out_ref):
+    latent = own_ref[...] + other_ref[...]
     content = latent[:, :KVL]
     scale = lax.rsqrt(jnp.mean(content * content, axis=1, keepdims=True) + 1e-06)
     content = (content * scale * gain_ref[...]).astype(bf16)
-    at = pl.ds(pl.multiple_of(layout_ref[BASE], PAD), PAD)
+    at = pl.ds(pl.multiple_of(layout_ref[BASE], PAD), latent.shape[0])
     pe = jnp.concatenate([latent[:, KVL:]] * 2, axis=1)
     pe = rotate(pe, cos_ref[at, :], sin_ref[at, :]).astype(bf16)
     for i in range(out_ref.shape[0]):
@@ -139,16 +140,16 @@
         out_ref[i, :, KVL:] = pe
 
 
-def norm_rows(layout, pieces, gain, cos_part, sin_part):
-    count, chunk, _ = pieces.shape
+def norm_rows(layout, own, other, gain, cos_part, sin_part):
+    count, chunk = 8, own.shape[0]
     return pl.pallas_call(
         norm_kernel,
-        in_specs=[SMEM] + [VMEM] * 4,
+        in_specs=[SMEM] + [VMEM] * 5,
         out_specs=VMEM,
         out_shape=jax.ShapeDtypeStruct((count, chunk, WIDE), bf16),
-        cost_estimate=pl.CostEstimate(flops=1_000_000, bytes_accessed=1_000_000, transcendentals=16),
+        cost_estimate=pl.CostEstimate(flops=NORM_FLOPS, bytes_accessed=1_000_000, transcendentals=16),
         name="norm_rows",
-    )(layout, pieces, gain, cos_part, sin_part)
+    )(layout, own, other, gain, cos_part, sin_part)
 
 
 def query_kernel(layout_ref, cq_ref, w_ref, cos_ref, sin_ref, out_ref):
@@ -346,39 +347,43 @@
 
 def body(hidden, comp_query, kv_down, kv_gain, q_up, kv_up, req_blocks, dest_slot, dec_query, dec_latent):
     ids = jnp.stack(
-        [lax.axis_index("rep"), lax.axis_index("x"), lax.axis_index("yh"), lax.axis_index(("yh", "z"))]
+        [lax.axis_index("rep"), lax.axis_index("x"), lax.axis_index("yh"), lax.axis_index("z")]
     ).astype(i32)
     rows, features = hidden.shape[1:]
     per_x = rows // NX
-    chunk = per_x // 16
+    chunk = per_x // 8
     cos_part, sin_part = rotary_table()
 
     own = comp_query[0]
     other = lax.ppermute(own, "yh", shift(2, 1))
-    packed = lax.all_to_all(pack(hidden[0], kv_down), "x", 0, 0, tiled=True)
+    pair = jnp.stack([own, other])
+    packed, pair = lax.optimization_barrier((pack(hidden[0], kv_down), pair))
+    packed = lax.all_to_all(packed, "x", 0, 0, tiled=True)
     layout = request_layout(ids, req_blocks, dest_slot)
-    pair = jnp.stack([own, other])
     line = [pair] + [lax.ppermute(pair, "x", shift(NX, d)) for d in range(1, NX)]
-    cq = lax.all_gather(jnp.concatenate(line).reshape(BLK, -1), "z", axis=0, tiled=True)
-
-    packed, dec_query, dec_latent = lax.optimization_barrier((packed, dec_query, dec_latent))
+    line = jnp.concatenate(line).reshape(BLK, -1)
+    packed, line, dec_query, dec_latent = lax.optimization_barrier((packed, line, dec_query, dec_latent))
+    cq = lax.all_gather(line, "z", axis=0, tiled=True)
     packed = packed.reshape(NX * features, -1)
     partial = lax.dot_general(
         packed[:, :per_x], packed[:, per_x:], (((0,), (0,)), ((), ())), preferred_element_type=f32
     )
-    pieces = lax.all_to_all(partial.reshape(16, chunk, -1), ("yh", "z"), 0, 0, tiled=True)
-    copies = norm_rows(layout, pieces, kv_gain[None, :], cos_part, sin_part)
-    cache = lax.all_to_all(copies, ("yh", "z"), 0, 0, tiled=True).reshape(per_x, -1)
-    cache = spread(cache, "x", NX).reshape(rows, -1)
+    pieces = lax.all_to_all(partial.reshape(8, chunk, -1), "z", 0, 0, tiled=True)
+    summed = jnp.sum(pieces, axis=0)
+    met = lax.ppermute(summed, "yh", shift(2, 1))
+    copies = norm_rows(layout, summed, met, kv_gain[None, :], cos_part, sin_part)
+    cache = lax.all_to_all(copies, "z", 0, 0, tiled=True).reshape(per_x, -1)
 
     rep_in = jnp.concatenate([dec_query, dec_latent], axis=2)
     for d in (1, 2):
         met = lax.ppermute(rep_in, "rep", [(i, i ^ d) for i in range(NREP)])
         rep_in = jnp.concatenate([rep_in, met])
     ready = prepare_decode(layout, rep_in, q_up, kv_up, cos_part, sin_part)
+    cache, ready = lax.optimization_barrier((cache, ready))
+    cache = spread(cache, "x", NX).reshape(rows, -1)
 
     queries = project_queries(layout, cq.reshape(8, 8, PAD, -1), q_up, cos_part, sin_part)
-    cache, queries, ready = lax.optimization_barrier((cache, queries, ready))
+    cache, queries = lax.optimization_barrier((cache, queries))
     result = decode(layout, ready, cache, kv_up)
     pool = lax.all_to_all(result, "rep", 0, 0, tiled=True)
     prefill_out = prefill(layout, queries, cache, kv_up)[None]

time: 167 us -> 151 us (0.904)
  the two profiles are of different devices: /device:TPU:56 before, /device:TPU:8 now
where the time goes in v5:
time: 151 us; the launch traced here: 150 us
  starting transfers between devices  57.5 us (38%)
  waiting for transfers between devices  45.7 us (30%)
  Pallas kernels  21 us (14%)
  between operations  14.3 us (9%)
  local copies, waits for them, and re-layouts  8.15 us (5%)
  other arithmetic  1.73 us (1%)
    all_to_all x1, waiting for transfers between devices, body(): lax.all_to_all(partial.reshape(8, chunk, -1), 'z', 0, 0, tiled=True)  20.3 us
    ppermute x3, starting transfers between devices, body(): lax.ppermute(pair, 'x', shift(NX, d))  10.7 us
    all_to_all x1, starting transfers between devices, body(): lax.all_to_all(partial.reshape(8, chunk, -1), 'z', 0, 0, tiled=True)  10.3 us
    all_to_all x1, starting transfers between devices, body(): pool = lax.all_to_all(result, 'rep', 0, 0, tiled=True)  7.67 us
    unnamed x34, local copies, waits for them, and re-layouts  6.98 us
    ppermute x1, starting transfers between devices, body(): other = lax.ppermute(own, 'yh', shift(2, 1))  6.97 us
    pallas_call x1, Pallas kernels, prefill(): pl.pallas_call(prefill_kernel, in_specs=[SMEM] + [VMEM] * 3, out_specs=VM...  5.89 us
    ppermute x3, waiting for transfers between devices, body(): lax.ppermute(pair, 'x', shift(NX, d))  5.71 us
  transfers between devices with their start and end apart: 13, of which 8 were waited for; matrix products, arithmetic and copies ran while one was open for 4% of the time, Pallas kernels for 11%

profile of v5, /device:TPU:8, one launch (start us, length us, event | category | flops | bytes accessed | tf_op | source)
XLA Modules:
  0.0 149.5 jit_solution(13618907140018716630)
XLA Ops:
  7.2 7.0 %collective-permute-start = (bf16[16,1536]{1,0:T(8,128)(2,1)}, bf16[16,1536]{1,0:T(8,128)(2,1)S(1)}, u32[]{:S(2)}, u32[]{:S(2)}) collective-permute-start(bf16[16,1536]{1,0:T(8,128)(2,1)} %bitcast.22), channel_id=1, source_target_pairs={{0,128},{128,0},{1,129},{129,1},{2,130},{130,2},{3,131},{131,3},{4... | collective-permute-start | bytes 147464 | tf_op jit(solution)/shard_map/ppermute | solution.py:358
  14.1 1.8 %copy.15 = bf16[1,1024,112]{2,1,0:T(8,128)(2,1)} copy(bf16[1,1024,112]{1,2,0:T(8,128)(2,1)} %param.12) | data formatting | bytes 458752 | tf_op args[0]
  15.9 2.1 %pack_hidden.1 = bf16[4,112,832]{2,1,0:T(8,128)(2,1)} custom-call(bf16[1024,112]{1,0:T(8,128)(2,1)} %bitcast.21, bf16[112,576]{1,0:T(8,128)(2,1)} %down_ref.1), custom_call_target="tpu_custom_call" | custom-call | flops 26000000 | bytes 1200000 | tf_op jit(solution)/shard_map/pack_hidden/pallas_call | solution.py:120
  18.1 4.3 %all-to-all-start = ((bf16[4,112,832]{2,1,0:T(8,128)(2,1)}), bf16[4,112,832]{2,1,0:T(8,128)(2,1)S(1)}, u32[]{:S(2)}, u32[]{:S(2)}) async-start(bf16[4,112,832]{2,1,0:T(8,128)(2,1)} %pack_hidden.1), calls=%async_computation | async-start | bytes 1605632 | tf_op jit(solution)/shard_map/all_to_all | solution.py:361
  22.4 5.1 %collective-permute-start.3 = (bf16[2,16,1536]{2,1,0:T(8,128)(2,1)S(1)}, bf16[2,16,1536]{2,1,0:T(8,128)(2,1)S(1)}, u32[]{:S(2)}, u32[]{:S(2)}) collective-permute-start(bf16[2,16,1536]{2,1,0:T(8,128)(2,1)S(1)} %pad_maximum_fusion.3), channel_id=1, source_target_pairs={{0,96},{32,0},{64,32},{96,64},{1,97},{33,1},{65,33},{97,65},{2,98}... | collective-permute-start | bytes 294920 | tf_op jit(solution)/shard_map/ppermute | solution.py:363
  27.5 2.8 %collective-permute-start.2 = (bf16[2,16,1536]{2,1,0:T(8,128)(2,1)S(1)}, bf16[2,16,1536]{2,1,0:T(8,128)(2,1)S(1)}, u32[]{:S(2)}, u32[]{:S(2)}) collective-permute-start(bf16[2,16,1536]{2,1,0:T(8,128)(2,1)S(1)} %pad_maximum_fusion.3), channel_id=1, source_target_pairs={{0,64},{32,96},{64,0},{96,32},{1,65},{33,97},{65,1},{97,33},{2,66}... | collective-permute-start | bytes 294920 | tf_op jit(solution)/shard_map/ppermute | solution.py:363
  30.3 2.8 %collective-permute-start.1 = (bf16[2,16,1536]{2,1,0:T(8,128)(2,1)S(1)}, bf16[2,16,1536]{2,1,0:T(8,128)(2,1)S(1)}, u32[]{:S(2)}, u32[]{:S(2)}) collective-permute-start(bf16[2,16,1536]{2,1,0:T(8,128)(2,1)S(1)} %pad_maximum_fusion.3), channel_id=1, source_target_pairs={{0,32},{32,64},{64,96},{96,0},{1,33},{33,65},{65,97},{97,1},{2,34}... | collective-permute-start | bytes 294920 | tf_op jit(solution)/shard_map/ppermute | solution.py:363
  33.1 3.2 %collective-permute-done.3 = bf16[2,16,1536]{2,1,0:T(8,128)(2,1)S(1)} collective-permute-done((bf16[2,16,1536]{2,1,0:T(8,128)(2,1)S(1)}, bf16[2,16,1536]{2,1,0:T(8,128)(2,1)S(1)}, u32[]{:S(2)}, u32[]{:S(2)}) %collective-permute-start.3) | collective-permute-done | bytes 98336 | tf_op jit(solution)/shard_map/ppermute | solution.py:363
  36.2 1.6 %collective-permute-done.2 = bf16[2,16,1536]{2,1,0:T(8,128)(2,1)S(1)} collective-permute-done((bf16[2,16,1536]{2,1,0:T(8,128)(2,1)S(1)}, bf16[2,16,1536]{2,1,0:T(8,128)(2,1)S(1)}, u32[]{:S(2)}, u32[]{:S(2)}) %collective-permute-start.2) | collective-permute-done | bytes 98336 | tf_op jit(solution)/shard_map/ppermute | solution.py:363
  37.8 1.0 collective-permute-done.1
  38.8 0.8 pad_maximum_fusion
  39.6 0.0 all-gather.2.cloned.1.call-update
  39.6 0.0 copy-start.14
  39.6 0.0 copy-start.15
  39.6 1.2 fusion
  40.8 10.3 %all-to-all-start.1 = ((f32[8,32,576]{2,1,0:T(8,128)}), f32[8,32,576]{2,1,0:T(8,128)S(1)}, u32[]{:S(2)}, u32[]{:S(2)}) async-start(f32[8,32,576]{2,1,0:T(8,128)} %bitcast.9), calls=%async_computation.1 | async-start | bytes 1310720 | tf_op jit(solution)/shard_map/all_to_all | solution.py:371
  51.2 3.3 %collective-permute-start.5 = (bf16[3,4,2112]{2,1,0:T(4,128)(2,1)S(1)}, bf16[3,4,2112]{2,1,0:T(4,128)(2,1)S(1)}, u32[]{:S(2)}, u32[]{:S(2)}) collective-permute-start(bf16[3,4,2112]{2,1,0:T(4,128)(2,1)S(1)} %constant_dynamic-update-slice_fusion), channel_id=1, source_target_pairs={{0,1},{1,0},{2,3},{3,2},{4,5},{5,4},{6,7},{7,6},{8,9},{9,8},{10,11... | collective-permute-start | bytes 152072 | tf_op jit(solution)/shard_map/ppermute | solution.py:379
  54.5 20.3 %all-to-all-done.1 = f32[8,32,576]{2,1,0:T(8,128)S(1)} async-done(((f32[8,32,576]{2,1,0:T(8,128)}), f32[8,32,576]{2,1,0:T(8,128)S(1)}, u32[]{:S(2)}, u32[]{:S(2)}) %all-to-all-start.1) | async-done | bytes 589856 | tf_op jit(solution)/shard_map/all_to_all | solution.py:371
  74.8 0.0 copy-start
  74.9 0.0 copy-start.2
  74.9 0.0 copy-start.3
  74.9 0.0 copy-start.4
  74.9 5.4 %collective-permute-start.4 = (f32[32,576]{1,0:T(8,128)S(1)}, f32[32,576]{1,0:T(8,128)S(1)}, u32[]{:S(2)}, u32[]{:S(2)}) collective-permute-start(f32[32,576]{1,0:T(8,128)S(1)} %reduce_sum.9.own_ref), channel_id=1, source_target_pairs={{0,128},{128,0},{1,129},{129,1},{2,130},{130,2},{3,131},{131,3},{4... | collective-permute-start | bytes 221192 | tf_op jit(solution)/shard_map/ppermute | solution.py:373
  80.3 0.7 pad_add_fusion.ids_ref
  81.0 1.3 request_layout.1.layout_ref
  82.3 3.8 %collective-permute-done.4.other_ref = f32[32,576]{1,0:T(8,128)S(1)} collective-permute-done((f32[32,576]{1,0:T(8,128)S(1)}, f32[32,576]{1,0:T(8,128)S(1)}, u32[]{:S(2)}, u32[]{:S(2)}) %collective-permute-start.4) | collective-permute-done | bytes 73760 | tf_op jit(solution)/shard_map/ppermute | solution.py:373
  86.1 0.6 copy-done.12
  86.7 2.0 %norm_rows.1 = bf16[8,32,640]{2,1,0:T(8,128)(2,1)} custom-call(s32[64]{0:T(128)} %request_layout.1.layout_ref, f32[32,576]{1,0:T(8,128)} %copy-done.10, f32[32,576]{1,0:T(8,128)} %copy-done.12, f32[1,512]{1,0:T(1,128)} %bitcast.24, f32[640,128]{1,0:T(8,128)} %constant.24.clone.cos_ref, f32[640,128]{1,0:T(8,128)} %constant.25.clone.sin_ref), custom_call_target="tpu_custom_call" | custom-call | flops 1000000 | bytes 1000000 | tf_op jit(solution)/shard_map/norm_rows/pallas_call | solution.py:145
  88.8 3.4 %all-to-all-start.2 = ((bf16[8,32,640]{2,1,0:T(8,128)(2,1)}), bf16[8,32,640]{2,1,0:T(8,128)(2,1)S(1)}, u32[]{:S(2)}, u32[]{:S(2)}) async-start(bf16[8,32,640]{2,1,0:T(8,128)(2,1)} %norm_rows.1), calls=%async_computation.2 | async-start | bytes 655360 | tf_op jit(solution)/shard_map/all_to_all | solution.py:375
  92.2 0.1 pad_maximum_fusion.2
  92.3 1.9 %collective-permute-start.6 = (bf16[6,4,2112]{2,1,0:T(4,128)(2,1)S(1)}, bf16[6,4,2112]{2,1,0:T(4,128)(2,1)S(1)}, u32[]{:S(2)}, u32[]{:S(2)}) collective-permute-start(bf16[6,4,2112]{2,1,0:T(4,128)(2,1)S(1)} %pad_maximum_fusion.2), channel_id=1, source_target_pairs={{0,2},{1,3},{2,0},{3,1},{4,6},{5,7},{6,4},{7,5},{8,10},{9,11},{10,... | collective-permute-start | bytes 304136 | tf_op jit(solution)/shard_map/ppermute | solution.py:379
  94.2 5.6 %collective-permute-done.6 = bf16[6,4,2112]{2,1,0:T(4,128)(2,1)S(1)} collective-permute-done((bf16[6,4,2112]{2,1,0:T(4,128)(2,1)S(1)}, bf16[6,4,2112]{2,1,0:T(4,128)(2,1)S(1)}, u32[]{:S(2)}, u32[]{:S(2)}) %collective-permute-start.6) | collective-permute-done | bytes 101408 | tf_op jit(solution)/shard_map/ppermute | solution.py:379
  99.9 0.1 pad_maximum_fusion.1.rows_ref
  100.1 1.1 prepare_decode.1.ready_ref
  101.1 5.4 %all-to-all-done.2 = bf16[8,32,640]{2,1,0:T(8,128)(2,1)S(1)} async-done(((bf16[8,32,640]{2,1,0:T(8,128)(2,1)}), bf16[8,32,640]{2,1,0:T(8,128)(2,1)S(1)}, u32[]{:S(2)}, u32[]{:S(2)}) %all-to-all-start.2) | async-done | bytes 327712 | tf_op jit(solution)/shard_map/all_to_all | solution.py:375
  106.5 1.2 broadcast_in_dim.13
  107.7 3.5 %all-to-all-start.3 = ((bf16[4,256,640]{2,1,0:T(8,128)(2,1)}), bf16[4,256,640]{2,1,0:T(8,128)(2,1)S(1)}, u32[]{:S(2)}, u32[]{:S(2)}) async-start(bf16[4,256,640]{2,1,0:T(8,128)(2,1)} %broadcast_in_dim.13), calls=%async_computation.3 | async-start | bytes 2621440 | tf_op jit(solution)/shard_map/all_to_all | solution.py:57
  111.3 0.0 all-gather.2.cloned.1.call-done
  111.3 1.9 %copy-done.1 = bf16[1024,1536]{1,0:T(8,128)(2,1)S(1)} copy-done((bf16[1024,1536]{1,0:T(8,128)(2,1)S(1)}, bf16[1024,1536]{1,0:T(8,128)(2,1)}, u32[]{:S(2)}) %copy-start.1) | copy-done | bytes 3145752
  113.2 4.6 %project_queries.1.q_ref = bf16[2,1024,256]{2,1,0:T(8,128)(2,1)S(1)} custom-call(s32[64]{0:T(128)S(1)} %copy-done.9, bf16[8,8,16,1536]{3,2,1,0:T(8,128)(2,1)S(1)} %bitcast.17, bf16[1536,384]{1,0:T(8,128)(2,1)S(1)} %copy-done, f32[640,128]{1,0:T(8,128)S(1)} %copy-done.3, f32[640,128]{1,0:T(8,128)S(1)} %copy-done.2), custom_call_target="tpu_custom_call" | custom-call | flops 1200000000 | bytes 5000000 | tf_op jit(solution)/shard_map/project_queries/pallas_call | solution.py:170
  117.8 1.0 copy-done.7
  118.8 4.8 %all-to-all-done.3 = bf16[4,256,640]{2,1,0:T(8,128)(2,1)S(1)} async-done(((bf16[4,256,640]{2,1,0:T(8,128)(2,1)}), bf16[4,256,640]{2,1,0:T(8,128)(2,1)S(1)}, u32[]{:S(2)}, u32[]{:S(2)}) %all-to-all-start.3) | async-done | bytes 1310752 | tf_op jit(solution)/shard_map/all_to_all | solution.py:57
  123.5 1.0 copy-done.5
  124.6 2.5 %decode_attention.1 = bf16[4,16,256]{2,1,0:T(8,128)(2,1)} custom-call(s32[64]{0:T(128)S(1)} %copy-done.9, bf16[48,640]{1,0:T(8,128)(2,1)S(1)} %prepare_decode.1.ready_ref, bf16[1024,640]{1,0:T(8,128)(2,1)S(1)} %bitcast.15, bf16[512,512]{1,0:T(8,128)(2,1)S(1)} %copy-done.5), custom_call_target="tpu_custom_call" | custom-call | flops 100000000 | bytes 2000000 | tf_op jit(solution)/shard_map/decode_attention/pallas_call | solution.py:272
  127.0 7.7 %all-to-all-start.4 = ((bf16[4,16,256]{2,1,0:T(8,128)(2,1)}), bf16[4,16,256]{2,1,0:T(8,128)(2,1)S(1)}, u32[]{:S(2)}, u32[]{:S(2)}) async-start(bf16[4,16,256]{2,1,0:T(8,128)(2,1)} %decode_attention.1), calls=%async_computation.4 | async-start | bytes 65536 | tf_op jit(solution)/shard_map/all_to_all | solution.py:388
  134.7 5.9 %prefill_attention.1 = bf16[1024,256]{1,0:T(8,128)(2,1)} custom-call(s32[64]{0:T(128)S(1)} %copy-done.9, bf16[2,1024,256]{2,1,0:T(8,128)(2,1)S(1)} %copy-done.8, bf16[1024,640]{1,0:T(8,128)(2,1)S(1)} %bitcast.16, bf16[512,512]{1,0:T(8,128)(2,1)S(1)} %copy-done.6), custom_call_target="tpu_custom_call" | custom-call | flops 1500000000 | bytes 4000000 | tf_op jit(solution)/shard_map/prefill_attention/pallas_call | solution.py:333
  140.6 0.6 copy-done.11
  141.2 1.5 select_slots.1
  (30 shorter events, 0.1 us)
Async XLA Ops:
  7.2 10.9 %copy-start.13 = (bf16[1,16,1536]{2,1,0:T(8,128)(2,1)S(1)}, bf16[1,16,1536]{2,1,0:T(8,128)(2,1)}, u32[]{:S(2)}) copy-start(bf16[1,16,1536]{2,1,0:T(8,128)(2,1)} %param.13) | copy-start | bytes 147460
  7.2 10.9 %collective-permute-start = (bf16[16,1536]{1,0:T(8,128)(2,1)}, bf16[16,1536]{1,0:T(8,128)(2,1)S(1)}, u32[]{:S(2)}, u32[]{:S(2)}) collective-permute-start(bf16[16,1536]{1,0:T(8,128)(2,1)} %bitcast.22), channel_id=1, source_target_pairs={{0,128},{128,0},{1,129},{129,1},{2,130},{130,2},{3,131},{131,3},{4... | collective-permute-start | bytes 147464 | tf_op jit(solution)/shard_map/ppermute | solution.py:358
  18.1 21.5 %all-to-all-start = ((bf16[4,112,832]{2,1,0:T(8,128)(2,1)}), bf16[4,112,832]{2,1,0:T(8,128)(2,1)S(1)}, u32[]{:S(2)}, u32[]{:S(2)}) async-start(bf16[4,112,832]{2,1,0:T(8,128)(2,1)} %pack_hidden.1), calls=%async_computation | async-start | bytes 1605632 | tf_op jit(solution)/shard_map/all_to_all | solution.py:361
  22.4 88.9 %all-gather.2.cloned.1.call-start = ((), (), s32[]{:S(2)}) async-start(), calls=%async_computation.5 | async-start | bytes 3538944 | tf_op jit(solution)/shard_map/all_gather | solution.py:366
  22.4 13.8 %collective-permute-start.3 = (bf16[2,16,1536]{2,1,0:T(8,128)(2,1)S(1)}, bf16[2,16,1536]{2,1,0:T(8,128)(2,1)S(1)}, u32[]{:S(2)}, u32[]{:S(2)}) collective-permute-start(bf16[2,16,1536]{2,1,0:T(8,128)(2,1)S(1)} %pad_maximum_fusion.3), channel_id=1, source_target_pairs={{0,96},{32,0},{64,32},{96,64},{1,97},{33,1},{65,33},{97,65},{2,98}... | collective-permute-start | bytes 294920 | tf_op jit(solution)/shard_map/ppermute | solution.py:363
  27.5 10.3 %collective-permute-start.2 = (bf16[2,16,1536]{2,1,0:T(8,128)(2,1)S(1)}, bf16[2,16,1536]{2,1,0:T(8,128)(2,1)S(1)}, u32[]{:S(2)}, u32[]{:S(2)}) collective-permute-start(bf16[2,16,1536]{2,1,0:T(8,128)(2,1)S(1)} %pad_maximum_fusion.3), channel_id=1, source_target_pairs={{0,64},{32,96},{64,0},{96,32},{1,65},{33,97},{65,1},{97,33},{2,66}... | collective-permute-start | bytes 294920 | tf_op jit(solution)/shard_map/ppermute | solution.py:363
  30.3 8.5 %collective-permute-start.1 = (bf16[2,16,1536]{2,1,0:T(8,128)(2,1)S(1)}, bf16[2,16,1536]{2,1,0:T(8,128)(2,1)S(1)}, u32[]{:S(2)}, u32[]{:S(2)}) collective-permute-start(bf16[2,16,1536]{2,1,0:T(8,128)(2,1)S(1)} %pad_maximum_fusion.3), channel_id=1, source_target_pairs={{0,32},{32,64},{64,96},{96,0},{1,33},{33,65},{65,97},{97,1},{2,34}... | collective-permute-start | bytes 294920 | tf_op jit(solution)/shard_map/ppermute | solution.py:363
  39.6 11.6 %copy-start.14 = (bf16[3,4,1536]{2,1,0:T(4,128)(2,1)S(1)}, bf16[3,4,1536]{2,1,0:T(4,128)(2,1)}, u32[]{:S(2)}) copy-start(bf16[3,4,1536]{2,1,0:T(4,128)(2,1)} %param.20) | copy-start | bytes 110596
  39.6 11.6 %copy-start.15 = (bf16[3,4,576]{2,1,0:T(4,128)(2,1)S(1)}, bf16[3,4,576]{2,1,0:T(4,128)(2,1)}, u32[]{:S(2)}) copy-start(bf16[3,4,576]{2,1,0:T(4,128)(2,1)} %param.21) | copy-start | bytes 41476
  40.8 33.9 %all-to-all-start.1 = ((f32[8,32,576]{2,1,0:T(8,128)}), f32[8,32,576]{2,1,0:T(8,128)S(1)}, u32[]{:S(2)}, u32[]{:S(2)}) async-start(f32[8,32,576]{2,1,0:T(8,128)} %bitcast.9), calls=%async_computation.1 | async-start | bytes 1310720 | tf_op jit(solution)/shard_map/all_to_all | solution.py:371
  51.2 41.0 %collective-permute-start.5 = (bf16[3,4,2112]{2,1,0:T(4,128)(2,1)S(1)}, bf16[3,4,2112]{2,1,0:T(4,128)(2,1)S(1)}, u32[]{:S(2)}, u32[]{:S(2)}) collective-permute-start(bf16[3,4,2112]{2,1,0:T(4,128)(2,1)S(1)} %constant_dynamic-update-slice_fusion), channel_id=1, source_target_pairs={{0,1},{1,0},{2,3},{3,2},{4,5},{5,4},{6,7},{7,6},{8,9},{9,8},{10,11... | collective-permute-start | bytes 152072 | tf_op jit(solution)/shard_map/ppermute | solution.py:379
  74.8 11.3 %copy-start.10 = (f32[32,576]{1,0:T(8,128)}, f32[32,576]{1,0:T(8,128)S(1)}, u32[]{:S(2)}) copy-start(f32[32,576]{1,0:T(8,128)S(1)} %reduce_sum.9.own_ref) | copy-start | bytes 221188
  74.8 25.2 %copy-start = (bf16[1536,384]{1,0:T(8,128)(2,1)S(1)}, bf16[1536,384]{1,0:T(8,128)(2,1)}, u32[]{:S(2)}) copy-start(bf16[1536,384]{1,0:T(8,128)(2,1)} %w_ref.3) | copy-start | bytes 3538948
  74.9 25.2 %copy-start.2 = (f32[640,128]{1,0:T(8,128)S(1)}, f32[640,128]{1,0:T(8,128)}, u32[]{:S(2)}) copy-start(f32[640,128]{1,0:T(8,128)} %constant.25.clone.sin_ref) | copy-start | bytes 983044
  74.9 25.2 %copy-start.3 = (f32[640,128]{1,0:T(8,128)S(1)}, f32[640,128]{1,0:T(8,128)}, u32[]{:S(2)}) copy-start(f32[640,128]{1,0:T(8,128)} %constant.24.clone.cos_ref) | copy-start | bytes 983044
  74.9 25.2 %copy-start.4 = (bf16[512,512]{1,0:T(8,128)(2,1)S(1)}, bf16[512,512]{1,0:T(8,128)(2,1)}, u32[]{:S(2)}) copy-start(bf16[512,512]{1,0:T(8,128)(2,1)} %kv_ref.5) | copy-start | bytes 1572868
  74.9 11.2 %collective-permute-start.4 = (f32[32,576]{1,0:T(8,128)S(1)}, f32[32,576]{1,0:T(8,128)S(1)}, u32[]{:S(2)}, u32[]{:S(2)}) collective-permute-start(f32[32,576]{1,0:T(8,128)S(1)} %reduce_sum.9.own_ref), channel_id=1, source_target_pairs={{0,128},{128,0},{1,129},{129,1},{2,130},{130,2},{3,131},{131,3},{4... | collective-permute-start | bytes 221192 | tf_op jit(solution)/shard_map/ppermute | solution.py:373
  82.3 17.8 %copy-start.9 = (s32[64]{0:T(128)S(1)}, s32[64]{0:T(128)}, u32[]{:S(2)}) copy-start(s32[64]{0:T(128)} %request_layout.1.layout_ref) | copy-start | bytes 772
  86.1 0.6 copy-start.12
  88.8 17.8 %all-to-all-start.2 = ((bf16[8,32,640]{2,1,0:T(8,128)(2,1)}), bf16[8,32,640]{2,1,0:T(8,128)(2,1)S(1)}, u32[]{:S(2)}, u32[]{:S(2)}) async-start(bf16[8,32,640]{2,1,0:T(8,128)(2,1)} %norm_rows.1), calls=%async_computation.2 | async-start | bytes 655360 | tf_op jit(solution)/shard_map/all_to_all | solution.py:375
  92.3 7.6 %collective-permute-start.6 = (bf16[6,4,2112]{2,1,0:T(4,128)(2,1)S(1)}, bf16[6,4,2112]{2,1,0:T(4,128)(2,1)S(1)}, u32[]{:S(2)}, u32[]{:S(2)}) collective-permute-start(bf16[6,4,2112]{2,1,0:T(4,128)(2,1)S(1)} %pad_maximum_fusion.2), channel_id=1, source_target_pairs={{0,2},{1,3},{2,0},{3,1},{4,6},{5,7},{6,4},{7,5},{8,10},{9,11},{10,... | collective-permute-start | bytes 304136 | tf_op jit(solution)/shard_map/ppermute | solution.py:379
  107.7 15.8 %all-to-all-start.3 = ((bf16[4,256,640]{2,1,0:T(8,128)(2,1)}), bf16[4,256,640]{2,1,0:T(8,128)(2,1)S(1)}, u32[]{:S(2)}, u32[]{:S(2)}) async-start(bf16[4,256,640]{2,1,0:T(8,128)(2,1)} %broadcast_in_dim.13), calls=%async_computation.3 | async-start | bytes 2621440 | tf_op jit(solution)/shard_map/all_to_all | solution.py:57
  111.3 1.9 %copy-start.1 = (bf16[1024,1536]{1,0:T(8,128)(2,1)S(1)}, bf16[1024,1536]{1,0:T(8,128)(2,1)}, u32[]{:S(2)}) copy-start(bf16[1024,1536]{1,0:T(8,128)(2,1)} %all-gather.2.cloned.1.call-done) | copy-start | bytes 9437188
  117.8 1.0 copy-start.7
  123.5 1.0 copy-start.5
  124.6 10.2 %copy-start.6 = (bf16[512,512]{1,0:T(8,128)(2,1)S(1)}, bf16[512,512]{1,0:T(8,128)(2,1)}, u32[]{:S(2)}) copy-start(bf16[512,512]{1,0:T(8,128)(2,1)} %kv_ref.5) | copy-start | bytes 1572868
  124.6 10.2 %copy-start.8 = (bf16[2,1024,256]{2,1,0:T(8,128)(2,1)S(1)}, bf16[2,1024,256]{2,1,0:T(8,128)(2,1)}, u32[]{:S(2)}) copy-start(bf16[2,1024,256]{2,1,0:T(8,128)(2,1)} %copy-done.7) | copy-start | bytes 3145732
  127.0 13.6 %all-to-all-start.4 = ((bf16[4,16,256]{2,1,0:T(8,128)(2,1)}), bf16[4,16,256]{2,1,0:T(8,128)(2,1)S(1)}, u32[]{:S(2)}, u32[]{:S(2)}) async-start(bf16[4,16,256]{2,1,0:T(8,128)(2,1)} %decode_attention.1), calls=%async_computation.4 | async-start | bytes 65536 | tf_op jit(solution)/shard_map/all_to_all | solution.py:388
  140.6 0.6 copy-start.11
Sparse Core Ops, SparseCore 0:
  39.7 63.7 all-gather.1

commit v6 on v5

--- a/solution.py
+++ b/solution.py
@@ -86,7 +86,7 @@
     for i in range(8):
         out_ref[PLACE + i] = i - start_of(i)
         out_ref[FIRST + i] = start_of(i) * BLK
-        out_ref[BLOCK + i] = lax.rem(x + NX - i % NX, NX) * 2 + (yh ^ (i // NX))
+        out_ref[BLOCK + i] = (yh ^ (i % 2)) * NX + lax.rem(x + NX - i // 2, NX)
 
 
 SMEM = pl.BlockSpec(memory_space=pltpu.SMEM)
@@ -125,6 +125,54 @@
         cost_estimate=pl.CostEstimate(flops=26_000_000, bytes_accessed=1_200_000, transcendentals=0),
         name="pack_hidden",
     )(hidden, kv_down)
+
+
+def mix_kernel(packed_ref, pair_ref, out_ref):
+    count, chunk, _ = out_ref.shape
+    width = pair_ref.shape[1]
+    per_x = count * chunk
+    packed = packed_ref[...].reshape(-1, packed_ref.shape[2])
+    partial = lax.dot_general(
+        packed[:, :per_x], packed[:, per_x:], (((0,), (0,)), ((), ())), preferred_element_type=f32
+    ).astype(bf16)
+    for i in range(count):
+        out_ref[i, :, :width] = pair_ref[...]
+        out_ref[i, :, width:] = partial[i * chunk : (i + 1) * chunk]
+
+
+def mix(packed, pair):
+    chunk, width = pair.shape
+    return pl.pallas_call(
+        mix_kernel,
+        in_specs=[VMEM] * 2,
+        out_specs=VMEM,
+        out_shape=jax.ShapeDtypeStruct((8, chunk, width + KVL + ROPE), bf16),
+        compiler_params=pltpu.CompilerParams(vmem_limit_bytes=VMEM_LIMIT),
+        cost_estimate=pl.CostEstimate(flops=130_000_000, bytes_accessed=2_000_000, transcendentals=0),
+        name="partial_and_rows",
+    )(packed, pair)
+
+
+def unmix_kernel(mixed_ref, rows_ref, sum_ref):
+    width = rows_ref.shape[2]
+    rows_ref[...] = mixed_ref[:, :, :width]
+    sum_ref[...] = jnp.sum(mixed_ref[:, :, width:].astype(f32), axis=0)
+
+
+def unmix(mixed, width):
+    count, chunk, both = mixed.shape
+    return pl.pallas_call(
+        unmix_kernel,
+        in_specs=[VMEM],
+        out_specs=[VMEM, VMEM],
+        out_shape=[
+            jax.ShapeDtypeStruct((count, chunk, width), bf16),
+            jax.ShapeDtypeStruct((chunk, both - width), f32),
+        ],
+        compiler_params=pltpu.CompilerParams(vmem_limit_bytes=VMEM_LIMIT),
+        cost_estimate=pl.CostEstimate(flops=1_000_000, bytes_accessed=2_000_000, transcendentals=0),
+        name="rows_and_sum",
+    )(mixed)
 
 
 def norm_kernel(layout_ref, own_ref, other_ref, gain_ref, cos_ref, sin_ref, out_ref):
@@ -152,7 +200,8 @@
     )(layout, own, other, gain, cos_part, sin_part)
 
 
-def query_kernel(layout_ref, cq_ref, w_ref, cos_ref, sin_ref, out_ref):
+def query_kernel(layout_ref, cq_ref, w_ref, cos_ref, sin_ref, *refs):
+    out_ref = refs[-1]
     rows = cq_ref[...].reshape(BLK, -1)
     u = jnp.dot(rows, w_ref[...], preferred_element_type=f32)
     first, second, pe = split_heads(u)
@@ -164,27 +213,34 @@
     out_ref[1, :, NOPE:] = jnp.where(low, 0.0, pe).astype(bf16)
 
 
-def project_queries(layout, cq, weights, cos_part, sin_part):
+def project_queries(d, layout, cq, weights, cos_part, sin_part, queries):
     width = cq.shape[-1]
-    table = pl.BlockSpec((BLK, 2 * ROPE), lambda i, place: (place[PLACE + i], 0))
+
+    def block(j, place):
+        return place[BLOCK + 2 * d + j]
+
+    table = pl.BlockSpec((BLK, 2 * ROPE), lambda j, place: (place[PLACE + block(j, place)], 0))
+    earlier = [] if queries is None else [queries]
     return pl.pallas_call(
         query_kernel,
         grid_spec=pltpu.PrefetchScalarGridSpec(
             num_scalar_prefetch=1,
-            grid=(8,),
+            grid=(2,),
             in_specs=[
-                pl.BlockSpec((8, 1, PAD, width), lambda i, place: (0, place[BLOCK + i], 0, 0)),
-                pl.BlockSpec(weights.shape, lambda i, place: (0, 0)),
+                pl.BlockSpec((8, 1, PAD, width), lambda j, place: (0, j, 0, 0)),
+                pl.BlockSpec(weights.shape, lambda j, place: (0, 0)),
                 table,
                 table,
-            ],
-            out_specs=pl.BlockSpec((HEADS, BLK, 2 * NOPE), lambda i, place: (0, i, 0)),
+            ]
+            + [pl.BlockSpec(memory_space=pl.ANY)] * len(earlier),
+            out_specs=pl.BlockSpec((HEADS, BLK, 2 * NOPE), lambda j, place: (0, block(j, place), 0)),
         ),
         out_shape=jax.ShapeDtypeStruct((HEADS, 8 * BLK, 2 * NOPE), bf16),
-        compiler_params=pltpu.CompilerParams(vmem_limit_bytes=VMEM_LIMIT),
-        cost_estimate=pl.CostEstimate(flops=1_200_000_000, bytes_accessed=5_000_000, transcendentals=0),
+        input_output_aliases={5: 0} if earlier else {},
+        compiler_params=pltpu.CompilerParams(vmem_limit_bytes=VMEM_LIMIT),
+        cost_estimate=pl.CostEstimate(flops=300_000_000, bytes_accessed=2_500_000, transcendentals=0),
         name="project_queries",
-    )(layout, cq, weights, cos_part, sin_part)
+    )(layout, cq, weights, cos_part, sin_part, *earlier)
 
 
 def prepare_kernel(layout_ref, rows_ref, w_ref, kv_ref, cos_ref, sin_ref, out_ref, in_ref, cos_at, sin_at):
@@ -349,28 +405,21 @@
     ids = jnp.stack(
         [lax.axis_index("rep"), lax.axis_index("x"), lax.axis_index("yh"), lax.axis_index("z")]
     ).astype(i32)
-    rows, features = hidden.shape[1:]
+    rows = hidden.shape[1]
     per_x = rows // NX
-    chunk = per_x // 8
     cos_part, sin_part = rotary_table()
 
     own = comp_query[0]
     other = lax.ppermute(own, "yh", shift(2, 1))
-    pair = jnp.stack([own, other])
-    packed, pair = lax.optimization_barrier((pack(hidden[0], kv_down), pair))
-    packed = lax.all_to_all(packed, "x", 0, 0, tiled=True)
+    packed = lax.all_to_all(pack(hidden[0], kv_down), "x", 0, 0, tiled=True)
     layout = request_layout(ids, req_blocks, dest_slot)
-    line = [pair] + [lax.ppermute(pair, "x", shift(NX, d)) for d in range(1, NX)]
-    line = jnp.concatenate(line).reshape(BLK, -1)
-    packed, line, dec_query, dec_latent = lax.optimization_barrier((packed, line, dec_query, dec_latent))
-    cq = lax.all_gather(line, "z", axis=0, tiled=True)
-    packed = packed.reshape(NX * features, -1)
-    partial = lax.dot_general(
-        packed[:, :per_x], packed[:, per_x:], (((0,), (0,)), ((), ())), preferred_element_type=f32
-    )
-    pieces = lax.all_to_all(partial.reshape(8, chunk, -1), "z", 0, 0, tiled=True)
-    summed = jnp.sum(pieces, axis=0)
+    pair = jnp.concatenate([own, other])
+    packed, pair, dec_query, dec_latent = lax.optimization_barrier((packed, pair, dec_query, dec_latent))
+
+    mixed = lax.all_to_all(mix(packed, pair), "z", 0, 0, tiled=True)
+    near, summed = unmix(mixed, own.shape[1])
     met = lax.ppermute(summed, "yh", shift(2, 1))
+    chunks = [near] + [lax.ppermute(near, "x", shift(NX, d)) for d in range(1, NX)]
     copies = norm_rows(layout, summed, met, kv_gain[None, :], cos_part, sin_part)
     cache = lax.all_to_all(copies, "z", 0, 0, tiled=True).reshape(per_x, -1)
 
@@ -379,10 +428,14 @@
         met = lax.ppermute(rep_in, "rep", [(i, i ^ d) for i in range(NREP)])
         rep_in = jnp.concatenate([rep_in, met])
     ready = prepare_decode(layout, rep_in, q_up, kv_up, cos_part, sin_part)
-    cache, ready = lax.optimization_barrier((cache, ready))
+    cache, ready, *chunks = lax.optimization_barrier((cache, ready, *chunks))
     cache = spread(cache, "x", NX).reshape(rows, -1)
 
-    queries = project_queries(layout, cq.reshape(8, 8, PAD, -1), q_up, cos_part, sin_part)
+    queries = None
+    for d, chunk_rows in enumerate(chunks):
+        queries = project_queries(
+            d, layout, chunk_rows.reshape(8, 2, PAD, -1), q_up, cos_part, sin_part, queries
+        )
     cache, queries = lax.optimization_barrier((cache, queries))
     result = decode(layout, ready, cache, kv_up)
     pool = lax.all_to_all(result, "rep", 0, 0, tiled=True)

time: 151 us -> 157 us (1.040)
  the two profiles are of different devices: /device:TPU:8 before, /device:TPU:56 now
where the time goes in v6:
time: 157 us; the launch traced here: 154 us
  waiting for transfers between devices  66.2 us (42%)
  starting transfers between devices  51.5 us (33%)
  Pallas kernels  29.7 us (19%)
  local copies, waits for them, and re-layouts  5.21 us (3%)
    all_to_all x1, waiting for transfers between devices, body(): mixed = lax.all_to_all(mix(packed, pair), 'z', 0, 0, tiled=True)  25.6 us
    ppermute x3, waiting for transfers between devices, body(): lax.ppermute(near, 'x', shift(NX, d))  14.3 us
    all_to_all x1, starting transfers between devices, body(): mixed = lax.all_to_all(mix(packed, pair), 'z', 0, 0, tiled=True)  10.4 us
    all_to_all x1, waiting for transfers between devices, spread(): return lax.all_to_all(copies, axes, 0, 0, tiled=True)  9.22 us
    pallas_call x4, Pallas kernels, project_queries(): pl.pallas_call(query_kernel, grid_spec=pltpu.PrefetchScalarGridSpec(num_s...  9.15 us
    ppermute x3, starting transfers between devices, body(): lax.ppermute(near, 'x', shift(NX, d))  8.37 us
    ppermute x2, waiting for transfers between devices, body(): met = lax.ppermute(rep_in, 'rep', [(i, i ^ d) for i in range(NREP)])  6.68 us
    pallas_call x1, Pallas kernels, prefill(): pl.pallas_call(prefill_kernel, in_specs=[SMEM] + [VMEM] * 3, out_specs=VM...  6.67 us
  transfers between devices with their start and end apart: 12, of which 7 were waited for; matrix products, arithmetic and copies ran while one was open for 1% of the time, Pallas kernels for 14%

profile of v6, /device:TPU:56, one launch (start us, length us, event | category | flops | bytes accessed | tf_op | source)
XLA Modules:
  0.0 154.3 jit_solution(2769047837313197177)
XLA Ops:
  0.6 1.8 %copy.17 = bf16[1,1024,112]{2,1,0:T(8,128)(2,1)} copy(bf16[1,1024,112]{1,2,0:T(8,128)(2,1)} %param.12) | data formatting | bytes 458752 | tf_op args[0]
  2.4 2.1 %pack_hidden.1 = bf16[4,112,832]{2,1,0:T(8,128)(2,1)} custom-call(bf16[1024,112]{1,0:T(8,128)(2,1)} %bitcast.15, bf16[112,576]{1,0:T(8,128)(2,1)} %down_ref.1), custom_call_target="tpu_custom_call" | custom-call | flops 26000000 | bytes 1200000 | tf_op jit(solution)/shard_map/pack_hidden/pallas_call | solution.py:120
  4.5 4.3 %all-to-all-start = ((bf16[4,112,832]{2,1,0:T(8,128)(2,1)}), bf16[4,112,832]{2,1,0:T(8,128)(2,1)S(1)}, u32[]{:S(2)}, u32[]{:S(2)}) async-start(bf16[4,112,832]{2,1,0:T(8,128)(2,1)} %pack_hidden.1), calls=%async_computation | async-start | bytes 1605632 | tf_op jit(solution)/shard_map/all_to_all | solution.py:414
  8.8 0.0 copy-done.10
  8.8 4.7 %collective-permute-start = (bf16[16,1536]{1,0:T(8,128)(2,1)S(1)}, bf16[16,1536]{1,0:T(8,128)(2,1)S(1)}, u32[]{:S(2)}, u32[]{:S(2)}) collective-permute-start(bf16[16,1536]{1,0:T(8,128)(2,1)S(1)} %bitcast.16), channel_id=1, source_target_pairs={{0,128},{128,0},{1,129},{129,1},{2,130},{130,2},{3,131},{131,3},{4... | collective-permute-start | bytes 147464 | tf_op jit(solution)/shard_map/ppermute | solution.py:413
  13.5 5.7 %collective-permute-done = bf16[16,1536]{1,0:T(8,128)(2,1)S(1)} collective-permute-done((bf16[16,1536]{1,0:T(8,128)(2,1)S(1)}, bf16[16,1536]{1,0:T(8,128)(2,1)S(1)}, u32[]{:S(2)}, u32[]{:S(2)}) %collective-permute-start) | collective-permute-done | bytes 49184 | tf_op jit(solution)/shard_map/ppermute | solution.py:413
  19.2 2.0 %all-to-all-done.packed_ref = bf16[4,112,832]{2,1,0:T(8,128)(2,1)S(1)} async-done(((bf16[4,112,832]{2,1,0:T(8,128)(2,1)}), bf16[4,112,832]{2,1,0:T(8,128)(2,1)S(1)}, u32[]{:S(2)}, u32[]{:S(2)}) %all-to-all-start) | async-done | bytes 745504 | tf_op jit(solution)/shard_map/all_to_all | solution.py:414
  21.3 1.4 partial_and_rows.1
  22.7 10.4 %all-to-all-start.1 = ((bf16[8,32,2112]{2,1,0:T(8,128)(2,1)}), bf16[8,32,2112]{2,1,0:T(8,128)(2,1)S(1)}, u32[]{:S(2)}, u32[]{:S(2)}) async-start(bf16[8,32,2112]{2,1,0:T(8,128)(2,1)} %partial_and_rows.1), calls=%async_computation.1 | async-start | bytes 2228224 | tf_op jit(solution)/shard_map/all_to_all | solution.py:419
  33.2 0.0 copy-done.11
  33.2 3.3 %collective-permute-start.2 = (bf16[3,4,2112]{2,1,0:T(4,128)(2,1)S(1)}, bf16[3,4,2112]{2,1,0:T(4,128)(2,1)S(1)}, u32[]{:S(2)}, u32[]{:S(2)}) collective-permute-start(bf16[3,4,2112]{2,1,0:T(4,128)(2,1)S(1)} %constant_dynamic-update-slice_fusion), channel_id=1, source_target_pairs={{0,1},{1,0},{2,3},{3,2},{4,5},{5,4},{6,7},{7,6},{8,9},{9,8},{10,11... | collective-permute-start | bytes 152072 | tf_op jit(solution)/shard_map/ppermute | solution.py:428
  36.5 25.6 %all-to-all-done.1.mixed_ref = bf16[8,32,2112]{2,1,0:T(8,128)(2,1)S(1)} async-done(((bf16[8,32,2112]{2,1,0:T(8,128)(2,1)}), bf16[8,32,2112]{2,1,0:T(8,128)(2,1)S(1)}, u32[]{:S(2)}, u32[]{:S(2)}) %all-to-all-start.1) | async-done | bytes 1081376 | tf_op jit(solution)/shard_map/all_to_all | solution.py:419
  62.1 0.9 rows_and_sum.1
  63.1 4.7 %collective-permute-start.1 = (f32[32,576]{1,0:T(8,128)S(1)}, f32[32,576]{1,0:T(8,128)S(1)}, u32[]{:S(2)}, u32[]{:S(2)}) collective-permute-start(f32[32,576]{1,0:T(8,128)S(1)} %get-tuple-element.20.own_ref), channel_id=1, source_target_pairs={{0,128},{128,0},{1,129},{129,1},{2,130},{130,2},{3,131},{131,3},{4... | collective-permute-start | bytes 221192 | tf_op jit(solution)/shard_map/ppermute | solution.py:421
  67.8 0.6 pad_add_fusion.ids_ref
  68.4 1.3 request_layout.1.layout_ref
  69.7 3.1 %collective-permute-start.6 = (bf16[8,32,1536]{2,1,0:T(8,128)(2,1)}, bf16[8,32,1536]{2,1,0:T(8,128)(2,1)S(1)}, u32[]{:S(2)}, u32[]{:S(2)}) collective-permute-start(bf16[8,32,1536]{2,1,0:T(8,128)(2,1)} %get-tuple-element.29), channel_id=1, source_target_pairs={{0,96},{32,0},{64,32},{96,64},{1,97},{33,1},{65,33},{97,65},{2,98}... | collective-permute-start | bytes 2359304 | tf_op jit(solution)/shard_map/ppermute | solution.py:422
  72.8 3.4 %collective-permute-start.5 = (bf16[8,32,1536]{2,1,0:T(8,128)(2,1)}, bf16[8,32,1536]{2,1,0:T(8,128)(2,1)}, u32[]{:S(2)}, u32[]{:S(2)}) collective-permute-start(bf16[8,32,1536]{2,1,0:T(8,128)(2,1)} %get-tuple-element.29), channel_id=1, source_target_pairs={{0,64},{32,96},{64,0},{96,32},{1,65},{33,97},{65,1},{97,33},{2,66}... | collective-permute-start | bytes 2359304 | tf_op jit(solution)/shard_map/ppermute | solution.py:422
  76.2 1.9 %collective-permute-start.4 = (bf16[8,32,1536]{2,1,0:T(8,128)(2,1)}, bf16[8,32,1536]{2,1,0:T(8,128)(2,1)}, u32[]{:S(2)}, u32[]{:S(2)}) collective-permute-start(bf16[8,32,1536]{2,1,0:T(8,128)(2,1)} %get-tuple-element.29), channel_id=1, source_target_pairs={{0,32},{32,64},{64,96},{96,0},{1,33},{33,65},{65,97},{97,1},{2,34}... | collective-permute-start | bytes 2359304 | tf_op jit(solution)/shard_map/ppermute | solution.py:422
  78.1 0.0 collective-permute-done.1.other_ref
  78.1 0.0 copy-start.9
  78.1 0.0 copy-done.6
  78.1 0.6 copy-done.9
  78.8 2.2 %norm_rows.1 = bf16[8,32,640]{2,1,0:T(8,128)(2,1)} custom-call(s32[64]{0:T(128)} %request_layout.1.layout_ref, f32[32,576]{1,0:T(8,128)} %copy-done.6, f32[32,576]{1,0:T(8,128)} %copy-done.9, f32[1,512]{1,0:T(1,128)} %bitcast.18, f32[640,128]{1,0:T(8,128)} %constant.22.clone.cos_ref, f32[640,128]{1,0:T(8,128)} %constant.23.clone.sin_ref), custom_call_target="tpu_custom_call" | custom-call | flops 1000000 | bytes 1000000 | tf_op jit(solution)/shard_map/norm_rows/pallas_call | solution.py:193
  80.9 4.1 %all-to-all-start.2 = ((bf16[8,32,640]{2,1,0:T(8,128)(2,1)}), bf16[8,32,640]{2,1,0:T(8,128)(2,1)}, u32[]{:S(2)}, u32[]{:S(2)}) async-start(bf16[8,32,640]{2,1,0:T(8,128)(2,1)} %norm_rows.1), calls=%async_computation.2 | async-start | bytes 655360 | tf_op jit(solution)/shard_map/all_to_all | solution.py:424
  85.0 0.0 collective-permute-done.2
  85.0 0.1 pad_maximum_fusion.1
  85.1 2.2 %collective-permute-start.3 = (bf16[6,4,2112]{2,1,0:T(4,128)(2,1)S(1)}, bf16[6,4,2112]{2,1,0:T(4,128)(2,1)S(1)}, u32[]{:S(2)}, u32[]{:S(2)}) collective-permute-start(bf16[6,4,2112]{2,1,0:T(4,128)(2,1)S(1)} %pad_maximum_fusion.1), channel_id=1, source_target_pairs={{0,2},{1,3},{2,0},{3,1},{4,6},{5,7},{6,4},{7,5},{8,10},{9,11},{10,... | collective-permute-start | bytes 304136 | tf_op jit(solution)/shard_map/ppermute | solution.py:428
  87.4 6.7 %collective-permute-done.3 = bf16[6,4,2112]{2,1,0:T(4,128)(2,1)S(1)} collective-permute-done((bf16[6,4,2112]{2,1,0:T(4,128)(2,1)S(1)}, bf16[6,4,2112]{2,1,0:T(4,128)(2,1)S(1)}, u32[]{:S(2)}, u32[]{:S(2)}) %collective-permute-start.3) | collective-permute-done | bytes 101408 | tf_op jit(solution)/shard_map/ppermute | solution.py:428
  94.0 0.1 pad_maximum_fusion.rows_ref
  94.2 1.1 prepare_decode.1.ready_ref
  95.3 2.6 %all-to-all-done.2 = bf16[8,32,640]{2,1,0:T(8,128)(2,1)} async-done(((bf16[8,32,640]{2,1,0:T(8,128)(2,1)}), bf16[8,32,640]{2,1,0:T(8,128)(2,1)}, u32[]{:S(2)}, u32[]{:S(2)}) %all-to-all-start.2) | async-done | bytes 327712 | tf_op jit(solution)/shard_map/all_to_all | solution.py:424
  97.9 0.0 collective-permute-done.6
  97.9 0.0 collective-permute-done.5
  97.9 14.3 %collective-permute-done.4 = bf16[8,32,1536]{2,1,0:T(8,128)(2,1)} collective-permute-done((bf16[8,32,1536]{2,1,0:T(8,128)(2,1)}, bf16[8,32,1536]{2,1,0:T(8,128)(2,1)}, u32[]{:S(2)}, u32[]{:S(2)}) %collective-permute-start.4) | collective-permute-done | bytes 786464 | tf_op jit(solution)/shard_map/ppermute | solution.py:422
  112.2 2.1 %broadcast_in_dim.13 = bf16[4,256,640]{2,1,0:T(8,128)(2,1)} broadcast(bf16[256,640]{1,0:T(8,128)(2,1)} %bitcast.7), dimensions={1,2} | broadcast | bytes 1638400 | tf_op jit(solution)/shard_map/broadcast_in_dim | solution.py:56
  114.4 4.3 %all-to-all-start.3 = ((bf16[4,256,640]{2,1,0:T(8,128)(2,1)}), bf16[4,256,640]{2,1,0:T(8,128)(2,1)}, u32[]{:S(2)}, u32[]{:S(2)}) async-start(bf16[4,256,640]{2,1,0:T(8,128)(2,1)} %broadcast_in_dim.13), calls=%async_computation.3 | async-start | bytes 2621440 | tf_op jit(solution)/shard_map/all_to_all | solution.py:57
  118.7 2.5 %project_queries.4.refs_0_ = bf16[2,1024,256]{2,1,0:T(8,128)(2,1)S(1)} custom-call(s32[64]{0:T(128)S(1)} %copy-done.7, bf16[8,2,16,1536]{3,2,1,0:T(8,128)(2,1)} %bitcast.12.cq_ref, bf16[1536,384]{1,0:T(8,128)(2,1)S(1)} %copy-done, f32[640,128]{1,0:T(8,128)S(1)} %copy-done.2, f32[640,128]{1,0:T(8,128)S(1)} %copy-done.1), custom_call_target="tpu_custom_call" | custom-call | flops 300000000 | bytes 2500000 | tf_op jit(solution)/shard_map/project_queries/pallas_call | solution.py:224
  121.2 2.5 %project_queries.5.refs_0_ = bf16[2,1024,256]{2,1,0:T(8,128)(2,1)S(1)} custom-call(s32[64]{0:T(128)S(1)} %copy-done.7, bf16[8,2,16,1536]{3,2,1,0:T(8,128)(2,1)} %bitcast.11.cq_ref, bf16[1536,384]{1,0:T(8,128)(2,1)S(1)} %copy-done, f32[640,128]{1,0:T(8,128)S(1)} %copy-done.2, f32[640,128]{1,0:T(8,128)S(1)} %copy-done.1, ...), custom_call_target="tpu_custom_call", output_to_operand_aliasing={{}: (5, {})} | custom-call | flops 300000000 | bytes 2500000 | tf_op jit(solution)/shard_map/project_queries/pallas_call | solution.py:224
  123.8 2.5 %project_queries.6.refs_0_ = bf16[2,1024,256]{2,1,0:T(8,128)(2,1)S(1)} custom-call(s32[64]{0:T(128)S(1)} %copy-done.7, bf16[8,2,16,1536]{3,2,1,0:T(8,128)(2,1)} %bitcast.10.cq_ref, bf16[1536,384]{1,0:T(8,128)(2,1)S(1)} %copy-done, f32[640,128]{1,0:T(8,128)S(1)} %copy-done.2, f32[640,128]{1,0:T(8,128)S(1)} %copy-done.1, ...), custom_call_target="tpu_custom_call", output_to_operand_aliasing={{}: (5, {})} | custom-call | flops 300000000 | bytes 2500000 | tf_op jit(solution)/shard_map/project_queries/pallas_call | solution.py:224
  126.3 1.6 %project_queries.7.q_ref = bf16[2,1024,256]{2,1,0:T(8,128)(2,1)S(1)} custom-call(s32[64]{0:T(128)S(1)} %copy-done.7, bf16[8,2,16,1536]{3,2,1,0:T(8,128)(2,1)S(1)} %bitcast.14, bf16[1536,384]{1,0:T(8,128)(2,1)S(1)} %copy-done, f32[640,128]{1,0:T(8,128)S(1)} %copy-done.2, f32[640,128]{1,0:T(8,128)S(1)} %copy-done.1, ...), custom_call_target="tpu_custom_call", output_to_operand_aliasing={{}: (5, {})} | custom-call | flops 300000000 | bytes 2500000 | tf_op jit(solution)/shard_map/project_queries/pallas_call | solution.py:224
  127.9 9.2 %all-to-all-done.3 = bf16[4,256,640]{2,1,0:T(8,128)(2,1)} async-done(((bf16[4,256,640]{2,1,0:T(8,128)(2,1)}), bf16[4,256,640]{2,1,0:T(8,128)(2,1)}, u32[]{:S(2)}, u32[]{:S(2)}) %all-to-all-start.3) | async-done | bytes 1310752 | tf_op jit(solution)/shard_map/all_to_all | solution.py:57
  137.1 3.3 %decode_attention.1 = bf16[4,16,256]{2,1,0:T(8,128)(2,1)} custom-call(s32[64]{0:T(128)S(1)} %copy-done.7, bf16[48,640]{1,0:T(8,128)(2,1)S(1)} %prepare_decode.1.ready_ref, bf16[1024,640]{1,0:T(8,128)(2,1)} %bitcast.8.cache_ref, bf16[512,512]{1,0:T(8,128)(2,1)S(1)} %copy-done.3), custom_call_target="tpu_custom_call" | custom-call | flops 100000000 | bytes 2000000 | tf_op jit(solution)/shard_map/decode_attention/pallas_call | solution.py:328
  140.4 5.1 %all-to-all-start.4 = ((bf16[4,16,256]{2,1,0:T(8,128)(2,1)}), bf16[4,16,256]{2,1,0:T(8,128)(2,1)S(1)}, u32[]{:S(2)}, u32[]{:S(2)}) async-start(bf16[4,16,256]{2,1,0:T(8,128)(2,1)} %decode_attention.1), calls=%async_computation.4 | async-start | bytes 65536 | tf_op jit(solution)/shard_map/all_to_all | solution.py:441
  145.5 6.7 %prefill_attention.1 = bf16[1024,256]{1,0:T(8,128)(2,1)} custom-call(s32[64]{0:T(128)S(1)} %copy-done.7, bf16[2,1024,256]{2,1,0:T(8,128)(2,1)S(1)} %project_queries.7.q_ref, bf16[1024,640]{1,0:T(8,128)(2,1)} %bitcast.8.cache_ref, bf16[512,512]{1,0:T(8,128)(2,1)S(1)} %copy-done.3), custom_call_target="tpu_custom_call" | custom-call | flops 1500000000 | bytes 4000000 | tf_op jit(solution)/shard_map/prefill_attention/pallas_call | solution.py:389
  152.2 0.0 all-to-all-done.4.pool_ref
  152.2 0.6 copy-done.8
  152.8 1.5 select_slots.1
  (23 shorter events, 0.1 us)
Async XLA Ops:
  2.4 6.4 %copy-start.10 = (bf16[1,16,1536]{2,1,0:T(8,128)(2,1)S(1)}, bf16[1,16,1536]{2,1,0:T(8,128)(2,1)}, u32[]{:S(2)}) copy-start(bf16[1,16,1536]{2,1,0:T(8,128)(2,1)} %param.13) | copy-start | bytes 147460
  4.5 16.8 %all-to-all-start = ((bf16[4,112,832]{2,1,0:T(8,128)(2,1)}), bf16[4,112,832]{2,1,0:T(8,128)(2,1)S(1)}, u32[]{:S(2)}, u32[]{:S(2)}) async-start(bf16[4,112,832]{2,1,0:T(8,128)(2,1)} %pack_hidden.1), calls=%async_computation | async-start | bytes 1605632 | tf_op jit(solution)/shard_map/all_to_all | solution.py:414
  8.8 10.4 %collective-permute-start = (bf16[16,1536]{1,0:T(8,128)(2,1)S(1)}, bf16[16,1536]{1,0:T(8,128)(2,1)S(1)}, u32[]{:S(2)}, u32[]{:S(2)}) collective-permute-start(bf16[16,1536]{1,0:T(8,128)(2,1)S(1)} %bitcast.16), channel_id=1, source_target_pairs={{0,128},{128,0},{1,129},{129,1},{2,130},{130,2},{3,131},{131,3},{4... | collective-permute-start | bytes 147464 | tf_op jit(solution)/shard_map/ppermute | solution.py:413
  22.7 10.5 %copy-start.11 = (bf16[3,4,1536]{2,1,0:T(4,128)(2,1)S(1)}, bf16[3,4,1536]{2,1,0:T(4,128)(2,1)}, u32[]{:S(2)}) copy-start(bf16[3,4,1536]{2,1,0:T(4,128)(2,1)} %param.20) | copy-start | bytes 110596
  22.7 10.5 %copy-start.12 = (bf16[3,4,576]{2,1,0:T(4,128)(2,1)S(1)}, bf16[3,4,576]{2,1,0:T(4,128)(2,1)}, u32[]{:S(2)}) copy-start(bf16[3,4,576]{2,1,0:T(4,128)(2,1)} %param.21) | copy-start | bytes 41476
  22.7 39.4 %all-to-all-start.1 = ((bf16[8,32,2112]{2,1,0:T(8,128)(2,1)}), bf16[8,32,2112]{2,1,0:T(8,128)(2,1)S(1)}, u32[]{:S(2)}, u32[]{:S(2)}) async-start(bf16[8,32,2112]{2,1,0:T(8,128)(2,1)} %partial_and_rows.1), calls=%async_computation.1 | async-start | bytes 2228224 | tf_op jit(solution)/shard_map/all_to_all | solution.py:419
  33.2 51.8 %collective-permute-start.2 = (bf16[3,4,2112]{2,1,0:T(4,128)(2,1)S(1)}, bf16[3,4,2112]{2,1,0:T(4,128)(2,1)S(1)}, u32[]{:S(2)}, u32[]{:S(2)}) collective-permute-start(bf16[3,4,2112]{2,1,0:T(4,128)(2,1)S(1)} %constant_dynamic-update-slice_fusion), channel_id=1, source_target_pairs={{0,1},{1,0},{2,3},{3,2},{4,5},{5,4},{6,7},{7,6},{8,9},{9,8},{10,11... | collective-permute-start | bytes 152072 | tf_op jit(solution)/shard_map/ppermute | solution.py:428
  63.1 15.0 %copy-start.6 = (f32[32,576]{1,0:T(8,128)}, f32[32,576]{1,0:T(8,128)S(1)}, u32[]{:S(2)}) copy-start(f32[32,576]{1,0:T(8,128)S(1)} %get-tuple-element.20.own_ref) | copy-start | bytes 221188
  63.1 15.0 %collective-permute-start.1 = (f32[32,576]{1,0:T(8,128)S(1)}, f32[32,576]{1,0:T(8,128)S(1)}, u32[]{:S(2)}, u32[]{:S(2)}) collective-permute-start(f32[32,576]{1,0:T(8,128)S(1)} %get-tuple-element.20.own_ref), channel_id=1, source_target_pairs={{0,128},{128,0},{1,129},{129,1},{2,130},{130,2},{3,131},{131,3},{4... | collective-permute-start | bytes 221192 | tf_op jit(solution)/shard_map/ppermute | solution.py:421
  69.7 28.2 %collective-permute-start.6 = (bf16[8,32,1536]{2,1,0:T(8,128)(2,1)}, bf16[8,32,1536]{2,1,0:T(8,128)(2,1)S(1)}, u32[]{:S(2)}, u32[]{:S(2)}) collective-permute-start(bf16[8,32,1536]{2,1,0:T(8,128)(2,1)} %get-tuple-element.29), channel_id=1, source_target_pairs={{0,96},{32,0},{64,32},{96,64},{1,97},{33,1},{65,33},{97,65},{2,98}... | collective-permute-start | bytes 2359304 | tf_op jit(solution)/shard_map/ppermute | solution.py:422
  72.8 25.1 %collective-permute-start.5 = (bf16[8,32,1536]{2,1,0:T(8,128)(2,1)}, bf16[8,32,1536]{2,1,0:T(8,128)(2,1)}, u32[]{:S(2)}, u32[]{:S(2)}) collective-permute-start(bf16[8,32,1536]{2,1,0:T(8,128)(2,1)} %get-tuple-element.29), channel_id=1, source_target_pairs={{0,64},{32,96},{64,0},{96,32},{1,65},{33,97},{65,1},{97,33},{2,66}... | collective-permute-start | bytes 2359304 | tf_op jit(solution)/shard_map/ppermute | solution.py:422
  76.2 36.1 %collective-permute-start.4 = (bf16[8,32,1536]{2,1,0:T(8,128)(2,1)}, bf16[8,32,1536]{2,1,0:T(8,128)(2,1)}, u32[]{:S(2)}, u32[]{:S(2)}) collective-permute-start(bf16[8,32,1536]{2,1,0:T(8,128)(2,1)} %get-tuple-element.29), channel_id=1, source_target_pairs={{0,32},{32,64},{64,96},{96,0},{1,33},{33,65},{65,97},{97,1},{2,34}... | collective-permute-start | bytes 2359304 | tf_op jit(solution)/shard_map/ppermute | solution.py:422
  78.1 0.6 copy-start.9
  78.7 15.5 %copy-start = (bf16[1536,384]{1,0:T(8,128)(2,1)S(1)}, bf16[1536,384]{1,0:T(8,128)(2,1)}, u32[]{:S(2)}) copy-start(bf16[1536,384]{1,0:T(8,128)(2,1)} %w_ref.9) | copy-start | bytes 3538948
  78.7 15.5 %copy-start.1 = (f32[640,128]{1,0:T(8,128)S(1)}, f32[640,128]{1,0:T(8,128)}, u32[]{:S(2)}) copy-start(f32[640,128]{1,0:T(8,128)} %constant.23.clone.sin_ref) | copy-start | bytes 983044
  78.7 15.5 %copy-start.2 = (f32[640,128]{1,0:T(8,128)S(1)}, f32[640,128]{1,0:T(8,128)}, u32[]{:S(2)}) copy-start(f32[640,128]{1,0:T(8,128)} %constant.22.clone.cos_ref) | copy-start | bytes 983044
  78.7 15.5 %copy-start.3 = (bf16[512,512]{1,0:T(8,128)(2,1)S(1)}, bf16[512,512]{1,0:T(8,128)(2,1)}, u32[]{:S(2)}) copy-start(bf16[512,512]{1,0:T(8,128)(2,1)} %kv_ref.5) | copy-start | bytes 1572868
  78.7 15.5 %copy-start.7 = (s32[64]{0:T(128)S(1)}, s32[64]{0:T(128)}, u32[]{:S(2)}) copy-start(s32[64]{0:T(128)} %request_layout.1.layout_ref) | copy-start | bytes 772
  80.9 17.0 %all-to-all-start.2 = ((bf16[8,32,640]{2,1,0:T(8,128)(2,1)}), bf16[8,32,640]{2,1,0:T(8,128)(2,1)}, u32[]{:S(2)}, u32[]{:S(2)}) async-start(bf16[8,32,640]{2,1,0:T(8,128)(2,1)} %norm_rows.1), calls=%async_computation.2 | async-start | bytes 655360 | tf_op jit(solution)/shard_map/all_to_all | solution.py:424
  85.1 8.9 %collective-permute-start.3 = (bf16[6,4,2112]{2,1,0:T(4,128)(2,1)S(1)}, bf16[6,4,2112]{2,1,0:T(4,128)(2,1)S(1)}, u32[]{:S(2)}, u32[]{:S(2)}) collective-permute-start(bf16[6,4,2112]{2,1,0:T(4,128)(2,1)S(1)} %pad_maximum_fusion.1), channel_id=1, source_target_pairs={{0,2},{1,3},{2,0},{3,1},{4,6},{5,7},{6,4},{7,5},{8,10},{9,11},{10,... | collective-permute-start | bytes 304136 | tf_op jit(solution)/shard_map/ppermute | solution.py:428
  97.9 16.5 %copy-start.4 = (bf16[8,32,1536]{2,1,0:T(8,128)(2,1)}, bf16[8,32,1536]{2,1,0:T(8,128)(2,1)S(1)}, u32[]{:S(2)}) copy-start(bf16[8,32,1536]{2,1,0:T(8,128)(2,1)S(1)} %collective-permute-done.6) | copy-start | bytes 2359300
  114.4 22.7 %all-to-all-start.3 = ((bf16[4,256,640]{2,1,0:T(8,128)(2,1)}), bf16[4,256,640]{2,1,0:T(8,128)(2,1)}, u32[]{:S(2)}, u32[]{:S(2)}) async-start(bf16[4,256,640]{2,1,0:T(8,128)(2,1)} %broadcast_in_dim.13), calls=%async_computation.3 | async-start | bytes 2621440 | tf_op jit(solution)/shard_map/all_to_all | solution.py:57
  123.8 2.5 %copy-start.5 = (bf16[8,32,1536]{2,1,0:T(8,128)(2,1)S(1)}, bf16[8,32,1536]{2,1,0:T(8,128)(2,1)}, u32[]{:S(2)}) copy-start(bf16[8,32,1536]{2,1,0:T(8,128)(2,1)} %copy-done.4) | copy-start | bytes 2359300
  140.4 11.8 %all-to-all-start.4 = ((bf16[4,16,256]{2,1,0:T(8,128)(2,1)}), bf16[4,16,256]{2,1,0:T(8,128)(2,1)S(1)}, u32[]{:S(2)}, u32[]{:S(2)}) async-start(bf16[4,16,256]{2,1,0:T(8,128)(2,1)} %decode_attention.1), calls=%async_computation.4 | async-start | bytes 65536 | tf_op jit(solution)/shard_map/all_to_all | solution.py:441
  152.2 0.6 copy-start.8

commit v7 on v5

--- a/solution.py
+++ b/solution.py
@@ -66,7 +66,7 @@
 
 
 def layout_kernel(ids_ref, req_ref, slot_ref, out_ref):
-    rep, x, yh, z = ids_ref[0], ids_ref[1], ids_ref[2], ids_ref[3]
+    rep, x, z = ids_ref[0], ids_ref[1], ids_ref[2]
     lengths = [req_ref[rep, r] for r in range(NREQ)]
     starts = [0, lengths[0], lengths[0] + lengths[1]]
 
@@ -86,7 +86,7 @@
     for i in range(8):
         out_ref[PLACE + i] = i - start_of(i)
         out_ref[FIRST + i] = start_of(i) * BLK
-        out_ref[BLOCK + i] = lax.rem(x + NX - i % NX, NX) * 2 + (yh ^ (i // NX))
+        out_ref[BLOCK + i] = (i % 2) * NX + lax.rem(x + NX - i // 2, NX)
 
 
 SMEM = pl.BlockSpec(memory_space=pltpu.SMEM)
@@ -152,8 +152,9 @@
     )(layout, own, other, gain, cos_part, sin_part)
 
 
-def query_kernel(layout_ref, cq_ref, w_ref, cos_ref, sin_ref, out_ref):
-    rows = cq_ref[...].reshape(BLK, -1)
+def query_kernel(layout_ref, cq_ref, w_ref, cos_ref, sin_ref, *refs):
+    out_ref = refs[-1]
+    rows = cq_ref[0]
     u = jnp.dot(rows, w_ref[...], preferred_element_type=f32)
     first, second, pe = split_heads(u)
     pe = rotate(pe, cos_ref[...], sin_ref[...])
@@ -164,27 +165,34 @@
     out_ref[1, :, NOPE:] = jnp.where(low, 0.0, pe).astype(bf16)
 
 
-def project_queries(layout, cq, weights, cos_part, sin_part):
+def project_queries(d, layout, cq, weights, cos_part, sin_part, queries):
     width = cq.shape[-1]
-    table = pl.BlockSpec((BLK, 2 * ROPE), lambda i, place: (place[PLACE + i], 0))
+
+    def block(j, place):
+        return place[BLOCK + 2 * d + j]
+
+    table = pl.BlockSpec((BLK, 2 * ROPE), lambda j, place: (place[PLACE + block(j, place)], 0))
+    earlier = [] if queries is None else [queries]
     return pl.pallas_call(
         query_kernel,
         grid_spec=pltpu.PrefetchScalarGridSpec(
             num_scalar_prefetch=1,
-            grid=(8,),
+            grid=(2,),
             in_specs=[
-                pl.BlockSpec((8, 1, PAD, width), lambda i, place: (0, place[BLOCK + i], 0, 0)),
-                pl.BlockSpec(weights.shape, lambda i, place: (0, 0)),
+                pl.BlockSpec((1, BLK, width), lambda j, place: (j, 0, 0)),
+                pl.BlockSpec(weights.shape, lambda j, place: (0, 0)),
                 table,
                 table,
-            ],
-            out_specs=pl.BlockSpec((HEADS, BLK, 2 * NOPE), lambda i, place: (0, i, 0)),
+            ]
+            + [pl.BlockSpec(memory_space=pl.ANY)] * len(earlier),
+            out_specs=pl.BlockSpec((HEADS, BLK, 2 * NOPE), lambda j, place: (0, block(j, place), 0)),
         ),
         out_shape=jax.ShapeDtypeStruct((HEADS, 8 * BLK, 2 * NOPE), bf16),
+        input_output_aliases={5: 0} if earlier else {},
         compiler_params=pltpu.CompilerParams(vmem_limit_bytes=VMEM_LIMIT),
-        cost_estimate=pl.CostEstimate(flops=1_200_000_000, bytes_accessed=5_000_000, transcendentals=0),
+        cost_estimate=pl.CostEstimate(flops=300_000_000, bytes_accessed=2_500_000, transcendentals=0),
         name="project_queries",
-    )(layout, cq, weights, cos_part, sin_part)
+    )(layout, cq, weights, cos_part, sin_part, *earlier)
 
 
 def prepare_kernel(layout_ref, rows_ref, w_ref, kv_ref, cos_ref, sin_ref, out_ref, in_ref, cos_at, sin_at):
@@ -347,28 +355,24 @@
 
 def body(hidden, comp_query, kv_down, kv_gain, q_up, kv_up, req_blocks, dest_slot, dec_query, dec_latent):
     ids = jnp.stack(
-        [lax.axis_index("rep"), lax.axis_index("x"), lax.axis_index("yh"), lax.axis_index("z")]
+        [lax.axis_index("rep"), lax.axis_index("x"), lax.axis_index("z"), lax.axis_index("yh")]
     ).astype(i32)
-    rows, features = hidden.shape[1:]
+    rows = hidden.shape[1]
     per_x = rows // NX
-    chunk = per_x // 8
     cos_part, sin_part = rotary_table()
 
-    own = comp_query[0]
-    other = lax.ppermute(own, "yh", shift(2, 1))
-    pair = jnp.stack([own, other])
-    packed, pair = lax.optimization_barrier((pack(hidden[0], kv_down), pair))
+    layout = request_layout(ids, req_blocks, dest_slot)
+    near = spread(comp_query[0], ("yh", "z"), 16).reshape(2, BLK, -1)
+    packed, near = lax.optimization_barrier((pack(hidden[0], kv_down), near))
+    chunks = [near] + [lax.ppermute(near, "x", shift(NX, d)) for d in range(1, NX)]
     packed = lax.all_to_all(packed, "x", 0, 0, tiled=True)
-    layout = request_layout(ids, req_blocks, dest_slot)
-    line = [pair] + [lax.ppermute(pair, "x", shift(NX, d)) for d in range(1, NX)]
-    line = jnp.concatenate(line).reshape(BLK, -1)
-    packed, line, dec_query, dec_latent = lax.optimization_barrier((packed, line, dec_query, dec_latent))
-    cq = lax.all_gather(line, "z", axis=0, tiled=True)
-    packed = packed.reshape(NX * features, -1)
+    packed, dec_query, dec_latent = lax.optimization_barrier((packed, dec_query, dec_latent))
+    packed = packed.reshape(-1, packed.shape[2])
     partial = lax.dot_general(
         packed[:, :per_x], packed[:, per_x:], (((0,), (0,)), ((), ())), preferred_element_type=f32
     )
-    pieces = lax.all_to_all(partial.reshape(8, chunk, -1), "z", 0, 0, tiled=True)
+    pieces = lax.all_to_all(partial.reshape(8, per_x // 8, -1), "z", 0, 0, tiled=True)
+    pieces, chunks[1], chunks[3] = lax.optimization_barrier((pieces, chunks[1], chunks[3]))
     summed = jnp.sum(pieces, axis=0)
     met = lax.ppermute(summed, "yh", shift(2, 1))
     copies = norm_rows(layout, summed, met, kv_gain[None, :], cos_part, sin_part)
@@ -379,10 +383,14 @@
         met = lax.ppermute(rep_in, "rep", [(i, i ^ d) for i in range(NREP)])
         rep_in = jnp.concatenate([rep_in, met])
     ready = prepare_decode(layout, rep_in, q_up, kv_up, cos_part, sin_part)
-    cache, ready = lax.optimization_barrier((cache, ready))
+    cache, ready, *chunks = lax.optimization_barrier((cache, ready, *chunks))
     cache = spread(cache, "x", NX).reshape(rows, -1)
 
-    queries = project_queries(layout, cq.reshape(8, 8, PAD, -1), q_up, cos_part, sin_part)
+    queries = None
+    for d, chunk_rows in enumerate(chunks):
+        queries = project_queries(
+            d, layout, chunk_rows, q_up, cos_part, sin_part, queries
+        )
     cache, queries = lax.optimization_barrier((cache, queries))
     result = decode(layout, ready, cache, kv_up)
     pool = lax.all_to_all(result, "rep", 0, 0, tiled=True)

time: 151 us -> 158 us (1.046)
  the two profiles are of different devices: /device:TPU:8 before, /device:TPU:56 now
where the time goes in v7:
time: 158 us; the launch traced here: 155 us
  starting transfers between devices  60 us (38%)
  waiting for transfers between devices  44 us (28%)
  Pallas kernels  25 us (16%)
  blocking collectives  14.3 us (9%)
  local copies, waits for them, and re-layouts  9.06 us (6%)
    all_to_all x2, waiting for transfers between devices, spread(): return lax.all_to_all(copies, axes, 0, 0, tiled=True)  22.3 us
    all_to_all x2, starting transfers between devices, spread(): return lax.all_to_all(copies, axes, 0, 0, tiled=True)  20 us
    all_to_all x1, blocking collectives, body(): packed = lax.all_to_all(packed, 'x', 0, 0, tiled=True)  14.3 us
    ppermute x3, waiting for transfers between devices, body(): lax.ppermute(near, 'x', shift(NX, d))  14 us
    ppermute x2, starting transfers between devices, body(): met = lax.ppermute(rep_in, 'rep', [(i, i ^ d) for i in range(NREP)])  9.18 us
    ppermute x3, starting transfers between devices, body(): lax.ppermute(near, 'x', shift(NX, d))  7.99 us
    all_to_all x1, starting transfers between devices, body(): pool = lax.all_to_all(result, 'rep', 0, 0, tiled=True)  7.08 us
    pallas_call x4, Pallas kernels, project_queries(): pl.pallas_call(query_kernel, grid_spec=pltpu.PrefetchScalarGridSpec(num_s...  7.03 us
  transfers between devices with their start and end apart: 11, of which 7 were waited for; matrix products, arithmetic and copies ran while one was open for 1% of the time, Pallas kernels for 13%

profile of v7, /device:TPU:56, one launch (start us, length us, event | category | flops | bytes accessed | tf_op | source)
XLA Modules:
  0.0 155.4 jit_solution(15491202743113333020)
XLA Ops:
  0.6 1.9 %broadcast_in_dim.20 = bf16[16,16,1536]{2,1,0:T(8,128)(2,1)} broadcast(bf16[16,1536]{1,0:T(8,128)(2,1)} %bitcast.19), dimensions={1,2} | broadcast | bytes 835584 | tf_op jit(solution)/shard_map/broadcast_in_dim | solution.py:56
  2.5 15.7 %all-to-all-start = ((bf16[16,16,1536]{2,1,0:T(8,128)(2,1)}), bf16[16,16,1536]{2,1,0:T(8,128)(2,1)S(1)}, u32[]{:S(2)}, u32[]{:S(2)}) async-start(bf16[16,16,1536]{2,1,0:T(8,128)(2,1)} %broadcast_in_dim.20), calls=%async_computation | async-start | bytes 1572864 | tf_op jit(solution)/shard_map/all_to_all | solution.py:57
  18.2 0.8 copy.18
  19.0 2.1 %pack_hidden.1 = bf16[4,112,832]{2,1,0:T(8,128)(2,1)} custom-call(bf16[1024,112]{1,0:T(8,128)(2,1)} %bitcast.18, bf16[112,576]{1,0:T(8,128)(2,1)} %down_ref.1), custom_call_target="tpu_custom_call" | custom-call | flops 26000000 | bytes 1200000 | tf_op jit(solution)/shard_map/pack_hidden/pallas_call | solution.py:120
  21.2 17.7 %all-to-all-done = bf16[16,16,1536]{2,1,0:T(8,128)(2,1)S(1)} async-done(((bf16[16,16,1536]{2,1,0:T(8,128)(2,1)}), bf16[16,16,1536]{2,1,0:T(8,128)(2,1)S(1)}, u32[]{:S(2)}, u32[]{:S(2)}) %all-to-all-start) | async-done | bytes 786464 | tf_op jit(solution)/shard_map/all_to_all | solution.py:57
  38.9 14.3 %all_to_all.30 = bf16[4,112,832]{2,1,0:T(8,128)(2,1)S(1)} all-to-all(bf16[4,112,832]{2,1,0:T(8,128)(2,1)} %pack_hidden.1), channel_id=1, replica_groups=mesh['section'=2,'yh'=2,'x'=4,'z'=8,'rep'=4] {'x'}, dimensions={0} | all-to-all | bytes 1490944 | tf_op jit(solution)/shard_map/all_to_all | solution.py:368
  53.2 1.2 fusion
  54.4 6.8 %all-to-all-start.2 = ((f32[8,32,576]{2,1,0:T(8,128)}), f32[8,32,576]{2,1,0:T(8,128)S(1)}, u32[]{:S(2)}, u32[]{:S(2)}) async-start(f32[8,32,576]{2,1,0:T(8,128)} %bitcast.8), calls=%async_computation.2 | async-start | bytes 1310720 | tf_op jit(solution)/shard_map/all_to_all | solution.py:374
  61.2 3.1 %collective-permute-start.1 = (bf16[2,128,1536]{2,1,0:T(8,128)(2,1)S(1)}, bf16[2,128,1536]{2,1,0:T(8,128)(2,1)S(1)}, u32[]{:S(2)}, u32[]{:S(2)}) collective-permute-start(bf16[2,128,1536]{2,1,0:T(8,128)(2,1)S(1)} %bitcast.13), channel_id=1, source_target_pairs={{0,96},{32,0},{64,32},{96,64},{1,97},{33,1},{65,33},{97,65},{2,98}... | collective-permute-start | bytes 2359304 | tf_op jit(solution)/shard_map/ppermute | solution.py:367
  64.3 2.8 %collective-permute-start = (bf16[2,128,1536]{2,1,0:T(8,128)(2,1)S(1)}, bf16[2,128,1536]{2,1,0:T(8,128)(2,1)S(1)}, u32[]{:S(2)}, u32[]{:S(2)}) collective-permute-start(bf16[2,128,1536]{2,1,0:T(8,128)(2,1)S(1)} %bitcast.14), channel_id=1, source_target_pairs={{0,32},{32,64},{64,96},{96,0},{1,33},{33,65},{65,97},{97,1},{2,34}... | collective-permute-start | bytes 2359304 | tf_op jit(solution)/shard_map/ppermute | solution.py:367
  67.1 2.8 %collective-permute-start.3 = (bf16[3,4,2112]{2,1,0:T(4,128)(2,1)S(1)}, bf16[3,4,2112]{2,1,0:T(4,128)(2,1)S(1)}, u32[]{:S(2)}, u32[]{:S(2)}) collective-permute-start(bf16[3,4,2112]{2,1,0:T(4,128)(2,1)S(1)} %constant_dynamic-update-slice_fusion), channel_id=1, source_target_pairs={{0,1},{1,0},{2,3},{3,2},{4,5},{5,4},{6,7},{7,6},{8,9},{9,8},{10,11... | collective-permute-start | bytes 152072 | tf_op jit(solution)/shard_map/ppermute | solution.py:383
  69.9 10.9 %collective-permute-done.1.cq_ref = bf16[2,128,1536]{2,1,0:T(8,128)(2,1)S(1)} collective-permute-done((bf16[2,128,1536]{2,1,0:T(8,128)(2,1)S(1)}, bf16[2,128,1536]{2,1,0:T(8,128)(2,1)S(1)}, u32[]{:S(2)}, u32[]{:S(2)}) %collective-permute-start.1) | collective-permute-done | bytes 786464 | tf_op jit(solution)/shard_map/ppermute | solution.py:367
  80.8 0.9 copy-done.6
  81.7 3.1 %collective-permute-done.cq_ref = bf16[2,128,1536]{2,1,0:T(8,128)(2,1)S(1)} collective-permute-done((bf16[2,128,1536]{2,1,0:T(8,128)(2,1)S(1)}, bf16[2,128,1536]{2,1,0:T(8,128)(2,1)S(1)}, u32[]{:S(2)}, u32[]{:S(2)}) %collective-permute-start) | collective-permute-done | bytes 786464 | tf_op jit(solution)/shard_map/ppermute | solution.py:367
  84.8 0.9 copy-done.8
  85.7 0.0 all-to-all-done.2
  85.7 0.0 copy-start
  85.8 0.0 copy-start.1
  85.8 0.0 copy-start.2
  85.8 0.0 copy-start.5
  85.8 2.1 %collective-permute-start.2 = (f32[32,576]{1,0:T(8,128)S(1)}, f32[32,576]{1,0:T(8,128)S(1)}, u32[]{:S(2)}, u32[]{:S(2)}) collective-permute-start(f32[32,576]{1,0:T(8,128)S(1)} %reduce_sum.9.own_ref), channel_id=1, source_target_pairs={{0,128},{128,0},{1,129},{129,1},{2,130},{130,2},{3,131},{131,3},{4... | collective-permute-start | bytes 221192 | tf_op jit(solution)/shard_map/ppermute | solution.py:377
  87.8 0.6 pad_add_fusion.ids_ref
  88.4 1.3 request_layout.1.layout_ref
  89.8 2.2 %collective-permute-start.5 = (bf16[2,128,1536]{2,1,0:T(8,128)(2,1)S(1)}, bf16[2,128,1536]{2,1,0:T(8,128)(2,1)}, u32[]{:S(2)}, u32[]{:S(2)}) collective-permute-start(bf16[2,128,1536]{2,1,0:T(8,128)(2,1)S(1)} %bitcast.15), channel_id=1, source_target_pairs={{0,64},{32,96},{64,0},{96,32},{1,65},{33,97},{65,1},{97,33},{2,66}... | collective-permute-start | bytes 2359304 | tf_op jit(solution)/shard_map/ppermute | solution.py:367
  92.0 4.2 %collective-permute-done.2.other_ref = f32[32,576]{1,0:T(8,128)S(1)} collective-permute-done((f32[32,576]{1,0:T(8,128)S(1)}, f32[32,576]{1,0:T(8,128)S(1)}, u32[]{:S(2)}, u32[]{:S(2)}) %collective-permute-start.2) | collective-permute-done | bytes 73760 | tf_op jit(solution)/shard_map/ppermute | solution.py:377
  96.2 0.6 copy-done.14
  96.8 2.1 %norm_rows.1 = bf16[8,32,640]{2,1,0:T(8,128)(2,1)} custom-call(s32[64]{0:T(128)} %request_layout.1.layout_ref, f32[32,576]{1,0:T(8,128)} %copy-done.11, f32[32,576]{1,0:T(8,128)} %copy-done.14, f32[1,512]{1,0:T(1,128)} %bitcast.20, f32[640,128]{1,0:T(8,128)} %constant.24.clone.cos_ref, f32[640,128]{1,0:T(8,128)} %constant.25.clone.sin_ref), custom_call_target="tpu_custom_call" | custom-call | flops 1000000 | bytes 1000000 | tf_op jit(solution)/shard_map/norm_rows/pallas_call | solution.py:145
  98.9 6.9 %all-to-all-start.3 = ((bf16[8,32,640]{2,1,0:T(8,128)(2,1)}), bf16[8,32,640]{2,1,0:T(8,128)(2,1)}, u32[]{:S(2)}, u32[]{:S(2)}) async-start(bf16[8,32,640]{2,1,0:T(8,128)(2,1)} %norm_rows.1), calls=%async_computation.3 | async-start | bytes 655360 | tf_op jit(solution)/shard_map/all_to_all | solution.py:379
  105.8 0.0 collective-permute-done.3
  105.8 0.1 pad_maximum_fusion.1
  105.9 6.4 %collective-permute-start.4 = (bf16[6,4,2112]{2,1,0:T(4,128)(2,1)S(1)}, bf16[6,4,2112]{2,1,0:T(4,128)(2,1)S(1)}, u32[]{:S(2)}, u32[]{:S(2)}) collective-permute-start(bf16[6,4,2112]{2,1,0:T(4,128)(2,1)S(1)} %pad_maximum_fusion.1), channel_id=1, source_target_pairs={{0,2},{1,3},{2,0},{3,1},{4,6},{5,7},{6,4},{7,5},{8,10},{9,11},{10,... | collective-permute-start | bytes 304136 | tf_op jit(solution)/shard_map/ppermute | solution.py:383
  112.3 3.2 %collective-permute-done.4 = bf16[6,4,2112]{2,1,0:T(4,128)(2,1)S(1)} collective-permute-done((bf16[6,4,2112]{2,1,0:T(4,128)(2,1)S(1)}, bf16[6,4,2112]{2,1,0:T(4,128)(2,1)S(1)}, u32[]{:S(2)}, u32[]{:S(2)}) %collective-permute-start.4) | collective-permute-done | bytes 101408 | tf_op jit(solution)/shard_map/ppermute | solution.py:383
  115.5 0.1 pad_maximum_fusion.rows_ref
  115.7 1.1 prepare_decode.1.ready_ref
  116.8 0.3 all-to-all-done.3
  117.1 2.1 %broadcast_in_dim.22 = bf16[4,256,640]{2,1,0:T(8,128)(2,1)} broadcast(bf16[256,640]{1,0:T(8,128)(2,1)} %bitcast.10), dimensions={1,2} | broadcast | bytes 1638400 | tf_op jit(solution)/shard_map/broadcast_in_dim | solution.py:56
  119.2 4.3 %all-to-all-start.4 = ((bf16[4,256,640]{2,1,0:T(8,128)(2,1)}), bf16[4,256,640]{2,1,0:T(8,128)(2,1)}, u32[]{:S(2)}, u32[]{:S(2)}) async-start(bf16[4,256,640]{2,1,0:T(8,128)(2,1)} %broadcast_in_dim.22), calls=%async_computation.4 | async-start | bytes 2621440 | tf_op jit(solution)/shard_map/all_to_all | solution.py:57
  123.6 1.1 copy-done.4
  124.7 1.5 project_queries.4.refs_0_
  126.2 1.5 project_queries.5.refs_0_
  127.7 2.5 %project_queries.6.refs_0_ = bf16[2,1024,256]{2,1,0:T(8,128)(2,1)S(1)} custom-call(s32[64]{0:T(128)S(1)} %copy-done.10, bf16[2,128,1536]{2,1,0:T(8,128)(2,1)} %collective-permute-done.5.cq_ref, bf16[1536,384]{1,0:T(8,128)(2,1)S(1)} %copy-done, f32[640,128]{1,0:T(8,128)S(1)} %copy-done.2, f32[640,128]{1,0:T(8,128)S(1)} %copy-done.1, ...), custom_call_target="tpu_custom_call", output_to_operand_aliasing={{}: (5, {})} | custom-call | flops 300000000 | bytes 2500000 | tf_op jit(solution)/shard_map/project_queries/pallas_call | solution.py:176
  130.3 1.5 project_queries.7.q_ref
  131.8 4.5 %all-to-all-done.4 = bf16[4,256,640]{2,1,0:T(8,128)(2,1)} async-done(((bf16[4,256,640]{2,1,0:T(8,128)(2,1)}), bf16[4,256,640]{2,1,0:T(8,128)(2,1)}, u32[]{:S(2)}, u32[]{:S(2)}) %all-to-all-start.4) | async-done | bytes 1310752 | tf_op jit(solution)/shard_map/all_to_all | solution.py:57
  136.3 3.3 %decode_attention.1 = bf16[4,16,256]{2,1,0:T(8,128)(2,1)} custom-call(s32[64]{0:T(128)S(1)} %copy-done.10, bf16[48,640]{1,0:T(8,128)(2,1)S(1)} %prepare_decode.1.ready_ref, bf16[1024,640]{1,0:T(8,128)(2,1)} %bitcast.11.cache_ref, bf16[512,512]{1,0:T(8,128)(2,1)S(1)} %copy-done.5), custom_call_target="tpu_custom_call" | custom-call | flops 100000000 | bytes 2000000 | tf_op jit(solution)/shard_map/decode_attention/pallas_call | solution.py:280
  139.6 7.1 %all-to-all-start.5 = ((bf16[4,16,256]{2,1,0:T(8,128)(2,1)}), bf16[4,16,256]{2,1,0:T(8,128)(2,1)S(1)}, u32[]{:S(2)}, u32[]{:S(2)}) async-start(bf16[4,16,256]{2,1,0:T(8,128)(2,1)} %decode_attention.1), calls=%async_computation.5 | async-start | bytes 65536 | tf_op jit(solution)/shard_map/all_to_all | solution.py:396
  146.7 6.7 %prefill_attention.1 = bf16[1024,256]{1,0:T(8,128)(2,1)} custom-call(s32[64]{0:T(128)S(1)} %copy-done.10, bf16[2,1024,256]{2,1,0:T(8,128)(2,1)S(1)} %project_queries.7.q_ref, bf16[1024,640]{1,0:T(8,128)(2,1)} %bitcast.11.cache_ref, bf16[512,512]{1,0:T(8,128)(2,1)S(1)} %copy-done.5), custom_call_target="tpu_custom_call" | custom-call | flops 1500000000 | bytes 4000000 | tf_op jit(solution)/shard_map/prefill_attention/pallas_call | solution.py:341
  153.4 0.6 copy-done.13
  154.0 1.5 select_slots.1
  (30 shorter events, 0.1 us)
Async XLA Ops:
  0.6 17.6 %copy-start.12 = (bf16[1,1024,112]{1,2,0:T(8,128)(2,1)S(1)}, bf16[1,1024,112]{1,2,0:T(8,128)(2,1)}, u32[]{:S(2)}) copy-start(bf16[1,1024,112]{1,2,0:T(8,128)(2,1)} %param.12) | copy-start | bytes 688132
  2.5 36.4 %all-to-all-start = ((bf16[16,16,1536]{2,1,0:T(8,128)(2,1)}), bf16[16,16,1536]{2,1,0:T(8,128)(2,1)S(1)}, u32[]{:S(2)}, u32[]{:S(2)}) async-start(bf16[16,16,1536]{2,1,0:T(8,128)(2,1)} %broadcast_in_dim.20), calls=%async_computation | async-start | bytes 1572864 | tf_op jit(solution)/shard_map/all_to_all | solution.py:57
  38.9 50.9 %copy-start.3 = (bf16[16,16,1536]{2,1,0:T(8,128)(2,1)}, bf16[16,16,1536]{2,1,0:T(8,128)(2,1)S(1)}, u32[]{:S(2)}) copy-start(bf16[16,16,1536]{2,1,0:T(8,128)(2,1)S(1)} %all-to-all-done) | copy-start | bytes 2359300
  53.2 13.9 %copy-start.15 = (bf16[3,4,1536]{2,1,0:T(4,128)(2,1)S(1)}, bf16[3,4,1536]{2,1,0:T(4,128)(2,1)}, u32[]{:S(2)}) copy-start(bf16[3,4,1536]{2,1,0:T(4,128)(2,1)} %param.20) | copy-start | bytes 110596
  53.2 13.9 %copy-start.16 = (bf16[3,4,576]{2,1,0:T(4,128)(2,1)S(1)}, bf16[3,4,576]{2,1,0:T(4,128)(2,1)}, u32[]{:S(2)}) copy-start(bf16[3,4,576]{2,1,0:T(4,128)(2,1)} %param.21) | copy-start | bytes 41476
  54.4 31.3 %all-to-all-start.2 = ((f32[8,32,576]{2,1,0:T(8,128)}), f32[8,32,576]{2,1,0:T(8,128)S(1)}, u32[]{:S(2)}, u32[]{:S(2)}) async-start(f32[8,32,576]{2,1,0:T(8,128)} %bitcast.8), calls=%async_computation.2 | async-start | bytes 1310720 | tf_op jit(solution)/shard_map/all_to_all | solution.py:374
  61.2 19.6 %collective-permute-start.1 = (bf16[2,128,1536]{2,1,0:T(8,128)(2,1)S(1)}, bf16[2,128,1536]{2,1,0:T(8,128)(2,1)S(1)}, u32[]{:S(2)}, u32[]{:S(2)}) collective-permute-start(bf16[2,128,1536]{2,1,0:T(8,128)(2,1)S(1)} %bitcast.13), channel_id=1, source_target_pairs={{0,96},{32,0},{64,32},{96,64},{1,97},{33,1},{65,33},{97,65},{2,98}... | collective-permute-start | bytes 2359304 | tf_op jit(solution)/shard_map/ppermute | solution.py:367
  64.3 20.5 %collective-permute-start = (bf16[2,128,1536]{2,1,0:T(8,128)(2,1)S(1)}, bf16[2,128,1536]{2,1,0:T(8,128)(2,1)S(1)}, u32[]{:S(2)}, u32[]{:S(2)}) collective-permute-start(bf16[2,128,1536]{2,1,0:T(8,128)(2,1)S(1)} %bitcast.14), channel_id=1, source_target_pairs={{0,32},{32,64},{64,96},{96,0},{1,33},{33,65},{65,97},{97,1},{2,34}... | collective-permute-start | bytes 2359304 | tf_op jit(solution)/shard_map/ppermute | solution.py:367
  67.1 38.7 %collective-permute-start.3 = (bf16[3,4,2112]{2,1,0:T(4,128)(2,1)S(1)}, bf16[3,4,2112]{2,1,0:T(4,128)(2,1)S(1)}, u32[]{:S(2)}, u32[]{:S(2)}) collective-permute-start(bf16[3,4,2112]{2,1,0:T(4,128)(2,1)S(1)} %constant_dynamic-update-slice_fusion), channel_id=1, source_target_pairs={{0,1},{1,0},{2,3},{3,2},{4,5},{5,4},{6,7},{7,6},{8,9},{9,8},{10,11... | collective-permute-start | bytes 152072 | tf_op jit(solution)/shard_map/ppermute | solution.py:383
  80.8 0.9 copy-start.6
  84.8 0.9 copy-start.8
  85.7 10.5 %copy-start.11 = (f32[32,576]{1,0:T(8,128)}, f32[32,576]{1,0:T(8,128)S(1)}, u32[]{:S(2)}) copy-start(f32[32,576]{1,0:T(8,128)S(1)} %reduce_sum.9.own_ref) | copy-start | bytes 221188
  85.7 29.9 %copy-start = (bf16[1536,384]{1,0:T(8,128)(2,1)S(1)}, bf16[1536,384]{1,0:T(8,128)(2,1)}, u32[]{:S(2)}) copy-start(bf16[1536,384]{1,0:T(8,128)(2,1)} %w_ref.9) | copy-start | bytes 3538948
  85.8 29.9 %copy-start.1 = (f32[640,128]{1,0:T(8,128)S(1)}, f32[640,128]{1,0:T(8,128)}, u32[]{:S(2)}) copy-start(f32[640,128]{1,0:T(8,128)} %constant.25.clone.sin_ref) | copy-start | bytes 983044
  85.8 29.9 %copy-start.2 = (f32[640,128]{1,0:T(8,128)S(1)}, f32[640,128]{1,0:T(8,128)}, u32[]{:S(2)}) copy-start(f32[640,128]{1,0:T(8,128)} %constant.24.clone.cos_ref) | copy-start | bytes 983044
  85.8 29.9 %copy-start.5 = (bf16[512,512]{1,0:T(8,128)(2,1)S(1)}, bf16[512,512]{1,0:T(8,128)(2,1)}, u32[]{:S(2)}) copy-start(bf16[512,512]{1,0:T(8,128)(2,1)} %kv_ref.5) | copy-start | bytes 1572868
  85.8 10.4 %collective-permute-start.2 = (f32[32,576]{1,0:T(8,128)S(1)}, f32[32,576]{1,0:T(8,128)S(1)}, u32[]{:S(2)}, u32[]{:S(2)}) collective-permute-start(f32[32,576]{1,0:T(8,128)S(1)} %reduce_sum.9.own_ref), channel_id=1, source_target_pairs={{0,128},{128,0},{1,129},{129,1},{2,130},{130,2},{3,131},{131,3},{4... | collective-permute-start | bytes 221192 | tf_op jit(solution)/shard_map/ppermute | solution.py:377
  89.8 25.9 %copy-start.10 = (s32[64]{0:T(128)S(1)}, s32[64]{0:T(128)}, u32[]{:S(2)}) copy-start(s32[64]{0:T(128)} %request_layout.1.layout_ref) | copy-start | bytes 772
  89.8 27.0 %collective-permute-start.5 = (bf16[2,128,1536]{2,1,0:T(8,128)(2,1)S(1)}, bf16[2,128,1536]{2,1,0:T(8,128)(2,1)}, u32[]{:S(2)}, u32[]{:S(2)}) collective-permute-start(bf16[2,128,1536]{2,1,0:T(8,128)(2,1)S(1)} %bitcast.15), channel_id=1, source_target_pairs={{0,64},{32,96},{64,0},{96,32},{1,65},{33,97},{65,1},{97,33},{2,66}... | collective-permute-start | bytes 2359304 | tf_op jit(solution)/shard_map/ppermute | solution.py:367
  96.2 0.6 copy-start.14
  98.9 18.2 %all-to-all-start.3 = ((bf16[8,32,640]{2,1,0:T(8,128)(2,1)}), bf16[8,32,640]{2,1,0:T(8,128)(2,1)}, u32[]{:S(2)}, u32[]{:S(2)}) async-start(bf16[8,32,640]{2,1,0:T(8,128)(2,1)} %norm_rows.1), calls=%async_computation.3 | async-start | bytes 655360 | tf_op jit(solution)/shard_map/all_to_all | solution.py:379
  105.9 9.6 %collective-permute-start.4 = (bf16[6,4,2112]{2,1,0:T(4,128)(2,1)S(1)}, bf16[6,4,2112]{2,1,0:T(4,128)(2,1)S(1)}, u32[]{:S(2)}, u32[]{:S(2)}) collective-permute-start(bf16[6,4,2112]{2,1,0:T(4,128)(2,1)S(1)} %pad_maximum_fusion.1), channel_id=1, source_target_pairs={{0,2},{1,3},{2,0},{3,1},{4,6},{5,7},{6,4},{7,5},{8,10},{9,11},{10,... | collective-permute-start | bytes 304136 | tf_op jit(solution)/shard_map/ppermute | solution.py:383
  119.2 17.1 %all-to-all-start.4 = ((bf16[4,256,640]{2,1,0:T(8,128)(2,1)}), bf16[4,256,640]{2,1,0:T(8,128)(2,1)}, u32[]{:S(2)}, u32[]{:S(2)}) async-start(bf16[4,256,640]{2,1,0:T(8,128)(2,1)} %broadcast_in_dim.22), calls=%async_computation.4 | async-start | bytes 2621440 | tf_op jit(solution)/shard_map/all_to_all | solution.py:57
  123.5 1.1 copy-start.4
  124.7 1.5 copy-start.9
  127.7 2.5 %copy-start.7 = (bf16[2,128,1536]{2,1,0:T(8,128)(2,1)S(1)}, bf16[2,128,1536]{2,1,0:T(8,128)(2,1)}, u32[]{:S(2)}) copy-start(bf16[2,128,1536]{2,1,0:T(8,128)(2,1)} %copy-done.6) | copy-start | bytes 2359300
  139.6 13.8 %all-to-all-start.5 = ((bf16[4,16,256]{2,1,0:T(8,128)(2,1)}), bf16[4,16,256]{2,1,0:T(8,128)(2,1)S(1)}, u32[]{:S(2)}, u32[]{:S(2)}) async-start(bf16[4,16,256]{2,1,0:T(8,128)(2,1)} %decode_attention.1), calls=%async_computation.5 | async-start | bytes 65536 | tf_op jit(solution)/shard_map/all_to_all | solution.py:396
  153.4 0.6 copy-start.13

commit v8 on v4

--- a/solution.py
+++ b/solution.py
@@ -127,11 +127,11 @@
 
 
 def norm_kernel(layout_ref, pieces_ref, gain_ref, cos_ref, sin_ref, out_ref):
-    latent = jnp.sum(pieces_ref[...].astype(f32), axis=0)
+    latent = jnp.sum(pieces_ref[...], axis=0)
     content = latent[:, :KVL]
     scale = lax.rsqrt(jnp.mean(content * content, axis=1, keepdims=True) + 1e-06)
     content = (content * scale * gain_ref[...]).astype(bf16)
-    at = pl.ds(pl.multiple_of(layout_ref[BASE], PAD), PAD)
+    at = pl.ds(pl.multiple_of(layout_ref[BASE], PAD), latent.shape[0])
     pe = jnp.concatenate([latent[:, KVL:]] * 2, axis=1)
     pe = rotate(pe, cos_ref[at, :], sin_ref[at, :]).astype(bf16)
     for i in range(out_ref.shape[0]):
@@ -355,13 +355,13 @@
 
     own = comp_query[0]
     other = lax.ppermute(own, "yh", shift(2, 1))
+    pair = jnp.stack([own, other])
     packed = lax.all_to_all(pack(hidden[0], kv_down), "x", 0, 0, tiled=True)
     layout = request_layout(ids, req_blocks, dest_slot)
-    pair = jnp.stack([own, other])
     line = [pair] + [lax.ppermute(pair, "x", shift(NX, d)) for d in range(1, NX)]
-    cq = lax.all_gather(jnp.concatenate(line).reshape(BLK, -1), "z", axis=0, tiled=True)
-
-    packed, dec_query, dec_latent = lax.optimization_barrier((packed, dec_query, dec_latent))
+    line = jnp.concatenate(line).reshape(BLK, -1)
+    packed, line, dec_query, dec_latent = lax.optimization_barrier((packed, line, dec_query, dec_latent))
+    cq = lax.all_gather(line, "z", axis=0, tiled=True)
     packed = packed.reshape(NX * features, -1)
     partial = lax.dot_general(
         packed[:, :per_x], packed[:, per_x:], (((0,), (0,)), ((), ())), preferred_element_type=f32
@@ -369,16 +369,17 @@
     pieces = lax.all_to_all(partial.reshape(16, chunk, -1), ("yh", "z"), 0, 0, tiled=True)
     copies = norm_rows(layout, pieces, kv_gain[None, :], cos_part, sin_part)
     cache = lax.all_to_all(copies, ("yh", "z"), 0, 0, tiled=True).reshape(per_x, -1)
-    cache = spread(cache, "x", NX).reshape(rows, -1)
 
     rep_in = jnp.concatenate([dec_query, dec_latent], axis=2)
     for d in (1, 2):
         met = lax.ppermute(rep_in, "rep", [(i, i ^ d) for i in range(NREP)])
         rep_in = jnp.concatenate([rep_in, met])
     ready = prepare_decode(layout, rep_in, q_up, kv_up, cos_part, sin_part)
+    cache, ready = lax.optimization_barrier((cache, ready))
+    cache = spread(cache, "x", NX).reshape(rows, -1)
 
     queries = project_queries(layout, cq.reshape(8, 8, PAD, -1), q_up, cos_part, sin_part)
-    cache, queries, ready = lax.optimization_barrier((cache, queries, ready))
+    cache, queries = lax.optimization_barrier((cache, queries))
     result = decode(layout, ready, cache, kv_up)
     pool = lax.all_to_all(result, "rep", 0, 0, tiled=True)
     prefill_out = prefill(layout, queries, cache, kv_up)[None]

time: 167 us -> 148 us (0.89); the launches traced: 164 us -> 147 us
  blocking collectives: 14.5 us -> 0 us
    all_to_all x1 -> x0, blocking collectives: 14.5 us -> none  [body(): packed = lax.all_to_all(pack(hidden[0], kv_down), 'x', 0, 0, tiled=True)]
    all_to_all x1, waiting for transfers between devices: 9.5 us -> 0.01 us  [body(): lax.all_to_all(copies, ('yh', 'z'), 0, 0, tiled=True).reshape(per_x, -1)]
    all_to_all x1, waiting for transfers between devices: 0.01 us -> 8.64 us  [spread(): return lax.all_to_all(copies, axes, 0, 0, tiled=True)]
    ppermute x1, waiting for transfers between devices: 5.09 us -> 0.01 us  [body(): other = lax.ppermute(own, 'yh', shift(2, 1))]
    all_to_all x0 -> x1, starting transfers between devices: none -> 4.3 us  [body(): packed = lax.all_to_all(pack(hidden[0], kv_down), 'x', 0, 0, tiled=True)]
    ppermute x2, starting transfers between devices: 7.52 us -> 4.3 us  [body(): met = lax.ppermute(rep_in, 'rep', [(i, i ^ d) for i in range(NREP)])]
    ppermute x2, waiting for transfers between devices: 7.07 us -> 9.77 us  [body(): met = lax.ppermute(rep_in, 'rep', [(i, i ^ d) for i in range(NREP)])]
    all_gather x1, waiting for transfers between devices: 0.01 us -> 2.29 us  [body(): cq = lax.all_gather(line, 'z', axis=0, tiled=True)]
  transfers between devices with their start and end apart: 11 -> 12, of which waited for: 6 -> 5; matrix products, arithmetic and copies ran while one was open for 3% -> 4% of each run, Pallas kernels for 11% -> 12%
where the time goes in v8:
time: 148 us; the launch traced here: 147 us
  starting transfers between devices  59.3 us (40%)
  waiting for transfers between devices  40.4 us (27%)
  Pallas kernels  21.4 us (14%)
  between operations  14.3 us (10%)
  local copies, waits for them, and re-layouts  9.16 us (6%)
    all_to_all x1, starting transfers between devices, body(): lax.all_to_all(partial.reshape(16, chunk, -1), ('yh', 'z'), 0, 0, tiled=T...  15.7 us
    all_to_all x1, waiting for transfers between devices, body(): lax.all_to_all(partial.reshape(16, chunk, -1), ('yh', 'z'), 0, 0, tiled=T...  14 us
    all_to_all x1, starting transfers between devices, body(): lax.all_to_all(copies, ('yh', 'z'), 0, 0, tiled=True).reshape(per_x, -1)  11 us
    ppermute x3, starting transfers between devices, body(): lax.ppermute(pair, 'x', shift(NX, d))  10.7 us
    ppermute x2, waiting for transfers between devices, body(): met = lax.ppermute(rep_in, 'rep', [(i, i ^ d) for i in range(NREP)])  9.77 us
    all_to_all x1, waiting for transfers between devices, spread(): return lax.all_to_all(copies, axes, 0, 0, tiled=True)  8.64 us
    unnamed x38, local copies, waits for them, and re-layouts  7.95 us
    pallas_call x1, Pallas kernels, prefill(): pl.pallas_call(prefill_kernel, in_specs=[SMEM] + [VMEM] * 3, out_specs=VM...  5.92 us
  transfers between devices with their start and end apart: 12, of which 5 were waited for; matrix products, arithmetic and copies ran while one was open for 4% of the time, Pallas kernels for 12%

profile of v8, /device:TPU:56, one launch (start us, length us, event | category | flops | bytes accessed | tf_op | source)
XLA Modules:
  0.0 146.6 jit_solution(18136134952561045977)
XLA Ops:
  7.2 4.7 %collective-permute-start = (bf16[16,1536]{1,0:T(8,128)(2,1)}, bf16[16,1536]{1,0:T(8,128)(2,1)S(1)}, u32[]{:S(2)}, u32[]{:S(2)}) collective-permute-start(bf16[16,1536]{1,0:T(8,128)(2,1)} %bitcast.23), channel_id=1, source_target_pairs={{0,128},{128,0},{1,129},{129,1},{2,130},{130,2},{3,131},{131,3},{4... | collective-permute-start | bytes 147464 | tf_op jit(solution)/shard_map/ppermute | solution.py:357
  11.9 1.8 %copy.14 = bf16[1,1024,112]{2,1,0:T(8,128)(2,1)} copy(bf16[1,1024,112]{1,2,0:T(8,128)(2,1)} %param.12) | data formatting | bytes 458752 | tf_op args[0]
  13.7 2.1 %pack_hidden.1 = bf16[4,112,832]{2,1,0:T(8,128)(2,1)} custom-call(bf16[1024,112]{1,0:T(8,128)(2,1)} %bitcast.21, bf16[112,576]{1,0:T(8,128)(2,1)} %down_ref.1), custom_call_target="tpu_custom_call" | custom-call | flops 26000000 | bytes 1200000 | tf_op jit(solution)/shard_map/pack_hidden/pallas_call | solution.py:119
  15.8 4.3 %all-to-all-start = ((bf16[4,112,832]{2,1,0:T(8,128)(2,1)}), bf16[4,112,832]{2,1,0:T(8,128)(2,1)S(1)}, u32[]{:S(2)}, u32[]{:S(2)}) async-start(bf16[4,112,832]{2,1,0:T(8,128)(2,1)} %pack_hidden.1), calls=%async_computation | async-start | bytes 1605632 | tf_op jit(solution)/shard_map/all_to_all | solution.py:359
  20.1 0.0 collective-permute-done
  20.1 5.1 %collective-permute-start.3 = (bf16[2,16,1536]{2,1,0:T(8,128)(2,1)S(1)}, bf16[2,16,1536]{2,1,0:T(8,128)(2,1)S(1)}, u32[]{:S(2)}, u32[]{:S(2)}) collective-permute-start(bf16[2,16,1536]{2,1,0:T(8,128)(2,1)S(1)} %pad_maximum_fusion.2), channel_id=1, source_target_pairs={{0,96},{32,0},{64,32},{96,64},{1,97},{33,1},{65,33},{97,65},{2,98}... | collective-permute-start | bytes 294920 | tf_op jit(solution)/shard_map/ppermute | solution.py:361
  25.3 2.8 %collective-permute-start.2 = (bf16[2,16,1536]{2,1,0:T(8,128)(2,1)S(1)}, bf16[2,16,1536]{2,1,0:T(8,128)(2,1)S(1)}, u32[]{:S(2)}, u32[]{:S(2)}) collective-permute-start(bf16[2,16,1536]{2,1,0:T(8,128)(2,1)S(1)} %pad_maximum_fusion.2), channel_id=1, source_target_pairs={{0,64},{32,96},{64,0},{96,32},{1,65},{33,97},{65,1},{97,33},{2,66}... | collective-permute-start | bytes 294920 | tf_op jit(solution)/shard_map/ppermute | solution.py:361
  28.1 2.8 %collective-permute-start.1 = (bf16[2,16,1536]{2,1,0:T(8,128)(2,1)S(1)}, bf16[2,16,1536]{2,1,0:T(8,128)(2,1)S(1)}, u32[]{:S(2)}, u32[]{:S(2)}) collective-permute-start(bf16[2,16,1536]{2,1,0:T(8,128)(2,1)S(1)} %pad_maximum_fusion.2), channel_id=1, source_target_pairs={{0,32},{32,64},{64,96},{96,0},{1,33},{33,65},{65,97},{97,1},{2,34}... | collective-permute-start | bytes 294920 | tf_op jit(solution)/shard_map/ppermute | solution.py:361
  30.8 5.6 %collective-permute-done.1 = bf16[2,16,1536]{2,1,0:T(8,128)(2,1)S(1)} collective-permute-done((bf16[2,16,1536]{2,1,0:T(8,128)(2,1)S(1)}, bf16[2,16,1536]{2,1,0:T(8,128)(2,1)S(1)}, u32[]{:S(2)}, u32[]{:S(2)}) %collective-permute-start.1) | collective-permute-done | bytes 98336 | tf_op jit(solution)/shard_map/ppermute | solution.py:361
  36.5 0.0 collective-permute-done.2
  36.5 0.0 collective-permute-done.3
  36.5 0.0 copy-start.11
  36.6 0.0 all-to-all-done
  36.6 0.7 copy-done.11
  37.3 0.0 all-gather.2.cloned.1.call-update
  37.3 0.0 copy-start.14
  37.3 0.0 copy-start.15
  37.3 1.2 fusion
  38.6 15.7 %all-to-all-start.1 = ((f32[16,16,576]{2,1,0:T(8,128)}), f32[16,16,576]{2,1,0:T(8,128)S(1)}, u32[]{:S(2)}, u32[]{:S(2)}) async-start(f32[16,16,576]{2,1,0:T(8,128)} %bitcast.9), calls=%async_computation.1 | async-start | bytes 1310720 | tf_op jit(solution)/shard_map/all_to_all | solution.py:369
  54.3 2.4 %collective-permute-start.4 = (bf16[3,4,2112]{2,1,0:T(4,128)(2,1)S(1)}, bf16[3,4,2112]{2,1,0:T(4,128)(2,1)S(1)}, u32[]{:S(2)}, u32[]{:S(2)}) collective-permute-start(bf16[3,4,2112]{2,1,0:T(4,128)(2,1)S(1)} %constant_dynamic-update-slice_fusion.5), channel_id=1, source_target_pairs={{0,1},{1,0},{2,3},{3,2},{4,5},{5,4},{6,7},{7,6},{8,9},{9,8},{10,11... | collective-permute-start | bytes 152072 | tf_op jit(solution)/shard_map/ppermute | solution.py:375
  56.7 0.7 pad_add_fusion.ids_ref
  57.4 1.3 request_layout.1.layout_ref
  58.7 14.0 %all-to-all-done.1.pieces_ref = f32[16,16,576]{2,1,0:T(8,128)S(1)} async-done(((f32[16,16,576]{2,1,0:T(8,128)}), f32[16,16,576]{2,1,0:T(8,128)S(1)}, u32[]{:S(2)}, u32[]{:S(2)}) %all-to-all-start.1) | async-done | bytes 589856 | tf_op jit(solution)/shard_map/all_to_all | solution.py:369
  72.7 0.8 copy-done.10
  73.5 2.3 %norm_rows.1 = bf16[16,16,640]{2,1,0:T(8,128)(2,1)} custom-call(s32[64]{0:T(128)} %request_layout.1.layout_ref, f32[16,16,576]{2,1,0:T(8,128)} %copy-done.10, f32[1,512]{1,0:T(1,128)} %bitcast.25, f32[640,128]{1,0:T(8,128)} %constant.24.clone.cos_ref, f32[640,128]{1,0:T(8,128)} %constant.25.clone.sin_ref), custom_call_target="tpu_custom_call" | custom-call | flops 1000000 | bytes 1000000 | tf_op jit(solution)/shard_map/norm_rows/pallas_call | solution.py:144
  75.9 11.0 %all-to-all-start.2 = ((bf16[16,16,640]{2,1,0:T(8,128)(2,1)}), bf16[16,16,640]{2,1,0:T(8,128)(2,1)S(1)}, u32[]{:S(2)}, u32[]{:S(2)}) async-start(bf16[16,16,640]{2,1,0:T(8,128)(2,1)} %norm_rows.1), calls=%async_computation.2 | async-start | bytes 655360 | tf_op jit(solution)/shard_map/all_to_all | solution.py:371
  86.9 0.0 collective-permute-done.4
  86.9 0.1 pad_maximum_fusion.1
  87.0 1.9 %collective-permute-start.5 = (bf16[6,4,2112]{2,1,0:T(4,128)(2,1)S(1)}, bf16[6,4,2112]{2,1,0:T(4,128)(2,1)S(1)}, u32[]{:S(2)}, u32[]{:S(2)}) collective-permute-start(bf16[6,4,2112]{2,1,0:T(4,128)(2,1)S(1)} %pad_maximum_fusion.1), channel_id=1, source_target_pairs={{0,2},{1,3},{2,0},{3,1},{4,6},{5,7},{6,4},{7,5},{8,10},{9,11},{10,... | collective-permute-start | bytes 304136 | tf_op jit(solution)/shard_map/ppermute | solution.py:375
  88.9 9.8 %collective-permute-done.5 = bf16[6,4,2112]{2,1,0:T(4,128)(2,1)S(1)} collective-permute-done((bf16[6,4,2112]{2,1,0:T(4,128)(2,1)S(1)}, bf16[6,4,2112]{2,1,0:T(4,128)(2,1)S(1)}, u32[]{:S(2)}, u32[]{:S(2)}) %collective-permute-start.5) | collective-permute-done | bytes 101408 | tf_op jit(solution)/shard_map/ppermute | solution.py:375
  98.7 0.1 pad_maximum_fusion.rows_ref
  98.9 1.1 prepare_decode.1.ready_ref
  99.9 0.0 all-to-all-done.2
  99.9 1.2 broadcast_in_dim.13
  101.1 3.5 %all-to-all-start.3 = ((bf16[4,256,640]{2,1,0:T(8,128)(2,1)}), bf16[4,256,640]{2,1,0:T(8,128)(2,1)S(1)}, u32[]{:S(2)}, u32[]{:S(2)}) async-start(bf16[4,256,640]{2,1,0:T(8,128)(2,1)} %broadcast_in_dim.13), calls=%async_computation.3 | async-start | bytes 2621440 | tf_op jit(solution)/shard_map/all_to_all | solution.py:56
  104.7 2.3 %all-gather.2.cloned.1.call-done = bf16[1024,1536]{1,0:T(8,128)(2,1)} async-done(((bf16[128,1536]{1,0:T(8,128)(2,1)}), bf16[1024,1536]{1,0:T(8,128)(2,1)}) %all-gather.2.cloned.1.call-update) | async-done | bytes 3145744 | tf_op jit(solution)/shard_map/all_gather | solution.py:364
  107.0 1.9 %copy-done.1 = bf16[1024,1536]{1,0:T(8,128)(2,1)S(1)} copy-done((bf16[1024,1536]{1,0:T(8,128)(2,1)S(1)}, bf16[1024,1536]{1,0:T(8,128)(2,1)}, u32[]{:S(2)}) %copy-start.1) | copy-done | bytes 3145752
  108.9 4.6 %project_queries.1.q_ref = bf16[2,1024,256]{2,1,0:T(8,128)(2,1)S(1)} custom-call(s32[64]{0:T(128)S(1)} %copy-done.9, bf16[8,8,16,1536]{3,2,1,0:T(8,128)(2,1)S(1)} %bitcast.18, bf16[1536,384]{1,0:T(8,128)(2,1)S(1)} %copy-done, f32[640,128]{1,0:T(8,128)S(1)} %copy-done.3, f32[640,128]{1,0:T(8,128)S(1)} %copy-done.2), custom_call_target="tpu_custom_call" | custom-call | flops 1200000000 | bytes 5000000 | tf_op jit(solution)/shard_map/project_queries/pallas_call | solution.py:169
  113.5 1.0 copy-done.7
  114.5 8.6 %all-to-all-done.3 = bf16[4,256,640]{2,1,0:T(8,128)(2,1)S(1)} async-done(((bf16[4,256,640]{2,1,0:T(8,128)(2,1)}), bf16[4,256,640]{2,1,0:T(8,128)(2,1)S(1)}, u32[]{:S(2)}, u32[]{:S(2)}) %all-to-all-start.3) | async-done | bytes 1310752 | tf_op jit(solution)/shard_map/all_to_all | solution.py:56
  123.1 1.0 copy-done.5
  124.2 2.5 %decode_attention.1 = bf16[4,16,256]{2,1,0:T(8,128)(2,1)} custom-call(s32[64]{0:T(128)S(1)} %copy-done.9, bf16[48,640]{1,0:T(8,128)(2,1)S(1)} %prepare_decode.1.ready_ref, bf16[1024,640]{1,0:T(8,128)(2,1)S(1)} %bitcast.16, bf16[512,512]{1,0:T(8,128)(2,1)S(1)} %copy-done.5), custom_call_target="tpu_custom_call" | custom-call | flops 100000000 | bytes 2000000 | tf_op jit(solution)/shard_map/decode_attention/pallas_call | solution.py:271
  126.6 5.1 %all-to-all-start.4 = ((bf16[4,16,256]{2,1,0:T(8,128)(2,1)}), bf16[4,16,256]{2,1,0:T(8,128)(2,1)S(1)}, u32[]{:S(2)}, u32[]{:S(2)}) async-start(bf16[4,16,256]{2,1,0:T(8,128)(2,1)} %decode_attention.1), calls=%async_computation.4 | async-start | bytes 65536 | tf_op jit(solution)/shard_map/all_to_all | solution.py:384
  131.7 0.0 copy-done.6
  131.7 5.9 %prefill_attention.1 = bf16[1024,256]{1,0:T(8,128)(2,1)} custom-call(s32[64]{0:T(128)S(1)} %copy-done.9, bf16[2,1024,256]{2,1,0:T(8,128)(2,1)S(1)} %copy-done.8, bf16[1024,640]{1,0:T(8,128)(2,1)S(1)} %bitcast.17, bf16[512,512]{1,0:T(8,128)(2,1)S(1)} %copy-done.6), custom_call_target="tpu_custom_call" | custom-call | flops 1500000000 | bytes 4000000 | tf_op jit(solution)/shard_map/prefill_attention/pallas_call | solution.py:332
  137.7 0.0 all-to-all-done.4.pool_ref
  137.7 0.6 copy-done.13
  138.3 1.5 %select_slots.1 = bf16[3,4,256]{2,1,0:T(4,128)(2,1)} custom-call(s32[64]{0:T(128)} %request_layout.1.layout_ref, bf16[4,16,256]{2,1,0:T(8,128)(2,1)} %copy-done.13), custom_call_target="tpu_custom_call" | custom-call | flops 1000000 | bytes 50000 | tf_op jit(solution)/shard_map/select_slots/pallas_call | solution.py:292
  (31 shorter events, 0.1 us)
Async XLA Ops:
  7.2 12.9 %collective-permute-start = (bf16[16,1536]{1,0:T(8,128)(2,1)}, bf16[16,1536]{1,0:T(8,128)(2,1)S(1)}, u32[]{:S(2)}, u32[]{:S(2)}) collective-permute-start(bf16[16,1536]{1,0:T(8,128)(2,1)} %bitcast.23), channel_id=1, source_target_pairs={{0,128},{128,0},{1,129},{129,1},{2,130},{130,2},{3,131},{131,3},{4... | collective-permute-start | bytes 147464 | tf_op jit(solution)/shard_map/ppermute | solution.py:357
  13.7 6.4 %copy-start.12 = (bf16[1,16,1536]{2,1,0:T(8,128)(2,1)S(1)}, bf16[1,16,1536]{2,1,0:T(8,128)(2,1)}, u32[]{:S(2)}) copy-start(bf16[1,16,1536]{2,1,0:T(8,128)(2,1)} %param.13) | copy-start | bytes 147460
  15.8 20.8 %all-to-all-start = ((bf16[4,112,832]{2,1,0:T(8,128)(2,1)}), bf16[4,112,832]{2,1,0:T(8,128)(2,1)S(1)}, u32[]{:S(2)}, u32[]{:S(2)}) async-start(bf16[4,112,832]{2,1,0:T(8,128)(2,1)} %pack_hidden.1), calls=%async_computation | async-start | bytes 1605632 | tf_op jit(solution)/shard_map/all_to_all | solution.py:359
  20.1 86.9 %all-gather.2.cloned.1.call-start = ((), (), s32[]{:S(2)}) async-start(), calls=%async_computation.5 | async-start | bytes 3538944 | tf_op jit(solution)/shard_map/all_gather | solution.py:364
  20.1 16.4 %collective-permute-start.3 = (bf16[2,16,1536]{2,1,0:T(8,128)(2,1)S(1)}, bf16[2,16,1536]{2,1,0:T(8,128)(2,1)S(1)}, u32[]{:S(2)}, u32[]{:S(2)}) collective-permute-start(bf16[2,16,1536]{2,1,0:T(8,128)(2,1)S(1)} %pad_maximum_fusion.2), channel_id=1, source_target_pairs={{0,96},{32,0},{64,32},{96,64},{1,97},{33,1},{65,33},{97,65},{2,98}... | collective-permute-start | bytes 294920 | tf_op jit(solution)/shard_map/ppermute | solution.py:361
  25.3 11.2 %collective-permute-start.2 = (bf16[2,16,1536]{2,1,0:T(8,128)(2,1)S(1)}, bf16[2,16,1536]{2,1,0:T(8,128)(2,1)S(1)}, u32[]{:S(2)}, u32[]{:S(2)}) collective-permute-start(bf16[2,16,1536]{2,1,0:T(8,128)(2,1)S(1)} %pad_maximum_fusion.2), channel_id=1, source_target_pairs={{0,64},{32,96},{64,0},{96,32},{1,65},{33,97},{65,1},{97,33},{2,66}... | collective-permute-start | bytes 294920 | tf_op jit(solution)/shard_map/ppermute | solution.py:361
  28.1 8.4 %collective-permute-start.1 = (bf16[2,16,1536]{2,1,0:T(8,128)(2,1)S(1)}, bf16[2,16,1536]{2,1,0:T(8,128)(2,1)S(1)}, u32[]{:S(2)}, u32[]{:S(2)}) collective-permute-start(bf16[2,16,1536]{2,1,0:T(8,128)(2,1)S(1)} %pad_maximum_fusion.2), channel_id=1, source_target_pairs={{0,32},{32,64},{64,96},{96,0},{1,33},{33,65},{65,97},{97,1},{2,34}... | collective-permute-start | bytes 294920 | tf_op jit(solution)/shard_map/ppermute | solution.py:361
  36.5 0.7 copy-start.11
  37.3 16.9 %copy-start.14 = (bf16[3,4,1536]{2,1,0:T(4,128)(2,1)S(1)}, bf16[3,4,1536]{2,1,0:T(4,128)(2,1)}, u32[]{:S(2)}) copy-start(bf16[3,4,1536]{2,1,0:T(4,128)(2,1)} %param.20) | copy-start | bytes 110596
  37.3 17.0 %copy-start.15 = (bf16[3,4,576]{2,1,0:T(4,128)(2,1)S(1)}, bf16[3,4,576]{2,1,0:T(4,128)(2,1)}, u32[]{:S(2)}) copy-start(bf16[3,4,576]{2,1,0:T(4,128)(2,1)} %param.21) | copy-start | bytes 41476
  38.6 34.1 %all-to-all-start.1 = ((f32[16,16,576]{2,1,0:T(8,128)}), f32[16,16,576]{2,1,0:T(8,128)S(1)}, u32[]{:S(2)}, u32[]{:S(2)}) async-start(f32[16,16,576]{2,1,0:T(8,128)} %bitcast.9), calls=%async_computation.1 | async-start | bytes 1310720 | tf_op jit(solution)/shard_map/all_to_all | solution.py:369
  54.3 32.6 %collective-permute-start.4 = (bf16[3,4,2112]{2,1,0:T(4,128)(2,1)S(1)}, bf16[3,4,2112]{2,1,0:T(4,128)(2,1)S(1)}, u32[]{:S(2)}, u32[]{:S(2)}) collective-permute-start(bf16[3,4,2112]{2,1,0:T(4,128)(2,1)S(1)} %constant_dynamic-update-slice_fusion.5), channel_id=1, source_target_pairs={{0,1},{1,0},{2,3},{3,2},{4,5},{5,4},{6,7},{7,6},{8,9},{9,8},{10,11... | collective-permute-start | bytes 152072 | tf_op jit(solution)/shard_map/ppermute | solution.py:375
  72.7 0.8 copy-start.10
  73.5 25.3 %copy-start = (bf16[1536,384]{1,0:T(8,128)(2,1)S(1)}, bf16[1536,384]{1,0:T(8,128)(2,1)}, u32[]{:S(2)}) copy-start(bf16[1536,384]{1,0:T(8,128)(2,1)} %w_ref.3) | copy-start | bytes 3538948
  73.5 25.3 %copy-start.2 = (f32[640,128]{1,0:T(8,128)S(1)}, f32[640,128]{1,0:T(8,128)}, u32[]{:S(2)}) copy-start(f32[640,128]{1,0:T(8,128)} %constant.25.clone.sin_ref) | copy-start | bytes 983044
  73.5 25.3 %copy-start.3 = (f32[640,128]{1,0:T(8,128)S(1)}, f32[640,128]{1,0:T(8,128)}, u32[]{:S(2)}) copy-start(f32[640,128]{1,0:T(8,128)} %constant.24.clone.cos_ref) | copy-start | bytes 983044
  73.5 25.3 %copy-start.4 = (bf16[512,512]{1,0:T(8,128)(2,1)S(1)}, bf16[512,512]{1,0:T(8,128)(2,1)}, u32[]{:S(2)}) copy-start(bf16[512,512]{1,0:T(8,128)(2,1)} %kv_ref.5) | copy-start | bytes 1572868
  73.5 25.3 %copy-start.9 = (s32[64]{0:T(128)S(1)}, s32[64]{0:T(128)}, u32[]{:S(2)}) copy-start(s32[64]{0:T(128)} %request_layout.1.layout_ref) | copy-start | bytes 772
  75.9 24.1 %all-to-all-start.2 = ((bf16[16,16,640]{2,1,0:T(8,128)(2,1)}), bf16[16,16,640]{2,1,0:T(8,128)(2,1)S(1)}, u32[]{:S(2)}, u32[]{:S(2)}) async-start(bf16[16,16,640]{2,1,0:T(8,128)(2,1)} %norm_rows.1), calls=%async_computation.2 | async-start | bytes 655360 | tf_op jit(solution)/shard_map/all_to_all | solution.py:371
  87.0 11.7 %collective-permute-start.5 = (bf16[6,4,2112]{2,1,0:T(4,128)(2,1)S(1)}, bf16[6,4,2112]{2,1,0:T(4,128)(2,1)S(1)}, u32[]{:S(2)}, u32[]{:S(2)}) collective-permute-start(bf16[6,4,2112]{2,1,0:T(4,128)(2,1)S(1)} %pad_maximum_fusion.1), channel_id=1, source_target_pairs={{0,2},{1,3},{2,0},{3,1},{4,6},{5,7},{6,4},{7,5},{8,10},{9,11},{10,... | collective-permute-start | bytes 304136 | tf_op jit(solution)/shard_map/ppermute | solution.py:375
  101.1 22.0 %all-to-all-start.3 = ((bf16[4,256,640]{2,1,0:T(8,128)(2,1)}), bf16[4,256,640]{2,1,0:T(8,128)(2,1)S(1)}, u32[]{:S(2)}, u32[]{:S(2)}) async-start(bf16[4,256,640]{2,1,0:T(8,128)(2,1)} %broadcast_in_dim.13), calls=%async_computation.3 | async-start | bytes 2621440 | tf_op jit(solution)/shard_map/all_to_all | solution.py:56
  107.0 1.9 %copy-start.1 = (bf16[1024,1536]{1,0:T(8,128)(2,1)S(1)}, bf16[1024,1536]{1,0:T(8,128)(2,1)}, u32[]{:S(2)}) copy-start(bf16[1024,1536]{1,0:T(8,128)(2,1)} %all-gather.2.cloned.1.call-done) | copy-start | bytes 9437188
  113.5 1.0 copy-start.7
  123.1 1.0 copy-start.5
  124.2 7.6 %copy-start.6 = (bf16[512,512]{1,0:T(8,128)(2,1)S(1)}, bf16[512,512]{1,0:T(8,128)(2,1)}, u32[]{:S(2)}) copy-start(bf16[512,512]{1,0:T(8,128)(2,1)} %kv_ref.5) | copy-start | bytes 1572868
  124.2 7.6 %copy-start.8 = (bf16[2,1024,256]{2,1,0:T(8,128)(2,1)S(1)}, bf16[2,1024,256]{2,1,0:T(8,128)(2,1)}, u32[]{:S(2)}) copy-start(bf16[2,1024,256]{2,1,0:T(8,128)(2,1)} %copy-done.7) | copy-start | bytes 3145732
  126.6 11.0 %all-to-all-start.4 = ((bf16[4,16,256]{2,1,0:T(8,128)(2,1)}), bf16[4,16,256]{2,1,0:T(8,128)(2,1)S(1)}, u32[]{:S(2)}, u32[]{:S(2)}) async-start(bf16[4,16,256]{2,1,0:T(8,128)(2,1)} %decode_attention.1), calls=%async_computation.4 | async-start | bytes 65536 | tf_op jit(solution)/shard_map/all_to_all | solution.py:384
  137.7 0.6 copy-start.13
Sparse Core Ops, SparseCore 0:
  37.4 69.4 all-gather.1

commit v9 on v8

--- a/solution.py
+++ b/solution.py
@@ -21,6 +21,7 @@
 HEADS = 2
 PAD = 16
 TABLE = 640
+NORM_FLOPS = 30_000_000_000
 WIDE = KVL + 2 * ROPE
 START, LENGTH, BASE, PLACE, FIRST, SOURCE, SLOT, BLOCK = 0, 3, 6, 8, 16, 24, 28, 32
 
@@ -85,7 +86,7 @@
     for i in range(8):
         out_ref[PLACE + i] = i - start_of(i)
         out_ref[FIRST + i] = start_of(i) * BLK
-        out_ref[BLOCK + i] = lax.rem(x + NX - i % NX, NX) * 2 + (yh ^ (i // NX))
+        out_ref[BLOCK + i] = (yh ^ (i // NX)) * NX + lax.rem(x + NX - i % NX, NX)
 
 
 SMEM = pl.BlockSpec(memory_space=pltpu.SMEM)
@@ -104,26 +105,22 @@
 
 
 def pack_kernel(hidden_ref, down_ref, out_ref):
-    features = hidden_ref.shape[1]
-    per_x = hidden_ref.shape[0] // NX
-    row = lax.broadcasted_iota(i32, (features, features), 0)
-    column = lax.broadcasted_iota(i32, (features, features), 1)
-    unit = jnp.where(row == column, 1.0, 0.0).astype(bf16)
+    per_x = hidden_ref.shape[1] // NX
     for i in range(NX):
-        out_ref[i, :, :per_x] = dot_t(unit, hidden_ref[i * per_x : (i + 1) * per_x, :]).astype(bf16)
+        out_ref[i, :, :per_x] = hidden_ref[:, i * per_x : (i + 1) * per_x]
         out_ref[i, :, per_x:] = down_ref[...]
 
 
-def pack(hidden, kv_down):
-    rows, features = hidden.shape
+def pack(hidden_t, kv_down):
+    features, rows = hidden_t.shape
     return pl.pallas_call(
         pack_kernel,
         in_specs=[VMEM] * 2,
         out_specs=VMEM,
         out_shape=jax.ShapeDtypeStruct((NX, features, rows // NX + kv_down.shape[1]), bf16),
-        cost_estimate=pl.CostEstimate(flops=26_000_000, bytes_accessed=1_200_000, transcendentals=0),
+        cost_estimate=pl.CostEstimate(flops=0, bytes_accessed=1_200_000, transcendentals=0),
         name="pack_hidden",
-    )(hidden, kv_down)
+    )(hidden_t, kv_down)
 
 
 def norm_kernel(layout_ref, pieces_ref, gain_ref, cos_ref, sin_ref, out_ref):
@@ -146,7 +143,7 @@
         in_specs=[SMEM] + [VMEM] * 4,
         out_specs=VMEM,
         out_shape=jax.ShapeDtypeStruct((count, chunk, WIDE), bf16),
-        cost_estimate=pl.CostEstimate(flops=1_000_000, bytes_accessed=1_000_000, transcendentals=16),
+        cost_estimate=pl.CostEstimate(flops=NORM_FLOPS, bytes_accessed=1_000_000, transcendentals=16),
         name="norm_rows",
     )(layout, pieces, gain, cos_part, sin_part)
 
@@ -354,14 +351,13 @@
     cos_part, sin_part = rotary_table()
 
     own = comp_query[0]
-    other = lax.ppermute(own, "yh", shift(2, 1))
-    pair = jnp.stack([own, other])
-    packed = lax.all_to_all(pack(hidden[0], kv_down), "x", 0, 0, tiled=True)
+    packed = lax.all_to_all(pack(hidden[0].T, kv_down), "x", 0, 0, tiled=True)
     layout = request_layout(ids, req_blocks, dest_slot)
-    line = [pair] + [lax.ppermute(pair, "x", shift(NX, d)) for d in range(1, NX)]
-    line = jnp.concatenate(line).reshape(BLK, -1)
+    line = jnp.concatenate([own] + [lax.ppermute(own, "x", shift(NX, d)) for d in range(1, NX)])
     packed, line, dec_query, dec_latent = lax.optimization_barrier((packed, line, dec_query, dec_latent))
+    line = jnp.concatenate([line, lax.ppermute(line, "yh", shift(2, 1))])
     cq = lax.all_gather(line, "z", axis=0, tiled=True)
+
     packed = packed.reshape(NX * features, -1)
     partial = lax.dot_general(
         packed[:, :per_x], packed[:, per_x:], (((0,), (0,)), ((), ())), preferred_element_type=f32

time: 148 us -> 139 us (0.939)
  waiting for transfers between devices: 40.4 us -> 31.8 us
  local copies, waits for them, and re-layouts: 9.16 us -> 6.51 us
  starting transfers between devices: 59.3 us -> 61.7 us
    all_to_all x1, waiting for transfers between devices: 8.64 us -> 0.69 us  [spread(): return lax.all_to_all(copies, axes, 0, 0, tiled=True)]
    all_gather x1, waiting for transfers between devices: 2.29 us -> 8.58 us  [body(): cq = lax.all_gather(line, 'z', axis=0, tiled=True)]
    all_to_all x1, waiting for transfers between devices: 14 us -> 10 us  [body(): lax.all_to_all(partial.reshape(16, chunk, -1), ('yh', 'z'), 0, 0, tiled=T...]
    unnamed x38 -> x29, local copies, waits for them, and re-layouts: 7.95 us -> 5.32 us
    ppermute x2, starting transfers between devices: 4.3 us -> 6.4 us  [body(): met = lax.ppermute(rep_in, 'rep', [(i, i ^ d) for i in range(NREP)])]
    ppermute x2, waiting for transfers between devices: 9.77 us -> 8.08 us  [body(): met = lax.ppermute(rep_in, 'rep', [(i, i ^ d) for i in range(NREP)])]
  transfers between devices with their start and end apart: 12 -> 12, of which waited for: 5 -> 7; matrix products, arithmetic and copies ran while one was open for 4% -> 3% of each run, Pallas kernels for 12% -> 11%
where the time goes in v9:
time: 139 us; the launch traced here: 138 us
  starting transfers between devices  61.7 us (44%)
  waiting for transfers between devices  31.8 us (23%)
  Pallas kernels  21.2 us (15%)
  between operations  14.2 us (10%)
  local copies, waits for them, and re-layouts  6.51 us (5%)
  other arithmetic  1.61 us (1%)
    all_to_all x1, starting transfers between devices, body(): lax.all_to_all(partial.reshape(16, chunk, -1), ('yh', 'z'), 0, 0, tiled=T...  15.8 us
    ppermute x3, starting transfers between devices, body(): lax.ppermute(own, 'x', shift(NX, d))  10.7 us
    all_to_all x1, starting transfers between devices, body(): lax.all_to_all(copies, ('yh', 'z'), 0, 0, tiled=True).reshape(per_x, -1)  10.4 us
    all_to_all x1, waiting for transfers between devices, body(): lax.all_to_all(partial.reshape(16, chunk, -1), ('yh', 'z'), 0, 0, tiled=T...  10 us
    all_gather x1, waiting for transfers between devices, body(): cq = lax.all_gather(line, 'z', axis=0, tiled=True)  8.58 us
    ppermute x2, waiting for transfers between devices, body(): met = lax.ppermute(rep_in, 'rep', [(i, i ^ d) for i in range(NREP)])  8.08 us
    ppermute x2, starting transfers between devices, body(): met = lax.ppermute(rep_in, 'rep', [(i, i ^ d) for i in range(NREP)])  6.4 us
    pallas_call x1, Pallas kernels, prefill(): pl.pallas_call(prefill_kernel, in_specs=[SMEM] + [VMEM] * 3, out_specs=VM...  5.91 us
  transfers between devices with their start and end apart: 12, of which 7 were waited for; matrix products, arithmetic and copies ran while one was open for 3% of the time, Pallas kernels for 11%

profile of v9, /device:TPU:56, one launch (start us, length us, event | category | flops | bytes accessed | tf_op | source)
XLA Modules:
  0.0 138.2 jit_solution(1457515209798118636)
XLA Ops:
  7.2 0.0 copy-start.11
  7.2 2.0 %pack_hidden.1 = bf16[4,112,832]{2,1,0:T(8,128)(2,1)} custom-call(bf16[112,1024]{1,0:T(8,128)(2,1)} %bitcast.20, bf16[112,576]{1,0:T(8,128)(2,1)} %down_ref.1), custom_call_target="tpu_custom_call" | custom-call | bytes 1200000 | tf_op jit(solution)/shard_map/pack_hidden/pallas_call | solution.py:116
  9.2 4.3 %all-to-all-start = ((bf16[4,112,832]{2,1,0:T(8,128)(2,1)}), bf16[4,112,832]{2,1,0:T(8,128)(2,1)S(1)}, u32[]{:S(2)}, u32[]{:S(2)}) async-start(bf16[4,112,832]{2,1,0:T(8,128)(2,1)} %pack_hidden.1), calls=%async_computation | async-start | bytes 1605632 | tf_op jit(solution)/shard_map/all_to_all | solution.py:354
  13.5 0.0 copy-done.11
  13.5 5.1 %collective-permute-start.2 = (bf16[16,1536]{1,0:T(8,128)(2,1)S(1)}, bf16[16,1536]{1,0:T(8,128)(2,1)S(1)}, u32[]{:S(2)}, u32[]{:S(2)}) collective-permute-start(bf16[16,1536]{1,0:T(8,128)(2,1)S(1)} %bitcast.21), channel_id=1, source_target_pairs={{0,96},{32,0},{64,32},{96,64},{1,97},{33,1},{65,33},{97,65},{2,98}... | collective-permute-start | bytes 147464 | tf_op jit(solution)/shard_map/ppermute | solution.py:356
  18.6 2.8 %collective-permute-start.1 = (bf16[16,1536]{1,0:T(8,128)(2,1)S(1)}, bf16[16,1536]{1,0:T(8,128)(2,1)S(1)}, u32[]{:S(2)}, u32[]{:S(2)}) collective-permute-start(bf16[16,1536]{1,0:T(8,128)(2,1)S(1)} %bitcast.22), channel_id=1, source_target_pairs={{0,64},{32,96},{64,0},{96,32},{1,65},{33,97},{65,1},{97,33},{2,66}... | collective-permute-start | bytes 147464 | tf_op jit(solution)/shard_map/ppermute | solution.py:356
  21.4 2.8 %collective-permute-start = (bf16[16,1536]{1,0:T(8,128)(2,1)S(1)}, bf16[16,1536]{1,0:T(8,128)(2,1)S(1)}, u32[]{:S(2)}, u32[]{:S(2)}) collective-permute-start(bf16[16,1536]{1,0:T(8,128)(2,1)S(1)} %bitcast.23), channel_id=1, source_target_pairs={{0,32},{32,64},{64,96},{96,0},{1,33},{33,65},{65,97},{97,1},{2,34}... | collective-permute-start | bytes 147464 | tf_op jit(solution)/shard_map/ppermute | solution.py:356
  24.2 1.9 %collective-permute-done.2 = bf16[16,1536]{1,0:T(8,128)(2,1)S(1)} collective-permute-done((bf16[16,1536]{1,0:T(8,128)(2,1)S(1)}, bf16[16,1536]{1,0:T(8,128)(2,1)S(1)}, u32[]{:S(2)}, u32[]{:S(2)}) %collective-permute-start.2) | collective-permute-done | bytes 49184 | tf_op jit(solution)/shard_map/ppermute | solution.py:356
  26.0 1.6 %collective-permute-done.1 = bf16[16,1536]{1,0:T(8,128)(2,1)S(1)} collective-permute-done((bf16[16,1536]{1,0:T(8,128)(2,1)S(1)}, bf16[16,1536]{1,0:T(8,128)(2,1)S(1)}, u32[]{:S(2)}, u32[]{:S(2)}) %collective-permute-start.1) | collective-permute-done | bytes 49184 | tf_op jit(solution)/shard_map/ppermute | solution.py:356
  27.6 1.0 collective-permute-done
  28.6 0.0 all-to-all-done
  28.6 4.7 %collective-permute-start.5 = (bf16[64,1536]{1,0:T(8,128)(2,1)S(1)}, bf16[64,1536]{1,0:T(8,128)(2,1)S(1)}, u32[]{:S(2)}, u32[]{:S(2)}) collective-permute-start(bf16[64,1536]{1,0:T(8,128)(2,1)S(1)} %pad_maximum_fusion.2), channel_id=1, source_target_pairs={{0,128},{128,0},{1,129},{129,1},{2,130},{130,2},{3,131},{131,3},{4... | collective-permute-start | bytes 589832 | tf_op jit(solution)/shard_map/ppermute | solution.py:358
  33.3 1.2 fusion
  34.6 15.8 %all-to-all-start.1 = ((f32[16,16,576]{2,1,0:T(8,128)}), f32[16,16,576]{2,1,0:T(8,128)S(1)}, u32[]{:S(2)}, u32[]{:S(2)}) async-start(f32[16,16,576]{2,1,0:T(8,128)} %bitcast.8), calls=%async_computation.1 | async-start | bytes 1310720 | tf_op jit(solution)/shard_map/all_to_all | solution.py:365
  50.4 0.0 all-gather.2.cloned.1.call-start
  50.4 0.0 collective-permute-done.5
  50.4 0.8 pad_maximum_fusion
  51.2 0.0 all-gather.2.cloned.1.call-update
  51.2 0.6 pad_add_fusion.ids_ref
  51.8 1.3 request_layout.1.layout_ref
  53.2 0.0 copy-done.12
  53.2 0.0 copy-done.13
  53.2 2.4 %collective-permute-start.3 = (bf16[3,4,2112]{2,1,0:T(4,128)(2,1)S(1)}, bf16[3,4,2112]{2,1,0:T(4,128)(2,1)S(1)}, u32[]{:S(2)}, u32[]{:S(2)}) collective-permute-start(bf16[3,4,2112]{2,1,0:T(4,128)(2,1)S(1)} %constant_dynamic-update-slice_fusion), channel_id=1, source_target_pairs={{0,1},{1,0},{2,3},{3,2},{4,5},{5,4},{6,7},{7,6},{8,9},{9,8},{10,11... | collective-permute-start | bytes 152072 | tf_op jit(solution)/shard_map/ppermute | solution.py:371
  55.6 10.0 %all-to-all-done.1.pieces_ref = f32[16,16,576]{2,1,0:T(8,128)S(1)} async-done(((f32[16,16,576]{2,1,0:T(8,128)}), f32[16,16,576]{2,1,0:T(8,128)S(1)}, u32[]{:S(2)}, u32[]{:S(2)}) %all-to-all-start.1) | async-done | bytes 589856 | tf_op jit(solution)/shard_map/all_to_all | solution.py:365
  65.6 0.8 copy-done.9
  66.5 2.3 %norm_rows.1 = bf16[16,16,640]{2,1,0:T(8,128)(2,1)} custom-call(s32[64]{0:T(128)} %request_layout.1.layout_ref, f32[16,16,576]{2,1,0:T(8,128)} %copy-done.9, f32[1,512]{1,0:T(1,128)} %bitcast.25, f32[640,128]{1,0:T(8,128)} %constant.24.clone.cos_ref, f32[640,128]{1,0:T(8,128)} %constant.25.clone.sin_ref), custom_call_target="tpu_custom_call" | custom-call | flops 30000001024 | bytes 1000000 | tf_op jit(solution)/shard_map/norm_rows/pallas_call | solution.py:141
  68.7 10.4 %all-to-all-start.2 = ((bf16[16,16,640]{2,1,0:T(8,128)(2,1)}), bf16[16,16,640]{2,1,0:T(8,128)(2,1)S(1)}, u32[]{:S(2)}, u32[]{:S(2)}) async-start(bf16[16,16,640]{2,1,0:T(8,128)(2,1)} %norm_rows.1), calls=%async_computation.2 | async-start | bytes 655360 | tf_op jit(solution)/shard_map/all_to_all | solution.py:367
  79.1 0.0 collective-permute-done.3
  79.1 0.1 pad_maximum_fusion.3
  79.2 4.0 %collective-permute-start.4 = (bf16[6,4,2112]{2,1,0:T(4,128)(2,1)S(1)}, bf16[6,4,2112]{2,1,0:T(4,128)(2,1)S(1)}, u32[]{:S(2)}, u32[]{:S(2)}) collective-permute-start(bf16[6,4,2112]{2,1,0:T(4,128)(2,1)S(1)} %pad_maximum_fusion.3), channel_id=1, source_target_pairs={{0,2},{1,3},{2,0},{3,1},{4,6},{5,7},{6,4},{7,5},{8,10},{9,11},{10,... | collective-permute-start | bytes 304136 | tf_op jit(solution)/shard_map/ppermute | solution.py:371
  83.3 8.1 %collective-permute-done.4 = bf16[6,4,2112]{2,1,0:T(4,128)(2,1)S(1)} collective-permute-done((bf16[6,4,2112]{2,1,0:T(4,128)(2,1)S(1)}, bf16[6,4,2112]{2,1,0:T(4,128)(2,1)S(1)}, u32[]{:S(2)}, u32[]{:S(2)}) %collective-permute-start.4) | collective-permute-done | bytes 101408 | tf_op jit(solution)/shard_map/ppermute | solution.py:371
  91.3 0.1 pad_maximum_fusion.1.rows_ref
  91.5 1.1 prepare_decode.1.ready_ref
  92.6 0.0 all-to-all-done.2
  92.6 1.2 broadcast_in_dim.13
  93.8 3.5 %all-to-all-start.3 = ((bf16[4,256,640]{2,1,0:T(8,128)(2,1)}), bf16[4,256,640]{2,1,0:T(8,128)(2,1)S(1)}, u32[]{:S(2)}, u32[]{:S(2)}) async-start(bf16[4,256,640]{2,1,0:T(8,128)(2,1)} %broadcast_in_dim.13), calls=%async_computation.3 | async-start | bytes 2621440 | tf_op jit(solution)/shard_map/all_to_all | solution.py:57
  97.3 8.6 %all-gather.2.cloned.1.call-done = bf16[1024,1536]{1,0:T(8,128)(2,1)} async-done(((bf16[128,1536]{1,0:T(8,128)(2,1)}), bf16[1024,1536]{1,0:T(8,128)(2,1)}) %all-gather.2.cloned.1.call-update) | async-done | bytes 3145744 | tf_op jit(solution)/shard_map/all_gather | solution.py:359
  105.9 1.9 %copy-done.1 = bf16[1024,1536]{1,0:T(8,128)(2,1)S(1)} copy-done((bf16[1024,1536]{1,0:T(8,128)(2,1)S(1)}, bf16[1024,1536]{1,0:T(8,128)(2,1)}, u32[]{:S(2)}) %copy-start.1) | copy-done | bytes 3145752
  107.8 1.0 copy-done.5
  108.8 4.6 %project_queries.1.q_ref = bf16[2,1024,256]{2,1,0:T(8,128)(2,1)S(1)} custom-call(s32[64]{0:T(128)S(1)} %copy-done.8, bf16[8,8,16,1536]{3,2,1,0:T(8,128)(2,1)S(1)} %bitcast.17, bf16[1536,384]{1,0:T(8,128)(2,1)S(1)} %copy-done, f32[640,128]{1,0:T(8,128)S(1)} %copy-done.5, f32[640,128]{1,0:T(8,128)S(1)} %copy-done.3), custom_call_target="tpu_custom_call" | custom-call | flops 1200000000 | bytes 5000000 | tf_op jit(solution)/shard_map/project_queries/pallas_call | solution.py:166
  113.4 1.0 copy-done.6
  114.4 0.7 all-to-all-done.3
  115.1 2.5 %decode_attention.1 = bf16[4,16,256]{2,1,0:T(8,128)(2,1)} custom-call(s32[64]{0:T(128)S(1)} %copy-done.8, bf16[48,640]{1,0:T(8,128)(2,1)S(1)} %prepare_decode.1.ready_ref, bf16[1024,640]{1,0:T(8,128)(2,1)S(1)} %bitcast.15, bf16[512,512]{1,0:T(8,128)(2,1)S(1)} %copy-done.2), custom_call_target="tpu_custom_call" | custom-call | flops 100000000 | bytes 2000000 | tf_op jit(solution)/shard_map/decode_attention/pallas_call | solution.py:268
  117.6 5.8 %all-to-all-start.4 = ((bf16[4,16,256]{2,1,0:T(8,128)(2,1)}), bf16[4,16,256]{2,1,0:T(8,128)(2,1)S(1)}, u32[]{:S(2)}, u32[]{:S(2)}) async-start(bf16[4,16,256]{2,1,0:T(8,128)(2,1)} %decode_attention.1), calls=%async_computation.4 | async-start | bytes 65536 | tf_op jit(solution)/shard_map/all_to_all | solution.py:380
  123.4 5.9 %prefill_attention.1 = bf16[1024,256]{1,0:T(8,128)(2,1)} custom-call(s32[64]{0:T(128)S(1)} %copy-done.8, bf16[2,1024,256]{2,1,0:T(8,128)(2,1)S(1)} %copy-done.7, bf16[1024,640]{1,0:T(8,128)(2,1)S(1)} %bitcast.16, bf16[512,512]{1,0:T(8,128)(2,1)S(1)} %copy-done.2), custom_call_target="tpu_custom_call" | custom-call | flops 1500000000 | bytes 4000000 | tf_op jit(solution)/shard_map/prefill_attention/pallas_call | solution.py:329
  129.3 0.0 all-to-all-done.4.pool_ref
  129.3 0.6 copy-done.10
  129.9 1.5 %select_slots.1 = bf16[3,4,256]{2,1,0:T(4,128)(2,1)} custom-call(s32[64]{0:T(128)} %request_layout.1.layout_ref, bf16[4,16,256]{2,1,0:T(8,128)(2,1)} %copy-done.10), custom_call_target="tpu_custom_call" | custom-call | flops 1000000 | bytes 50000 | tf_op jit(solution)/shard_map/select_slots/pallas_call | solution.py:289
  (22 shorter events, 0.1 us)
Async XLA Ops:
  7.2 6.3 %copy-start.11 = (bf16[1,16,1536]{2,1,0:T(8,128)(2,1)S(1)}, bf16[1,16,1536]{2,1,0:T(8,128)(2,1)}, u32[]{:S(2)}) copy-start(bf16[1,16,1536]{2,1,0:T(8,128)(2,1)} %param.13) | copy-start | bytes 147460
  9.2 19.4 %all-to-all-start = ((bf16[4,112,832]{2,1,0:T(8,128)(2,1)}), bf16[4,112,832]{2,1,0:T(8,128)(2,1)S(1)}, u32[]{:S(2)}, u32[]{:S(2)}) async-start(bf16[4,112,832]{2,1,0:T(8,128)(2,1)} %pack_hidden.1), calls=%async_computation | async-start | bytes 1605632 | tf_op jit(solution)/shard_map/all_to_all | solution.py:354
  13.5 12.6 %collective-permute-start.2 = (bf16[16,1536]{1,0:T(8,128)(2,1)S(1)}, bf16[16,1536]{1,0:T(8,128)(2,1)S(1)}, u32[]{:S(2)}, u32[]{:S(2)}) collective-permute-start(bf16[16,1536]{1,0:T(8,128)(2,1)S(1)} %bitcast.21), channel_id=1, source_target_pairs={{0,96},{32,0},{64,32},{96,64},{1,97},{33,1},{65,33},{97,65},{2,98}... | collective-permute-start | bytes 147464 | tf_op jit(solution)/shard_map/ppermute | solution.py:356
  18.6 9.0 %collective-permute-start.1 = (bf16[16,1536]{1,0:T(8,128)(2,1)S(1)}, bf16[16,1536]{1,0:T(8,128)(2,1)S(1)}, u32[]{:S(2)}, u32[]{:S(2)}) collective-permute-start(bf16[16,1536]{1,0:T(8,128)(2,1)S(1)} %bitcast.22), channel_id=1, source_target_pairs={{0,64},{32,96},{64,0},{96,32},{1,65},{33,97},{65,1},{97,33},{2,66}... | collective-permute-start | bytes 147464 | tf_op jit(solution)/shard_map/ppermute | solution.py:356
  21.4 7.2 %collective-permute-start = (bf16[16,1536]{1,0:T(8,128)(2,1)S(1)}, bf16[16,1536]{1,0:T(8,128)(2,1)S(1)}, u32[]{:S(2)}, u32[]{:S(2)}) collective-permute-start(bf16[16,1536]{1,0:T(8,128)(2,1)S(1)} %bitcast.23), channel_id=1, source_target_pairs={{0,32},{32,64},{64,96},{96,0},{1,33},{33,65},{65,97},{97,1},{2,34}... | collective-permute-start | bytes 147464 | tf_op jit(solution)/shard_map/ppermute | solution.py:356
  28.6 21.8 %collective-permute-start.5 = (bf16[64,1536]{1,0:T(8,128)(2,1)S(1)}, bf16[64,1536]{1,0:T(8,128)(2,1)S(1)}, u32[]{:S(2)}, u32[]{:S(2)}) collective-permute-start(bf16[64,1536]{1,0:T(8,128)(2,1)S(1)} %pad_maximum_fusion.2), channel_id=1, source_target_pairs={{0,128},{128,0},{1,129},{129,1},{2,130},{130,2},{3,131},{131,3},{4... | collective-permute-start | bytes 589832 | tf_op jit(solution)/shard_map/ppermute | solution.py:358
  34.6 18.6 %copy-start.12 = (bf16[3,4,1536]{2,1,0:T(4,128)(2,1)S(1)}, bf16[3,4,1536]{2,1,0:T(4,128)(2,1)}, u32[]{:S(2)}) copy-start(bf16[3,4,1536]{2,1,0:T(4,128)(2,1)} %param.20) | copy-start | bytes 110596
  34.6 18.7 %copy-start.13 = (bf16[3,4,576]{2,1,0:T(4,128)(2,1)S(1)}, bf16[3,4,576]{2,1,0:T(4,128)(2,1)}, u32[]{:S(2)}) copy-start(bf16[3,4,576]{2,1,0:T(4,128)(2,1)} %param.21) | copy-start | bytes 41476
  34.6 31.1 %all-to-all-start.1 = ((f32[16,16,576]{2,1,0:T(8,128)}), f32[16,16,576]{2,1,0:T(8,128)S(1)}, u32[]{:S(2)}, u32[]{:S(2)}) async-start(f32[16,16,576]{2,1,0:T(8,128)} %bitcast.8), calls=%async_computation.1 | async-start | bytes 1310720 | tf_op jit(solution)/shard_map/all_to_all | solution.py:365
  50.4 55.5 %all-gather.2.cloned.1.call-start = ((), (), s32[]{:S(2)}) async-start(), calls=%async_computation.5 | async-start | bytes 3538944 | tf_op jit(solution)/shard_map/all_gather | solution.py:359
  53.2 25.9 %collective-permute-start.3 = (bf16[3,4,2112]{2,1,0:T(4,128)(2,1)S(1)}, bf16[3,4,2112]{2,1,0:T(4,128)(2,1)S(1)}, u32[]{:S(2)}, u32[]{:S(2)}) collective-permute-start(bf16[3,4,2112]{2,1,0:T(4,128)(2,1)S(1)} %constant_dynamic-update-slice_fusion), channel_id=1, source_target_pairs={{0,1},{1,0},{2,3},{3,2},{4,5},{5,4},{6,7},{7,6},{8,9},{9,8},{10,11... | collective-permute-start | bytes 152072 | tf_op jit(solution)/shard_map/ppermute | solution.py:371
  65.6 0.8 copy-start.9
  66.5 25.0 %copy-start.2 = (bf16[512,512]{1,0:T(8,128)(2,1)S(1)}, bf16[512,512]{1,0:T(8,128)(2,1)}, u32[]{:S(2)}) copy-start(bf16[512,512]{1,0:T(8,128)(2,1)} %kv_ref.5) | copy-start | bytes 1572868
  66.5 25.0 %copy-start.3 = (f32[640,128]{1,0:T(8,128)S(1)}, f32[640,128]{1,0:T(8,128)}, u32[]{:S(2)}) copy-start(f32[640,128]{1,0:T(8,128)} %constant.25.clone.sin_ref) | copy-start | bytes 983044
  66.5 25.1 %copy-start.4 = (f32[640,128]{1,0:T(8,128)S(1)}, f32[640,128]{1,0:T(8,128)}, u32[]{:S(2)}) copy-start(f32[640,128]{1,0:T(8,128)} %constant.24.clone.cos_ref) | copy-start | bytes 983044
  66.5 25.1 %copy-start.8 = (s32[64]{0:T(128)S(1)}, s32[64]{0:T(128)}, u32[]{:S(2)}) copy-start(s32[64]{0:T(128)} %request_layout.1.layout_ref) | copy-start | bytes 772
  68.7 22.8 %copy-start = (bf16[1536,384]{1,0:T(8,128)(2,1)S(1)}, bf16[1536,384]{1,0:T(8,128)(2,1)}, u32[]{:S(2)}) copy-start(bf16[1536,384]{1,0:T(8,128)(2,1)} %w_ref.3) | copy-start | bytes 3538948
  68.7 23.9 %all-to-all-start.2 = ((bf16[16,16,640]{2,1,0:T(8,128)(2,1)}), bf16[16,16,640]{2,1,0:T(8,128)(2,1)S(1)}, u32[]{:S(2)}, u32[]{:S(2)}) async-start(bf16[16,16,640]{2,1,0:T(8,128)(2,1)} %norm_rows.1), calls=%async_computation.2 | async-start | bytes 655360 | tf_op jit(solution)/shard_map/all_to_all | solution.py:367
  79.2 12.1 %collective-permute-start.4 = (bf16[6,4,2112]{2,1,0:T(4,128)(2,1)S(1)}, bf16[6,4,2112]{2,1,0:T(4,128)(2,1)S(1)}, u32[]{:S(2)}, u32[]{:S(2)}) collective-permute-start(bf16[6,4,2112]{2,1,0:T(4,128)(2,1)S(1)} %pad_maximum_fusion.3), channel_id=1, source_target_pairs={{0,2},{1,3},{2,0},{3,1},{4,6},{5,7},{6,4},{7,5},{8,10},{9,11},{10,... | collective-permute-start | bytes 304136 | tf_op jit(solution)/shard_map/ppermute | solution.py:371
  93.8 21.3 %all-to-all-start.3 = ((bf16[4,256,640]{2,1,0:T(8,128)(2,1)}), bf16[4,256,640]{2,1,0:T(8,128)(2,1)S(1)}, u32[]{:S(2)}, u32[]{:S(2)}) async-start(bf16[4,256,640]{2,1,0:T(8,128)(2,1)} %broadcast_in_dim.13), calls=%async_computation.3 | async-start | bytes 2621440 | tf_op jit(solution)/shard_map/all_to_all | solution.py:57
  105.9 1.9 %copy-start.1 = (bf16[1024,1536]{1,0:T(8,128)(2,1)S(1)}, bf16[1024,1536]{1,0:T(8,128)(2,1)}, u32[]{:S(2)}) copy-start(bf16[1024,1536]{1,0:T(8,128)(2,1)} %all-gather.2.cloned.1.call-done) | copy-start | bytes 9437188
  107.8 1.0 copy-start.5
  113.4 1.0 copy-start.6
  115.1 8.3 %copy-start.7 = (bf16[2,1024,256]{2,1,0:T(8,128)(2,1)S(1)}, bf16[2,1024,256]{2,1,0:T(8,128)(2,1)}, u32[]{:S(2)}) copy-start(bf16[2,1024,256]{2,1,0:T(8,128)(2,1)} %copy-done.6) | copy-start | bytes 3145732
  117.6 11.7 %all-to-all-start.4 = ((bf16[4,16,256]{2,1,0:T(8,128)(2,1)}), bf16[4,16,256]{2,1,0:T(8,128)(2,1)S(1)}, u32[]{:S(2)}, u32[]{:S(2)}) async-start(bf16[4,16,256]{2,1,0:T(8,128)(2,1)} %decode_attention.1), calls=%async_computation.4 | async-start | bytes 65536 | tf_op jit(solution)/shard_map/all_to_all | solution.py:380
  129.3 0.6 copy-start.10
Sparse Core Ops, SparseCore 0:
  53.9 51.9 all-gather.1

commit v10 on v9

--- a/solution.py
+++ b/solution.py
@@ -23,13 +23,12 @@
 TABLE = 640
 NORM_FLOPS = 30_000_000_000
 WIDE = KVL + 2 * ROPE
-START, LENGTH, BASE, PLACE, FIRST, SOURCE, SLOT, BLOCK = 0, 3, 6, 8, 16, 24, 28, 32
+START, LENGTH, BASE, PLACE, FIRST, SOURCE, SLOT, HALF, LINE = 0, 3, 6, 8, 16, 24, 28, 32, 40
 
 SIGMA = (1.0 + 0.1 * math.log(40.0)) ** 2 * (NOPE + ROPE) ** (-0.5)
 bf16 = jnp.bfloat16
 f32 = jnp.float32
 i32 = jnp.int32
-VMEM_LIMIT = 40 * 1024 * 1024
 
 
 def rotary_table():
@@ -82,11 +81,14 @@
         for m in range(NREP * NREQ):
             source += jnp.where(slot_ref[0, m] == rep * NREQ + r, m, 0)
         out_ref[SOURCE + r] = lax.div(source, NREQ) * PAD + lax.rem(source, NREQ) * STEPS
+    for j in range(2):
+        out_ref[HALF + j] = yh ^ j
+    for d in range(NX):
+        out_ref[LINE + d] = lax.rem(x + NX - d, NX)
     out_ref[BASE] = x * 2 * BLK + yz * PAD - start_of(x * 2 + lax.div(yz, 8)) * BLK
     for i in range(8):
         out_ref[PLACE + i] = i - start_of(i)
         out_ref[FIRST + i] = start_of(i) * BLK
-        out_ref[BLOCK + i] = (yh ^ (i // NX)) * NX + lax.rem(x + NX - i % NX, NX)
 
 
 SMEM = pl.BlockSpec(memory_space=pltpu.SMEM)
@@ -149,35 +151,41 @@
 
 
 def query_kernel(layout_ref, cq_ref, w_ref, cos_ref, sin_ref, out_ref):
-    rows = cq_ref[...].reshape(BLK, -1)
+    half = pl.program_id(0)
+    rows = jnp.concatenate([cq_ref[:, d].reshape(BLK, -1) for d in range(NX)])
     u = jnp.dot(rows, w_ref[...], preferred_element_type=f32)
     first, second, pe = split_heads(u)
-    pe = rotate(pe, cos_ref[...], sin_ref[...])
-    low = lax.broadcasted_iota(i32, pe.shape, 1) < ROPE
-    out_ref[0, :, :NOPE] = first.astype(bf16)
-    out_ref[0, :, NOPE:] = jnp.where(low, pe, 0.0).astype(bf16)
-    out_ref[1, :, :NOPE] = second.astype(bf16)
-    out_ref[1, :, NOPE:] = jnp.where(low, 0.0, pe).astype(bf16)
+    low = lax.broadcasted_iota(i32, (BLK, 2 * ROPE), 1) < ROPE
+    for d in range(NX):
+        here = slice(d * BLK, (d + 1) * BLK)
+        line = layout_ref[LINE + d]
+        to = pl.ds(pl.multiple_of(line * BLK, BLK), BLK)
+        at = pl.ds(pl.multiple_of(layout_ref[PLACE + half * NX + line] * BLK, BLK), BLK)
+        turned = rotate(pe[here], cos_ref[at, :], sin_ref[at, :])
+        out_ref[0, to, :NOPE] = first[here].astype(bf16)
+        out_ref[0, to, NOPE:] = jnp.where(low, turned, 0.0).astype(bf16)
+        out_ref[1, to, :NOPE] = second[here].astype(bf16)
+        out_ref[1, to, NOPE:] = jnp.where(low, 0.0, turned).astype(bf16)
 
 
 def project_queries(layout, cq, weights, cos_part, sin_part):
     width = cq.shape[-1]
-    table = pl.BlockSpec((BLK, 2 * ROPE), lambda i, place: (place[PLACE + i], 0))
+    table = pl.BlockSpec(cos_part.shape, lambda j, place: (0, 0))
     return pl.pallas_call(
         query_kernel,
         grid_spec=pltpu.PrefetchScalarGridSpec(
             num_scalar_prefetch=1,
-            grid=(8,),
+            grid=(2,),
             in_specs=[
-                pl.BlockSpec((8, 1, PAD, width), lambda i, place: (0, place[BLOCK + i], 0, 0)),
-                pl.BlockSpec(weights.shape, lambda i, place: (0, 0)),
+                pl.BlockSpec((8, NX, PAD, width), lambda j, place: (0, place[HALF + j], 0, 0)),
+                pl.BlockSpec(weights.shape, lambda j, place: (0, 0)),
                 table,
                 table,
             ],
-            out_specs=pl.BlockSpec((HEADS, BLK, 2 * NOPE), lambda i, place: (0, i, 0)),
+            out_specs=pl.BlockSpec((HEADS, NX * BLK, 2 * NOPE), lambda j, place: (0, j, 0)),
         ),
         out_shape=jax.ShapeDtypeStruct((HEADS, 8 * BLK, 2 * NOPE), bf16),
-        compiler_params=pltpu.CompilerParams(vmem_limit_bytes=VMEM_LIMIT),
+        compiler_params=pltpu.CompilerParams(vmem_limit_bytes=60 * 1024 * 1024),
         cost_estimate=pl.CostEstimate(flops=1_200_000_000, bytes_accessed=5_000_000, transcendentals=0),
         name="project_queries",
     )(layout, cq, weights, cos_part, sin_part)
@@ -222,7 +230,7 @@
             pltpu.VMEM((PAD, 2 * ROPE), f32),
             pltpu.VMEM((PAD, 2 * ROPE), f32),
         ],
-        compiler_params=pltpu.CompilerParams(vmem_limit_bytes=VMEM_LIMIT),
+        compiler_params=pltpu.CompilerParams(vmem_limit_bytes=16 * 1024 * 1024),
         cost_estimate=pl.CostEstimate(flops=30_000_000, bytes_accessed=2_500_000, transcendentals=0),
         name="prepare_decode",
     )(layout, rows, q_up, kv_up, cos_part, sin_part)
@@ -270,7 +278,7 @@
         in_specs=[SMEM] + [VMEM] * 3,
         out_specs=VMEM,
         out_shape=jax.ShapeDtypeStruct((NREP, PAD, HEADS * VD), bf16),
-        compiler_params=pltpu.CompilerParams(vmem_limit_bytes=VMEM_LIMIT),
+        compiler_params=pltpu.CompilerParams(vmem_limit_bytes=16 * 1024 * 1024),
         cost_estimate=pl.CostEstimate(flops=100_000_000, bytes_accessed=2_000_000, transcendentals=40_000),
         name="decode_attention",
     )(layout, ready, cache, kv_up)
@@ -335,7 +343,7 @@
             pltpu.VMEM((HEADS, rows, 2 * NOPE), bf16),
             pltpu.VMEM((HEADS, rows, VD), bf16),
         ],
-        compiler_params=pltpu.CompilerParams(vmem_limit_bytes=VMEM_LIMIT),
+        compiler_params=pltpu.CompilerParams(vmem_limit_bytes=32 * 1024 * 1024),
         cost_estimate=pl.CostEstimate(flops=1_500_000_000, bytes_accessed=4_000_000, transcendentals=1_000_000),
         name="prefill_attention",
     )(layout, queries, cache, kv_up)

time: 139 us -> 139 us (level)
  local copies, waits for them, and re-layouts: 6.51 us -> 2.7 us
  waiting for transfers between devices: 31.8 us -> 34.8 us
    unnamed x29 -> x25, local copies, waits for them, and re-layouts: 5.32 us -> 1.5 us
    all_to_all x1, waiting for transfers between devices: 0.69 us -> 3.66 us  [spread(): return lax.all_to_all(copies, axes, 0, 0, tiled=True)]
  transfers between devices with their start and end apart: 12 -> 12, of which waited for: 7 -> 7; matrix products, arithmetic and copies ran while one was open for 3% -> 3% of each run, Pallas kernels for 11% -> 12%
where the time goes in v10:
time: 139 us; the launch traced here: 138 us
  starting transfers between devices  61.3 us (44%)
  waiting for transfers between devices  34.8 us (25%)
  Pallas kernels  22.3 us (16%)
  between operations  14.2 us (10%)
  local copies, waits for them, and re-layouts  2.7 us (2%)
  other arithmetic  1.61 us (1%)
    all_to_all x1, starting transfers between devices, body(): lax.all_to_all(partial.reshape(16, chunk, -1), ('yh', 'z'), 0, 0, tiled=T...  15.8 us
    ppermute x3, starting transfers between devices, body(): lax.ppermute(own, 'x', shift(NX, d))  10.7 us
    all_to_all x1, starting transfers between devices, body(): lax.all_to_all(copies, ('yh', 'z'), 0, 0, tiled=True).reshape(per_x, -1)  10.4 us
    all_to_all x1, waiting for transfers between devices, body(): lax.all_to_all(partial.reshape(16, chunk, -1), ('yh', 'z'), 0, 0, tiled=T...  10 us
    all_gather x1, waiting for transfers between devices, body(): cq = lax.all_gather(line, 'z', axis=0, tiled=True)  8.39 us
    ppermute x2, waiting for transfers between devices, body(): met = lax.ppermute(rep_in, 'rep', [(i, i ^ d) for i in range(NREP)])  8.28 us
    ppermute x2, starting transfers between devices, body(): met = lax.ppermute(rep_in, 'rep', [(i, i ^ d) for i in range(NREP)])  6.37 us
    pallas_call x1, Pallas kernels, prefill(): pl.pallas_call(prefill_kernel, in_specs=[SMEM] + [VMEM] * 3, out_specs=VM...  5.89 us
  transfers between devices with their start and end apart: 12, of which 7 were waited for; matrix products, arithmetic and copies ran while one was open for 3% of the time, Pallas kernels for 12%

profile of v10, /device:TPU:56, one launch (start us, length us, event | category | flops | bytes accessed | tf_op | source)
XLA Modules:
  0.0 138.2 jit_solution(538135897233130049)
XLA Ops:
  7.2 0.0 copy-start.9
  7.2 2.0 %pack_hidden.1 = bf16[4,112,832]{2,1,0:T(8,128)(2,1)} custom-call(bf16[112,1024]{1,0:T(8,128)(2,1)} %bitcast.20, bf16[112,576]{1,0:T(8,128)(2,1)} %down_ref.1), custom_call_target="tpu_custom_call" | custom-call | bytes 1200000 | tf_op jit(solution)/shard_map/pack_hidden/pallas_call | solution.py:118
  9.2 4.3 %all-to-all-start = ((bf16[4,112,832]{2,1,0:T(8,128)(2,1)}), bf16[4,112,832]{2,1,0:T(8,128)(2,1)S(1)}, u32[]{:S(2)}, u32[]{:S(2)}) async-start(bf16[4,112,832]{2,1,0:T(8,128)(2,1)} %pack_hidden.1), calls=%async_computation | async-start | bytes 1605632 | tf_op jit(solution)/shard_map/all_to_all | solution.py:362
  13.5 0.0 copy-done.9
  13.5 5.1 %collective-permute-start.2 = (bf16[16,1536]{1,0:T(8,128)(2,1)S(1)}, bf16[16,1536]{1,0:T(8,128)(2,1)S(1)}, u32[]{:S(2)}, u32[]{:S(2)}) collective-permute-start(bf16[16,1536]{1,0:T(8,128)(2,1)S(1)} %bitcast.21), channel_id=1, source_target_pairs={{0,96},{32,0},{64,32},{96,64},{1,97},{33,1},{65,33},{97,65},{2,98}... | collective-permute-start | bytes 147464 | tf_op jit(solution)/shard_map/ppermute | solution.py:364
  18.6 2.8 %collective-permute-start.1 = (bf16[16,1536]{1,0:T(8,128)(2,1)S(1)}, bf16[16,1536]{1,0:T(8,128)(2,1)S(1)}, u32[]{:S(2)}, u32[]{:S(2)}) collective-permute-start(bf16[16,1536]{1,0:T(8,128)(2,1)S(1)} %bitcast.22), channel_id=1, source_target_pairs={{0,64},{32,96},{64,0},{96,32},{1,65},{33,97},{65,1},{97,33},{2,66}... | collective-permute-start | bytes 147464 | tf_op jit(solution)/shard_map/ppermute | solution.py:364
  21.4 2.8 %collective-permute-start = (bf16[16,1536]{1,0:T(8,128)(2,1)S(1)}, bf16[16,1536]{1,0:T(8,128)(2,1)S(1)}, u32[]{:S(2)}, u32[]{:S(2)}) collective-permute-start(bf16[16,1536]{1,0:T(8,128)(2,1)S(1)} %bitcast.23), channel_id=1, source_target_pairs={{0,32},{32,64},{64,96},{96,0},{1,33},{33,65},{65,97},{97,1},{2,34}... | collective-permute-start | bytes 147464 | tf_op jit(solution)/shard_map/ppermute | solution.py:364
  24.2 1.9 %collective-permute-done.2 = bf16[16,1536]{1,0:T(8,128)(2,1)S(1)} collective-permute-done((bf16[16,1536]{1,0:T(8,128)(2,1)S(1)}, bf16[16,1536]{1,0:T(8,128)(2,1)S(1)}, u32[]{:S(2)}, u32[]{:S(2)}) %collective-permute-start.2) | collective-permute-done | bytes 49184 | tf_op jit(solution)/shard_map/ppermute | solution.py:364
  26.0 1.6 %collective-permute-done.1 = bf16[16,1536]{1,0:T(8,128)(2,1)S(1)} collective-permute-done((bf16[16,1536]{1,0:T(8,128)(2,1)S(1)}, bf16[16,1536]{1,0:T(8,128)(2,1)S(1)}, u32[]{:S(2)}, u32[]{:S(2)}) %collective-permute-start.1) | collective-permute-done | bytes 49184 | tf_op jit(solution)/shard_map/ppermute | solution.py:364
  27.6 1.0 collective-permute-done
  28.6 0.0 all-to-all-done
  28.6 4.7 %collective-permute-start.5 = (bf16[64,1536]{1,0:T(8,128)(2,1)S(1)}, bf16[64,1536]{1,0:T(8,128)(2,1)S(1)}, u32[]{:S(2)}, u32[]{:S(2)}) collective-permute-start(bf16[64,1536]{1,0:T(8,128)(2,1)S(1)} %pad_maximum_fusion.2), channel_id=1, source_target_pairs={{0,128},{128,0},{1,129},{129,1},{2,130},{130,2},{3,131},{131,3},{4... | collective-permute-start | bytes 589832 | tf_op jit(solution)/shard_map/ppermute | solution.py:366
  33.3 1.2 fusion
  34.6 15.8 %all-to-all-start.1 = ((f32[16,16,576]{2,1,0:T(8,128)}), f32[16,16,576]{2,1,0:T(8,128)S(1)}, u32[]{:S(2)}, u32[]{:S(2)}) async-start(f32[16,16,576]{2,1,0:T(8,128)} %bitcast.8), calls=%async_computation.1 | async-start | bytes 1310720 | tf_op jit(solution)/shard_map/all_to_all | solution.py:373
  50.4 0.0 all-gather.2.cloned.1.call-start
  50.4 0.0 collective-permute-done.5
  50.5 0.8 pad_maximum_fusion
  51.2 0.0 all-gather.2.cloned.1.call-update
  51.3 0.6 pad_add_fusion.ids_ref
  51.9 1.3 request_layout.1.layout_ref
  53.2 0.0 copy-done.10
  53.2 0.0 copy-done.11
  53.2 2.4 %collective-permute-start.3 = (bf16[3,4,2112]{2,1,0:T(4,128)(2,1)S(1)}, bf16[3,4,2112]{2,1,0:T(4,128)(2,1)S(1)}, u32[]{:S(2)}, u32[]{:S(2)}) collective-permute-start(bf16[3,4,2112]{2,1,0:T(4,128)(2,1)S(1)} %constant_dynamic-update-slice_fusion), channel_id=1, source_target_pairs={{0,1},{1,0},{2,3},{3,2},{4,5},{5,4},{6,7},{7,6},{8,9},{9,8},{10,11... | collective-permute-start | bytes 152072 | tf_op jit(solution)/shard_map/ppermute | solution.py:379
  55.6 10.0 %all-to-all-done.1.pieces_ref = f32[16,16,576]{2,1,0:T(8,128)S(1)} async-done(((f32[16,16,576]{2,1,0:T(8,128)}), f32[16,16,576]{2,1,0:T(8,128)S(1)}, u32[]{:S(2)}, u32[]{:S(2)}) %all-to-all-start.1) | async-done | bytes 589856 | tf_op jit(solution)/shard_map/all_to_all | solution.py:373
  65.6 0.8 copy-done.7
  66.5 2.3 %norm_rows.1 = bf16[16,16,640]{2,1,0:T(8,128)(2,1)} custom-call(s32[64]{0:T(128)} %request_layout.1.layout_ref, f32[16,16,576]{2,1,0:T(8,128)} %copy-done.7, f32[1,512]{1,0:T(1,128)} %bitcast.25, f32[640,128]{1,0:T(8,128)} %constant.24.clone.cos_ref, f32[640,128]{1,0:T(8,128)} %constant.25.clone.sin_ref), custom_call_target="tpu_custom_call" | custom-call | flops 30000001024 | bytes 1000000 | tf_op jit(solution)/shard_map/norm_rows/pallas_call | solution.py:143
  68.8 10.4 %all-to-all-start.2 = ((bf16[16,16,640]{2,1,0:T(8,128)(2,1)}), bf16[16,16,640]{2,1,0:T(8,128)(2,1)S(1)}, u32[]{:S(2)}, u32[]{:S(2)}) async-start(bf16[16,16,640]{2,1,0:T(8,128)(2,1)} %norm_rows.1), calls=%async_computation.2 | async-start | bytes 655360 | tf_op jit(solution)/shard_map/all_to_all | solution.py:375
  79.1 0.0 collective-permute-done.3
  79.1 0.1 pad_maximum_fusion.3
  79.2 4.0 %collective-permute-start.4 = (bf16[6,4,2112]{2,1,0:T(4,128)(2,1)S(1)}, bf16[6,4,2112]{2,1,0:T(4,128)(2,1)S(1)}, u32[]{:S(2)}, u32[]{:S(2)}) collective-permute-start(bf16[6,4,2112]{2,1,0:T(4,128)(2,1)S(1)} %pad_maximum_fusion.3), channel_id=1, source_target_pairs={{0,2},{1,3},{2,0},{3,1},{4,6},{5,7},{6,4},{7,5},{8,10},{9,11},{10,... | collective-permute-start | bytes 304136 | tf_op jit(solution)/shard_map/ppermute | solution.py:379
  83.2 8.3 %collective-permute-done.4 = bf16[6,4,2112]{2,1,0:T(4,128)(2,1)S(1)} collective-permute-done((bf16[6,4,2112]{2,1,0:T(4,128)(2,1)S(1)}, bf16[6,4,2112]{2,1,0:T(4,128)(2,1)S(1)}, u32[]{:S(2)}, u32[]{:S(2)}) %collective-permute-start.4) | collective-permute-done | bytes 101408 | tf_op jit(solution)/shard_map/ppermute | solution.py:379
  91.5 0.1 pad_maximum_fusion.1.rows_ref
  91.7 0.0 copy-done.1
  91.7 0.0 copy-done.2
  91.7 1.1 prepare_decode.1.ready_ref
  92.8 0.0 all-to-all-done.2
  92.8 1.2 broadcast_in_dim.13
  94.0 3.5 %all-to-all-start.3 = ((bf16[4,256,640]{2,1,0:T(8,128)(2,1)}), bf16[4,256,640]{2,1,0:T(8,128)(2,1)S(1)}, u32[]{:S(2)}, u32[]{:S(2)}) async-start(bf16[4,256,640]{2,1,0:T(8,128)(2,1)} %broadcast_in_dim.13), calls=%async_computation.3 | async-start | bytes 2621440 | tf_op jit(solution)/shard_map/all_to_all | solution.py:56
  97.5 8.4 %all-gather.2.cloned.1.call-done = bf16[1024,1536]{1,0:T(8,128)(2,1)} async-done(((bf16[128,1536]{1,0:T(8,128)(2,1)}), bf16[1024,1536]{1,0:T(8,128)(2,1)}) %all-gather.2.cloned.1.call-update) | async-done | bytes 3145744 | tf_op jit(solution)/shard_map/all_gather | solution.py:367
  105.9 5.8 %project_queries.1.q_ref = bf16[2,1024,256]{2,1,0:T(8,128)(2,1)} custom-call(s32[64]{0:T(128)} %request_layout.1.layout_ref, bf16[8,8,16,1536]{3,2,1,0:T(8,128)(2,1)} %bitcast.18, bf16[1536,384]{1,0:T(8,128)(2,1)} %w_ref.3, f32[640,128]{1,0:T(8,128)} %constant.24.clone.cos_ref, f32[640,128]{1,0:T(8,128)} %constant.25.clone.sin_ref), custom_call_target="tpu_custom_call" | custom-call | flops 1200000000 | bytes 5000000 | tf_op jit(solution)/shard_map/project_queries/pallas_call | solution.py:174
  111.7 3.7 %all-to-all-done.3 = bf16[4,256,640]{2,1,0:T(8,128)(2,1)S(1)} async-done(((bf16[4,256,640]{2,1,0:T(8,128)(2,1)}), bf16[4,256,640]{2,1,0:T(8,128)(2,1)S(1)}, u32[]{:S(2)}, u32[]{:S(2)}) %all-to-all-start.3) | async-done | bytes 1310752 | tf_op jit(solution)/shard_map/all_to_all | solution.py:56
  115.4 0.0 copy-done.6
  115.4 2.5 %decode_attention.1 = bf16[4,16,256]{2,1,0:T(8,128)(2,1)} custom-call(s32[64]{0:T(128)S(1)} %copy-done.6, bf16[48,640]{1,0:T(8,128)(2,1)S(1)} %prepare_decode.1.ready_ref, bf16[1024,640]{1,0:T(8,128)(2,1)S(1)} %bitcast.15, bf16[512,512]{1,0:T(8,128)(2,1)S(1)} %copy-done.1), custom_call_target="tpu_custom_call" | custom-call | flops 100000000 | bytes 2000000 | tf_op jit(solution)/shard_map/decode_attention/pallas_call | solution.py:276
  117.9 5.5 %all-to-all-start.4 = ((bf16[4,16,256]{2,1,0:T(8,128)(2,1)}), bf16[4,16,256]{2,1,0:T(8,128)(2,1)S(1)}, u32[]{:S(2)}, u32[]{:S(2)}) async-start(bf16[4,16,256]{2,1,0:T(8,128)(2,1)} %decode_attention.1), calls=%async_computation.4 | async-start | bytes 65536 | tf_op jit(solution)/shard_map/all_to_all | solution.py:388
  123.4 5.9 %prefill_attention.1 = bf16[1024,256]{1,0:T(8,128)(2,1)} custom-call(s32[64]{0:T(128)S(1)} %copy-done.6, bf16[2,1024,256]{2,1,0:T(8,128)(2,1)S(1)} %copy-done.4, bf16[1024,640]{1,0:T(8,128)(2,1)S(1)} %bitcast.16, bf16[512,512]{1,0:T(8,128)(2,1)S(1)} %copy-done.1), custom_call_target="tpu_custom_call" | custom-call | flops 1500000000 | bytes 4000000 | tf_op jit(solution)/shard_map/prefill_attention/pallas_call | solution.py:337
  129.3 0.0 all-to-all-done.4.pool_ref
  129.3 0.6 copy-done.8
  129.9 1.5 %select_slots.1 = bf16[3,4,256]{2,1,0:T(4,128)(2,1)} custom-call(s32[64]{0:T(128)} %request_layout.1.layout_ref, bf16[4,16,256]{2,1,0:T(8,128)(2,1)} %copy-done.8), custom_call_target="tpu_custom_call" | custom-call | flops 1000000 | bytes 50000 | tf_op jit(solution)/shard_map/select_slots/pallas_call | solution.py:297
  (18 shorter events, 0.1 us)
Async XLA Ops:
  7.2 6.3 %copy-start.9 = (bf16[1,16,1536]{2,1,0:T(8,128)(2,1)S(1)}, bf16[1,16,1536]{2,1,0:T(8,128)(2,1)}, u32[]{:S(2)}) copy-start(bf16[1,16,1536]{2,1,0:T(8,128)(2,1)} %param.13) | copy-start | bytes 147460
  9.2 19.4 %all-to-all-start = ((bf16[4,112,832]{2,1,0:T(8,128)(2,1)}), bf16[4,112,832]{2,1,0:T(8,128)(2,1)S(1)}, u32[]{:S(2)}, u32[]{:S(2)}) async-start(bf16[4,112,832]{2,1,0:T(8,128)(2,1)} %pack_hidden.1), calls=%async_computation | async-start | bytes 1605632 | tf_op jit(solution)/shard_map/all_to_all | solution.py:362
  13.5 12.6 %collective-permute-start.2 = (bf16[16,1536]{1,0:T(8,128)(2,1)S(1)}, bf16[16,1536]{1,0:T(8,128)(2,1)S(1)}, u32[]{:S(2)}, u32[]{:S(2)}) collective-permute-start(bf16[16,1536]{1,0:T(8,128)(2,1)S(1)} %bitcast.21), channel_id=1, source_target_pairs={{0,96},{32,0},{64,32},{96,64},{1,97},{33,1},{65,33},{97,65},{2,98}... | collective-permute-start | bytes 147464 | tf_op jit(solution)/shard_map/ppermute | solution.py:364
  18.6 9.0 %collective-permute-start.1 = (bf16[16,1536]{1,0:T(8,128)(2,1)S(1)}, bf16[16,1536]{1,0:T(8,128)(2,1)S(1)}, u32[]{:S(2)}, u32[]{:S(2)}) collective-permute-start(bf16[16,1536]{1,0:T(8,128)(2,1)S(1)} %bitcast.22), channel_id=1, source_target_pairs={{0,64},{32,96},{64,0},{96,32},{1,65},{33,97},{65,1},{97,33},{2,66}... | collective-permute-start | bytes 147464 | tf_op jit(solution)/shard_map/ppermute | solution.py:364
  21.4 7.2 %collective-permute-start = (bf16[16,1536]{1,0:T(8,128)(2,1)S(1)}, bf16[16,1536]{1,0:T(8,128)(2,1)S(1)}, u32[]{:S(2)}, u32[]{:S(2)}) collective-permute-start(bf16[16,1536]{1,0:T(8,128)(2,1)S(1)} %bitcast.23), channel_id=1, source_target_pairs={{0,32},{32,64},{64,96},{96,0},{1,33},{33,65},{65,97},{97,1},{2,34}... | collective-permute-start | bytes 147464 | tf_op jit(solution)/shard_map/ppermute | solution.py:364
  28.6 21.8 %collective-permute-start.5 = (bf16[64,1536]{1,0:T(8,128)(2,1)S(1)}, bf16[64,1536]{1,0:T(8,128)(2,1)S(1)}, u32[]{:S(2)}, u32[]{:S(2)}) collective-permute-start(bf16[64,1536]{1,0:T(8,128)(2,1)S(1)} %pad_maximum_fusion.2), channel_id=1, source_target_pairs={{0,128},{128,0},{1,129},{129,1},{2,130},{130,2},{3,131},{131,3},{4... | collective-permute-start | bytes 589832 | tf_op jit(solution)/shard_map/ppermute | solution.py:366
  34.6 18.6 %copy-start.10 = (bf16[3,4,1536]{2,1,0:T(4,128)(2,1)S(1)}, bf16[3,4,1536]{2,1,0:T(4,128)(2,1)}, u32[]{:S(2)}) copy-start(bf16[3,4,1536]{2,1,0:T(4,128)(2,1)} %param.20) | copy-start | bytes 110596
  34.6 18.7 %copy-start.11 = (bf16[3,4,576]{2,1,0:T(4,128)(2,1)S(1)}, bf16[3,4,576]{2,1,0:T(4,128)(2,1)}, u32[]{:S(2)}) copy-start(bf16[3,4,576]{2,1,0:T(4,128)(2,1)} %param.21) | copy-start | bytes 41476
  34.6 31.1 %all-to-all-start.1 = ((f32[16,16,576]{2,1,0:T(8,128)}), f32[16,16,576]{2,1,0:T(8,128)S(1)}, u32[]{:S(2)}, u32[]{:S(2)}) async-start(f32[16,16,576]{2,1,0:T(8,128)} %bitcast.8), calls=%async_computation.1 | async-start | bytes 1310720 | tf_op jit(solution)/shard_map/all_to_all | solution.py:373
  50.4 55.5 %all-gather.2.cloned.1.call-start = ((), (), s32[]{:S(2)}) async-start(), calls=%async_computation.5 | async-start | bytes 3538944 | tf_op jit(solution)/shard_map/all_gather | solution.py:367
  53.2 25.9 %collective-permute-start.3 = (bf16[3,4,2112]{2,1,0:T(4,128)(2,1)S(1)}, bf16[3,4,2112]{2,1,0:T(4,128)(2,1)S(1)}, u32[]{:S(2)}, u32[]{:S(2)}) collective-permute-start(bf16[3,4,2112]{2,1,0:T(4,128)(2,1)S(1)} %constant_dynamic-update-slice_fusion), channel_id=1, source_target_pairs={{0,1},{1,0},{2,3},{3,2},{4,5},{5,4},{6,7},{7,6},{8,9},{9,8},{10,11... | collective-permute-start | bytes 152072 | tf_op jit(solution)/shard_map/ppermute | solution.py:379
  65.6 0.8 copy-start.7
  66.5 25.2 %copy-start.1 = (bf16[512,512]{1,0:T(8,128)(2,1)S(1)}, bf16[512,512]{1,0:T(8,128)(2,1)}, u32[]{:S(2)}) copy-start(bf16[512,512]{1,0:T(8,128)(2,1)} %kv_ref.5) | copy-start | bytes 1572868
  66.5 25.2 %copy-start.2 = (f32[640,128]{1,0:T(8,128)S(1)}, f32[640,128]{1,0:T(8,128)}, u32[]{:S(2)}) copy-start(f32[640,128]{1,0:T(8,128)} %constant.25.clone.sin_ref) | copy-start | bytes 983044
  66.5 25.2 %copy-start.3 = (f32[640,128]{1,0:T(8,128)S(1)}, f32[640,128]{1,0:T(8,128)}, u32[]{:S(2)}) copy-start(f32[640,128]{1,0:T(8,128)} %constant.24.clone.cos_ref) | copy-start | bytes 983044
  66.5 25.2 %copy-start.5 = (s32[64]{0:T(128)S(1)}, s32[64]{0:T(128)}, u32[]{:S(2)}) copy-start(s32[64]{0:T(128)} %request_layout.1.layout_ref) | copy-start | bytes 772
  68.8 22.9 %copy-start = (bf16[1536,384]{1,0:T(8,128)(2,1)S(1)}, bf16[1536,384]{1,0:T(8,128)(2,1)}, u32[]{:S(2)}) copy-start(bf16[1536,384]{1,0:T(8,128)(2,1)} %w_ref.3) | copy-start | bytes 3538948
  68.8 24.0 %all-to-all-start.2 = ((bf16[16,16,640]{2,1,0:T(8,128)(2,1)}), bf16[16,16,640]{2,1,0:T(8,128)(2,1)S(1)}, u32[]{:S(2)}, u32[]{:S(2)}) async-start(bf16[16,16,640]{2,1,0:T(8,128)(2,1)} %norm_rows.1), calls=%async_computation.2 | async-start | bytes 655360 | tf_op jit(solution)/shard_map/all_to_all | solution.py:375
  79.2 12.3 %collective-permute-start.4 = (bf16[6,4,2112]{2,1,0:T(4,128)(2,1)S(1)}, bf16[6,4,2112]{2,1,0:T(4,128)(2,1)S(1)}, u32[]{:S(2)}, u32[]{:S(2)}) collective-permute-start(bf16[6,4,2112]{2,1,0:T(4,128)(2,1)S(1)} %pad_maximum_fusion.3), channel_id=1, source_target_pairs={{0,2},{1,3},{2,0},{3,1},{4,6},{5,7},{6,4},{7,5},{8,10},{9,11},{10,... | collective-permute-start | bytes 304136 | tf_op jit(solution)/shard_map/ppermute | solution.py:379
  94.0 21.4 %all-to-all-start.3 = ((bf16[4,256,640]{2,1,0:T(8,128)(2,1)}), bf16[4,256,640]{2,1,0:T(8,128)(2,1)S(1)}, u32[]{:S(2)}, u32[]{:S(2)}) async-start(bf16[4,256,640]{2,1,0:T(8,128)(2,1)} %broadcast_in_dim.13), calls=%async_computation.3 | async-start | bytes 2621440 | tf_op jit(solution)/shard_map/all_to_all | solution.py:56
  105.9 9.5 %copy-start.6 = (s32[64]{0:T(128)S(1)}, s32[64]{0:T(128)}, u32[]{:S(2)}) copy-start(s32[64]{0:T(128)} %request_layout.1.layout_ref) | copy-start | bytes 772
  111.7 11.7 %copy-start.4 = (bf16[2,1024,256]{2,1,0:T(8,128)(2,1)S(1)}, bf16[2,1024,256]{2,1,0:T(8,128)(2,1)}, u32[]{:S(2)}) copy-start(bf16[2,1024,256]{2,1,0:T(8,128)(2,1)} %project_queries.1.q_ref) | copy-start | bytes 3145732
  117.9 11.4 %all-to-all-start.4 = ((bf16[4,16,256]{2,1,0:T(8,128)(2,1)}), bf16[4,16,256]{2,1,0:T(8,128)(2,1)S(1)}, u32[]{:S(2)}, u32[]{:S(2)}) async-start(bf16[4,16,256]{2,1,0:T(8,128)(2,1)} %decode_attention.1), calls=%async_computation.4 | async-start | bytes 65536 | tf_op jit(solution)/shard_map/all_to_all | solution.py:388
  129.3 0.6 copy-start.8
Sparse Core Ops, SparseCore 0:
  53.9 51.9 all-gather.1

commit v11 on v10

--- a/solution.py
+++ b/solution.py
@@ -84,7 +84,7 @@
     for j in range(2):
         out_ref[HALF + j] = yh ^ j
     for d in range(NX):
-        out_ref[LINE + d] = lax.rem(x + NX - d, NX)
+        out_ref[LINE + d] = d
     out_ref[BASE] = x * 2 * BLK + yz * PAD - start_of(x * 2 + lax.div(yz, 8)) * BLK
     for i in range(8):
         out_ref[PLACE + i] = i - start_of(i)
@@ -106,23 +106,58 @@
     )(ids, req_blocks, dest_slot)
 
 
-def pack_kernel(hidden_ref, down_ref, out_ref):
+def pack_kernel(hidden_ref, down_ref, own_ref, out_ref):
     per_x = hidden_ref.shape[1] // NX
+    count = own_ref.shape[1] // per_x
     for i in range(NX):
         out_ref[i, :, :per_x] = hidden_ref[:, i * per_x : (i + 1) * per_x]
-        out_ref[i, :, per_x:] = down_ref[...]
-
-
-def pack(hidden_t, kv_down):
+        for j in range(count):
+            out_ref[i, j * PAD : (j + 1) * PAD, per_x : 2 * per_x] = own_ref[:, j * per_x : (j + 1) * per_x]
+        left = out_ref.shape[1] - count * PAD
+        out_ref[i, count * PAD :, per_x : 2 * per_x] = jnp.zeros((left, per_x), bf16)
+        out_ref[i, :, 2 * per_x :] = down_ref[...]
+
+
+def pack(hidden_t, kv_down, own):
     features, rows = hidden_t.shape
     return pl.pallas_call(
         pack_kernel,
-        in_specs=[VMEM] * 2,
-        out_specs=VMEM,
-        out_shape=jax.ShapeDtypeStruct((NX, features, rows // NX + kv_down.shape[1]), bf16),
-        cost_estimate=pl.CostEstimate(flops=0, bytes_accessed=1_200_000, transcendentals=0),
+        in_specs=[VMEM] * 3,
+        out_specs=VMEM,
+        out_shape=jax.ShapeDtypeStruct((NX, features, 2 * (rows // NX) + kv_down.shape[1]), bf16),
+        cost_estimate=pl.CostEstimate(flops=0, bytes_accessed=1_500_000, transcendentals=0),
         name="pack_hidden",
-    )(hidden_t, kv_down)
+    )(hidden_t, kv_down, own)
+
+
+def meet_kernel(packed_ref, partial_ref, line_ref):
+    per_x = line_ref.shape[1] // 6
+    packed = packed_ref[...].reshape(-1, packed_ref.shape[2])
+    partial = lax.dot_general(
+        packed[:, :per_x], packed[:, 2 * per_x :], (((0,), (0,)), ((), ())), preferred_element_type=f32
+    )
+    partial_ref[...] = partial.reshape(partial_ref.shape)
+    for d in range(NX):
+        for j in range(6):
+            line_ref[d * PAD : (d + 1) * PAD, j * per_x : (j + 1) * per_x] = packed_ref[
+                d, j * PAD : (j + 1) * PAD, per_x : 2 * per_x
+            ]
+
+
+def meet(packed, per_x, width):
+    latent = packed.shape[2] - 2 * per_x
+    return pl.pallas_call(
+        meet_kernel,
+        in_specs=[VMEM],
+        out_specs=[VMEM, VMEM],
+        out_shape=[
+            jax.ShapeDtypeStruct((16, per_x // 16, latent), f32),
+            jax.ShapeDtypeStruct((NX * PAD, width), bf16),
+        ],
+        compiler_params=pltpu.CompilerParams(vmem_limit_bytes=16 * 1024 * 1024),
+        cost_estimate=pl.CostEstimate(flops=130_000_000, bytes_accessed=2_000_000, transcendentals=0),
+        name="partial_and_rows",
+    )(packed)
 
 
 def norm_kernel(layout_ref, pieces_ref, gain_ref, cos_ref, sin_ref, out_ref):
@@ -353,24 +388,19 @@
     ids = jnp.stack(
         [lax.axis_index("rep"), lax.axis_index("x"), lax.axis_index("yh"), lax.axis_index(("yh", "z"))]
     ).astype(i32)
-    rows, features = hidden.shape[1:]
+    rows = hidden.shape[1]
     per_x = rows // NX
-    chunk = per_x // 16
     cos_part, sin_part = rotary_table()
 
     own = comp_query[0]
-    packed = lax.all_to_all(pack(hidden[0].T, kv_down), "x", 0, 0, tiled=True)
+    packed = lax.all_to_all(pack(hidden[0].T, kv_down, own), "x", 0, 0, tiled=True)
     layout = request_layout(ids, req_blocks, dest_slot)
-    line = jnp.concatenate([own] + [lax.ppermute(own, "x", shift(NX, d)) for d in range(1, NX)])
-    packed, line, dec_query, dec_latent = lax.optimization_barrier((packed, line, dec_query, dec_latent))
+    packed, dec_query, dec_latent = lax.optimization_barrier((packed, dec_query, dec_latent))
+    partial, line = meet(packed, per_x, own.shape[1])
     line = jnp.concatenate([line, lax.ppermute(line, "yh", shift(2, 1))])
     cq = lax.all_gather(line, "z", axis=0, tiled=True)
 
-    packed = packed.reshape(NX * features, -1)
-    partial = lax.dot_general(
-        packed[:, :per_x], packed[:, per_x:], (((0,), (0,)), ((), ())), preferred_element_type=f32
-    )
-    pieces = lax.all_to_all(partial.reshape(16, chunk, -1), ("yh", "z"), 0, 0, tiled=True)
+    pieces = lax.all_to_all(partial, ("yh", "z"), 0, 0, tiled=True)
     copies = norm_rows(layout, pieces, kv_gain[None, :], cos_part, sin_part)
     cache = lax.all_to_all(copies, ("yh", "z"), 0, 0, tiled=True).reshape(per_x, -1)
 

time: 139 us -> 140 us (level)
  blocking collectives: 0 us -> 19.2 us
  starting transfers between devices: 61.3 us -> 45.8 us
  waiting for transfers between devices: 34.8 us -> 31.8 us
    all_to_all x0 -> x1, blocking collectives: none -> 19.2 us  [body(): lax.all_to_all(pack(hidden[0].T, kv_down, own), 'x', 0, 0, tiled=True)]
    ppermute x3 -> x0, starting transfers between devices: 10.7 us -> none  [body(): lax.ppermute(own, 'x', shift(NX, d))]
    all_to_all x2 -> x1, starting transfers between devices: 20.1 us -> 15.7 us  [body(): pieces = lax.all_to_all(partial, ('yh', 'z'), 0, 0, tiled=True)]
    ppermute x3 -> x0, waiting for transfers between devices: 4.42 us -> none  [body(): lax.ppermute(own, 'x', shift(NX, d))]
    pallas_call x1 -> x2, Pallas kernels: 1.99 us -> 3.3 us  [the longest x1 2.07 us: pack(): pl.pallas_call(pack_kernel, in_specs=[VMEM] * 3, out_specs=VMEM, out_shap...]
    all_to_all x2 -> x1, waiting for transfers between devices: 10 us -> 11 us  [body(): pieces = lax.all_to_all(partial, ('yh', 'z'), 0, 0, tiled=True)]
  transfers between devices with their start and end apart: 12 -> 8, of which waited for: 7 -> 4; matrix products, arithmetic and copies ran while one was open for 3% -> 2% of each run, Pallas kernels for 12% -> 12%
where the time goes in v11:
time: 140 us; the launch traced here: 139 us
  starting transfers between devices  45.8 us (33%)
  waiting for transfers between devices  31.8 us (23%)
  Pallas kernels  23.6 us (17%)
  blocking collectives  19.2 us (14%)
  between operations  14.2 us (10%)
  local copies, waits for them, and re-layouts  2.7 us (2%)
  other arithmetic  1.66 us (1%)
    all_to_all x1, blocking collectives, body(): lax.all_to_all(pack(hidden[0].T, kv_down, own), 'x', 0, 0, tiled=True)  19.2 us
    all_to_all x1, starting transfers between devices, body(): pieces = lax.all_to_all(partial, ('yh', 'z'), 0, 0, tiled=True)  15.7 us
    all_to_all x1, waiting for transfers between devices, body(): pieces = lax.all_to_all(partial, ('yh', 'z'), 0, 0, tiled=True)  11 us
    all_to_all x1, starting transfers between devices, body(): lax.all_to_all(copies, ('yh', 'z'), 0, 0, tiled=True).reshape(per_x, -1)  10.2 us
    ppermute x2, waiting for transfers between devices, body(): met = lax.ppermute(rep_in, 'rep', [(i, i ^ d) for i in range(NREP)])  8.23 us
    all_gather x1, waiting for transfers between devices, body(): cq = lax.all_gather(line, 'z', axis=0, tiled=True)  8.03 us
    ppermute x2, starting transfers between devices, body(): met = lax.ppermute(rep_in, 'rep', [(i, i ^ d) for i in range(NREP)])  6.37 us
    pallas_call x1, Pallas kernels, prefill(): pl.pallas_call(prefill_kernel, in_specs=[SMEM] + [VMEM] * 3, out_specs=VM...  5.89 us
  transfers between devices with their start and end apart: 8, of which 4 were waited for; matrix products, arithmetic and copies ran while one was open for 2% of the time, Pallas kernels for 12%

profile of v11, /device:TPU:56, one launch (start us, length us, event | category | flops | bytes accessed | tf_op | source)
XLA Modules:
  0.0 139.0 jit_solution(1832909205453828280)
XLA Ops:
  7.2 2.1 %pack_hidden.1 = bf16[4,112,1088]{2,1,0:T(8,128)(2,1)} custom-call(bf16[112,1024]{1,0:T(8,128)(2,1)} %bitcast.17, bf16[112,576]{1,0:T(8,128)(2,1)} %down_ref.1, bf16[16,1536]{1,0:T(8,128)(2,1)} %bitcast.18), custom_call_target="tpu_custom_call" | custom-call | bytes 1500000 | tf_op jit(solution)/shard_map/pack_hidden/pallas_call | solution.py:123
  9.2 19.2 %all_to_all.25.packed_ref = bf16[4,112,1088]{2,1,0:T(8,128)(2,1)S(1)} all-to-all(bf16[4,112,1088]{2,1,0:T(8,128)(2,1)} %pack_hidden.1), channel_id=1, replica_groups=mesh['section'=2,'yh'=2,'x'=4,'z'=8,'rep'=4] {'x'}, dimensions={0} | all-to-all | bytes 1949696 | tf_op jit(solution)/shard_map/all_to_all | solution.py:396
  28.4 1.2 partial_and_rows.1
  29.7 0.0 copy-start.9
  29.7 0.0 copy-start.10
  29.7 4.8 %collective-permute-start.2 = (bf16[64,1536]{1,0:T(8,128)(2,1)S(1)}, bf16[64,1536]{1,0:T(8,128)(2,1)S(1)}, u32[]{:S(2)}, u32[]{:S(2)}) collective-permute-start(bf16[64,1536]{1,0:T(8,128)(2,1)S(1)} %get-tuple-element.19), channel_id=1, source_target_pairs={{0,128},{128,0},{1,129},{129,1},{2,130},{130,2},{3,131},{131,3},{4... | collective-permute-start | bytes 589832 | tf_op jit(solution)/shard_map/ppermute | solution.py:400
  34.5 15.7 %all-to-all-start.1 = ((f32[16,16,576]{2,1,0:T(8,128)}), f32[16,16,576]{2,1,0:T(8,128)S(1)}, u32[]{:S(2)}, u32[]{:S(2)}) async-start(f32[16,16,576]{2,1,0:T(8,128)} %get-tuple-element.14), calls=%async_computation.1 | async-start | bytes 1310720 | tf_op jit(solution)/shard_map/all_to_all | solution.py:403
  50.2 0.0 all-gather.2.cloned.1.call-start
  50.3 0.0 collective-permute-done.2
  50.3 0.8 pad_maximum_fusion
  51.1 0.0 all-gather.2.cloned.1.call-update
  51.1 0.7 pad_add_fusion.ids_ref
  51.8 1.3 request_layout.1.layout_ref
  53.1 0.0 copy-done.9
  53.1 0.0 copy-done.10
  53.2 2.4 %collective-permute-start = (bf16[3,4,2112]{2,1,0:T(4,128)(2,1)S(1)}, bf16[3,4,2112]{2,1,0:T(4,128)(2,1)S(1)}, u32[]{:S(2)}, u32[]{:S(2)}) collective-permute-start(bf16[3,4,2112]{2,1,0:T(4,128)(2,1)S(1)} %constant_dynamic-update-slice_fusion), channel_id=1, source_target_pairs={{0,1},{1,0},{2,3},{3,2},{4,5},{5,4},{6,7},{7,6},{8,9},{9,8},{10,11... | collective-permute-start | bytes 152072 | tf_op jit(solution)/shard_map/ppermute | solution.py:409
  55.5 11.0 %all-to-all-done.1.pieces_ref = f32[16,16,576]{2,1,0:T(8,128)S(1)} async-done(((f32[16,16,576]{2,1,0:T(8,128)}), f32[16,16,576]{2,1,0:T(8,128)S(1)}, u32[]{:S(2)}, u32[]{:S(2)}) %all-to-all-start.1) | async-done | bytes 589856 | tf_op jit(solution)/shard_map/all_to_all | solution.py:403
  66.5 0.0 copy-start.7
  66.5 0.8 copy-done.7
  67.4 0.0 copy-start.2
  67.4 0.0 copy-start.3
  67.4 2.3 %norm_rows.1 = bf16[16,16,640]{2,1,0:T(8,128)(2,1)} custom-call(s32[64]{0:T(128)} %request_layout.1.layout_ref, f32[16,16,576]{2,1,0:T(8,128)} %copy-done.7, f32[1,512]{1,0:T(1,128)} %bitcast.19, f32[640,128]{1,0:T(8,128)} %constant.24.clone.cos_ref, f32[640,128]{1,0:T(8,128)} %constant.25.clone.sin_ref), custom_call_target="tpu_custom_call" | custom-call | flops 30000001024 | bytes 1000000 | tf_op jit(solution)/shard_map/norm_rows/pallas_call | solution.py:178
  69.7 10.2 %all-to-all-start.2 = ((bf16[16,16,640]{2,1,0:T(8,128)(2,1)}), bf16[16,16,640]{2,1,0:T(8,128)(2,1)S(1)}, u32[]{:S(2)}, u32[]{:S(2)}) async-start(bf16[16,16,640]{2,1,0:T(8,128)(2,1)} %norm_rows.1), calls=%async_computation.2 | async-start | bytes 655360 | tf_op jit(solution)/shard_map/all_to_all | solution.py:405
  79.9 0.0 collective-permute-done
  79.9 0.1 pad_maximum_fusion.2
  80.0 4.0 %collective-permute-start.1 = (bf16[6,4,2112]{2,1,0:T(4,128)(2,1)S(1)}, bf16[6,4,2112]{2,1,0:T(4,128)(2,1)S(1)}, u32[]{:S(2)}, u32[]{:S(2)}) collective-permute-start(bf16[6,4,2112]{2,1,0:T(4,128)(2,1)S(1)} %pad_maximum_fusion.2), channel_id=1, source_target_pairs={{0,2},{1,3},{2,0},{3,1},{4,6},{5,7},{6,4},{7,5},{8,10},{9,11},{10,... | collective-permute-start | bytes 304136 | tf_op jit(solution)/shard_map/ppermute | solution.py:409
  84.0 8.2 %collective-permute-done.1 = bf16[6,4,2112]{2,1,0:T(4,128)(2,1)S(1)} collective-permute-done((bf16[6,4,2112]{2,1,0:T(4,128)(2,1)S(1)}, bf16[6,4,2112]{2,1,0:T(4,128)(2,1)S(1)}, u32[]{:S(2)}, u32[]{:S(2)}) %collective-permute-start.1) | collective-permute-done | bytes 101408 | tf_op jit(solution)/shard_map/ppermute | solution.py:409
  92.3 0.1 pad_maximum_fusion.1.rows_ref
  92.4 0.0 copy-done.1
  92.4 0.0 copy-done.2
  92.4 0.0 copy-done.3
  92.4 0.0 copy-done.5
  92.4 0.0 copy-done
  92.5 1.1 prepare_decode.1.ready_ref
  93.5 0.0 all-to-all-done.2
  93.5 1.2 broadcast_in_dim.13
  94.7 3.5 %all-to-all-start.3 = ((bf16[4,256,640]{2,1,0:T(8,128)(2,1)}), bf16[4,256,640]{2,1,0:T(8,128)(2,1)S(1)}, u32[]{:S(2)}, u32[]{:S(2)}) async-start(bf16[4,256,640]{2,1,0:T(8,128)(2,1)} %broadcast_in_dim.13), calls=%async_computation.3 | async-start | bytes 2621440 | tf_op jit(solution)/shard_map/all_to_all | solution.py:56
  98.3 8.0 %all-gather.2.cloned.1.call-done = bf16[1024,1536]{1,0:T(8,128)(2,1)} async-done(((bf16[128,1536]{1,0:T(8,128)(2,1)}), bf16[1024,1536]{1,0:T(8,128)(2,1)}) %all-gather.2.cloned.1.call-update) | async-done | bytes 3145744 | tf_op jit(solution)/shard_map/all_gather | solution.py:401
  106.3 5.8 %project_queries.1.q_ref = bf16[2,1024,256]{2,1,0:T(8,128)(2,1)} custom-call(s32[64]{0:T(128)} %request_layout.1.layout_ref, bf16[8,8,16,1536]{3,2,1,0:T(8,128)(2,1)} %bitcast.15, bf16[1536,384]{1,0:T(8,128)(2,1)} %w_ref.3, f32[640,128]{1,0:T(8,128)} %constant.24.clone.cos_ref, f32[640,128]{1,0:T(8,128)} %constant.25.clone.sin_ref), custom_call_target="tpu_custom_call" | custom-call | flops 1200000000 | bytes 5000000 | tf_op jit(solution)/shard_map/project_queries/pallas_call | solution.py:209
  112.1 4.5 %all-to-all-done.3 = bf16[4,256,640]{2,1,0:T(8,128)(2,1)S(1)} async-done(((bf16[4,256,640]{2,1,0:T(8,128)(2,1)}), bf16[4,256,640]{2,1,0:T(8,128)(2,1)S(1)}, u32[]{:S(2)}, u32[]{:S(2)}) %all-to-all-start.3) | async-done | bytes 1310752 | tf_op jit(solution)/shard_map/all_to_all | solution.py:56
  116.6 0.0 copy-done.6
  116.6 2.5 %decode_attention.1 = bf16[4,16,256]{2,1,0:T(8,128)(2,1)} custom-call(s32[64]{0:T(128)S(1)} %copy-done.6, bf16[48,640]{1,0:T(8,128)(2,1)S(1)} %prepare_decode.1.ready_ref, bf16[1024,640]{1,0:T(8,128)(2,1)S(1)} %bitcast.13, bf16[512,512]{1,0:T(8,128)(2,1)S(1)} %copy-done.1), custom_call_target="tpu_custom_call" | custom-call | flops 100000000 | bytes 2000000 | tf_op jit(solution)/shard_map/decode_attention/pallas_call | solution.py:311
  119.1 5.1 %all-to-all-start.4 = ((bf16[4,16,256]{2,1,0:T(8,128)(2,1)}), bf16[4,16,256]{2,1,0:T(8,128)(2,1)S(1)}, u32[]{:S(2)}, u32[]{:S(2)}) async-start(bf16[4,16,256]{2,1,0:T(8,128)(2,1)} %decode_attention.1), calls=%async_computation.4 | async-start | bytes 65536 | tf_op jit(solution)/shard_map/all_to_all | solution.py:418
  124.2 0.0 copy-done.4
  124.2 5.9 %prefill_attention.1 = bf16[1024,256]{1,0:T(8,128)(2,1)} custom-call(s32[64]{0:T(128)S(1)} %copy-done.6, bf16[2,1024,256]{2,1,0:T(8,128)(2,1)S(1)} %copy-done.4, bf16[1024,640]{1,0:T(8,128)(2,1)S(1)} %bitcast.14, bf16[512,512]{1,0:T(8,128)(2,1)S(1)} %copy-done.1), custom_call_target="tpu_custom_call" | custom-call | flops 1500000000 | bytes 4000000 | tf_op jit(solution)/shard_map/prefill_attention/pallas_call | solution.py:372
  130.0 0.0 all-to-all-done.4.pool_ref
  130.1 0.6 copy-done.8
  130.7 1.5 %select_slots.1 = bf16[3,4,256]{2,1,0:T(4,128)(2,1)} custom-call(s32[64]{0:T(128)} %request_layout.1.layout_ref, bf16[4,16,256]{2,1,0:T(8,128)(2,1)} %copy-done.8), custom_call_target="tpu_custom_call" | custom-call | flops 1000000 | bytes 50000 | tf_op jit(solution)/shard_map/select_slots/pallas_call | solution.py:332
  (8 shorter events, 0.0 us)
Async XLA Ops:
  29.7 23.4 %copy-start.9 = (bf16[3,4,1536]{2,1,0:T(4,128)(2,1)S(1)}, bf16[3,4,1536]{2,1,0:T(4,128)(2,1)}, u32[]{:S(2)}) copy-start(bf16[3,4,1536]{2,1,0:T(4,128)(2,1)} %param.20) | copy-start | bytes 110596
  29.7 23.4 %copy-start.10 = (bf16[3,4,576]{2,1,0:T(4,128)(2,1)S(1)}, bf16[3,4,576]{2,1,0:T(4,128)(2,1)}, u32[]{:S(2)}) copy-start(bf16[3,4,576]{2,1,0:T(4,128)(2,1)} %param.21) | copy-start | bytes 41476
  29.7 20.6 %collective-permute-start.2 = (bf16[64,1536]{1,0:T(8,128)(2,1)S(1)}, bf16[64,1536]{1,0:T(8,128)(2,1)S(1)}, u32[]{:S(2)}, u32[]{:S(2)}) collective-permute-start(bf16[64,1536]{1,0:T(8,128)(2,1)S(1)} %get-tuple-element.19), channel_id=1, source_target_pairs={{0,128},{128,0},{1,129},{129,1},{2,130},{130,2},{3,131},{131,3},{4... | collective-permute-start | bytes 589832 | tf_op jit(solution)/shard_map/ppermute | solution.py:400
  34.5 32.0 %all-to-all-start.1 = ((f32[16,16,576]{2,1,0:T(8,128)}), f32[16,16,576]{2,1,0:T(8,128)S(1)}, u32[]{:S(2)}, u32[]{:S(2)}) async-start(f32[16,16,576]{2,1,0:T(8,128)} %get-tuple-element.14), calls=%async_computation.1 | async-start | bytes 1310720 | tf_op jit(solution)/shard_map/all_to_all | solution.py:403
  50.2 56.1 %all-gather.2.cloned.1.call-start = ((), (), s32[]{:S(2)}) async-start(), calls=%async_computation.5 | async-start | bytes 3538944 | tf_op jit(solution)/shard_map/all_gather | solution.py:401
  53.2 26.8 %collective-permute-start = (bf16[3,4,2112]{2,1,0:T(4,128)(2,1)S(1)}, bf16[3,4,2112]{2,1,0:T(4,128)(2,1)S(1)}, u32[]{:S(2)}, u32[]{:S(2)}) collective-permute-start(bf16[3,4,2112]{2,1,0:T(4,128)(2,1)S(1)} %constant_dynamic-update-slice_fusion), channel_id=1, source_target_pairs={{0,1},{1,0},{2,3},{3,2},{4,5},{5,4},{6,7},{7,6},{8,9},{9,8},{10,11... | collective-permute-start | bytes 152072 | tf_op jit(solution)/shard_map/ppermute | solution.py:409
  66.5 0.8 copy-start.7
  67.4 25.0 %copy-start.1 = (bf16[512,512]{1,0:T(8,128)(2,1)S(1)}, bf16[512,512]{1,0:T(8,128)(2,1)}, u32[]{:S(2)}) copy-start(bf16[512,512]{1,0:T(8,128)(2,1)} %kv_ref.5) | copy-start | bytes 1572868
  67.4 25.0 %copy-start.2 = (f32[640,128]{1,0:T(8,128)S(1)}, f32[640,128]{1,0:T(8,128)}, u32[]{:S(2)}) copy-start(f32[640,128]{1,0:T(8,128)} %constant.25.clone.sin_ref) | copy-start | bytes 983044
  67.4 25.0 %copy-start.3 = (f32[640,128]{1,0:T(8,128)S(1)}, f32[640,128]{1,0:T(8,128)}, u32[]{:S(2)}) copy-start(f32[640,128]{1,0:T(8,128)} %constant.24.clone.cos_ref) | copy-start | bytes 983044
  67.4 25.0 %copy-start.5 = (s32[64]{0:T(128)S(1)}, s32[64]{0:T(128)}, u32[]{:S(2)}) copy-start(s32[64]{0:T(128)} %request_layout.1.layout_ref) | copy-start | bytes 772
  69.7 22.8 %copy-start = (bf16[1536,384]{1,0:T(8,128)(2,1)S(1)}, bf16[1536,384]{1,0:T(8,128)(2,1)}, u32[]{:S(2)}) copy-start(bf16[1536,384]{1,0:T(8,128)(2,1)} %w_ref.3) | copy-start | bytes 3538948
  69.7 23.8 %all-to-all-start.2 = ((bf16[16,16,640]{2,1,0:T(8,128)(2,1)}), bf16[16,16,640]{2,1,0:T(8,128)(2,1)S(1)}, u32[]{:S(2)}, u32[]{:S(2)}) async-start(bf16[16,16,640]{2,1,0:T(8,128)(2,1)} %norm_rows.1), calls=%async_computation.2 | async-start | bytes 655360 | tf_op jit(solution)/shard_map/all_to_all | solution.py:405
  80.0 12.2 %collective-permute-start.1 = (bf16[6,4,2112]{2,1,0:T(4,128)(2,1)S(1)}, bf16[6,4,2112]{2,1,0:T(4,128)(2,1)S(1)}, u32[]{:S(2)}, u32[]{:S(2)}) collective-permute-start(bf16[6,4,2112]{2,1,0:T(4,128)(2,1)S(1)} %pad_maximum_fusion.2), channel_id=1, source_target_pairs={{0,2},{1,3},{2,0},{3,1},{4,6},{5,7},{6,4},{7,5},{8,10},{9,11},{10,... | collective-permute-start | bytes 304136 | tf_op jit(solution)/shard_map/ppermute | solution.py:409
  94.7 21.9 %all-to-all-start.3 = ((bf16[4,256,640]{2,1,0:T(8,128)(2,1)}), bf16[4,256,640]{2,1,0:T(8,128)(2,1)S(1)}, u32[]{:S(2)}, u32[]{:S(2)}) async-start(bf16[4,256,640]{2,1,0:T(8,128)(2,1)} %broadcast_in_dim.13), calls=%async_computation.3 | async-start | bytes 2621440 | tf_op jit(solution)/shard_map/all_to_all | solution.py:56
  106.3 10.3 %copy-start.6 = (s32[64]{0:T(128)S(1)}, s32[64]{0:T(128)}, u32[]{:S(2)}) copy-start(s32[64]{0:T(128)} %request_layout.1.layout_ref) | copy-start | bytes 772
  112.1 12.1 %copy-start.4 = (bf16[2,1024,256]{2,1,0:T(8,128)(2,1)S(1)}, bf16[2,1024,256]{2,1,0:T(8,128)(2,1)}, u32[]{:S(2)}) copy-start(bf16[2,1024,256]{2,1,0:T(8,128)(2,1)} %project_queries.1.q_ref) | copy-start | bytes 3145732
  119.1 11.0 %all-to-all-start.4 = ((bf16[4,16,256]{2,1,0:T(8,128)(2,1)}), bf16[4,16,256]{2,1,0:T(8,128)(2,1)S(1)}, u32[]{:S(2)}, u32[]{:S(2)}) async-start(bf16[4,16,256]{2,1,0:T(8,128)(2,1)} %decode_attention.1), calls=%async_computation.4 | async-start | bytes 65536 | tf_op jit(solution)/shard_map/all_to_all | solution.py:418
  130.0 0.6 copy-start.8
Sparse Core Ops, SparseCore 0:
  53.7 52.5 all-gather.1

commit v12 on v11

--- a/solution.py
+++ b/solution.py
@@ -21,7 +21,7 @@
 HEADS = 2
 PAD = 16
 TABLE = 640
-NORM_FLOPS = 30_000_000_000
+NORM_FLOPS = 35_000_000_000
 WIDE = KVL + 2 * ROPE
 START, LENGTH, BASE, PLACE, FIRST, SOURCE, SLOT, HALF, LINE = 0, 3, 6, 8, 16, 24, 28, 32, 40
 
@@ -395,21 +395,24 @@
     own = comp_query[0]
     packed = lax.all_to_all(pack(hidden[0].T, kv_down, own), "x", 0, 0, tiled=True)
     layout = request_layout(ids, req_blocks, dest_slot)
-    packed, dec_query, dec_latent = lax.optimization_barrier((packed, dec_query, dec_latent))
+    rep_in = jnp.concatenate([dec_query, dec_latent], axis=2)
+
+    def rep_step(part, d):
+        met = lax.ppermute(part, "rep", [(i, i ^ d) for i in range(NREP)])
+        return jnp.concatenate([part, met])
+
+    rep_in = rep_step(rep_in, 1)
+    packed, rep_in, layout = lax.optimization_barrier((packed, rep_in, layout))
     partial, line = meet(packed, per_x, own.shape[1])
     line = jnp.concatenate([line, lax.ppermute(line, "yh", shift(2, 1))])
     cq = lax.all_gather(line, "z", axis=0, tiled=True)
 
+    ready = prepare_decode(layout, rep_step(rep_in, 2), q_up, kv_up, cos_part, sin_part)
     pieces = lax.all_to_all(partial, ("yh", "z"), 0, 0, tiled=True)
+    pieces, ready = lax.optimization_barrier((pieces, ready))
     copies = norm_rows(layout, pieces, kv_gain[None, :], cos_part, sin_part)
     cache = lax.all_to_all(copies, ("yh", "z"), 0, 0, tiled=True).reshape(per_x, -1)
 
-    rep_in = jnp.concatenate([dec_query, dec_latent], axis=2)
-    for d in (1, 2):
-        met = lax.ppermute(rep_in, "rep", [(i, i ^ d) for i in range(NREP)])
-        rep_in = jnp.concatenate([rep_in, met])
-    ready = prepare_decode(layout, rep_in, q_up, kv_up, cos_part, sin_part)
-    cache, ready = lax.optimization_barrier((cache, ready))
     cache = spread(cache, "x", NX).reshape(rows, -1)
 
     queries = project_queries(layout, cq.reshape(8, 8, PAD, -1), q_up, cos_part, sin_part)

time: 140 us -> 143 us (1.021)
  starting transfers between devices: 45.8 us -> 39.4 us
  blocking collectives: 19.2 us -> 23.6 us
  waiting for transfers between devices: 31.8 us -> 35 us
    all_to_all x1, waiting for transfers between devices: 11 us -> 0.01 us  [body(): pieces = lax.all_to_all(partial, ('yh', 'z'), 0, 0, tiled=True)]
    all_to_all x1, waiting for transfers between devices: 0.01 us -> 8.77 us  [body(): lax.all_to_all(pack(hidden[0].T, kv_down, own), 'x', 0, 0, tiled=True)]
    ppermute x2, waiting for transfers between devices: 8.23 us -> 14.5 us  [rep_step(): met = lax.ppermute(part, 'rep', [(i, i ^ d) for i in range(NREP)])]
    all_to_all x1, starting transfers between devices: 10.2 us -> 4.42 us  [body(): lax.all_to_all(pack(hidden[0].T, kv_down, own), 'x', 0, 0, tiled=True)]
    all_to_all x1, blocking collectives: 19.2 us -> 23.6 us  [body(): lax.all_to_all(copies, ('yh', 'z'), 0, 0, tiled=True).reshape(per_x, -1)]
    all_gather x1, waiting for transfers between devices: 8.03 us -> 6.54 us  [body(): cq = lax.all_gather(line, 'z', axis=0, tiled=True)]
  transfers between devices with their start and end apart: 8 -> 8, of which waited for: 4 -> 5; matrix products, arithmetic and copies ran while one was open for 2% -> 3% of each run, Pallas kernels for 12% -> 12%
where the time goes in v12:
time: 143 us; the launch traced here: 141 us
  starting transfers between devices  39.4 us (28%)
  waiting for transfers between devices  35 us (24%)
  blocking collectives  23.6 us (17%)
  Pallas kernels  23.5 us (16%)
  between operations  14.2 us (10%)
  local copies, waits for them, and re-layouts  2.71 us (2%)
  other arithmetic  2.57 us (2%)
    all_to_all x1, blocking collectives, body(): lax.all_to_all(copies, ('yh', 'z'), 0, 0, tiled=True).reshape(per_x, -1)  23.6 us
    all_to_all x1, starting transfers between devices, body(): pieces = lax.all_to_all(partial, ('yh', 'z'), 0, 0, tiled=True)  15.8 us
    ppermute x2, waiting for transfers between devices, rep_step(): met = lax.ppermute(part, 'rep', [(i, i ^ d) for i in range(NREP)])  14.5 us
    all_to_all x1, waiting for transfers between devices, body(): lax.all_to_all(pack(hidden[0].T, kv_down, own), 'x', 0, 0, tiled=True)  8.77 us
    all_gather x1, waiting for transfers between devices, body(): cq = lax.all_gather(line, 'z', axis=0, tiled=True)  6.54 us
    pallas_call x1, Pallas kernels, prefill(): pl.pallas_call(prefill_kernel, in_specs=[SMEM] + [VMEM] * 3, out_specs=VM...  5.9 us
    pallas_call x1, Pallas kernels, project_queries(): pl.pallas_call(query_kernel, grid_spec=pltpu.PrefetchScalarGridSpec(num_s...  5.79 us
    ppermute x2, starting transfers between devices, rep_step(): met = lax.ppermute(part, 'rep', [(i, i ^ d) for i in range(NREP)])  5.5 us
  transfers between devices with their start and end apart: 8, of which 5 were waited for; matrix products, arithmetic and copies ran while one was open for 3% of the time, Pallas kernels for 12%

profile of v12, /device:TPU:56, one launch (start us, length us, event | category | flops | bytes accessed | tf_op | source)
XLA Modules:
  0.0 140.9 jit_solution(3818253223523769536)
XLA Ops:
  7.2 2.1 %pack_hidden.1 = bf16[4,112,1088]{2,1,0:T(8,128)(2,1)} custom-call(bf16[112,1024]{1,0:T(8,128)(2,1)} %bitcast.17, bf16[112,576]{1,0:T(8,128)(2,1)} %down_ref.1, bf16[16,1536]{1,0:T(8,128)(2,1)} %bitcast.18), custom_call_target="tpu_custom_call" | custom-call | bytes 1500000 | tf_op jit(solution)/shard_map/pack_hidden/pallas_call | solution.py:123
  9.2 4.4 %all-to-all-start = ((bf16[4,112,1088]{2,1,0:T(8,128)(2,1)}), bf16[4,112,1088]{2,1,0:T(8,128)(2,1)S(1)}, u32[]{:S(2)}, u32[]{:S(2)}) async-start(bf16[4,112,1088]{2,1,0:T(8,128)(2,1)} %pack_hidden.1), calls=%async_computation | async-start | bytes 2064384 | tf_op jit(solution)/shard_map/all_to_all | solution.py:396
  13.7 0.0 copy-done.9
  13.7 0.0 copy-done.10
  13.7 3.3 %collective-permute-start = (bf16[3,4,2112]{2,1,0:T(4,128)(2,1)S(1)}, bf16[3,4,2112]{2,1,0:T(4,128)(2,1)S(1)}, u32[]{:S(2)}, u32[]{:S(2)}) collective-permute-start(bf16[3,4,2112]{2,1,0:T(4,128)(2,1)S(1)} %constant_dynamic-update-slice_fusion), channel_id=1, source_target_pairs={{0,1},{1,0},{2,3},{3,2},{4,5},{5,4},{6,7},{7,6},{8,9},{9,8},{10,11... | collective-permute-start | bytes 152072 | tf_op jit(solution)/shard_map/ppermute | solution.py:401
  17.0 0.7 pad_add_fusion.ids_ref
  17.6 1.3 request_layout.1.layout_ref
  19.0 0.8 collective-permute-done
  19.7 0.1 pad_maximum_fusion.2
  19.8 8.8 %all-to-all-done.packed_ref = bf16[4,112,1088]{2,1,0:T(8,128)(2,1)S(1)} async-done(((bf16[4,112,1088]{2,1,0:T(8,128)(2,1)}), bf16[4,112,1088]{2,1,0:T(8,128)(2,1)S(1)}, u32[]{:S(2)}, u32[]{:S(2)}) %all-to-all-start) | async-done | bytes 974880 | tf_op jit(solution)/shard_map/all_to_all | solution.py:396
  28.6 1.2 partial_and_rows.1
  29.8 4.7 %collective-permute-start.2 = (bf16[64,1536]{1,0:T(8,128)(2,1)S(1)}, bf16[64,1536]{1,0:T(8,128)(2,1)}, u32[]{:S(2)}, u32[]{:S(2)}) collective-permute-start(bf16[64,1536]{1,0:T(8,128)(2,1)S(1)} %get-tuple-element.19), channel_id=1, source_target_pairs={{0,128},{128,0},{1,129},{129,1},{2,130},{130,2},{3,131},{131,3},{4... | collective-permute-start | bytes 589832 | tf_op jit(solution)/shard_map/ppermute | solution.py:407
  34.5 0.0 copy-start
  34.5 0.0 copy-start.1
  34.5 0.0 copy-start.2
  34.6 0.0 copy-start.3
  34.6 0.0 copy-start.5
  34.6 15.8 %all-to-all-start.1 = ((f32[16,16,576]{2,1,0:T(8,128)}), f32[16,16,576]{2,1,0:T(8,128)S(1)}, u32[]{:S(2)}, u32[]{:S(2)}) async-start(f32[16,16,576]{2,1,0:T(8,128)} %get-tuple-element.15), calls=%async_computation.1 | async-start | bytes 1310720 | tf_op jit(solution)/shard_map/all_to_all | solution.py:411
  50.4 0.0 all-gather.2.cloned.1.call-start
  50.5 0.0 collective-permute-done.2
  50.5 1.7 %pad_maximum_fusion = bf16[128,1536]{1,0:T(8,128)(2,1)} fusion(bf16[64,1536]{1,0:T(8,128)(2,1)} %collective-permute-done.2, bf16[64,1536]{1,0:T(8,128)(2,1)S(1)} %get-tuple-element.19), kind=kLoop, calls=%fused_computation | loop fusion | flops 786432 | bytes 786432 | tf_op jit(solution)/shard_map/concatenate | solution.py:407
  52.2 0.0 all-gather.2.cloned.1.call-update
  52.2 2.2 %collective-permute-start.1 = (bf16[6,4,2112]{2,1,0:T(4,128)(2,1)S(1)}, bf16[6,4,2112]{2,1,0:T(4,128)(2,1)S(1)}, u32[]{:S(2)}, u32[]{:S(2)}) collective-permute-start(bf16[6,4,2112]{2,1,0:T(4,128)(2,1)S(1)} %pad_maximum_fusion.2), channel_id=1, source_target_pairs={{0,2},{1,3},{2,0},{3,1},{4,6},{5,7},{6,4},{7,5},{8,10},{9,11},{10,... | collective-permute-start | bytes 304136 | tf_op jit(solution)/shard_map/ppermute | solution.py:401
  54.5 13.7 %collective-permute-done.1 = bf16[6,4,2112]{2,1,0:T(4,128)(2,1)S(1)} collective-permute-done((bf16[6,4,2112]{2,1,0:T(4,128)(2,1)S(1)}, bf16[6,4,2112]{2,1,0:T(4,128)(2,1)S(1)}, u32[]{:S(2)}, u32[]{:S(2)}) %collective-permute-start.1) | collective-permute-done | bytes 101408 | tf_op jit(solution)/shard_map/ppermute | solution.py:401
  68.2 0.1 pad_maximum_fusion.1.rows_ref
  68.3 0.0 copy-done
  68.4 0.0 copy-done.1
  68.4 0.0 copy-done.2
  68.4 0.0 copy-done.3
  68.4 0.0 copy-done.5
  68.4 1.1 prepare_decode.1.ready_ref
  69.5 0.0 all-to-all-done.1.pieces_ref
  69.5 0.9 copy-done.7
  70.3 2.2 %norm_rows.1 = bf16[16,16,640]{2,1,0:T(8,128)(2,1)} custom-call(s32[64]{0:T(128)} %request_layout.1.layout_ref, f32[16,16,576]{2,1,0:T(8,128)} %copy-done.7, f32[1,512]{1,0:T(1,128)} %bitcast.19, f32[640,128]{1,0:T(8,128)} %constant.24.clone.cos_ref, f32[640,128]{1,0:T(8,128)} %constant.25.clone.sin_ref), custom_call_target="tpu_custom_call" | custom-call | flops 35000000512 | bytes 1000000 | tf_op jit(solution)/shard_map/norm_rows/pallas_call | solution.py:178
  72.5 23.6 %all_to_all.25 = bf16[16,16,640]{2,1,0:T(8,128)(2,1)S(1)} all-to-all(bf16[16,16,640]{2,1,0:T(8,128)(2,1)} %norm_rows.1), channel_id=1, replica_groups=mesh['section'=2,'yh'=2,'x'=4,'z'=8,'rep'=4] {'yh','z'}, dimensions={0} | all-to-all | bytes 655360 | tf_op jit(solution)/shard_map/all_to_all | solution.py:414
  96.1 1.2 broadcast_in_dim.15
  97.2 3.5 %all-to-all-start.3 = ((bf16[4,256,640]{2,1,0:T(8,128)(2,1)}), bf16[4,256,640]{2,1,0:T(8,128)(2,1)S(1)}, u32[]{:S(2)}, u32[]{:S(2)}) async-start(bf16[4,256,640]{2,1,0:T(8,128)(2,1)} %broadcast_in_dim.15), calls=%async_computation.3 | async-start | bytes 2621440 | tf_op jit(solution)/shard_map/all_to_all | solution.py:56
  100.8 6.5 %all-gather.2.cloned.1.call-done = bf16[1024,1536]{1,0:T(8,128)(2,1)} async-done(((bf16[128,1536]{1,0:T(8,128)(2,1)}), bf16[1024,1536]{1,0:T(8,128)(2,1)}) %all-gather.2.cloned.1.call-update) | async-done | bytes 3145744 | tf_op jit(solution)/shard_map/all_gather | solution.py:408
  107.3 5.8 %project_queries.1.q_ref = bf16[2,1024,256]{2,1,0:T(8,128)(2,1)} custom-call(s32[64]{0:T(128)} %request_layout.1.layout_ref, bf16[8,8,16,1536]{3,2,1,0:T(8,128)(2,1)} %bitcast.15, bf16[1536,384]{1,0:T(8,128)(2,1)} %w_ref.3, f32[640,128]{1,0:T(8,128)} %constant.24.clone.cos_ref, f32[640,128]{1,0:T(8,128)} %constant.25.clone.sin_ref), custom_call_target="tpu_custom_call" | custom-call | flops 1200000000 | bytes 5000000 | tf_op jit(solution)/shard_map/project_queries/pallas_call | solution.py:209
  113.1 5.1 %all-to-all-done.3 = bf16[4,256,640]{2,1,0:T(8,128)(2,1)S(1)} async-done(((bf16[4,256,640]{2,1,0:T(8,128)(2,1)}), bf16[4,256,640]{2,1,0:T(8,128)(2,1)S(1)}, u32[]{:S(2)}, u32[]{:S(2)}) %all-to-all-start.3) | async-done | bytes 1310752 | tf_op jit(solution)/shard_map/all_to_all | solution.py:56
  118.3 0.0 copy-done.6
  118.3 2.5 %decode_attention.1 = bf16[4,16,256]{2,1,0:T(8,128)(2,1)} custom-call(s32[64]{0:T(128)S(1)} %copy-done.6, bf16[48,640]{1,0:T(8,128)(2,1)S(1)} %prepare_decode.1.ready_ref, bf16[1024,640]{1,0:T(8,128)(2,1)S(1)} %bitcast.13, bf16[512,512]{1,0:T(8,128)(2,1)S(1)} %copy-done.1), custom_call_target="tpu_custom_call" | custom-call | flops 100000000 | bytes 2000000 | tf_op jit(solution)/shard_map/decode_attention/pallas_call | solution.py:311
  120.7 5.4 %all-to-all-start.4 = ((bf16[4,16,256]{2,1,0:T(8,128)(2,1)}), bf16[4,16,256]{2,1,0:T(8,128)(2,1)S(1)}, u32[]{:S(2)}, u32[]{:S(2)}) async-start(bf16[4,16,256]{2,1,0:T(8,128)(2,1)} %decode_attention.1), calls=%async_computation.4 | async-start | bytes 65536 | tf_op jit(solution)/shard_map/all_to_all | solution.py:421
  126.1 0.0 copy-done.4
  126.1 5.9 %prefill_attention.1 = bf16[1024,256]{1,0:T(8,128)(2,1)} custom-call(s32[64]{0:T(128)S(1)} %copy-done.6, bf16[2,1024,256]{2,1,0:T(8,128)(2,1)S(1)} %copy-done.4, bf16[1024,640]{1,0:T(8,128)(2,1)S(1)} %bitcast.14, bf16[512,512]{1,0:T(8,128)(2,1)S(1)} %copy-done.1), custom_call_target="tpu_custom_call" | custom-call | flops 1500000000 | bytes 4000000 | tf_op jit(solution)/shard_map/prefill_attention/pallas_call | solution.py:372
  132.0 0.0 all-to-all-done.4.pool_ref
  132.0 0.6 copy-done.8
  132.6 1.5 %select_slots.1 = bf16[3,4,256]{2,1,0:T(4,128)(2,1)} custom-call(s32[64]{0:T(128)} %request_layout.1.layout_ref, bf16[4,16,256]{2,1,0:T(8,128)(2,1)} %copy-done.8), custom_call_target="tpu_custom_call" | custom-call | flops 1000000 | bytes 50000 | tf_op jit(solution)/shard_map/select_slots/pallas_call | solution.py:332
  (8 shorter events, 0.0 us)
Async XLA Ops:
  9.2 4.4 %copy-start.9 = (bf16[3,4,1536]{2,1,0:T(4,128)(2,1)S(1)}, bf16[3,4,1536]{2,1,0:T(4,128)(2,1)}, u32[]{:S(2)}) copy-start(bf16[3,4,1536]{2,1,0:T(4,128)(2,1)} %param.20) | copy-start | bytes 110596
  9.2 4.5 %copy-start.10 = (bf16[3,4,576]{2,1,0:T(4,128)(2,1)S(1)}, bf16[3,4,576]{2,1,0:T(4,128)(2,1)}, u32[]{:S(2)}) copy-start(bf16[3,4,576]{2,1,0:T(4,128)(2,1)} %param.21) | copy-start | bytes 41476
  9.2 19.3 %all-to-all-start = ((bf16[4,112,1088]{2,1,0:T(8,128)(2,1)}), bf16[4,112,1088]{2,1,0:T(8,128)(2,1)S(1)}, u32[]{:S(2)}, u32[]{:S(2)}) async-start(bf16[4,112,1088]{2,1,0:T(8,128)(2,1)} %pack_hidden.1), calls=%async_computation | async-start | bytes 2064384 | tf_op jit(solution)/shard_map/all_to_all | solution.py:396
  13.7 6.0 %collective-permute-start = (bf16[3,4,2112]{2,1,0:T(4,128)(2,1)S(1)}, bf16[3,4,2112]{2,1,0:T(4,128)(2,1)S(1)}, u32[]{:S(2)}, u32[]{:S(2)}) collective-permute-start(bf16[3,4,2112]{2,1,0:T(4,128)(2,1)S(1)} %constant_dynamic-update-slice_fusion), channel_id=1, source_target_pairs={{0,1},{1,0},{2,3},{3,2},{4,5},{5,4},{6,7},{7,6},{8,9},{9,8},{10,11... | collective-permute-start | bytes 152072 | tf_op jit(solution)/shard_map/ppermute | solution.py:401
  29.8 20.7 %collective-permute-start.2 = (bf16[64,1536]{1,0:T(8,128)(2,1)S(1)}, bf16[64,1536]{1,0:T(8,128)(2,1)}, u32[]{:S(2)}, u32[]{:S(2)}) collective-permute-start(bf16[64,1536]{1,0:T(8,128)(2,1)S(1)} %get-tuple-element.19), channel_id=1, source_target_pairs={{0,128},{128,0},{1,129},{129,1},{2,130},{130,2},{3,131},{131,3},{4... | collective-permute-start | bytes 589832 | tf_op jit(solution)/shard_map/ppermute | solution.py:407
  34.5 33.8 %copy-start = (bf16[1536,384]{1,0:T(8,128)(2,1)S(1)}, bf16[1536,384]{1,0:T(8,128)(2,1)}, u32[]{:S(2)}) copy-start(bf16[1536,384]{1,0:T(8,128)(2,1)} %w_ref.3) | copy-start | bytes 3538948
  34.5 33.8 %copy-start.1 = (bf16[512,512]{1,0:T(8,128)(2,1)S(1)}, bf16[512,512]{1,0:T(8,128)(2,1)}, u32[]{:S(2)}) copy-start(bf16[512,512]{1,0:T(8,128)(2,1)} %kv_ref.5) | copy-start | bytes 1572868
  34.5 33.8 %copy-start.2 = (f32[640,128]{1,0:T(8,128)S(1)}, f32[640,128]{1,0:T(8,128)}, u32[]{:S(2)}) copy-start(f32[640,128]{1,0:T(8,128)} %constant.25.clone.sin_ref) | copy-start | bytes 983044
  34.6 33.8 %copy-start.3 = (f32[640,128]{1,0:T(8,128)S(1)}, f32[640,128]{1,0:T(8,128)}, u32[]{:S(2)}) copy-start(f32[640,128]{1,0:T(8,128)} %constant.24.clone.cos_ref) | copy-start | bytes 983044
  34.6 33.8 %copy-start.5 = (s32[64]{0:T(128)S(1)}, s32[64]{0:T(128)}, u32[]{:S(2)}) copy-start(s32[64]{0:T(128)} %request_layout.1.layout_ref) | copy-start | bytes 772
  34.6 34.9 %all-to-all-start.1 = ((f32[16,16,576]{2,1,0:T(8,128)}), f32[16,16,576]{2,1,0:T(8,128)S(1)}, u32[]{:S(2)}, u32[]{:S(2)}) async-start(f32[16,16,576]{2,1,0:T(8,128)} %get-tuple-element.15), calls=%async_computation.1 | async-start | bytes 1310720 | tf_op jit(solution)/shard_map/all_to_all | solution.py:411
  50.4 56.9 %all-gather.2.cloned.1.call-start = ((), (), s32[]{:S(2)}) async-start(), calls=%async_computation.5 | async-start | bytes 3538944 | tf_op jit(solution)/shard_map/all_gather | solution.py:408
  52.2 16.0 %collective-permute-start.1 = (bf16[6,4,2112]{2,1,0:T(4,128)(2,1)S(1)}, bf16[6,4,2112]{2,1,0:T(4,128)(2,1)S(1)}, u32[]{:S(2)}, u32[]{:S(2)}) collective-permute-start(bf16[6,4,2112]{2,1,0:T(4,128)(2,1)S(1)} %pad_maximum_fusion.2), channel_id=1, source_target_pairs={{0,2},{1,3},{2,0},{3,1},{4,6},{5,7},{6,4},{7,5},{8,10},{9,11},{10,... | collective-permute-start | bytes 304136 | tf_op jit(solution)/shard_map/ppermute | solution.py:401
  69.5 0.9 copy-start.7
  97.2 21.0 %all-to-all-start.3 = ((bf16[4,256,640]{2,1,0:T(8,128)(2,1)}), bf16[4,256,640]{2,1,0:T(8,128)(2,1)S(1)}, u32[]{:S(2)}, u32[]{:S(2)}) async-start(bf16[4,256,640]{2,1,0:T(8,128)(2,1)} %broadcast_in_dim.15), calls=%async_computation.3 | async-start | bytes 2621440 | tf_op jit(solution)/shard_map/all_to_all | solution.py:56
  107.3 10.9 %copy-start.6 = (s32[64]{0:T(128)S(1)}, s32[64]{0:T(128)}, u32[]{:S(2)}) copy-start(s32[64]{0:T(128)} %request_layout.1.layout_ref) | copy-start | bytes 772
  113.1 13.0 %copy-start.4 = (bf16[2,1024,256]{2,1,0:T(8,128)(2,1)S(1)}, bf16[2,1024,256]{2,1,0:T(8,128)(2,1)}, u32[]{:S(2)}) copy-start(bf16[2,1024,256]{2,1,0:T(8,128)(2,1)} %project_queries.1.q_ref) | copy-start | bytes 3145732
  120.7 11.3 %all-to-all-start.4 = ((bf16[4,16,256]{2,1,0:T(8,128)(2,1)}), bf16[4,16,256]{2,1,0:T(8,128)(2,1)S(1)}, u32[]{:S(2)}, u32[]{:S(2)}) async-start(bf16[4,16,256]{2,1,0:T(8,128)(2,1)} %decode_attention.1), calls=%async_computation.4 | async-start | bytes 65536 | tf_op jit(solution)/shard_map/all_to_all | solution.py:421
  132.0 0.6 copy-start.8
Sparse Core Ops, SparseCore 0:
  53.9 53.3 all-gather.1

commit v13 on v10

--- a/solution.py
+++ b/solution.py
@@ -375,11 +375,13 @@
     cache = lax.all_to_all(copies, ("yh", "z"), 0, 0, tiled=True).reshape(per_x, -1)
 
     rep_in = jnp.concatenate([dec_query, dec_latent], axis=2)
-    for d in (1, 2):
-        met = lax.ppermute(rep_in, "rep", [(i, i ^ d) for i in range(NREP)])
-        rep_in = jnp.concatenate([rep_in, met])
-    ready = prepare_decode(layout, rep_in, q_up, kv_up, cos_part, sin_part)
-    cache, ready = lax.optimization_barrier((cache, ready))
+
+    def rep_step(part, d):
+        met = lax.ppermute(part, "rep", [(i, i ^ d) for i in range(NREP)])
+        return jnp.concatenate([part, met])
+
+    cache, rep_in = lax.optimization_barrier((cache, rep_step(rep_in, 1)))
+    ready = prepare_decode(layout, rep_step(rep_in, 2), q_up, kv_up, cos_part, sin_part)
     cache = spread(cache, "x", NX).reshape(rows, -1)
 
     queries = project_queries(layout, cq.reshape(8, 8, PAD, -1), q_up, cos_part, sin_part)

time: 139 us -> 137 us (0.986)
  waiting for transfers between devices: 34.8 us -> 31.1 us
    all_gather x1, waiting for transfers between devices: 8.39 us -> 0.13 us  [body(): cq = lax.all_gather(line, 'z', axis=0, tiled=True)]
    all_to_all x1, waiting for transfers between devices: 0.01 us -> 3.58 us  [body(): lax.all_to_all(copies, ('yh', 'z'), 0, 0, tiled=True).reshape(per_x, -1)]
    all_to_all x1, waiting for transfers between devices: 3.66 us -> 0.83 us  [spread(): return lax.all_to_all(copies, axes, 0, 0, tiled=True)]
    all_to_all x1, waiting for transfers between devices: 10 us -> 12.3 us  [body(): lax.all_to_all(partial.reshape(16, chunk, -1), ('yh', 'z'), 0, 0, tiled=T...]
    ppermute x2, waiting for transfers between devices: 8.28 us -> 9.84 us  [rep_step(): met = lax.ppermute(part, 'rep', [(i, i ^ d) for i in range(NREP)])]
  transfers between devices with their start and end apart: 12 -> 12, of which waited for: 7 -> 9; matrix products, arithmetic and copies ran while one was open for 3% -> 3% of each run, Pallas kernels for 12% -> 12%
where the time goes in v13:
time: 137 us; the launch traced here: 135 us
  starting transfers between devices  61.3 us (45%)
  waiting for transfers between devices  31.1 us (23%)
  Pallas kernels  22.2 us (16%)
  between operations  14.2 us (10%)
  local copies, waits for them, and re-layouts  3.66 us (3%)
  other arithmetic  1.6 us (1%)
    all_to_all x1, starting transfers between devices, body(): lax.all_to_all(partial.reshape(16, chunk, -1), ('yh', 'z'), 0, 0, tiled=T...  15.7 us
    all_to_all x1, waiting for transfers between devices, body(): lax.all_to_all(partial.reshape(16, chunk, -1), ('yh', 'z'), 0, 0, tiled=T...  12.3 us
    ppermute x3, starting transfers between devices, body(): lax.ppermute(own, 'x', shift(NX, d))  10.7 us
    all_to_all x1, starting transfers between devices, body(): lax.all_to_all(copies, ('yh', 'z'), 0, 0, tiled=True).reshape(per_x, -1)  10.5 us
    ppermute x2, waiting for transfers between devices, rep_step(): met = lax.ppermute(part, 'rep', [(i, i ^ d) for i in range(NREP)])  9.84 us
    ppermute x2, starting transfers between devices, rep_step(): met = lax.ppermute(part, 'rep', [(i, i ^ d) for i in range(NREP)])  6.15 us
    pallas_call x1, Pallas kernels, prefill(): pl.pallas_call(prefill_kernel, in_specs=[SMEM] + [VMEM] * 3, out_specs=VM...  5.91 us
    pallas_call x1, Pallas kernels, project_queries(): pl.pallas_call(query_kernel, grid_spec=pltpu.PrefetchScalarGridSpec(num_s...  5.8 us
  transfers between devices with their start and end apart: 12, of which 9 were waited for; matrix products, arithmetic and copies ran while one was open for 3% of the time, Pallas kernels for 12%

profile of v13, /device:TPU:56, one launch (start us, length us, event | category | flops | bytes accessed | tf_op | source)
XLA Modules:
  0.0 135.4 jit_solution(12350293173291983283)
XLA Ops:
  7.2 0.0 copy-start.9
  7.2 2.0 %pack_hidden.1 = bf16[4,112,832]{2,1,0:T(8,128)(2,1)} custom-call(bf16[112,1024]{1,0:T(8,128)(2,1)} %bitcast.20, bf16[112,576]{1,0:T(8,128)(2,1)} %down_ref.1), custom_call_target="tpu_custom_call" | custom-call | bytes 1200000 | tf_op jit(solution)/shard_map/pack_hidden/pallas_call | solution.py:118
  9.2 4.3 %all-to-all-start = ((bf16[4,112,832]{2,1,0:T(8,128)(2,1)}), bf16[4,112,832]{2,1,0:T(8,128)(2,1)S(1)}, u32[]{:S(2)}, u32[]{:S(2)}) async-start(bf16[4,112,832]{2,1,0:T(8,128)(2,1)} %pack_hidden.1), calls=%async_computation | async-start | bytes 1605632 | tf_op jit(solution)/shard_map/all_to_all | solution.py:362
  13.5 0.0 copy-done.9
  13.5 5.1 %collective-permute-start.2 = (bf16[16,1536]{1,0:T(8,128)(2,1)S(1)}, bf16[16,1536]{1,0:T(8,128)(2,1)S(1)}, u32[]{:S(2)}, u32[]{:S(2)}) collective-permute-start(bf16[16,1536]{1,0:T(8,128)(2,1)S(1)} %bitcast.21), channel_id=1, source_target_pairs={{0,96},{32,0},{64,32},{96,64},{1,97},{33,1},{65,33},{97,65},{2,98}... | collective-permute-start | bytes 147464 | tf_op jit(solution)/shard_map/ppermute | solution.py:364
  18.6 2.8 %collective-permute-start.1 = (bf16[16,1536]{1,0:T(8,128)(2,1)S(1)}, bf16[16,1536]{1,0:T(8,128)(2,1)S(1)}, u32[]{:S(2)}, u32[]{:S(2)}) collective-permute-start(bf16[16,1536]{1,0:T(8,128)(2,1)S(1)} %bitcast.22), channel_id=1, source_target_pairs={{0,64},{32,96},{64,0},{96,32},{1,65},{33,97},{65,1},{97,33},{2,66}... | collective-permute-start | bytes 147464 | tf_op jit(solution)/shard_map/ppermute | solution.py:364
  21.4 2.8 %collective-permute-start = (bf16[16,1536]{1,0:T(8,128)(2,1)S(1)}, bf16[16,1536]{1,0:T(8,128)(2,1)S(1)}, u32[]{:S(2)}, u32[]{:S(2)}) collective-permute-start(bf16[16,1536]{1,0:T(8,128)(2,1)S(1)} %bitcast.23), channel_id=1, source_target_pairs={{0,32},{32,64},{64,96},{96,0},{1,33},{33,65},{65,97},{97,1},{2,34}... | collective-permute-start | bytes 147464 | tf_op jit(solution)/shard_map/ppermute | solution.py:364
  24.2 1.9 %collective-permute-done.2 = bf16[16,1536]{1,0:T(8,128)(2,1)S(1)} collective-permute-done((bf16[16,1536]{1,0:T(8,128)(2,1)S(1)}, bf16[16,1536]{1,0:T(8,128)(2,1)S(1)}, u32[]{:S(2)}, u32[]{:S(2)}) %collective-permute-start.2) | collective-permute-done | bytes 49184 | tf_op jit(solution)/shard_map/ppermute | solution.py:364
  26.0 1.6 %collective-permute-done.1 = bf16[16,1536]{1,0:T(8,128)(2,1)S(1)} collective-permute-done((bf16[16,1536]{1,0:T(8,128)(2,1)S(1)}, bf16[16,1536]{1,0:T(8,128)(2,1)S(1)}, u32[]{:S(2)}, u32[]{:S(2)}) %collective-permute-start.1) | collective-permute-done | bytes 49184 | tf_op jit(solution)/shard_map/ppermute | solution.py:364
  27.6 1.0 collective-permute-done
  28.6 0.0 all-to-all-done
  28.6 4.7 %collective-permute-start.5 = (bf16[64,1536]{1,0:T(8,128)(2,1)S(1)}, bf16[64,1536]{1,0:T(8,128)(2,1)S(1)}, u32[]{:S(2)}, u32[]{:S(2)}) collective-permute-start(bf16[64,1536]{1,0:T(8,128)(2,1)S(1)} %pad_maximum_fusion.2), channel_id=1, source_target_pairs={{0,128},{128,0},{1,129},{129,1},{2,130},{130,2},{3,131},{131,3},{4... | collective-permute-start | bytes 589832 | tf_op jit(solution)/shard_map/ppermute | solution.py:366
  33.3 1.2 fusion
  34.6 15.7 %all-to-all-start.1 = ((f32[16,16,576]{2,1,0:T(8,128)}), f32[16,16,576]{2,1,0:T(8,128)S(1)}, u32[]{:S(2)}, u32[]{:S(2)}) async-start(f32[16,16,576]{2,1,0:T(8,128)} %bitcast.8), calls=%async_computation.1 | async-start | bytes 1310720 | tf_op jit(solution)/shard_map/all_to_all | solution.py:373
  50.3 0.0 all-gather.2.cloned.1.call-start
  50.3 0.0 collective-permute-done.5
  50.3 0.8 pad_maximum_fusion
  51.1 0.0 all-gather.2.cloned.1.call-update
  51.1 0.6 pad_add_fusion.ids_ref
  51.7 1.3 request_layout.1.layout_ref
  53.0 12.3 %all-to-all-done.1.pieces_ref = f32[16,16,576]{2,1,0:T(8,128)S(1)} async-done(((f32[16,16,576]{2,1,0:T(8,128)}), f32[16,16,576]{2,1,0:T(8,128)S(1)}, u32[]{:S(2)}, u32[]{:S(2)}) %all-to-all-start.1) | async-done | bytes 589856 | tf_op jit(solution)/shard_map/all_to_all | solution.py:373
  65.3 0.8 copy-done.7
  66.2 2.2 %norm_rows.1 = bf16[16,16,640]{2,1,0:T(8,128)(2,1)} custom-call(s32[64]{0:T(128)} %request_layout.1.layout_ref, f32[16,16,576]{2,1,0:T(8,128)} %copy-done.7, f32[1,512]{1,0:T(1,128)} %bitcast.25, f32[640,128]{1,0:T(8,128)} %constant.24.clone.cos_ref, f32[640,128]{1,0:T(8,128)} %constant.25.clone.sin_ref), custom_call_target="tpu_custom_call" | custom-call | flops 30000001024 | bytes 1000000 | tf_op jit(solution)/shard_map/norm_rows/pallas_call | solution.py:143
  68.3 10.5 %all-to-all-start.2 = ((bf16[16,16,640]{2,1,0:T(8,128)(2,1)}), bf16[16,16,640]{2,1,0:T(8,128)(2,1)S(1)}, u32[]{:S(2)}, u32[]{:S(2)}) async-start(bf16[16,16,640]{2,1,0:T(8,128)(2,1)} %norm_rows.1), calls=%async_computation.2 | async-start | bytes 655360 | tf_op jit(solution)/shard_map/all_to_all | solution.py:375
  78.8 0.0 copy-done.10
  78.9 0.0 copy-done.11
  78.9 4.2 %collective-permute-start.3 = (bf16[3,4,2112]{2,1,0:T(4,128)(2,1)S(1)}, bf16[3,4,2112]{2,1,0:T(4,128)(2,1)S(1)}, u32[]{:S(2)}, u32[]{:S(2)}) collective-permute-start(bf16[3,4,2112]{2,1,0:T(4,128)(2,1)S(1)} %constant_dynamic-update-slice_fusion), channel_id=1, source_target_pairs={{0,1},{1,0},{2,3},{3,2},{4,5},{5,4},{6,7},{7,6},{8,9},{9,8},{10,11... | collective-permute-start | bytes 152072 | tf_op jit(solution)/shard_map/ppermute | solution.py:380
  83.1 4.3 %collective-permute-done.3 = bf16[3,4,2112]{2,1,0:T(4,128)(2,1)S(1)} collective-permute-done((bf16[3,4,2112]{2,1,0:T(4,128)(2,1)S(1)}, bf16[3,4,2112]{2,1,0:T(4,128)(2,1)S(1)}, u32[]{:S(2)}, u32[]{:S(2)}) %collective-permute-start.3) | collective-permute-done | bytes 50720 | tf_op jit(solution)/shard_map/ppermute | solution.py:380
  87.4 0.1 pad_maximum_fusion.3
  87.5 3.6 %all-to-all-done.2 = bf16[16,16,640]{2,1,0:T(8,128)(2,1)S(1)} async-done(((bf16[16,16,640]{2,1,0:T(8,128)(2,1)}), bf16[16,16,640]{2,1,0:T(8,128)(2,1)S(1)}, u32[]{:S(2)}, u32[]{:S(2)}) %all-to-all-start.2) | async-done | bytes 327712 | tf_op jit(solution)/shard_map/all_to_all | solution.py:375
  91.1 1.2 broadcast_in_dim.13
  92.3 3.7 %all-to-all-start.3 = ((bf16[4,256,640]{2,1,0:T(8,128)(2,1)}), bf16[4,256,640]{2,1,0:T(8,128)(2,1)S(1)}, u32[]{:S(2)}, u32[]{:S(2)}) async-start(bf16[4,256,640]{2,1,0:T(8,128)(2,1)} %broadcast_in_dim.13), calls=%async_computation.3 | async-start | bytes 2621440 | tf_op jit(solution)/shard_map/all_to_all | solution.py:56
  96.0 1.9 %collective-permute-start.4 = (bf16[6,4,2112]{2,1,0:T(4,128)(2,1)S(1)}, bf16[6,4,2112]{2,1,0:T(4,128)(2,1)S(1)}, u32[]{:S(2)}, u32[]{:S(2)}) collective-permute-start(bf16[6,4,2112]{2,1,0:T(4,128)(2,1)S(1)} %pad_maximum_fusion.3), channel_id=1, source_target_pairs={{0,2},{1,3},{2,0},{3,1},{4,6},{5,7},{6,4},{7,5},{8,10},{9,11},{10,... | collective-permute-start | bytes 304136 | tf_op jit(solution)/shard_map/ppermute | solution.py:380
  97.9 5.5 %collective-permute-done.4 = bf16[6,4,2112]{2,1,0:T(4,128)(2,1)S(1)} collective-permute-done((bf16[6,4,2112]{2,1,0:T(4,128)(2,1)S(1)}, bf16[6,4,2112]{2,1,0:T(4,128)(2,1)S(1)}, u32[]{:S(2)}, u32[]{:S(2)}) %collective-permute-start.4) | collective-permute-done | bytes 101408 | tf_op jit(solution)/shard_map/ppermute | solution.py:380
  103.4 0.1 pad_maximum_fusion.1.rows_ref
  103.6 0.0 copy-done
  103.6 0.0 copy-start.3
  103.6 1.0 copy-done.3
  104.6 1.1 prepare_decode.1.ready_ref
  105.7 0.1 all-gather.2.cloned.1.call-done
  105.8 5.8 %project_queries.1.q_ref = bf16[2,1024,256]{2,1,0:T(8,128)(2,1)} custom-call(s32[64]{0:T(128)} %request_layout.1.layout_ref, bf16[8,8,16,1536]{3,2,1,0:T(8,128)(2,1)} %bitcast.18, bf16[1536,384]{1,0:T(8,128)(2,1)} %w_ref.3, f32[640,128]{1,0:T(8,128)} %constant.24.clone.cos_ref, f32[640,128]{1,0:T(8,128)} %constant.25.clone.sin_ref), custom_call_target="tpu_custom_call" | custom-call | flops 1200000000 | bytes 5000000 | tf_op jit(solution)/shard_map/project_queries/pallas_call | solution.py:174
  111.6 0.8 all-to-all-done.3
  112.4 2.5 %decode_attention.1 = bf16[4,16,256]{2,1,0:T(8,128)(2,1)} custom-call(s32[64]{0:T(128)S(1)} %copy-done.6, bf16[48,640]{1,0:T(8,128)(2,1)S(1)} %prepare_decode.1.ready_ref, bf16[1024,640]{1,0:T(8,128)(2,1)S(1)} %bitcast.15, bf16[512,512]{1,0:T(8,128)(2,1)S(1)} %copy-done.1), custom_call_target="tpu_custom_call" | custom-call | flops 100000000 | bytes 2000000 | tf_op jit(solution)/shard_map/decode_attention/pallas_call | solution.py:276
  114.9 5.6 %all-to-all-start.4 = ((bf16[4,16,256]{2,1,0:T(8,128)(2,1)}), bf16[4,16,256]{2,1,0:T(8,128)(2,1)S(1)}, u32[]{:S(2)}, u32[]{:S(2)}) async-start(bf16[4,16,256]{2,1,0:T(8,128)(2,1)} %decode_attention.1), calls=%async_computation.4 | async-start | bytes 65536 | tf_op jit(solution)/shard_map/all_to_all | solution.py:390
  120.5 5.9 %prefill_attention.1 = bf16[1024,256]{1,0:T(8,128)(2,1)} custom-call(s32[64]{0:T(128)S(1)} %copy-done.6, bf16[2,1024,256]{2,1,0:T(8,128)(2,1)S(1)} %copy-done.4, bf16[1024,640]{1,0:T(8,128)(2,1)S(1)} %bitcast.16, bf16[512,512]{1,0:T(8,128)(2,1)S(1)} %copy-done.1), custom_call_target="tpu_custom_call" | custom-call | flops 1500000000 | bytes 4000000 | tf_op jit(solution)/shard_map/prefill_attention/pallas_call | solution.py:337
  126.4 0.0 all-to-all-done.4.pool_ref
  126.4 0.6 copy-done.8
  127.0 1.5 %select_slots.1 = bf16[3,4,256]{2,1,0:T(4,128)(2,1)} custom-call(s32[64]{0:T(128)} %request_layout.1.layout_ref, bf16[4,16,256]{2,1,0:T(8,128)(2,1)} %copy-done.8), custom_call_target="tpu_custom_call" | custom-call | flops 1000000 | bytes 50000 | tf_op jit(solution)/shard_map/select_slots/pallas_call | solution.py:297
  (18 shorter events, 0.1 us)
Async XLA Ops:
  7.2 6.3 %copy-start.9 = (bf16[1,16,1536]{2,1,0:T(8,128)(2,1)S(1)}, bf16[1,16,1536]{2,1,0:T(8,128)(2,1)}, u32[]{:S(2)}) copy-start(bf16[1,16,1536]{2,1,0:T(8,128)(2,1)} %param.13) | copy-start | bytes 147460
  9.2 19.4 %all-to-all-start = ((bf16[4,112,832]{2,1,0:T(8,128)(2,1)}), bf16[4,112,832]{2,1,0:T(8,128)(2,1)S(1)}, u32[]{:S(2)}, u32[]{:S(2)}) async-start(bf16[4,112,832]{2,1,0:T(8,128)(2,1)} %pack_hidden.1), calls=%async_computation | async-start | bytes 1605632 | tf_op jit(solution)/shard_map/all_to_all | solution.py:362
  13.5 12.6 %collective-permute-start.2 = (bf16[16,1536]{1,0:T(8,128)(2,1)S(1)}, bf16[16,1536]{1,0:T(8,128)(2,1)S(1)}, u32[]{:S(2)}, u32[]{:S(2)}) collective-permute-start(bf16[16,1536]{1,0:T(8,128)(2,1)S(1)} %bitcast.21), channel_id=1, source_target_pairs={{0,96},{32,0},{64,32},{96,64},{1,97},{33,1},{65,33},{97,65},{2,98}... | collective-permute-start | bytes 147464 | tf_op jit(solution)/shard_map/ppermute | solution.py:364
  18.6 9.0 %collective-permute-start.1 = (bf16[16,1536]{1,0:T(8,128)(2,1)S(1)}, bf16[16,1536]{1,0:T(8,128)(2,1)S(1)}, u32[]{:S(2)}, u32[]{:S(2)}) collective-permute-start(bf16[16,1536]{1,0:T(8,128)(2,1)S(1)} %bitcast.22), channel_id=1, source_target_pairs={{0,64},{32,96},{64,0},{96,32},{1,65},{33,97},{65,1},{97,33},{2,66}... | collective-permute-start | bytes 147464 | tf_op jit(solution)/shard_map/ppermute | solution.py:364
  21.4 7.2 %collective-permute-start = (bf16[16,1536]{1,0:T(8,128)(2,1)S(1)}, bf16[16,1536]{1,0:T(8,128)(2,1)S(1)}, u32[]{:S(2)}, u32[]{:S(2)}) collective-permute-start(bf16[16,1536]{1,0:T(8,128)(2,1)S(1)} %bitcast.23), channel_id=1, source_target_pairs={{0,32},{32,64},{64,96},{96,0},{1,33},{33,65},{65,97},{97,1},{2,34}... | collective-permute-start | bytes 147464 | tf_op jit(solution)/shard_map/ppermute | solution.py:364
  28.6 21.7 %collective-permute-start.5 = (bf16[64,1536]{1,0:T(8,128)(2,1)S(1)}, bf16[64,1536]{1,0:T(8,128)(2,1)S(1)}, u32[]{:S(2)}, u32[]{:S(2)}) collective-permute-start(bf16[64,1536]{1,0:T(8,128)(2,1)S(1)} %pad_maximum_fusion.2), channel_id=1, source_target_pairs={{0,128},{128,0},{1,129},{129,1},{2,130},{130,2},{3,131},{131,3},{4... | collective-permute-start | bytes 589832 | tf_op jit(solution)/shard_map/ppermute | solution.py:366
  34.6 30.8 %all-to-all-start.1 = ((f32[16,16,576]{2,1,0:T(8,128)}), f32[16,16,576]{2,1,0:T(8,128)S(1)}, u32[]{:S(2)}, u32[]{:S(2)}) async-start(f32[16,16,576]{2,1,0:T(8,128)} %bitcast.8), calls=%async_computation.1 | async-start | bytes 1310720 | tf_op jit(solution)/shard_map/all_to_all | solution.py:373
  50.3 55.5 %all-gather.2.cloned.1.call-start = ((), (), s32[]{:S(2)}) async-start(), calls=%async_computation.5 | async-start | bytes 3538944 | tf_op jit(solution)/shard_map/all_gather | solution.py:367
  65.3 0.8 copy-start.7
  66.2 12.7 %copy-start.10 = (bf16[3,4,1536]{2,1,0:T(4,128)(2,1)S(1)}, bf16[3,4,1536]{2,1,0:T(4,128)(2,1)}, u32[]{:S(2)}) copy-start(bf16[3,4,1536]{2,1,0:T(4,128)(2,1)} %param.20) | copy-start | bytes 110596
  66.2 12.7 %copy-start.11 = (bf16[3,4,576]{2,1,0:T(4,128)(2,1)S(1)}, bf16[3,4,576]{2,1,0:T(4,128)(2,1)}, u32[]{:S(2)}) copy-start(bf16[3,4,576]{2,1,0:T(4,128)(2,1)} %param.21) | copy-start | bytes 41476
  68.3 22.7 %all-to-all-start.2 = ((bf16[16,16,640]{2,1,0:T(8,128)(2,1)}), bf16[16,16,640]{2,1,0:T(8,128)(2,1)S(1)}, u32[]{:S(2)}, u32[]{:S(2)}) async-start(bf16[16,16,640]{2,1,0:T(8,128)(2,1)} %norm_rows.1), calls=%async_computation.2 | async-start | bytes 655360 | tf_op jit(solution)/shard_map/all_to_all | solution.py:375
  78.9 8.5 %collective-permute-start.3 = (bf16[3,4,2112]{2,1,0:T(4,128)(2,1)S(1)}, bf16[3,4,2112]{2,1,0:T(4,128)(2,1)S(1)}, u32[]{:S(2)}, u32[]{:S(2)}) collective-permute-start(bf16[3,4,2112]{2,1,0:T(4,128)(2,1)S(1)} %constant_dynamic-update-slice_fusion), channel_id=1, source_target_pairs={{0,1},{1,0},{2,3},{3,2},{4,5},{5,4},{6,7},{7,6},{8,9},{9,8},{10,11... | collective-permute-start | bytes 152072 | tf_op jit(solution)/shard_map/ppermute | solution.py:380
  92.2 11.3 %copy-start = (bf16[1536,384]{1,0:T(8,128)(2,1)S(1)}, bf16[1536,384]{1,0:T(8,128)(2,1)}, u32[]{:S(2)}) copy-start(bf16[1536,384]{1,0:T(8,128)(2,1)} %w_ref.3) | copy-start | bytes 3538948
  92.2 11.3 %copy-start.1 = (bf16[512,512]{1,0:T(8,128)(2,1)S(1)}, bf16[512,512]{1,0:T(8,128)(2,1)}, u32[]{:S(2)}) copy-start(bf16[512,512]{1,0:T(8,128)(2,1)} %kv_ref.5) | copy-start | bytes 1572868
  92.3 11.3 %copy-start.2 = (f32[640,128]{1,0:T(8,128)S(1)}, f32[640,128]{1,0:T(8,128)}, u32[]{:S(2)}) copy-start(f32[640,128]{1,0:T(8,128)} %constant.25.clone.sin_ref) | copy-start | bytes 983044
  92.3 11.4 %copy-start.5 = (s32[64]{0:T(128)S(1)}, s32[64]{0:T(128)}, u32[]{:S(2)}) copy-start(s32[64]{0:T(128)} %request_layout.1.layout_ref) | copy-start | bytes 772
  92.3 20.1 %all-to-all-start.3 = ((bf16[4,256,640]{2,1,0:T(8,128)(2,1)}), bf16[4,256,640]{2,1,0:T(8,128)(2,1)S(1)}, u32[]{:S(2)}, u32[]{:S(2)}) async-start(bf16[4,256,640]{2,1,0:T(8,128)(2,1)} %broadcast_in_dim.13), calls=%async_computation.3 | async-start | bytes 2621440 | tf_op jit(solution)/shard_map/all_to_all | solution.py:56
  96.0 7.5 %collective-permute-start.4 = (bf16[6,4,2112]{2,1,0:T(4,128)(2,1)S(1)}, bf16[6,4,2112]{2,1,0:T(4,128)(2,1)S(1)}, u32[]{:S(2)}, u32[]{:S(2)}) collective-permute-start(bf16[6,4,2112]{2,1,0:T(4,128)(2,1)S(1)} %pad_maximum_fusion.3), channel_id=1, source_target_pairs={{0,2},{1,3},{2,0},{3,1},{4,6},{5,7},{6,4},{7,5},{8,10},{9,11},{10,... | collective-permute-start | bytes 304136 | tf_op jit(solution)/shard_map/ppermute | solution.py:380
  103.6 1.0 copy-start.3
  105.8 6.6 %copy-start.6 = (s32[64]{0:T(128)S(1)}, s32[64]{0:T(128)}, u32[]{:S(2)}) copy-start(s32[64]{0:T(128)} %request_layout.1.layout_ref) | copy-start | bytes 772
  111.6 8.9 %copy-start.4 = (bf16[2,1024,256]{2,1,0:T(8,128)(2,1)S(1)}, bf16[2,1024,256]{2,1,0:T(8,128)(2,1)}, u32[]{:S(2)}) copy-start(bf16[2,1024,256]{2,1,0:T(8,128)(2,1)} %project_queries.1.q_ref) | copy-start | bytes 3145732
  114.9 11.5 %all-to-all-start.4 = ((bf16[4,16,256]{2,1,0:T(8,128)(2,1)}), bf16[4,16,256]{2,1,0:T(8,128)(2,1)S(1)}, u32[]{:S(2)}, u32[]{:S(2)}) async-start(bf16[4,16,256]{2,1,0:T(8,128)(2,1)} %decode_attention.1), calls=%async_computation.4 | async-start | bytes 65536 | tf_op jit(solution)/shard_map/all_to_all | solution.py:390
  126.4 0.6 copy-start.8
Sparse Core Ops, SparseCore 0:
  53.7 51.9 all-gather.1
